TPU v7x, 512 devices: a whole 4x4x16 slice. The times are simulated.
512 devices in a mesh: cfg: 2 (over core), band: 16 (over z_hi, x), seq: 16 (over y, z_lo).
Axes of the slice: x: 4, y: 4, z: 16 (z_hi: 4, z_lo: 4; z = z_hi * 4 + z_lo), core: 2. Of those that a mesh axis runs over, the one named last changes fastest.
Arguments:
- query: bfloat16 [2, 8192, 4096], P('cfg', 'seq', 'band'), may hold values from -8 to 8
- keys: bfloat16 [2, 8192, 4096], P('cfg', 'seq', 'band'), may hold values from -8 to 8
- values: bfloat16 [2, 8192, 4096], P('cfg', 'seq', 'band'), may hold values from -6 to 6
- lengths: int32 [1], replicated, may hold values from 6144 to 8192
- timestep: int32 [1], replicated, may hold values from 0 to 49
- latent: float32 [16, 32, 64, 16], P('seq', 'band'), may hold values from -6 to 6
- head_weight: bfloat16 [4096, 64], replicated, may hold values from -0.59765625 to 0.59765625
- conv_weight: bfloat16 [3, 3, 3, 16, 384], replicated, may hold values from -0.3125 to 0.3125
- conv_bias: float32 [384], replicated, may hold values from -4 to 4
- gain: float32 [384], replicated, may hold values from 0.1 to 1.9
Outputs:
- velocity: float32 [16, 32, 64, 16], P('seq', 'band', 'cfg')
- decoded: bfloat16 [16, 32, 64, 384], P('seq', 'band', 'cfg')
All inputs are finite; a program needn't handle non-finite values.
Results may differ from a plain program's by a relative error of at most 0.017.
Values may be sent and summed in bfloat16 or wider, within the bound.
No kernel may reach another device: no remote copies, remote signals or barrier semaphores. Data moves between devices by JAX's collectives and lax.ppermute only.
A program may use at most 64 MiB of HBM per device.

v0:
```python
import math

import jax
import jax.numpy as jnp
from jax import lax
from jax.sharding import PartitionSpec as P

DH = 128
STEPS = 50


GUIDE = 5.0
SHIFT_FACTOR = 5.0
NEG_FILL = -1e30
EPSILON = 1e-06


def swapped(value, axis, distance):
    mask = 2**distance
    pairs = [(source, source ^ mask) for source in range(lax.axis_size(axis))]
    return lax.ppermute(value, axis, pairs)


def from_behind(value, axis, steps):
    count = lax.axis_size(axis)
    first, last = (max(0, -steps), min(count, count - steps))
    return lax.ppermute(value, axis, [(source, source + steps) for source in range(first, last)])


def padded_2(block, sides, width):
    for axis, dim in sides:
        count = lax.axis_size(axis)
        forward = [(i, i + 1) for i in range(count - 1)]
        backward = [(target, source) for source, target in forward]
        low = lax.ppermute(
            lax.slice_in_dim(block, block.shape[dim] - width, None, axis=dim), axis, forward
        )
        high = lax.ppermute(lax.slice_in_dim(block, 0, width, axis=dim), axis, backward)
        block = jnp.concatenate([low, block, high], axis=dim)
    return block


def noise_level(timestep, total_steps):
    frac = 1.0 - timestep.astype(jnp.float32) / total_steps
    return SHIFT_FACTOR * frac / (1.0 + (SHIFT_FACTOR - 1.0) * frac)


def decode_cells(window, frames, conv_weight, conv_bias, gain):
    rows = window.shape[1] - 2
    cols = window.shape[2] - 2
    chans = window.shape[3]
    slices = [
        window[a : a + frames, b : b + rows, c : c + cols, :]
        for a in range(3)
        for b in range(3)
        for c in range(3)
    ]
    patches = jnp.concatenate(slices, 3).reshape(-1, 27 * chans)
    features = (
        jnp.dot(patches, conv_weight.reshape(27 * chans, -1), preferred_element_type=jnp.float32)
        + conv_bias
    )
    scaled = (
        features * lax.rsqrt(jnp.mean(features * features, axis=1, keepdims=True) + EPSILON) * gain
    )
    return jax.nn.silu(scaled).astype(jnp.bfloat16).reshape(frames, rows, cols, -1)


def unpatch(values_grid, channels):
    frames, rows, cols = (values_grid.shape[0], values_grid.shape[1], values_grid.shape[2])
    split = values_grid.reshape(frames, rows, cols, 2, 2, channels).transpose(0, 1, 3, 2, 4, 5)
    return split.reshape(frames, 2 * rows, 2 * cols, channels)


def make_folder(query_heads, length):
    groups = query_heads.shape[1]

    def fold_keys(carry, piece, start):
        key_piece = piece[0].reshape(-1, groups, DH)
        value_piece = piece[1].reshape(-1, groups, DH)
        count = key_piece.shape[0]
        block = math.gcd(count, 512)
        nblocks = count // block
        places = lax.broadcasted_iota(jnp.int32, (count,), 0)
        key_blocks = key_piece.reshape(nblocks, block, groups, DH)
        value_blocks = value_piece.reshape(nblocks, block, groups, DH)
        place_blocks = places.reshape(nblocks, block)

        def add_block(state, item):
            top, denom, accum = state
            key_blk, value_blk, place_blk = item
            scores = jnp.einsum(
                "qhd,khd->hqk", query_heads, key_blk, preferred_element_type=jnp.float32
            ) / math.sqrt(DH)
            valid = (place_blk < length)[None, None, :]
            scores = jnp.where(valid, scores, NEG_FILL)
            new_top = jnp.maximum(top, jnp.max(scores, axis=2))
            weights = jnp.where(valid, jnp.exp(scores - new_top[:, :, None]), 0.0)
            factor = jnp.exp(top - new_top)
            denom = denom * factor + jnp.sum(weights, axis=2)
            mixed = jnp.einsum(
                "hqk,khd->qhd",
                weights.astype(jnp.bfloat16),
                value_blk,
                preferred_element_type=jnp.float32,
            )
            accum = accum * jnp.transpose(factor)[:, :, None] + mixed
            return ((new_top, denom, accum), None)

        result, _ = lax.scan(add_block, carry, (key_blocks, value_blocks, place_blocks))
        return result

    return fold_keys


def start_state(rows, groups):
    return (
        jnp.full((groups, rows), NEG_FILL, jnp.float32),
        jnp.zeros((groups, rows), jnp.float32),
        jnp.zeros((rows, groups, DH), jnp.float32),
    )


def finish(state, rows, groups):
    top, denom, accum = state
    return (
        (accum / jnp.transpose(denom)[:, :, None]).astype(jnp.bfloat16).reshape(rows, groups * DH)
    )


def local(
    query, keys, values, lengths, timestep, latent, head_weight, conv_weight, conv_bias, gain
):
    tok = query.shape[1]
    width = query.shape[2]
    groups = width // DH
    length = lengths[0]
    query_rows = query.reshape(tok, width)
    key_rows = keys.reshape(tok, width)
    value_rows = values.reshape(tok, width)
    folder = make_folder(query_rows.reshape(tok, groups, DH), length)
    state = folder(
        start_state(tok, groups),
        (
            lax.all_gather(key_rows, "seq", axis=0, tiled=True),
            lax.all_gather(value_rows, "seq", axis=0, tiled=True),
        ),
        jnp.int32(0),
    )
    attention = finish(state, tok, groups)
    gathered = lax.all_to_all(attention, "band", split_axis=0, concat_axis=1, tiled=True)
    prediction = jnp.dot(gathered, head_weight, preferred_element_type=jnp.float32)
    frames, lrows, cols, channels = latent.shape
    trows = lrows // 2
    tcols = cols // 2
    cfg_index = lax.axis_index("cfg")
    sigma = noise_level(timestep[0], STEPS)
    other = swapped(prediction, "cfg", 0)
    guided = jnp.where(cfg_index == 0, prediction, other)
    plain = jnp.where(cfg_index == 0, other, prediction)
    combined = plain + GUIDE * (guided - plain)
    velocity_full = unpatch(combined.reshape(frames, trows, tcols, 4 * channels), channels)
    velocity = lax.dynamic_slice_in_dim(velocity_full, cfg_index * tcols, tcols, 2)
    current = (latent - sigma * velocity_full).astype(jnp.bfloat16)
    history = [current]
    for lag in range(2):
        history = [from_behind(history[0], "seq", 1)] + history
    stacked = jnp.concatenate(history, 0)
    rimmed = padded_2(stacked, (("band", 1),), 1)
    padded = jnp.pad(rimmed, ((0, 0), (0, 0), (1, 1), (0, 0)))
    window = lax.dynamic_slice_in_dim(padded, cfg_index * tcols, tcols + 2, 2)
    decoded = decode_cells(window, frames, conv_weight, conv_bias, gain)
    return (velocity, decoded)


def solution(mesh):
    placed = (
        P("cfg", "seq", "band"),
        P("cfg", "seq", "band"),
        P("cfg", "seq", "band"),
        P(),
        P(),
        P("seq", "band", None, None),
        P(),
        P(),
        P(),
        P(),
    )
    return jax.shard_map(
        local,
        mesh=mesh,
        in_specs=placed,
        out_specs=(P("seq", "band", "cfg", None), P("seq", "band", "cfg", None)),
        check_vma=False,
    )
```

profile of v0, /device:TPU:30, one launch (start us, length us, event | category | flops | bytes accessed | tf_op | source)
XLA Modules:
  0.0 407.2 jit_solution(17374939292168967106)
XLA Ops:
  8.7 1.1 copy.46
  10.0 109.5 %all-gather.5.cloned.1.call-done = bf16[1,8192,256]{2,1,0:T(8,128)(2,1)} async-done(((bf16[1,512,256]{2,1,0:T(8,128)(2,1)}), bf16[1,8192,256]{2,1,0:T(8,128)(2,1)}) %all-gather.5.cloned.1.call-update) | async-done | bytes 4194320 | tf_op jit(solution)/shard_map/all_gather | solution.py:145
  119.5 6.9 %reshape.91 = bf16[16,512,2,128]{3,2,1,0:T(2,128)(2,1)} reshape(bf16[1,8192,256]{2,1,0:T(8,128)(2,1)} %all-gather.5.cloned.1.call-done) | data formatting | bytes 8388608 | tf_op jit(solution)/shard_map/reshape;reshape | solution.py:85
  126.4 99.6 %all-gather.7.cloned.1.call-done = bf16[1,8192,256]{2,1,0:T(8,128)(2,1)} async-done(((bf16[1,512,256]{2,1,0:T(8,128)(2,1)}), bf16[1,8192,256]{2,1,0:T(8,128)(2,1)}) %all-gather.7.cloned.1.call-update) | async-done | bytes 4194320 | tf_op jit(solution)/shard_map/all_gather | solution.py:146
  226.0 7.0 %reshape.92 = bf16[16,512,2,128]{3,2,1,0:T(2,128)(2,1)} reshape(bf16[1,8192,256]{2,1,0:T(8,128)(2,1)} %all-gather.7.cloned.1.call-done) | data formatting | bytes 8388608 | tf_op jit(solution)/shard_map/reshape;reshape | solution.py:86
  232.9 94.2 %while.15 = (s32[]{:T(128)}, f32[2,512]{1,0:T(2,128)S(1)}, f32[2,512]{1,0:T(2,128)S(1)}, f32[512,2,128]{0,2,1:T(8,128)}, s32[16,512]{1,0:T(8,128)S(1)}, /*index=...) while((s32[]{:T(128)}, f32[2,512]{1,0:T(2,128)S(1)}, ...), condition=%wide.region_3.4_spmd.clone, body=%wide.region_0.3_spmd.clone.sunk | while | flops 275651072 | bytes 9769093 | solution.py:110
  233.6 1.4 constant_dynamic-slice_fusion.31
  235.7 1.5 fusion.40
  238.5 1.4 constant_dynamic-slice_fusion.31
  240.6 2.6 fusion.40
  244.5 1.4 constant_dynamic-slice_fusion.31
  246.6 2.6 fusion.40
  250.4 1.4 constant_dynamic-slice_fusion.31
  252.5 2.6 fusion.40
  256.4 1.4 constant_dynamic-slice_fusion.31
  258.5 2.6 fusion.40
  262.4 1.4 constant_dynamic-slice_fusion.31
  264.4 2.6 fusion.40
  268.3 1.4 constant_dynamic-slice_fusion.31
  270.4 2.6 fusion.40
  274.3 1.4 constant_dynamic-slice_fusion.31
  276.3 2.6 fusion.40
  280.2 1.4 constant_dynamic-slice_fusion.31
  282.3 2.6 fusion.40
  286.2 1.4 constant_dynamic-slice_fusion.31
  288.2 2.6 fusion.40
  292.1 1.4 constant_dynamic-slice_fusion.31
  294.2 2.6 fusion.40
  298.1 1.4 constant_dynamic-slice_fusion.31
  300.1 2.6 fusion.40
  304.0 1.4 constant_dynamic-slice_fusion.31
  306.1 2.6 fusion.40
  310.0 1.4 constant_dynamic-slice_fusion.31
  312.0 2.6 fusion.40
  315.9 1.4 constant_dynamic-slice_fusion.31
  318.0 2.6 fusion.40
  321.9 1.4 constant_dynamic-slice_fusion.31
  324.0 2.6 fusion.40
  327.2 1.1 divide_convert_fusion
  328.6 30.6 %all_to_all.19 = bf16[16,32,256]{2,1,0:T(8,128)(2,1)S(1)} all-to-all(bf16[16,32,256]{2,1,0:T(8,128)(2,1)S(1)} %all_to_all.14), channel_id=1, replica_groups=mesh['cfg'=2,'band'=16,'seq'=16] {'band'}, dimensions={0} | all-to-all | bytes 524288 | tf_op jit(solution)/shard_map/all_to_all | solution.py:151
  359.5 1.9 collective-permute-start
  362.9 5.5 %collective-permute-start.1 = (bf16[1,2,64,16]{2,3,1,0:T(8,128)(2,1)S(1)}, bf16[1,2,64,16]{2,3,1,0:T(8,128)(2,1)S(1)}, u32[]{:S(2)}, u32[]{:S(2)}) collective-permute-start(bf16[1,2,64,16]{2,3,1,0:T(8,128)(2,1)S(1)} %subtract_convert_fusion), channel_id=1, source_target_pairs={{0,1},{1,2},{2,3},{3,4},{4,5},{5,6},{6,7},{7,8},{8,9},{9,10},{10,1... | collective-permute-start | bytes 12296 | tf_op jit(solution)/shard_map/ppermute | solution.py:27
  368.4 2.7 collective-permute-done.1
  371.1 2.8 collective-permute-start.2
  374.0 5.4 %collective-permute-done.2 = bf16[1,2,64,16]{2,3,1,0:T(8,128)(2,1)S(1)} collective-permute-done((bf16[1,2,64,16]{2,3,1,0:T(8,128)(2,1)S(1)}, bf16[1,2,64,16]{2,3,1,0:T(8,128)(2,1)S(1)}, u32[]{:S(2)}, u32[]{:S(2)}) %collective-permute-start.2) | collective-permute-done | bytes 4128 | tf_op jit(solution)/shard_map/ppermute | solution.py:27
  379.4 7.6 %collective-permute-start.3 = (bf16[3,1,64,16]{2,3,1,0:T(8,128)(2,1)S(1)}, bf16[3,1,64,16]{2,3,1,0:T(8,128)(2,1)S(1)}, u32[]{:S(2)}, u32[]{:S(2)}) collective-permute-start(bf16[3,1,64,16]{2,3,1,0:T(8,128)(2,1)S(1)} %get-tuple-element.166), channel_id=1, source_target_pairs={{0,16},{16,32},{32,48},{48,64},{64,80},{80,96},{96,112},{112,128},... | collective-permute-start | bytes 18440 | tf_op jit(solution)/shard_map/ppermute | solution.py:35
  386.9 1.9 collective-permute-start.4
  389.6 9.0 %collective-permute-done.4 = bf16[3,1,64,16]{2,3,1,0:T(8,128)(2,1)S(1)} collective-permute-done((bf16[3,1,64,16]{2,3,1,0:T(8,128)(2,1)S(1)}, bf16[3,1,64,16]{2,3,1,0:T(8,128)(2,1)S(1)}, u32[]{:S(2)}, u32[]{:S(2)}) %collective-permute-start.4) | collective-permute-done | bytes 6176 | tf_op jit(solution)/shard_map/ppermute | solution.py:38
  (156 shorter events, 36.2 us)
Async XLA Ops:
  7.2 352.1 %copy-start = (bf16[4096,64]{0,1:T(8,128)(2,1)S(1)}, bf16[4096,64]{0,1:T(8,128)(2,1)}, u32[]{:S(2)}) copy-start(bf16[4096,64]{0,1:T(8,128)(2,1)} %param.18) | copy-start | bytes 1572868
  7.2 112.3 %all-gather.5.cloned.1.call-start = ((), (), s32[]{:S(2)}) async-start(), calls=%async_computation.1 | async-start | bytes 4456448 | tf_op jit(solution)/shard_map/all_gather | solution.py:145
  7.9 218.1 %all-gather.7.cloned.1.call-start = ((), (), s32[]{:S(2)}) async-start(), calls=%async_computation.2 | async-start | bytes 4456448 | tf_op jit(solution)/shard_map/all_gather | solution.py:146
  327.2 35.7 %copy-start.2 = (f32[1,2,64,16]{2,3,1,0:T(8,128)S(1)}, f32[1,2,64,16]{2,3,1,0:T(8,128)}, u32[]{:S(2)}) copy-start(f32[1,2,64,16]{2,3,1,0:T(8,128)} %param.17) | copy-start | bytes 24580
  359.2 40.1 %copy-start.1 = (bf16[3,3,3,16,384]{4,3,2,1,0:T(8,128)(2,1)S(1)}, bf16[3,3,3,16,384]{4,3,2,1,0:T(8,128)(2,1)}, u32[]{:S(2)}) copy-start(bf16[3,3,3,16,384]{4,3,2,1,0:T(8,128)(2,1)} %param.19) | copy-start | bytes 995332
  359.2 40.1 %copy-start.3 = (f32[384]{0:T(512)S(1)}, f32[384]{0:T(512)}, u32[]{:S(2)}) copy-start(f32[384]{0:T(512)} %param.20) | copy-start | bytes 4612
  359.2 40.4 %copy-start.4 = (f32[384]{0:T(512)S(1)}, f32[384]{0:T(512)}, u32[]{:S(2)}) copy-start(f32[384]{0:T(512)} %param.21) | copy-start | bytes 4612
  359.5 3.1 collective-permute-start
  362.9 8.2 %collective-permute-start.1 = (bf16[1,2,64,16]{2,3,1,0:T(8,128)(2,1)S(1)}, bf16[1,2,64,16]{2,3,1,0:T(8,128)(2,1)S(1)}, u32[]{:S(2)}, u32[]{:S(2)}) collective-permute-start(bf16[1,2,64,16]{2,3,1,0:T(8,128)(2,1)S(1)} %subtract_convert_fusion), channel_id=1, source_target_pairs={{0,1},{1,2},{2,3},{3,4},{4,5},{5,6},{6,7},{7,8},{8,9},{9,10},{10,1... | collective-permute-start | bytes 12296 | tf_op jit(solution)/shard_map/ppermute | solution.py:27
  371.1 8.2 %collective-permute-start.2 = (bf16[1,2,64,16]{2,3,1,0:T(8,128)(2,1)S(1)}, bf16[1,2,64,16]{2,3,1,0:T(8,128)(2,1)S(1)}, u32[]{:S(2)}, u32[]{:S(2)}) collective-permute-start(bf16[1,2,64,16]{2,3,1,0:T(8,128)(2,1)S(1)} %collective-permute-done.1), channel_id=1, source_target_pairs={{0,1},{1,2},{2,3},{3,4},{4,5},{5,6},{6,7},{7,8},{8,9},{9,10},{10,1... | collective-permute-start | bytes 12296 | tf_op jit(solution)/shard_map/ppermute | solution.py:27
  379.4 10.2 %collective-permute-start.3 = (bf16[3,1,64,16]{2,3,1,0:T(8,128)(2,1)S(1)}, bf16[3,1,64,16]{2,3,1,0:T(8,128)(2,1)S(1)}, u32[]{:S(2)}, u32[]{:S(2)}) collective-permute-start(bf16[3,1,64,16]{2,3,1,0:T(8,128)(2,1)S(1)} %get-tuple-element.166), channel_id=1, source_target_pairs={{0,16},{16,32},{32,48},{48,64},{64,80},{80,96},{96,112},{112,128},... | collective-permute-start | bytes 18440 | tf_op jit(solution)/shard_map/ppermute | solution.py:35
  386.9 11.6 %collective-permute-start.4 = (bf16[3,1,64,16]{2,3,1,0:T(8,128)(2,1)S(1)}, bf16[3,1,64,16]{2,3,1,0:T(8,128)(2,1)S(1)}, u32[]{:S(2)}, u32[]{:S(2)}) collective-permute-start(bf16[3,1,64,16]{2,3,1,0:T(8,128)(2,1)S(1)} %get-tuple-element.167), channel_id=1, source_target_pairs={{16,0},{32,16},{48,32},{64,48},{80,64},{96,80},{112,96},{128,112},... | collective-permute-start | bytes 18440 | tf_op jit(solution)/shard_map/ppermute | solution.py:38
Sparse Core Ops, SparseCore 0:
  10.1 109.3 all-gather.4
  121.6 104.3 all-gather.6
where the time goes:
time: 409 us; the launch traced here: 407 us
  waiting for transfers between devices  228 us (56%)
  matrix products  48 us (12%)
  local copies, waits for them, and re-layouts  42.1 us (10%)
  blocking collectives  30.6 us (7%)
  other arithmetic  22.7 us (6%)
  starting transfers between devices  19.8 us (5%)
  between operations  15 us (4%)
    all_gather x1, waiting for transfers between devices, local(): lax.all_gather(key_rows, 'seq', axis=0, tiled=True)  110 us
    all_gather x1, waiting for transfers between devices, local(): lax.all_gather(value_rows, 'seq', axis=0, tiled=True)  99.6 us
    dot_general x16, matrix products, add_block(): jnp.einsum('hqk,khd->qhd', weights.astype(jnp.bfloat16), value_blk, prefe...  40.1 us
    all_to_all x1, blocking collectives, local(): lax.all_to_all(attention, 'band', split_axis=0, concat_axis=1, tiled=True)  30.6 us
    dynamic_slice x32, local copies, waits for them, and re-layouts, fold_keys(): lax.scan(add_block, carry, (key_blocks, value_blocks, place_blocks))  25 us
    lt x16, other arithmetic, add_block(): valid = (place_blk < length)[None, None, :]  10.8 us
    reduce_sum x16, other arithmetic, add_block(): denom = denom * factor + jnp.sum(weights, axis=2)  9.49 us
    ppermute x1, waiting for transfers between devices, padded_2(): lax.ppermute(lax.slice_in_dim(block, 0, width, axis=dim), axis, backward)  8.98 us
  transfers between devices with their start and end apart: 7, of which 6 were waited for; matrix products, arithmetic and copies ran while one was open for 2% of the time, Pallas kernels for 0%

commit v1 on v0

v1 whole, which is shorter than its diff:
```python
import math

import jax
import jax.numpy as jnp
from jax import lax
from jax.experimental import pallas as pl
from jax.experimental.pallas import tpu as pltpu
from jax.sharding import Mesh
from jax.sharding import PartitionSpec as P

DH = 128
STEPS = 50
GUIDE = 5.0
SHIFT_FACTOR = 5.0
NEG_FILL = -1e30
EPSILON = 1e-06
SIDE = 4
TOK = 512
ROWS, TCOLS = 16, 32
CUT = 24
LOG2_SCALE = math.log2(math.e) / math.sqrt(DH)

VMEM = pl.BlockSpec(memory_space=pltpu.VMEM)
SMEM = pl.BlockSpec(memory_space=pltpu.SMEM)


def noise_level(timestep, total_steps):
    frac = 1.0 - timestep.astype(jnp.float32) / total_steps
    return SHIFT_FACTOR * frac / (1.0 + (SHIFT_FACTOR - 1.0) * frac)


def ring(steps):
    return [(i, (i + steps) % SIDE) for i in range(SIDE)]


def crossed(mask):
    return [(i, i ^ mask) for i in range(SIDE)]


def moved(steps):
    count = SIDE * SIDE
    return [(i, i + steps) for i in range(count) if 0 <= i + steps < count]


def attention_kernel(count_ref, slot_ref, *refs):
    q_refs, kv_refs = refs[0:4], refs[4:8]
    lse_ref, top_ref, acc_ref = refs[8:11]
    qs, ks, vs, denom = refs[11:]
    for j in range(4):
        qs[j] = q_refs[j][...]
        ks[j] = kv_refs[j][:, : 2 * DH]
        for h in range(2):
            vs[j, h] = jnp.transpose(kv_refs[j][:, (2 + h) * DH : (3 + h) * DH])

    def query_block(j, _):
        out = slot_ref[j]
        top_ref[out] = jnp.full((2, TOK), NEG_FILL, jnp.float32)
        denom[...] = jnp.zeros((2, TOK), jnp.float32)
        acc_ref[out] = jnp.zeros((2, DH, TOK), jnp.float32)

        def update(b, masked):
            for h in range(2):
                scores = lax.dot_general(
                    ks[b, :, h * DH : (h + 1) * DH],
                    qs[j, :, h * DH : (h + 1) * DH],
                    (((1,), (1,)), ((), ())),
                    preferred_element_type=jnp.float32,
                )
                if masked:
                    valid = lax.broadcasted_iota(jnp.int32, (TOK, TOK), 0) < count_ref[b]
                    scores = jnp.where(valid, scores, NEG_FILL)
                old = top_ref[out, h : h + 1]
                new = jnp.maximum(old, jnp.max(scores, axis=0, keepdims=True))
                weights = jnp.exp2((scores - new) * LOG2_SCALE)
                if masked:
                    weights = jnp.where(valid, weights, 0.0)
                factor = jnp.exp2((old - new) * LOG2_SCALE)
                top_ref[out, h : h + 1] = new
                denom[h : h + 1] = denom[h : h + 1] * factor + jnp.sum(
                    weights, axis=0, keepdims=True
                )
                acc_ref[out, h] = acc_ref[out, h] * factor + jnp.dot(
                    vs[b, h], weights.astype(jnp.bfloat16), preferred_element_type=jnp.float32
                )

        def key_block(b, _):
            count = count_ref[b]

            @pl.when(count >= TOK)
            def _():
                update(b, False)

            @pl.when((count > 0) & (count < TOK))
            def _():
                update(b, True)

            return 0

        lax.fori_loop(0, 4, key_block, 0)
        stat = top_ref[out] * LOG2_SCALE + jnp.log2(denom[...])
        for copy in range(4):
            lse_ref[copy, out] = stat
        return 0

    lax.fori_loop(0, 4, query_block, 0)


def attend(counts, slots, queries, key_values):
    f32 = jnp.float32
    return pl.pallas_call(
        attention_kernel,
        out_shape=(
            jax.ShapeDtypeStruct((4, 4, 2, TOK), f32),
            jax.ShapeDtypeStruct((4, 2, TOK), f32),
            jax.ShapeDtypeStruct((4, 2, DH, TOK), f32),
        ),
        in_specs=[SMEM, SMEM] + [VMEM] * 8,
        out_specs=(VMEM,) * 3,
        scratch_shapes=[
            pltpu.VMEM((4, TOK, 2 * DH), jnp.bfloat16),
            pltpu.VMEM((4, TOK, 2 * DH), jnp.bfloat16),
            pltpu.VMEM((4, 2, DH, TOK), jnp.bfloat16),
            pltpu.VMEM((2, TOK), f32),
        ],
        compiler_params=pltpu.CompilerParams(vmem_limit_bytes=40 * 2**20),
    )(counts, slots, *queries, *key_values)


def project_kernel(scale_ref, lse_ref, top_ref, acc_ref, weight_ref, out_ref):
    lane = lax.broadcasted_iota(jnp.int32, (ROWS, TCOLS, 128), 2)
    blank = jnp.zeros((1, TCOLS, 128), jnp.float32)
    for j in range(4):
        stats = [lse_ref[z, j] for z in range(4)]
        peak = jnp.maximum(jnp.maximum(stats[0], stats[1]), jnp.maximum(stats[2], stats[3]))
        total = sum(jnp.exp2(stat - peak) for stat in stats)
        factor = jnp.exp2(top_ref[j] * LOG2_SCALE - peak) / total * scale_ref[0]
        mixed = jnp.concatenate(
            [(acc_ref[j, h] * factor[h : h + 1]).astype(jnp.bfloat16) for h in range(2)], 0
        )
        values = lax.dot_general(
            mixed, weight_ref[...], (((0,), (0,)), ((), ())), preferred_element_type=jnp.float32
        ).reshape(ROWS, TCOLS, 128)
        above = jnp.concatenate([blank, values[:-1]], 0)
        below = jnp.concatenate([values[1:], blank], 0)
        window = jnp.where(lane < 32, above, jnp.where(lane < 96, values, below))
        for row in range(ROWS):
            for half in range(2):
                cut = window[row, half * 8 : half * 8 + CUT]
                out_ref[half * 4 + row % 4, row // 4 * 4 + j] = cut.astype(jnp.bfloat16)


def project(scale, lse, top, acc, weight):
    return pl.pallas_call(
        project_kernel,
        out_shape=jax.ShapeDtypeStruct((8, 16, CUT, 128), jnp.bfloat16),
        in_specs=[SMEM] + [VMEM] * 4,
        out_specs=VMEM,
        compiler_params=pltpu.CompilerParams(vmem_limit_bytes=32 * 2**20),
    )(scale, lse, top, acc, weight)


def decode_kernel(half_ref, own_ref, last_ref, older_ref, even_ref, odd_ref, bias_ref, gain_ref, out_ref):
    left = half_ref[0] == 0
    blank = jnp.zeros((1, 128), jnp.float32)
    even, odd = [], []
    for ref in (older_ref, last_ref, own_ref):
        block = ref[...].astype(jnp.float32)
        here = jnp.where(left, block[0:16], block[8:24])
        before = jnp.where(left, jnp.concatenate([blank, block[0:15]], 0), block[7:23])
        after = jnp.where(left, block[1:17], jnp.concatenate([block[9:24], blank], 0))
        rows = [
            jnp.concatenate([x, pltpu.roll(x, 96, 1)], 0).astype(jnp.bfloat16)
            for x in (before, here, after)
        ]
        even += rows[0:2]
        odd += rows[1:3]
    finished = []
    for parts, weight_ref in ((even, even_ref), (odd, odd_ref)):
        features = (
            jnp.dot(
                jnp.concatenate(parts, 1), weight_ref[...], preferred_element_type=jnp.float32
            )
            + bias_ref[...]
        )
        power = jnp.mean(features * features, axis=1, keepdims=True)
        scaled = features * lax.rsqrt(power + EPSILON) * gain_ref[...]
        finished.append((scaled / (1.0 + jnp.exp(-scaled))).astype(jnp.bfloat16))
    target = lax.broadcasted_iota(jnp.int32, (32, 32), 0)
    source = lax.broadcasted_iota(jnp.int32, (32, 32), 1)
    order = ((target & 1) * 16 + (target >> 1) == source).astype(jnp.float32).astype(jnp.bfloat16)
    for row in range(2):
        both = jnp.concatenate([x[row * 16 : row * 16 + 16] for x in finished], 0)
        out_ref[row] = jnp.dot(order, both, preferred_element_type=jnp.float32).astype(jnp.bfloat16)


def decode(half, own, last, older, even, odd, bias, gain):
    chans = bias.shape[1]
    return pl.pallas_call(
        decode_kernel,
        out_shape=jax.ShapeDtypeStruct((2, 32, chans), jnp.bfloat16),
        in_specs=[SMEM] + [VMEM] * 7,
        out_specs=VMEM,
        compiler_params=pltpu.CompilerParams(vmem_limit_bytes=32 * 2**20),
    )(half, own, last, older, even, odd, bias, gain)


def conv_matrices(conv_weight):
    taps, _, _, chans, outs = conv_weight.shape
    padded = jnp.pad(conv_weight, ((0, 0), (0, 1), (0, 0), (0, 0), (0, 0)))
    blank = jnp.zeros((taps, 4, 1, chans, outs), conv_weight.dtype)
    both = []
    for parts in ([blank, padded], [padded, blank]):
        spread = jnp.concatenate(parts, 2).reshape(taps, 4, 2, 2, chans, outs)
        both.append(spread.transpose(0, 2, 1, 3, 4, 5).reshape(taps * 16 * chans, outs))
    return both


def local(
    query, keys, values, lengths, timestep, latent, head_weight, conv_weight, conv_bias, gain
):
    cfg, zh, x = lax.axis_index("cfg"), lax.axis_index("zh"), lax.axis_index("x")
    y, zl = lax.axis_index("y"), lax.axis_index("zl")
    seq, band = ("y", "zl"), ("zh", "x")

    own = jnp.concatenate([keys[0], values[0]], 1)
    key_values = [own] + [lax.ppermute(own, "y", ring(d)) for d in (1, 3, 2)]
    queries = [query[0]] + [lax.ppermute(query[0], "zl", crossed(m)) for m in (1, 2, 3)]
    block = jnp.stack([((y - d) % SIDE) * SIDE + zl for d in (0, 1, 3, 2)])
    counts = jnp.clip(lengths[0] - block * TOK, 0, TOK).astype(jnp.int32)
    slots = jnp.stack([zl ^ m for m in range(4)]).astype(jnp.int32)

    rows = latent[0]
    above = lax.ppermute(rows[1:2], band, moved(1))
    below = lax.ppermute(rows[0:1], band, moved(-1))
    grid = jnp.concatenate([above, rows, below], 0).reshape(4, TCOLS, 2, -1)
    grid = grid.transpose(1, 0, 2, 3).reshape(TCOLS, 128)
    latent_window = lax.dynamic_slice_in_dim(grid, cfg * 8, CUT, 0)
    even, odd = conv_matrices(conv_weight)
    part = lax.dynamic_slice_in_dim(head_weight, (zh * SIDE + x) * 2 * DH, 2 * DH, 0)
    weight = jnp.concatenate([part[:, 32:], part, part[:, :32]], 1)
    scale = jnp.where(cfg == 0, GUIDE, 1.0 - GUIDE).astype(jnp.float32).reshape(1)

    lse, top, acc = attend(counts, slots, queries, key_values)
    lse = lax.all_to_all(lse, "zl", 0, 0, tiled=True)
    shares = project(scale, lse, top, acc, weight)
    shares = lax.all_to_all(shares, ("cfg", "x"), 0, 0, tiled=True)
    shares = jnp.sum(shares.astype(jnp.float32), 0).astype(jnp.bfloat16)
    shares = lax.all_to_all(shares, ("zh", "zl"), 0, 0, tiled=True)
    window = jnp.sum(shares.astype(jnp.float32), 0)

    sigma = noise_level(timestep[0], STEPS)
    current = (latent_window - sigma * window).astype(jnp.bfloat16)
    last = lax.ppermute(current, seq, moved(1))
    older = lax.ppermute(current, seq, moved(2))
    mine = lax.dynamic_slice_in_dim(window, cfg * 8, TCOLS // 2, 0)[:, 32:96]
    velocity = mine.reshape(TCOLS // 2, 2, 2, -1).transpose(1, 0, 2, 3).reshape(1, 2, TCOLS, -1)
    decoded = decode(
        cfg.astype(jnp.int32).reshape(1),
        current,
        last,
        older,
        even,
        odd,
        conv_bias.reshape(1, -1),
        gain.reshape(1, -1),
    )
    return (velocity, decoded[None])


def solution(mesh):
    split = Mesh(
        mesh.devices.reshape(2, SIDE, SIDE, SIDE, SIDE), ("cfg", "zh", "x", "y", "zl")
    )
    seq, band = ("y", "zl"), ("zh", "x")
    tokens = P("cfg", seq, band)
    return jax.shard_map(
        local,
        mesh=split,
        in_specs=(
            tokens,
            tokens,
            tokens,
            P(),
            P(),
            P(seq, band, None, None),
            P(),
            P(),
            P(),
            P(),
        ),
        out_specs=(P(seq, band, "cfg", None), P(seq, band, "cfg", None)),
        check_vma=False,
    )
```

time: 409 us -> 145 us (0.35)
  the two profiles are of different devices: /device:TPU:30 before, /device:TPU:14 now
where the time goes in v1:
time: 145 us; the launch traced here: 144 us
  starting transfers between devices  60.3 us (42%)
  waiting for transfers between devices  29.6 us (20%)
  Pallas kernels  22.5 us (16%)
  blocking collectives  15.8 us (11%)
  local copies, waits for them, and re-layouts  11.7 us (8%)
  between operations  2.38 us (2%)
  other arithmetic  2.12 us (1%)
    pallas_call x1, Pallas kernels, attend(): pl.pallas_call(attention_kernel, out_shape=(jax.ShapeDtypeStruct((4, 4, 2...  20.8 us
    all_to_all x1, blocking collectives, local(): shares = lax.all_to_all(shares, ('cfg', 'x'), 0, 0, tiled=True)  15.8 us
    ppermute x3, waiting for transfers between devices, local(): lax.ppermute(query[0], 'zl', crossed(m))  13.5 us
    all_to_all x1, starting transfers between devices, local(): shares = lax.all_to_all(shares, ('zh', 'zl'), 0, 0, tiled=True)  13.2 us
    ppermute x3, starting transfers between devices, local(): lax.ppermute(query[0], 'zl', crossed(m))  11.1 us
    unnamed x36, local copies, waits for them, and re-layouts  10.8 us
    ppermute x3, starting transfers between devices, local(): key_values = [own] + [lax.ppermute(own, 'y', ring(d)) for d in (1, 3, 2)]  10 us
    ppermute x1, waiting for transfers between devices, local(): below = lax.ppermute(rows[0:1], band, moved(-1))  8.69 us
  transfers between devices with their start and end apart: 12, of which 4 were waited for; matrix products, arithmetic and copies ran while one was open for 2% of the time, Pallas kernels for 0%

profile of v1, /device:TPU:14, one launch (start us, length us, event | category | flops | bytes accessed | tf_op | source)
XLA Modules:
  0.0 144.5 jit_solution(4355109798004001628)
XLA Ops:
  0.6 4.0 %collective-permute-start = (bf16[512,256]{1,0:T(8,128)(2,1)}, bf16[512,256]{1,0:T(8,128)(2,1)S(1)}, u32[]{:S(2)}, u32[]{:S(2)}) collective-permute-start(bf16[512,256]{1,0:T(8,128)(2,1)} %bitcast.40), channel_id=1, source_target_pairs={{0,1},{1,0},{2,3},{3,2},{4,5},{5,4},{6,7},{7,6},{8,9},{9,8},{10,11... | collective-permute-start | bytes 786440 | tf_op jit(solution)/shard_map/ppermute | solution.py:227
  4.6 1.1 pad_maximum_fusion.refs_4_
  5.7 3.5 %collective-permute-start.3 = (bf16[512,512]{1,0:T(8,128)(2,1)S(1)}, bf16[512,512]{1,0:T(8,128)(2,1)S(1)}, u32[]{:S(2)}, u32[]{:S(2)}) collective-permute-start(bf16[512,512]{1,0:T(8,128)(2,1)S(1)} %pad_maximum_fusion.refs_4_), channel_id=1, source_target_pairs={{0,4},{4,8},{8,12},{12,0},{1,5},{5,9},{9,13},{13,1},{2,6},{6,10},{... | collective-permute-start | bytes 1572872 | tf_op jit(solution)/shard_map/ppermute | solution.py:226
  9.2 2.4 %collective-permute-start.4 = (bf16[512,512]{1,0:T(8,128)(2,1)S(1)}, bf16[512,512]{1,0:T(8,128)(2,1)S(1)}, u32[]{:S(2)}, u32[]{:S(2)}) collective-permute-start(bf16[512,512]{1,0:T(8,128)(2,1)S(1)} %pad_maximum_fusion.refs_4_), channel_id=1, source_target_pairs={{0,12},{4,0},{8,4},{12,8},{1,13},{5,1},{9,5},{13,9},{2,14},{6,2},{... | collective-permute-start | bytes 1572872 | tf_op jit(solution)/shard_map/ppermute | solution.py:226
  11.5 4.2 %collective-permute-start.5 = (bf16[512,512]{1,0:T(8,128)(2,1)S(1)}, bf16[512,512]{1,0:T(8,128)(2,1)S(1)}, u32[]{:S(2)}, u32[]{:S(2)}) collective-permute-start(bf16[512,512]{1,0:T(8,128)(2,1)S(1)} %pad_maximum_fusion.refs_4_), channel_id=1, source_target_pairs={{0,8},{4,12},{8,0},{12,4},{1,9},{5,13},{9,1},{13,5},{2,10},{6,14},... | collective-permute-start | bytes 1572872 | tf_op jit(solution)/shard_map/ppermute | solution.py:226
  15.8 5.2 %collective-permute-start.1 = (bf16[512,256]{1,0:T(8,128)(2,1)}, bf16[512,256]{1,0:T(8,128)(2,1)S(1)}, u32[]{:S(2)}, u32[]{:S(2)}) collective-permute-start(bf16[512,256]{1,0:T(8,128)(2,1)} %bitcast.41), channel_id=1, source_target_pairs={{0,2},{1,3},{2,0},{3,1},{4,6},{5,7},{6,4},{7,5},{8,10},{9,11},{10,... | collective-permute-start | bytes 786440 | tf_op jit(solution)/shard_map/ppermute | solution.py:227
  21.0 1.9 %collective-permute-start.2 = (bf16[512,256]{1,0:T(8,128)(2,1)}, bf16[512,256]{1,0:T(8,128)(2,1)S(1)}, u32[]{:S(2)}, u32[]{:S(2)}) collective-permute-start(bf16[512,256]{1,0:T(8,128)(2,1)} %bitcast.42), channel_id=1, source_target_pairs={{0,3},{1,2},{2,1},{3,0},{4,7},{5,6},{6,5},{7,4},{8,11},{9,10},{10,... | collective-permute-start | bytes 786440 | tf_op jit(solution)/shard_map/ppermute | solution.py:227
  23.6 0.1 copy.39
  23.8 0.1 pad_add_fusion
  23.8 13.5 %collective-permute-done.1.refs_2_ = bf16[512,256]{1,0:T(8,128)(2,1)S(1)} collective-permute-done((bf16[512,256]{1,0:T(8,128)(2,1)}, bf16[512,256]{1,0:T(8,128)(2,1)S(1)}, u32[]{:S(2)}, u32[]{:S(2)}) %collective-permute-start.1) | collective-permute-done | bytes 262176 | tf_op jit(solution)/shard_map/ppermute | solution.py:227
  37.4 0.7 copy-done.8
  38.1 0.7 copy-done.10
  38.8 0.8 copy-done.1
  39.6 0.8 copy-done.3
  40.4 0.8 copy-done.5
  41.2 1.0 copy-done.2
  42.3 1.0 copy-done.4
  43.3 1.0 copy-done.6
  44.4 0.9 copy-done.7
  45.3 0.9 copy-done.9
  46.3 0.9 copy-done.11
  47.2 20.8 %shard_map.113 = (f32[4,4,2,512]{3,2,1,0:T(2,128)}, f32[4,2,512]{2,1,0:T(2,128)S(1)}, f32[4,2,128,512]{3,2,1,0:T(8,128)S(1)}) custom-call(s32[4]{0:T(128)S(1)} %get-tuple-element.19.count_ref, s32[4]{0:T(128)S(1)} %get-tuple-element.18.slot_ref, bf16[512,256]{1,0:T(8,128)(2,1)S(1)} %bitcast.43, bf16[512,256]{1,0:T(8,128)(2,1)S(1)} %collective-permute-done.refs_1_, ...), custom_call_target="tpu_custom_call" | custom-call | tf_op jit(solution)/shard_map/pallas_call | solution.py:110
  68.1 7.8 %all-to-all-start = ((f32[4,4,2,512]{3,2,1,0:T(2,128)}), f32[4,4,2,512]{3,2,1,0:T(2,128)S(1)}, u32[]{:S(2)}, u32[]{:S(2)}) async-start(f32[4,4,2,512]{3,2,1,0:T(2,128)} %get-tuple-element.5), calls=%async_computation | async-start | bytes 131072 | tf_op jit(solution)/shard_map/all_to_all | solution.py:244
  75.9 0.1 fusion.3
  76.0 0.1 pad_maximum_fusion.1.weight_ref
  76.1 5.5 %all-to-all-done.lse_ref = f32[4,4,2,512]{3,2,1,0:T(2,128)S(1)} async-done(((f32[4,4,2,512]{3,2,1,0:T(2,128)}), f32[4,4,2,512]{3,2,1,0:T(2,128)S(1)}, u32[]{:S(2)}, u32[]{:S(2)}) %all-to-all-start) | async-done | bytes 65568 | tf_op jit(solution)/shard_map/all_to_all | solution.py:244
  81.6 0.5 shard_map.114
  82.1 15.8 %all_to_all.15 = bf16[8,16,24,128]{3,2,1,0:T(8,128)(2,1)S(1)} all-to-all(bf16[8,16,24,128]{3,2,1,0:T(8,128)(2,1)S(1)} %shard_map.114), channel_id=1, replica_groups=mesh['cfg'=2,'zh'=4,'x'=4,'y'=4,'zl'=4] {'cfg','x'}, dimensions={0} | all-to-all | bytes 1572864 | tf_op jit(solution)/shard_map/all_to_all | solution.py:246
  97.9 0.7 reduce_sum.21
  98.7 13.2 %all-to-all-start.2 = ((bf16[16,24,128]{2,1,0:T(8,128)(2,1)}), bf16[16,24,128]{2,1,0:T(8,128)(2,1)S(1)}, u32[]{:S(2)}, u32[]{:S(2)}) async-start(bf16[16,24,128]{2,1,0:T(8,128)(2,1)} %reduce_sum.21), calls=%async_computation.2 | async-start | bytes 196608 | tf_op jit(solution)/shard_map/all_to_all | solution.py:248
  111.9 8.6 %collective-permute-start.6 = (f32[1,64,16]{1,2,0:T(8,128)S(1)}, f32[1,64,16]{1,2,0:T(8,128)S(1)}, u32[]{:S(2)}, u32[]{:S(2)}) collective-permute-start(f32[1,64,16]{1,2,0:T(8,128)S(1)} %get-tuple-element.16), channel_id=1, source_target_pairs={{0,16},{16,32},{32,48},{48,64},{64,80},{80,96},{96,112},{112,128},... | collective-permute-start | bytes 12296 | tf_op jit(solution)/shard_map/ppermute | solution.py:233
  120.6 1.9 %collective-permute-start.7 = (f32[1,64,16]{1,2,0:T(8,128)S(1)}, f32[1,64,16]{1,2,0:T(8,128)S(1)}, u32[]{:S(2)}, u32[]{:S(2)}) collective-permute-start(f32[1,64,16]{1,2,0:T(8,128)S(1)} %get-tuple-element.17), channel_id=1, source_target_pairs={{16,0},{32,16},{48,32},{64,48},{80,64},{96,80},{112,96},{128,112},... | collective-permute-start | bytes 12296 | tf_op jit(solution)/shard_map/ppermute | solution.py:234
  122.5 0.1 copy.32
  123.3 0.1 copy.31
  123.4 8.7 %collective-permute-done.7 = f32[1,64,16]{1,2,0:T(8,128)S(1)} collective-permute-done((f32[1,64,16]{1,2,0:T(8,128)S(1)}, f32[1,64,16]{1,2,0:T(8,128)S(1)}, u32[]{:S(2)}, u32[]{:S(2)}) %collective-permute-start.7) | collective-permute-done | bytes 4128 | tf_op jit(solution)/shard_map/ppermute | solution.py:234
  132.1 0.1 copy.33
  132.2 0.1 maximum_bitcast_fusion
  132.3 0.1 copy.34
  132.4 0.1 constant_dynamic-slice_fusion
  132.6 3.4 %collective-permute-start.8 = (bf16[24,128]{1,0:T(8,128)(2,1)S(1)}, bf16[24,128]{1,0:T(8,128)(2,1)S(1)}, u32[]{:S(2)}, u32[]{:S(2)}) collective-permute-start(bf16[24,128]{1,0:T(8,128)(2,1)S(1)} %subtract_convert_fusion.own_ref), channel_id=1, source_target_pairs={{0,1},{1,2},{2,3},{3,4},{4,5},{5,6},{6,7},{7,8},{8,9},{9,10},{10,1... | collective-permute-start | bytes 18440 | tf_op jit(solution)/shard_map/ppermute | solution.py:253
  136.0 4.3 %collective-permute-start.9 = (bf16[24,128]{1,0:T(8,128)(2,1)S(1)}, bf16[24,128]{1,0:T(8,128)(2,1)S(1)}, u32[]{:S(2)}, u32[]{:S(2)}) collective-permute-start(bf16[24,128]{1,0:T(8,128)(2,1)S(1)} %subtract_convert_fusion.own_ref), channel_id=1, source_target_pairs={{0,2},{1,3},{2,4},{3,5},{4,6},{5,7},{6,8},{7,9},{8,10},{9,11},{10,... | collective-permute-start | bytes 18440 | tf_op jit(solution)/shard_map/ppermute | solution.py:254
  140.3 0.1 fusion.2
  140.4 0.1 copy.36
  140.6 0.1 dynamic-slice
  140.7 0.1 reshape.54
  140.8 0.7 copy.38
  141.5 1.8 %collective-permute-done.9.older_ref = bf16[24,128]{1,0:T(8,128)(2,1)S(1)} collective-permute-done((bf16[24,128]{1,0:T(8,128)(2,1)S(1)}, bf16[24,128]{1,0:T(8,128)(2,1)S(1)}, u32[]{:S(2)}, u32[]{:S(2)}) %collective-permute-start.9) | collective-permute-done | bytes 6176 | tf_op jit(solution)/shard_map/ppermute | solution.py:254
  143.3 1.2 shard_map.115
  (39 shorter events, 0.3 us)
Async XLA Ops:
  0.6 23.0 %copy-start = (bf16[4096,64]{0,1:T(8,128)(2,1)S(1)}, bf16[4096,64]{0,1:T(8,128)(2,1)}, u32[]{:S(2)}) copy-start(bf16[4096,64]{0,1:T(8,128)(2,1)} %param.16) | copy-start | bytes 1572868
  0.6 20.3 %collective-permute-start = (bf16[512,256]{1,0:T(8,128)(2,1)}, bf16[512,256]{1,0:T(8,128)(2,1)S(1)}, u32[]{:S(2)}, u32[]{:S(2)}) collective-permute-start(bf16[512,256]{1,0:T(8,128)(2,1)} %bitcast.40), channel_id=1, source_target_pairs={{0,1},{1,0},{2,3},{3,2},{4,5},{5,4},{6,7},{7,6},{8,9},{9,8},{10,11... | collective-permute-start | bytes 786440 | tf_op jit(solution)/shard_map/ppermute | solution.py:227
  5.7 33.1 %collective-permute-start.3 = (bf16[512,512]{1,0:T(8,128)(2,1)S(1)}, bf16[512,512]{1,0:T(8,128)(2,1)S(1)}, u32[]{:S(2)}, u32[]{:S(2)}) collective-permute-start(bf16[512,512]{1,0:T(8,128)(2,1)S(1)} %pad_maximum_fusion.refs_4_), channel_id=1, source_target_pairs={{0,4},{4,8},{8,12},{12,0},{1,5},{5,9},{9,13},{13,1},{2,6},{6,10},{... | collective-permute-start | bytes 1572872 | tf_op jit(solution)/shard_map/ppermute | solution.py:226
  9.2 30.4 %collective-permute-start.4 = (bf16[512,512]{1,0:T(8,128)(2,1)S(1)}, bf16[512,512]{1,0:T(8,128)(2,1)S(1)}, u32[]{:S(2)}, u32[]{:S(2)}) collective-permute-start(bf16[512,512]{1,0:T(8,128)(2,1)S(1)} %pad_maximum_fusion.refs_4_), channel_id=1, source_target_pairs={{0,12},{4,0},{8,4},{12,8},{1,13},{5,1},{9,5},{13,9},{2,14},{6,2},{... | collective-permute-start | bytes 1572872 | tf_op jit(solution)/shard_map/ppermute | solution.py:226
  11.5 28.9 %collective-permute-start.5 = (bf16[512,512]{1,0:T(8,128)(2,1)S(1)}, bf16[512,512]{1,0:T(8,128)(2,1)S(1)}, u32[]{:S(2)}, u32[]{:S(2)}) collective-permute-start(bf16[512,512]{1,0:T(8,128)(2,1)S(1)} %pad_maximum_fusion.refs_4_), channel_id=1, source_target_pairs={{0,8},{4,12},{8,0},{12,4},{1,9},{5,13},{9,1},{13,5},{2,10},{6,14},... | collective-permute-start | bytes 1572872 | tf_op jit(solution)/shard_map/ppermute | solution.py:226
  15.8 21.6 %collective-permute-start.1 = (bf16[512,256]{1,0:T(8,128)(2,1)}, bf16[512,256]{1,0:T(8,128)(2,1)S(1)}, u32[]{:S(2)}, u32[]{:S(2)}) collective-permute-start(bf16[512,256]{1,0:T(8,128)(2,1)} %bitcast.41), channel_id=1, source_target_pairs={{0,2},{1,3},{2,0},{3,1},{4,6},{5,7},{6,4},{7,5},{8,10},{9,11},{10,... | collective-permute-start | bytes 786440 | tf_op jit(solution)/shard_map/ppermute | solution.py:227
  21.0 17.2 %collective-permute-start.2 = (bf16[512,256]{1,0:T(8,128)(2,1)}, bf16[512,256]{1,0:T(8,128)(2,1)S(1)}, u32[]{:S(2)}, u32[]{:S(2)}) collective-permute-start(bf16[512,256]{1,0:T(8,128)(2,1)} %bitcast.42), channel_id=1, source_target_pairs={{0,3},{1,2},{2,1},{3,0},{4,7},{5,6},{6,5},{7,4},{8,11},{9,10},{10,... | collective-permute-start | bytes 786440 | tf_op jit(solution)/shard_map/ppermute | solution.py:227
  37.4 0.7 copy-start.8
  38.1 0.7 copy-start.10
  38.8 0.8 copy-start.1
  39.6 0.8 copy-start.3
  40.4 0.8 copy-start.5
  41.2 1.0 copy-start.2
  42.3 1.0 copy-start.4
  43.3 1.0 copy-start.6
  44.4 0.9 copy-start.7
  45.3 0.9 copy-start.9
  46.3 0.9 copy-start.11
  68.1 13.5 %all-to-all-start = ((f32[4,4,2,512]{3,2,1,0:T(2,128)}), f32[4,4,2,512]{3,2,1,0:T(2,128)S(1)}, u32[]{:S(2)}, u32[]{:S(2)}) async-start(f32[4,4,2,512]{3,2,1,0:T(2,128)} %get-tuple-element.5), calls=%async_computation | async-start | bytes 131072 | tf_op jit(solution)/shard_map/all_to_all | solution.py:244
  81.6 30.3 %copy-start.13 = (f32[1,2,64,16]{2,3,1,0:T(8,128)S(1)}, f32[1,2,64,16]{2,3,1,0:T(8,128)}, u32[]{:S(2)}) copy-start(f32[1,2,64,16]{2,3,1,0:T(8,128)} %param.15) | copy-start | bytes 24580
  82.1 41.1 %copy-start.12 = (bf16[3,3,3,16,384]{4,3,2,1,0:T(8,128)(2,1)S(1)}, bf16[3,3,3,16,384]{4,3,2,1,0:T(8,128)(2,1)}, u32[]{:S(2)}) copy-start(bf16[3,3,3,16,384]{4,3,2,1,0:T(8,128)(2,1)} %param.17) | copy-start | bytes 995332
  98.7 33.9 %all-to-all-start.2 = ((bf16[16,24,128]{2,1,0:T(8,128)(2,1)}), bf16[16,24,128]{2,1,0:T(8,128)(2,1)S(1)}, u32[]{:S(2)}, u32[]{:S(2)}) async-start(bf16[16,24,128]{2,1,0:T(8,128)(2,1)} %reduce_sum.21), calls=%async_computation.2 | async-start | bytes 196608 | tf_op jit(solution)/shard_map/all_to_all | solution.py:248
  111.9 11.4 %collective-permute-start.6 = (f32[1,64,16]{1,2,0:T(8,128)S(1)}, f32[1,64,16]{1,2,0:T(8,128)S(1)}, u32[]{:S(2)}, u32[]{:S(2)}) collective-permute-start(f32[1,64,16]{1,2,0:T(8,128)S(1)} %get-tuple-element.16), channel_id=1, source_target_pairs={{0,16},{16,32},{32,48},{48,64},{64,80},{80,96},{96,112},{112,128},... | collective-permute-start | bytes 12296 | tf_op jit(solution)/shard_map/ppermute | solution.py:233
  120.6 11.6 %collective-permute-start.7 = (f32[1,64,16]{1,2,0:T(8,128)S(1)}, f32[1,64,16]{1,2,0:T(8,128)S(1)}, u32[]{:S(2)}, u32[]{:S(2)}) collective-permute-start(f32[1,64,16]{1,2,0:T(8,128)S(1)} %get-tuple-element.17), channel_id=1, source_target_pairs={{16,0},{32,16},{48,32},{64,48},{80,64},{96,80},{112,96},{128,112},... | collective-permute-start | bytes 12296 | tf_op jit(solution)/shard_map/ppermute | solution.py:234
  132.5 8.1 %copy-start.14 = (f32[384]{0:T(512)S(1)}, f32[384]{0:T(512)}, u32[]{:S(2)}) copy-start(f32[384]{0:T(512)} %param.18) | copy-start | bytes 4612
  132.5 8.1 %copy-start.15 = (f32[384]{0:T(512)S(1)}, f32[384]{0:T(512)}, u32[]{:S(2)}) copy-start(f32[384]{0:T(512)} %param.19) | copy-start | bytes 4612
  132.6 8.9 %collective-permute-start.8 = (bf16[24,128]{1,0:T(8,128)(2,1)S(1)}, bf16[24,128]{1,0:T(8,128)(2,1)S(1)}, u32[]{:S(2)}, u32[]{:S(2)}) collective-permute-start(bf16[24,128]{1,0:T(8,128)(2,1)S(1)} %subtract_convert_fusion.own_ref), channel_id=1, source_target_pairs={{0,1},{1,2},{2,3},{3,4},{4,5},{5,6},{6,7},{7,8},{8,9},{9,10},{10,1... | collective-permute-start | bytes 18440 | tf_op jit(solution)/shard_map/ppermute | solution.py:253
  136.0 7.3 %collective-permute-start.9 = (bf16[24,128]{1,0:T(8,128)(2,1)S(1)}, bf16[24,128]{1,0:T(8,128)(2,1)S(1)}, u32[]{:S(2)}, u32[]{:S(2)}) collective-permute-start(bf16[24,128]{1,0:T(8,128)(2,1)S(1)} %subtract_convert_fusion.own_ref), channel_id=1, source_target_pairs={{0,2},{1,3},{2,4},{3,5},{4,6},{5,7},{6,8},{7,9},{8,10},{9,11},{10,... | collective-permute-start | bytes 18440 | tf_op jit(solution)/shard_map/ppermute | solution.py:254

commit v2 on v1

--- a/solution.py
+++ b/solution.py
@@ -1,3 +1,4 @@
+import functools
 import math
 
 import jax
@@ -22,6 +23,7 @@
 
 VMEM = pl.BlockSpec(memory_space=pltpu.VMEM)
 SMEM = pl.BlockSpec(memory_space=pltpu.SMEM)
+ANY = pl.BlockSpec(memory_space=pl.ANY)
 
 
 def noise_level(timestep, total_steps):
@@ -42,88 +44,138 @@
     return [(i, i + steps) for i in range(count) if 0 <= i + steps < count]
 
 
-def attention_kernel(count_ref, slot_ref, *refs):
-    q_refs, kv_refs = refs[0:4], refs[4:8]
-    lse_ref, top_ref, acc_ref = refs[8:11]
-    qs, ks, vs, denom = refs[11:]
-    for j in range(4):
-        qs[j] = q_refs[j][...]
-        ks[j] = kv_refs[j][:, : 2 * DH]
+def attention_kernel(count_ref, slot_ref, *refs, parts, nq, nk, nx, last):
+    refs = list(refs)
+    if not parts and nx:
+        carried_ref = refs.pop(nq + nk)
+        refs.pop(nq + nk + 3)[...] = carried_ref[...]
+        nx = 0
+    q_refs, kv_refs = refs[:nq], refs[nq : nq + nk]
+    states = [refs[nq + nk + 3 * i : nq + nk + 3 * i + 3] for i in range(len(parts))]
+    at = nq + nk + 3 * len(parts) + nx
+    if last:
+        lse_ref, top_ref, acc_ref = refs[at : at + 3]
+        qs, kvs, vs, scores, sems, denom = refs[at + 3 :]
+    else:
+        top_ref, denom, acc_ref = refs[at : at + 3]
+        qs, kvs, vs, scores, sems = refs[at + 3 :]
+    copies = [pltpu.make_async_copy(q_refs[j], qs.at[j], sems.at[j]) for j in range(nq)]
+    copies += [pltpu.make_async_copy(kv_refs[b], kvs.at[b], sems.at[nq + b]) for b in range(nk)]
+    for copy in copies:
+        copy.start()
+    if not parts:
+        for j in range(nq):
+            top_ref[j] = jnp.full((2, TOK), NEG_FILL, jnp.float32)
+            denom[j] = jnp.zeros((2, TOK), jnp.float32)
+            acc_ref[j] = jnp.zeros((2, DH, TOK), jnp.float32)
+    j = 0
+    for size, (top_in, denom_in, acc_in) in zip(parts, states):
+        for i in range(size):
+            out = slot_ref[j] if last else j
+            top_ref[out] = top_in[i]
+            denom[out] = denom_in[i]
+            acc_ref[out] = acc_in[i]
+            j += 1
+    for copy in copies:
+        copy.wait()
+    for b in range(nk):
         for h in range(2):
-            vs[j, h] = jnp.transpose(kv_refs[j][:, (2 + h) * DH : (3 + h) * DH])
-
-    def query_block(j, _):
-        out = slot_ref[j]
-        top_ref[out] = jnp.full((2, TOK), NEG_FILL, jnp.float32)
-        denom[...] = jnp.zeros((2, TOK), jnp.float32)
-        acc_ref[out] = jnp.zeros((2, DH, TOK), jnp.float32)
-
-        def update(b, masked):
-            for h in range(2):
-                scores = lax.dot_general(
-                    ks[b, :, h * DH : (h + 1) * DH],
-                    qs[j, :, h * DH : (h + 1) * DH],
-                    (((1,), (1,)), ((), ())),
-                    preferred_element_type=jnp.float32,
-                )
-                if masked:
-                    valid = lax.broadcasted_iota(jnp.int32, (TOK, TOK), 0) < count_ref[b]
-                    scores = jnp.where(valid, scores, NEG_FILL)
-                old = top_ref[out, h : h + 1]
-                new = jnp.maximum(old, jnp.max(scores, axis=0, keepdims=True))
-                weights = jnp.exp2((scores - new) * LOG2_SCALE)
-                if masked:
-                    weights = jnp.where(valid, weights, 0.0)
-                factor = jnp.exp2((old - new) * LOG2_SCALE)
-                top_ref[out, h : h + 1] = new
-                denom[h : h + 1] = denom[h : h + 1] * factor + jnp.sum(
-                    weights, axis=0, keepdims=True
-                )
-                acc_ref[out, h] = acc_ref[out, h] * factor + jnp.dot(
-                    vs[b, h], weights.astype(jnp.bfloat16), preferred_element_type=jnp.float32
-                )
-
-        def key_block(b, _):
-            count = count_ref[b]
-
-            @pl.when(count >= TOK)
-            def _():
-                update(b, False)
-
-            @pl.when((count > 0) & (count < TOK))
-            def _():
-                update(b, True)
-
-            return 0
-
-        lax.fori_loop(0, 4, key_block, 0)
-        stat = top_ref[out] * LOG2_SCALE + jnp.log2(denom[...])
-        for copy in range(4):
-            lse_ref[copy, out] = stat
+            vs[b, h, :DH] = jnp.transpose(kvs[b, :, (2 + h) * DH : (3 + h) * DH])
+            vs[b, h, DH:] = jnp.ones((16, TOK), jnp.bfloat16)
+
+    def scored(j, b, h):
+        return lax.dot_general(
+            kvs[b, :, h * DH : (h + 1) * DH],
+            qs[j, :, h * DH : (h + 1) * DH],
+            (((1,), (1,)), ((), ())),
+            preferred_element_type=jnp.float32,
+        )
+
+    def folded(out, b, h, score, masked):
+        if masked:
+            valid = lax.broadcasted_iota(jnp.int32, (TOK, TOK), 0) < count_ref[b]
+            score = jnp.where(valid, score, NEG_FILL)
+        old = top_ref[out, h : h + 1]
+        new = jnp.maximum(old, jnp.max(score, axis=0, keepdims=True))
+        weights = jnp.exp2((score - new) * LOG2_SCALE)
+        if masked:
+            weights = jnp.where(valid, weights, 0.0)
+        factor = jnp.exp2((old - new) * LOG2_SCALE)
+        top_ref[out, h : h + 1] = new
+        mixed = jnp.dot(vs[b, h], weights.astype(jnp.bfloat16), preferred_element_type=jnp.float32)
+        denom[out, h : h + 1] = denom[out, h : h + 1] * factor + mixed[DH : DH + 1]
+        acc_ref[out, h] = acc_ref[out, h] * factor + mixed[:DH]
+
+    def step(t, _):
+        j, b = lax.div(t, nk), lax.rem(t, nk)
+        later = jnp.minimum(t + 1, nq * nk - 1)
+        next_j, next_b = lax.div(later, nk), lax.rem(later, nk)
+        out = slot_ref[j] if last else j
+        count = count_ref[b]
+
+        def update(masked):
+            scores[1] = scored(j, b, 1)
+            folded(out, b, 0, scores[0], masked)
+            scores[0] = scored(next_j, next_b, 0)
+            folded(out, b, 1, scores[1], masked)
+
+        @pl.when(count >= TOK)
+        def _():
+            update(False)
+
+        @pl.when((count > 0) & (count < TOK))
+        def _():
+            update(True)
+
+        @pl.when(count <= 0)
+        def _():
+            scores[0] = scored(next_j, next_b, 0)
+
         return 0
 
-    lax.fori_loop(0, 4, query_block, 0)
-
-
-def attend(counts, slots, queries, key_values):
-    f32 = jnp.float32
-    return pl.pallas_call(
-        attention_kernel,
-        out_shape=(
-            jax.ShapeDtypeStruct((4, 4, 2, TOK), f32),
-            jax.ShapeDtypeStruct((4, 2, TOK), f32),
-            jax.ShapeDtypeStruct((4, 2, DH, TOK), f32),
+    scores[0] = scored(0, 0, 0)
+    lax.fori_loop(0, nq * nk, step, 0)
+    if last:
+        for out in range(nq):
+            stat = top_ref[out] * LOG2_SCALE + jnp.log2(denom[out])
+            for copy in range(4):
+                lse_ref[copy, out] = stat
+
+
+def attend(counts, slots, queries, key_values, states=(), extras=(), last=False):
+    f32, bf16 = jnp.float32, jnp.bfloat16
+    nq, nk = len(queries), len(key_values)
+    parts = tuple(state[0].shape[0] for state in states)
+    stat = jax.ShapeDtypeStruct((nq, 2, TOK), f32)
+    acc = jax.ShapeDtypeStruct((nq, 2, DH, TOK), f32)
+    first = jax.ShapeDtypeStruct((4, nq, 2, TOK), f32) if last else stat
+    carried = () if parts else tuple(jax.ShapeDtypeStruct(x.shape, x.dtype) for x in extras)
+    scratch = [
+        pltpu.VMEM((nq, TOK, 2 * DH), bf16),
+        pltpu.VMEM((nk, TOK, 4 * DH), bf16),
+        pltpu.VMEM((nk, 2, DH + 16, TOK), bf16),
+        pltpu.VMEM((2, TOK, TOK), f32),
+        pltpu.SemaphoreType.DMA((nq + nk,)),
+    ]
+    if last:
+        scratch.append(pltpu.VMEM((nq, 2, TOK), f32))
+    work = nq * nk * 2 * TOK * TOK
+    return pl.pallas_call(
+        functools.partial(
+            attention_kernel, parts=parts, nq=nq, nk=nk, nx=len(extras), last=last
         ),
-        in_specs=[SMEM, SMEM] + [VMEM] * 8,
-        out_specs=(VMEM,) * 3,
-        scratch_shapes=[
-            pltpu.VMEM((4, TOK, 2 * DH), jnp.bfloat16),
-            pltpu.VMEM((4, TOK, 2 * DH), jnp.bfloat16),
-            pltpu.VMEM((4, 2, DH, TOK), jnp.bfloat16),
-            pltpu.VMEM((2, TOK), f32),
-        ],
-        compiler_params=pltpu.CompilerParams(vmem_limit_bytes=40 * 2**20),
-    )(counts, slots, *queries, *key_values)
+        out_shape=(first, stat, acc) + carried,
+        in_specs=[SMEM, SMEM]
+        + [ANY] * (nq + nk)
+        + [VMEM] * (3 * len(parts))
+        + [ANY if parts else VMEM] * len(extras),
+        out_specs=(VMEM,) * (3 + len(carried)),
+        scratch_shapes=scratch,
+        compiler_params=pltpu.CompilerParams(vmem_limit_bytes=20 * 2**20),
+        cost_estimate=pl.CostEstimate(
+            flops=work * DH * 4, transcendentals=work, bytes_accessed=(nq + 2 * nk) * TOK * 4 * DH
+        ),
+    )(counts, slots, *queries, *key_values, *(x for state in states for x in state), *extras)
 
 
 def project_kernel(scale_ref, lse_ref, top_ref, acc_ref, weight_ref, out_ref):
@@ -157,6 +209,42 @@
         out_specs=VMEM,
         compiler_params=pltpu.CompilerParams(vmem_limit_bytes=32 * 2**20),
     )(scale, lse, top, acc, weight)
+
+
+def added_kernel(shares_ref, out_ref):
+    total = shares_ref[0].astype(jnp.float32)
+    for source in range(1, shares_ref.shape[0]):
+        total += shares_ref[source].astype(jnp.float32)
+    out_ref[...] = total.astype(jnp.bfloat16)
+
+
+def added(shares):
+    return pl.pallas_call(
+        added_kernel,
+        out_shape=jax.ShapeDtypeStruct(shares.shape[1:], shares.dtype),
+        in_specs=[VMEM],
+        out_specs=VMEM,
+    )(shares)
+
+
+def denoised_kernel(sigma_ref, shares_ref, latent_ref, current_ref, window_ref):
+    total = shares_ref[0].astype(jnp.float32)
+    for source in range(1, shares_ref.shape[0]):
+        total += shares_ref[source].astype(jnp.float32)
+    window_ref[...] = total
+    current_ref[...] = (latent_ref[...] - sigma_ref[0] * total).astype(jnp.bfloat16)
+
+
+def denoised(sigma, shares, latent):
+    return pl.pallas_call(
+        denoised_kernel,
+        out_shape=(
+            jax.ShapeDtypeStruct(latent.shape, jnp.bfloat16),
+            jax.ShapeDtypeStruct(latent.shape, jnp.float32),
+        ),
+        in_specs=[SMEM, VMEM, VMEM],
+        out_specs=(VMEM, VMEM),
+    )(sigma, shares, latent)
 
 
 def decode_kernel(half_ref, own_ref, last_ref, older_ref, even_ref, odd_ref, bias_ref, gain_ref, out_ref):
@@ -229,7 +317,10 @@
     counts = jnp.clip(lengths[0] - block * TOK, 0, TOK).astype(jnp.int32)
     slots = jnp.stack([zl ^ m for m in range(4)]).astype(jnp.int32)
 
-    rows = latent[0]
+    *near, rows = attend(
+        counts[:3], slots, queries[:2], key_values[:3], extras=(latent.reshape(2, 8, 128),)
+    )
+    far = attend(counts[:3], slots, queries[2:], key_values[:3])
     above = lax.ppermute(rows[1:2], band, moved(1))
     below = lax.ppermute(rows[0:1], band, moved(-1))
     grid = jnp.concatenate([above, rows, below], 0).reshape(4, TCOLS, 2, -1)
@@ -240,16 +331,21 @@
     weight = jnp.concatenate([part[:, 32:], part, part[:, :32]], 1)
     scale = jnp.where(cfg == 0, GUIDE, 1.0 - GUIDE).astype(jnp.float32).reshape(1)
 
-    lse, top, acc = attend(counts, slots, queries, key_values)
+    lse, top, acc = attend(
+        counts[3:],
+        slots,
+        queries,
+        key_values[3:],
+        (near, far),
+        (latent_window, even, odd, weight),
+        last=True,
+    )
     lse = lax.all_to_all(lse, "zl", 0, 0, tiled=True)
     shares = project(scale, lse, top, acc, weight)
     shares = lax.all_to_all(shares, ("cfg", "x"), 0, 0, tiled=True)
-    shares = jnp.sum(shares.astype(jnp.float32), 0).astype(jnp.bfloat16)
-    shares = lax.all_to_all(shares, ("zh", "zl"), 0, 0, tiled=True)
-    window = jnp.sum(shares.astype(jnp.float32), 0)
-
-    sigma = noise_level(timestep[0], STEPS)
-    current = (latent_window - sigma * window).astype(jnp.bfloat16)
+    shares = lax.all_to_all(added(shares), ("zh", "zl"), 0, 0, tiled=True)
+    sigma = noise_level(timestep, STEPS)
+    current, window = denoised(sigma, shares, latent_window)
     last = lax.ppermute(current, seq, moved(1))
     older = lax.ppermute(current, seq, moved(2))
     mine = lax.dynamic_slice_in_dim(window, cfg * 8, TCOLS // 2, 0)[:, 32:96]

time: 145 us -> 143 us (0.986)
  the two profiles are of different devices: /device:TPU:14 before, /device:TPU:24 now
where the time goes in v2:
time: 143 us; the launch traced here: 141 us
  starting transfers between devices  46.3 us (32%)
  blocking collectives  24.8 us (17%)
  Pallas kernels  24.3 us (17%)
  waiting for transfers between devices  22 us (15%)
  local copies, waits for them, and re-layouts  18.6 us (13%)
  between operations  2.45 us (2%)
  other arithmetic  2.19 us (2%)
    all_to_all x1, blocking collectives, local(): shares = lax.all_to_all(shares, ('cfg', 'x'), 0, 0, tiled=True)  24.8 us
    pallas_call x3, Pallas kernels, attend(): pl.pallas_call(functools.partial(attention_kernel, parts=parts, nq=nq, nk...  19.2 us
    unnamed x42, local copies, waits for them, and re-layouts  13.8 us
    all_to_all x1, waiting for transfers between devices, local(): shares = lax.all_to_all(added(shares), ('zh', 'zl'), 0, 0, tiled=True)  13.3 us
    ppermute x3, starting transfers between devices, local(): key_values = [own] + [lax.ppermute(own, 'y', ring(d)) for d in (1, 3, 2)]  12.8 us
    all_to_all x1, starting transfers between devices, local(): shares = lax.all_to_all(added(shares), ('zh', 'zl'), 0, 0, tiled=True)  11.5 us
    ppermute x3, starting transfers between devices, local(): lax.ppermute(query[0], 'zl', crossed(m))  10.1 us
    all_to_all x1, waiting for transfers between devices, local(): lse = lax.all_to_all(lse, 'zl', 0, 0, tiled=True)  5.7 us
  transfers between devices with their start and end apart: 12, of which 4 were waited for; matrix products, arithmetic and copies ran while one was open for 4% of the time, Pallas kernels for 9%

profile of v2, /device:TPU:24, one launch (start us, length us, event | category | flops | bytes accessed | tf_op | source)
XLA Modules:
  0.0 140.6 jit_solution(9281095813863679960)
XLA Ops:
  0.7 1.9 %pad_maximum_fusion.refs_2_ = bf16[512,512]{1,0:T(8,128)(2,1)} fusion(bf16[512,256]{1,0:T(8,128)(2,1)} %bitcast.47, bf16[512,256]{1,0:T(8,128)(2,1)} %bitcast.48), kind=kLoop, calls=%fused_computation | loop fusion | flops 1048576 | bytes 1048576 | tf_op jit(solution)/shard_map/concatenate | solution.py:313
  2.6 7.5 %collective-permute-start.4 = (bf16[512,512]{1,0:T(8,128)(2,1)}, bf16[512,512]{1,0:T(8,128)(2,1)S(1)}, u32[]{:S(2)}, u32[]{:S(2)}) collective-permute-start(bf16[512,512]{1,0:T(8,128)(2,1)} %pad_maximum_fusion.refs_2_), channel_id=1, source_target_pairs={{0,4},{4,8},{8,12},{12,0},{1,5},{5,9},{9,13},{13,1},{2,6},{6,10},{... | collective-permute-start | bytes 1572872 | tf_op jit(solution)/shard_map/ppermute | solution.py:314
  10.1 1.9 %collective-permute-start.5 = (bf16[512,512]{1,0:T(8,128)(2,1)}, bf16[512,512]{1,0:T(8,128)(2,1)}, u32[]{:S(2)}, u32[]{:S(2)}) collective-permute-start(bf16[512,512]{1,0:T(8,128)(2,1)} %pad_maximum_fusion.refs_2_), channel_id=1, source_target_pairs={{0,12},{4,0},{8,4},{12,8},{1,13},{5,1},{9,5},{13,9},{2,14},{6,2},{... | collective-permute-start | bytes 1572872 | tf_op jit(solution)/shard_map/ppermute | solution.py:314
  12.0 1.9 %collective-permute-start = (bf16[512,256]{1,0:T(8,128)(2,1)}, bf16[512,256]{1,0:T(8,128)(2,1)S(1)}, u32[]{:S(2)}, u32[]{:S(2)}) collective-permute-start(bf16[512,256]{1,0:T(8,128)(2,1)} %bitcast.36), channel_id=1, source_target_pairs={{0,1},{1,0},{2,3},{3,2},{4,5},{5,4},{6,7},{7,6},{8,9},{9,8},{10,11... | collective-permute-start | bytes 786440 | tf_op jit(solution)/shard_map/ppermute | solution.py:315
  13.9 3.5 %collective-permute-start.1 = (bf16[512,256]{1,0:T(8,128)(2,1)}, bf16[512,256]{1,0:T(8,128)(2,1)}, u32[]{:S(2)}, u32[]{:S(2)}) collective-permute-start(bf16[512,256]{1,0:T(8,128)(2,1)} %bitcast.37), channel_id=1, source_target_pairs={{0,2},{1,3},{2,0},{3,1},{4,6},{5,7},{6,4},{7,5},{8,10},{9,11},{10,... | collective-permute-start | bytes 786440 | tf_op jit(solution)/shard_map/ppermute | solution.py:315
  17.4 4.7 %collective-permute-start.2 = (bf16[512,256]{1,0:T(8,128)(2,1)}, bf16[512,256]{1,0:T(8,128)(2,1)}, u32[]{:S(2)}, u32[]{:S(2)}) collective-permute-start(bf16[512,256]{1,0:T(8,128)(2,1)} %bitcast.38), channel_id=1, source_target_pairs={{0,3},{1,2},{2,1},{3,0},{4,7},{5,6},{6,5},{7,4},{8,11},{9,10},{10,... | collective-permute-start | bytes 786440 | tf_op jit(solution)/shard_map/ppermute | solution.py:315
  22.2 0.1 copy.27
  23.1 1.0 pad.6
  24.1 0.1 fusion.2
  24.5 0.6 slice.22.count_ref
  25.4 0.1 pad_maximum_fusion.1.refs_14_.weight_ref
  25.5 0.7 copy-done.7
  26.2 3.4 %collective-permute-start.3 = (bf16[512,512]{1,0:T(8,128)(2,1)}, bf16[512,512]{1,0:T(8,128)(2,1)S(1)}, u32[]{:S(2)}, u32[]{:S(2)}) collective-permute-start(bf16[512,512]{1,0:T(8,128)(2,1)} %pad_maximum_fusion.refs_2_), channel_id=1, source_target_pairs={{0,8},{4,12},{8,0},{12,4},{1,9},{5,13},{9,1},{13,5},{2,10},{6,14},... | collective-permute-start | bytes 1572872 | tf_op jit(solution)/shard_map/ppermute | solution.py:314
  29.6 0.8 copy-done.12
  30.4 0.9 copy-done.5
  31.3 0.9 copy-done.8
  32.3 1.0 copy-done.13
  33.3 6.5 %shard_map.113 = (f32[2,2,512]{2,1,0:T(2,128)S(1)}, f32[2,2,512]{2,1,0:T(2,128)S(1)}, f32[2,2,128,512]{3,2,1,0:T(8,128)S(1)}, f32[2,8,128]{2,1,0:T(8,128)S(1)}) custom-call(s32[3]{0:T(128)S(1)} %bitcast.41, s32[4]{0:T(128)S(1)} %pad_add_fusion.slot_ref, bf16[512,256]{1,0:T(8,128)(2,1)S(1)} %bitcast.39, bf16[512,256]{1,0:T(8,128)(2,1)S(1)} %copy-done.8, ...), custom_call_target="tpu_custom_call" | custom-call | flops 1610612736 | bytes 2097152 | tf_op jit(solution)/shard_map/pallas_call | solution.py:163
  39.8 1.3 collective-permute-start.6
  41.1 1.3 collective-permute-start.7
  42.4 6.6 %shard_map.114 = (f32[2,2,512]{2,1,0:T(2,128)S(1)}, f32[2,2,512]{2,1,0:T(2,128)S(1)}, f32[2,2,128,512]{3,2,1,0:T(8,128)S(1)}) custom-call(s32[3]{0:T(128)S(1)} %bitcast.42, s32[4]{0:T(128)S(1)} %pad_add_fusion.slot_ref, bf16[512,256]{1,0:T(8,128)(2,1)} %collective-permute-done.1.refs_0_.refs_2_, bf16[512,256]{1,0:T(8,128)(2,1)} %collective-permute-done.2.refs_1_.refs_3_, ...), custom_call_target="tpu_custom_call" | custom-call | flops 1610612736 | bytes 2097152 | tf_op jit(solution)/shard_map/pallas_call | solution.py:163
  49.1 1.0 copy-done.3
  50.1 0.2 reshape.45
  50.3 0.7 copy.19
  51.0 0.9 constant_dynamic-slice_fusion.1
  52.0 1.2 copy-done.4
  53.2 0.9 copy-done.6
  54.2 0.9 copy-done.9
  55.1 6.1 %shard_map.115 = (f32[4,4,2,512]{3,2,1,0:T(2,128)}, f32[4,2,512]{2,1,0:T(2,128)S(1)}, f32[4,2,128,512]{3,2,1,0:T(8,128)S(1)}) custom-call(s32[1]{0:T(128)} %slice.22.count_ref, s32[4]{0:T(128)S(1)} %pad_add_fusion.slot_ref, bf16[512,256]{1,0:T(8,128)(2,1)S(1)} %bitcast.40, bf16[512,256]{1,0:T(8,128)(2,1)S(1)} %copy-done.9, ...), custom_call_target="tpu_custom_call" | custom-call | flops 1073741824 | bytes 1572864 | tf_op jit(solution)/shard_map/pallas_call | solution.py:163
  61.3 1.4 copy-done.1
  62.6 3.3 %all-to-all-start = ((f32[4,4,2,512]{3,2,1,0:T(2,128)}), f32[4,4,2,512]{3,2,1,0:T(2,128)S(1)}, u32[]{:S(2)}, u32[]{:S(2)}) async-start(f32[4,4,2,512]{3,2,1,0:T(2,128)} %get-tuple-element.21), calls=%async_computation | async-start | bytes 131072 | tf_op jit(solution)/shard_map/all_to_all | solution.py:343
  65.9 5.7 %all-to-all-done.lse_ref = f32[4,4,2,512]{3,2,1,0:T(2,128)S(1)} async-done(((f32[4,4,2,512]{3,2,1,0:T(2,128)}), f32[4,4,2,512]{3,2,1,0:T(2,128)S(1)}, u32[]{:S(2)}, u32[]{:S(2)}) %all-to-all-start) | async-done | bytes 65568 | tf_op jit(solution)/shard_map/all_to_all | solution.py:343
  71.6 1.6 %copy-done.2 = f32[4,2,128,512]{3,2,1,0:T(8,128)S(1)} copy-done((f32[4,2,128,512]{3,2,1,0:T(8,128)S(1)}, f32[4,2,128,512]{3,2,1,0:T(8,128)}, u32[]{:S(2)}) %copy-start.2) | copy-done | bytes 2097176
  73.2 0.5 shard_map.116
  73.8 24.8 %all_to_all.15.shares_ref = bf16[8,16,24,128]{3,2,1,0:T(8,128)(2,1)} all-to-all(bf16[8,16,24,128]{3,2,1,0:T(8,128)(2,1)S(1)} %shard_map.116), channel_id=1, replica_groups=mesh['cfg'=2,'zh'=4,'x'=4,'y'=4,'zl'=4] {'cfg','x'}, dimensions={0} | all-to-all | bytes 1572864 | tf_op jit(solution)/shard_map/all_to_all | solution.py:345
  98.6 1.9 %shard_map.117 = bf16[16,24,128]{2,1,0:T(8,128)(2,1)} custom-call(bf16[8,16,24,128]{3,2,1,0:T(8,128)(2,1)} %all_to_all.15.shares_ref), custom_call_target="tpu_custom_call" | custom-call | tf_op jit(solution)/shard_map/pallas_call | solution.py:222
  100.4 11.5 %all-to-all-start.2 = ((bf16[16,24,128]{2,1,0:T(8,128)(2,1)}), bf16[16,24,128]{2,1,0:T(8,128)(2,1)S(1)}, u32[]{:S(2)}, u32[]{:S(2)}) async-start(bf16[16,24,128]{2,1,0:T(8,128)(2,1)} %shard_map.117), calls=%async_computation.2 | async-start | bytes 196608 | tf_op jit(solution)/shard_map/all_to_all | solution.py:346
  112.7 13.3 %all-to-all-done.2.shares_ref = bf16[16,24,128]{2,1,0:T(8,128)(2,1)S(1)} async-done(((bf16[16,24,128]{2,1,0:T(8,128)(2,1)}), bf16[16,24,128]{2,1,0:T(8,128)(2,1)S(1)}, u32[]{:S(2)}, u32[]{:S(2)}) %all-to-all-start.2) | async-done | bytes 98336 | tf_op jit(solution)/shard_map/all_to_all | solution.py:346
  125.9 0.6 copy-done.15
  126.6 1.5 %shard_map.118 = (bf16[24,128]{1,0:T(8,128)(2,1)}, f32[24,128]{1,0:T(8,128)}) custom-call(f32[1]{0:T(128)S(6)} %div.7.sigma_ref, bf16[16,24,128]{2,1,0:T(8,128)(2,1)} %copy-done.15, f32[24,128]{1,0:T(8,128)} %copy-done.10), custom_call_target="tpu_custom_call" | custom-call | tf_op jit(solution)/shard_map/pallas_call | solution.py:239
  128.1 3.1 %collective-permute-start.8 = (bf16[24,128]{1,0:T(8,128)(2,1)}, bf16[24,128]{1,0:T(8,128)(2,1)S(1)}, u32[]{:S(2)}, u32[]{:S(2)}) collective-permute-start(bf16[24,128]{1,0:T(8,128)(2,1)} %get-tuple-element.25.own_ref), channel_id=1, source_target_pairs={{0,1},{1,2},{2,3},{3,4},{4,5},{5,6},{6,7},{7,8},{8,9},{9,10},{10,1... | collective-permute-start | bytes 18440 | tf_op jit(solution)/shard_map/ppermute | solution.py:349
  131.2 2.9 %collective-permute-start.9 = (bf16[24,128]{1,0:T(8,128)(2,1)}, bf16[24,128]{1,0:T(8,128)(2,1)S(1)}, u32[]{:S(2)}, u32[]{:S(2)}) collective-permute-start(bf16[24,128]{1,0:T(8,128)(2,1)} %get-tuple-element.25.own_ref), channel_id=1, source_target_pairs={{0,2},{1,3},{2,4},{3,5},{4,6},{5,7},{6,8},{7,9},{8,10},{9,11},{10,... | collective-permute-start | bytes 18440 | tf_op jit(solution)/shard_map/ppermute | solution.py:350
  134.1 0.8 dynamic-slice
  135.0 0.7 copy.25
  135.7 0.8 collective-permute-done.8.last_ref
  136.5 2.2 %collective-permute-done.9.older_ref = bf16[24,128]{1,0:T(8,128)(2,1)S(1)} collective-permute-done((bf16[24,128]{1,0:T(8,128)(2,1)}, bf16[24,128]{1,0:T(8,128)(2,1)S(1)}, u32[]{:S(2)}, u32[]{:S(2)}) %collective-permute-start.9) | collective-permute-done | bytes 6176 | tf_op jit(solution)/shard_map/ppermute | solution.py:350
  138.7 0.7 copy-done.11
  139.4 1.2 shard_map.119
  (48 shorter events, 0.8 us)
Async XLA Ops:
  0.6 21.5 %copy-start = (bf16[4096,64]{0,1:T(8,128)(2,1)S(1)}, bf16[4096,64]{0,1:T(8,128)(2,1)}, u32[]{:S(2)}) copy-start(bf16[4096,64]{0,1:T(8,128)(2,1)} %param.16) | copy-start | bytes 1572868
  0.6 23.7 %copy-start.16 = (f32[1,2,64,16]{2,3,1,0:T(8,128)S(1)}, f32[1,2,64,16]{2,3,1,0:T(8,128)}, u32[]{:S(2)}) copy-start(f32[1,2,64,16]{2,3,1,0:T(8,128)} %param.15) | copy-start | bytes 24580
  2.6 27.0 %collective-permute-start.4 = (bf16[512,512]{1,0:T(8,128)(2,1)}, bf16[512,512]{1,0:T(8,128)(2,1)S(1)}, u32[]{:S(2)}, u32[]{:S(2)}) collective-permute-start(bf16[512,512]{1,0:T(8,128)(2,1)} %pad_maximum_fusion.refs_2_), channel_id=1, source_target_pairs={{0,4},{4,8},{8,12},{12,0},{1,5},{5,9},{9,13},{13,1},{2,6},{6,10},{... | collective-permute-start | bytes 1572872 | tf_op jit(solution)/shard_map/ppermute | solution.py:314
  10.1 20.3 %collective-permute-start.5 = (bf16[512,512]{1,0:T(8,128)(2,1)}, bf16[512,512]{1,0:T(8,128)(2,1)}, u32[]{:S(2)}, u32[]{:S(2)}) collective-permute-start(bf16[512,512]{1,0:T(8,128)(2,1)} %pad_maximum_fusion.refs_2_), channel_id=1, source_target_pairs={{0,12},{4,0},{8,4},{12,8},{1,13},{5,1},{9,5},{13,9},{2,14},{6,2},{... | collective-permute-start | bytes 1572872 | tf_op jit(solution)/shard_map/ppermute | solution.py:314
  12.0 13.5 %collective-permute-start = (bf16[512,256]{1,0:T(8,128)(2,1)}, bf16[512,256]{1,0:T(8,128)(2,1)S(1)}, u32[]{:S(2)}, u32[]{:S(2)}) collective-permute-start(bf16[512,256]{1,0:T(8,128)(2,1)} %bitcast.36), channel_id=1, source_target_pairs={{0,1},{1,0},{2,3},{3,2},{4,5},{5,4},{6,7},{7,6},{8,9},{9,8},{10,11... | collective-permute-start | bytes 786440 | tf_op jit(solution)/shard_map/ppermute | solution.py:315
  13.9 28.5 %collective-permute-start.1 = (bf16[512,256]{1,0:T(8,128)(2,1)}, bf16[512,256]{1,0:T(8,128)(2,1)}, u32[]{:S(2)}, u32[]{:S(2)}) collective-permute-start(bf16[512,256]{1,0:T(8,128)(2,1)} %bitcast.37), channel_id=1, source_target_pairs={{0,2},{1,3},{2,0},{3,1},{4,6},{5,7},{6,4},{7,5},{8,10},{9,11},{10,... | collective-permute-start | bytes 786440 | tf_op jit(solution)/shard_map/ppermute | solution.py:315
  17.4 25.0 %collective-permute-start.2 = (bf16[512,256]{1,0:T(8,128)(2,1)}, bf16[512,256]{1,0:T(8,128)(2,1)}, u32[]{:S(2)}, u32[]{:S(2)}) collective-permute-start(bf16[512,256]{1,0:T(8,128)(2,1)} %bitcast.38), channel_id=1, source_target_pairs={{0,3},{1,2},{2,1},{3,0},{4,7},{5,6},{6,5},{7,4},{8,11},{9,10},{10,... | collective-permute-start | bytes 786440 | tf_op jit(solution)/shard_map/ppermute | solution.py:315
  25.5 0.7 copy-start.7
  26.2 25.8 %collective-permute-start.3 = (bf16[512,512]{1,0:T(8,128)(2,1)}, bf16[512,512]{1,0:T(8,128)(2,1)S(1)}, u32[]{:S(2)}, u32[]{:S(2)}) collective-permute-start(bf16[512,512]{1,0:T(8,128)(2,1)} %pad_maximum_fusion.refs_2_), channel_id=1, source_target_pairs={{0,8},{4,12},{8,0},{12,4},{1,9},{5,13},{9,1},{13,5},{2,10},{6,14},... | collective-permute-start | bytes 1572872 | tf_op jit(solution)/shard_map/ppermute | solution.py:314
  29.6 0.8 copy-start.12
  30.4 1.0 copy-start.5
  31.3 0.9 copy-start.8
  32.3 1.0 copy-start.13
  33.3 9.1 %copy-start.14 = (bf16[512,512]{1,0:T(8,128)(2,1)S(1)}, bf16[512,512]{1,0:T(8,128)(2,1)}, u32[]{:S(2)}) copy-start(bf16[512,512]{1,0:T(8,128)(2,1)} %copy-done.12) | copy-start | bytes 1572868
  39.8 10.2 %collective-permute-start.6 = (f32[1,8,128]{2,1,0:T(8,128)S(1)}, f32[1,8,128]{2,1,0:T(8,128)S(1)}, u32[]{:S(2)}, u32[]{:S(2)}) collective-permute-start(f32[1,8,128]{2,1,0:T(8,128)S(1)} %get-tuple-element.32), channel_id=1, source_target_pairs={{0,16},{16,32},{32,48},{48,64},{64,80},{80,96},{96,112},{112,128},... | collective-permute-start | bytes 12296 | tf_op jit(solution)/shard_map/ppermute | solution.py:324
  41.1 8.9 %collective-permute-start.7 = (f32[1,8,128]{2,1,0:T(8,128)S(1)}, f32[1,8,128]{2,1,0:T(8,128)S(1)}, u32[]{:S(2)}, u32[]{:S(2)}) collective-permute-start(f32[1,8,128]{2,1,0:T(8,128)S(1)} %get-tuple-element.33), channel_id=1, source_target_pairs={{16,0},{32,16},{48,32},{64,48},{80,64},{96,80},{112,96},{128,112},... | collective-permute-start | bytes 12296 | tf_op jit(solution)/shard_map/ppermute | solution.py:325
  49.1 1.0 copy-start.3
  52.0 9.3 %copy-start.10 = (f32[24,128]{1,0:T(8,128)}, f32[24,128]{1,0:T(8,128)S(1)}, u32[]{:S(2)}) copy-start(f32[24,128]{1,0:T(8,128)S(1)} %copy.26.refs_11_.latent_ref) | copy-start | bytes 36868
  52.0 1.3 copy-start.4
  53.2 0.9 copy-start.6
  54.2 0.9 copy-start.9
  61.3 1.4 copy-start.1
  62.6 9.0 %all-to-all-start = ((f32[4,4,2,512]{3,2,1,0:T(2,128)}), f32[4,4,2,512]{3,2,1,0:T(2,128)S(1)}, u32[]{:S(2)}, u32[]{:S(2)}) async-start(f32[4,4,2,512]{3,2,1,0:T(2,128)} %get-tuple-element.21), calls=%async_computation | async-start | bytes 131072 | tf_op jit(solution)/shard_map/all_to_all | solution.py:343
  71.6 1.6 %copy-start.2 = (f32[4,2,128,512]{3,2,1,0:T(8,128)S(1)}, f32[4,2,128,512]{3,2,1,0:T(8,128)}, u32[]{:S(2)}) copy-start(f32[4,2,128,512]{3,2,1,0:T(8,128)} %copy-done.1) | copy-start | bytes 6291460
  73.8 60.3 %copy-start.17 = (f32[384]{0:T(512)S(1)}, f32[384]{0:T(512)}, u32[]{:S(2)}) copy-start(f32[384]{0:T(512)} %param.18) | copy-start | bytes 4612
  73.8 60.3 %copy-start.18 = (f32[384]{0:T(512)S(1)}, f32[384]{0:T(512)}, u32[]{:S(2)}) copy-start(f32[384]{0:T(512)} %param.19) | copy-start | bytes 4612
  100.4 25.5 %all-to-all-start.2 = ((bf16[16,24,128]{2,1,0:T(8,128)(2,1)}), bf16[16,24,128]{2,1,0:T(8,128)(2,1)S(1)}, u32[]{:S(2)}, u32[]{:S(2)}) async-start(bf16[16,24,128]{2,1,0:T(8,128)(2,1)} %shard_map.117), calls=%async_computation.2 | async-start | bytes 196608 | tf_op jit(solution)/shard_map/all_to_all | solution.py:346
  125.9 0.6 copy-start.15
  128.1 8.4 %collective-permute-start.8 = (bf16[24,128]{1,0:T(8,128)(2,1)}, bf16[24,128]{1,0:T(8,128)(2,1)S(1)}, u32[]{:S(2)}, u32[]{:S(2)}) collective-permute-start(bf16[24,128]{1,0:T(8,128)(2,1)} %get-tuple-element.25.own_ref), channel_id=1, source_target_pairs={{0,1},{1,2},{2,3},{3,4},{4,5},{5,6},{6,7},{7,8},{8,9},{9,10},{10,1... | collective-permute-start | bytes 18440 | tf_op jit(solution)/shard_map/ppermute | solution.py:349
  131.2 7.5 %collective-permute-start.9 = (bf16[24,128]{1,0:T(8,128)(2,1)}, bf16[24,128]{1,0:T(8,128)(2,1)S(1)}, u32[]{:S(2)}, u32[]{:S(2)}) collective-permute-start(bf16[24,128]{1,0:T(8,128)(2,1)} %get-tuple-element.25.own_ref), channel_id=1, source_target_pairs={{0,2},{1,3},{2,4},{3,5},{4,6},{5,7},{6,8},{7,9},{8,10},{9,11},{10,... | collective-permute-start | bytes 18440 | tf_op jit(solution)/shard_map/ppermute | solution.py:350
  138.7 0.7 copy-start.11

commit v3 on v2

--- a/solution.py
+++ b/solution.py
@@ -23,7 +23,12 @@
 
 VMEM = pl.BlockSpec(memory_space=pltpu.VMEM)
 SMEM = pl.BlockSpec(memory_space=pltpu.SMEM)
+HBM = pl.BlockSpec(memory_space=pltpu.HBM)
 ANY = pl.BlockSpec(memory_space=pl.ANY)
+
+
+def in_hbm(value):
+    return pltpu.with_memory_space_constraint(value, pltpu.HBM)
 
 
 def noise_level(timestep, total_steps):
@@ -44,39 +49,40 @@
     return [(i, i + steps) for i in range(count) if 0 <= i + steps < count]
 
 
-def attention_kernel(count_ref, slot_ref, *refs, parts, nq, nk, nx, last):
+def attention_kernel(count_ref, slot_ref, *refs, nq, nk, skip, parts, nx, last):
     refs = list(refs)
-    if not parts and nx:
-        carried_ref = refs.pop(nq + nk)
-        refs.pop(nq + nk + 3)[...] = carried_ref[...]
-        nx = 0
-    q_refs, kv_refs = refs[:nq], refs[nq : nq + nk]
-    states = [refs[nq + nk + 3 * i : nq + nk + 3 * i + 3] for i in range(len(parts))]
-    at = nq + nk + 3 * len(parts) + nx
+    whole = 3
+    at = nq + nk + (nk > whole)
+    q_refs, kv_refs = refs[:nq], refs[nq:at]
+    if parts:
+        top_in, denom_in, acc_in = refs[at : at + 3]
+        at += 3
+    at += nx
     if last:
-        lse_ref, top_ref, acc_ref = refs[at : at + 3]
-        qs, kvs, vs, scores, sems, denom = refs[at + 3 :]
+        lse_ref, top_ref, acc_out = refs[at : at + 3]
+        qs, kvs, vs, scores, sems, denom, acc_ref = refs[at + 3 :]
     else:
-        top_ref, denom, acc_ref = refs[at : at + 3]
-        qs, kvs, vs, scores, sems = refs[at + 3 :]
+        top_ref, denom, acc_out = refs[at : at + 3]
+        qs, kvs, vs, scores, sems, acc_ref = refs[at + 3 :]
+    slots = [slot_ref[j] if last else j for j in range(nq)]
     copies = [pltpu.make_async_copy(q_refs[j], qs.at[j], sems.at[j]) for j in range(nq)]
-    copies += [pltpu.make_async_copy(kv_refs[b], kvs.at[b], sems.at[nq + b]) for b in range(nk)]
+    for b, kv_ref in enumerate(kv_refs):
+        place = kvs.at[b] if b < whole else kvs.at[whole, :, pl.ds((b - whole) * 2 * DH, 2 * DH)]
+        copies.append(pltpu.make_async_copy(kv_ref, place, sems.at[nq + b]))
     for copy in copies:
         copy.start()
-    if not parts:
-        for j in range(nq):
-            top_ref[j] = jnp.full((2, TOK), NEG_FILL, jnp.float32)
-            denom[j] = jnp.zeros((2, TOK), jnp.float32)
-            acc_ref[j] = jnp.zeros((2, DH, TOK), jnp.float32)
-    j = 0
-    for size, (top_in, denom_in, acc_in) in zip(parts, states):
-        for i in range(size):
-            out = slot_ref[j] if last else j
-            top_ref[out] = top_in[i]
-            denom[out] = denom_in[i]
-            acc_ref[out] = acc_in[i]
-            j += 1
-    for copy in copies:
+    carried = []
+    for j in range(parts):
+        copy = pltpu.make_async_copy(acc_in.at[j], acc_ref.at[slots[j]], sems.at[len(copies) + j])
+        copy.start()
+        carried.append(copy)
+        top_ref[slots[j]] = top_in[j]
+        denom[slots[j]] = denom_in[j]
+    for j in range(parts, nq):
+        top_ref[slots[j]] = jnp.full((2, TOK), NEG_FILL, jnp.float32)
+        denom[slots[j]] = jnp.zeros((2, TOK), jnp.float32)
+        acc_ref[slots[j]] = jnp.zeros((2, DH, TOK), jnp.float32)
+    for copy in copies + carried:
         copy.wait()
     for b in range(nk):
         for h in range(2):
@@ -106,10 +112,21 @@
         denom[out, h : h + 1] = denom[out, h : h + 1] * factor + mixed[DH : DH + 1]
         acc_ref[out, h] = acc_ref[out, h] * factor + mixed[:DH]
 
+    done = parts * (nk - skip) if parts else 0
+    total = done + (nq - parts) * nk
+
+    def tile(t):
+        if not parts:
+            return lax.div(t, nk), lax.rem(t, nk)
+        fresh = t >= done
+        rest = nk - skip
+        j = jnp.where(fresh, parts + lax.div(t - done, nk), lax.div(t, rest))
+        b = jnp.where(fresh, lax.rem(t - done, nk), skip + lax.rem(t, rest))
+        return j, b
+
     def step(t, _):
-        j, b = lax.div(t, nk), lax.rem(t, nk)
-        later = jnp.minimum(t + 1, nq * nk - 1)
-        next_j, next_b = lax.div(later, nk), lax.rem(later, nk)
+        j, b = tile(t)
+        next_j, next_b = tile(jnp.minimum(t + 1, total - 1))
         out = slot_ref[j] if last else j
         count = count_ref[b]
 
@@ -133,52 +150,67 @@
 
         return 0
 
-    scores[0] = scored(0, 0, 0)
-    lax.fori_loop(0, nq * nk, step, 0)
+    scores[0] = scored(0, skip if parts else 0, 0)
+    lax.fori_loop(0, total, step, 0)
+    copy = pltpu.make_async_copy(acc_ref, acc_out, sems.at[0])
+    copy.start()
     if last:
         for out in range(nq):
             stat = top_ref[out] * LOG2_SCALE + jnp.log2(denom[out])
-            for copy in range(4):
-                lse_ref[copy, out] = stat
-
-
-def attend(counts, slots, queries, key_values, states=(), extras=(), last=False):
+            for place in range(4):
+                lse_ref[place, out] = stat
+    copy.wait()
+
+
+def attend(counts, slots, queries, key_values, state=(), skip=0, extras=(), last=False):
     f32, bf16 = jnp.float32, jnp.bfloat16
-    nq, nk = len(queries), len(key_values)
-    parts = tuple(state[0].shape[0] for state in states)
+    nq, nk = len(queries), min(len(key_values), 4)
+    parts = state[0].shape[0] if state else 0
     stat = jax.ShapeDtypeStruct((nq, 2, TOK), f32)
-    acc = jax.ShapeDtypeStruct((nq, 2, DH, TOK), f32)
+    acc = pltpu.HBM((nq, 2, DH, TOK), f32)
     first = jax.ShapeDtypeStruct((4, nq, 2, TOK), f32) if last else stat
-    carried = () if parts else tuple(jax.ShapeDtypeStruct(x.shape, x.dtype) for x in extras)
     scratch = [
         pltpu.VMEM((nq, TOK, 2 * DH), bf16),
         pltpu.VMEM((nk, TOK, 4 * DH), bf16),
         pltpu.VMEM((nk, 2, DH + 16, TOK), bf16),
         pltpu.VMEM((2, TOK, TOK), f32),
-        pltpu.SemaphoreType.DMA((nq + nk,)),
+        pltpu.SemaphoreType.DMA((nq + len(key_values) + parts,)),
     ]
     if last:
         scratch.append(pltpu.VMEM((nq, 2, TOK), f32))
-    work = nq * nk * 2 * TOK * TOK
+    scratch.append(pltpu.VMEM((nq, 2, DH, TOK), f32))
+    tiles = nq * nk - parts * skip
+    work = tiles * 2 * TOK * TOK
     return pl.pallas_call(
         functools.partial(
-            attention_kernel, parts=parts, nq=nq, nk=nk, nx=len(extras), last=last
+            attention_kernel, nq=nq, nk=nk, skip=skip, parts=parts, nx=len(extras), last=last
         ),
-        out_shape=(first, stat, acc) + carried,
+        out_shape=(first, stat, acc),
         in_specs=[SMEM, SMEM]
-        + [ANY] * (nq + nk)
-        + [VMEM] * (3 * len(parts))
-        + [ANY if parts else VMEM] * len(extras),
-        out_specs=(VMEM,) * (3 + len(carried)),
+        + [HBM] * (nq + len(key_values))
+        + ([VMEM, VMEM, HBM] if parts else [])
+        + [ANY] * len(extras),
+        out_specs=(VMEM, VMEM, HBM),
         scratch_shapes=scratch,
-        compiler_params=pltpu.CompilerParams(vmem_limit_bytes=20 * 2**20),
+        compiler_params=pltpu.CompilerParams(vmem_limit_bytes=24 * 2**20),
         cost_estimate=pl.CostEstimate(
             flops=work * DH * 4, transcendentals=work, bytes_accessed=(nq + 2 * nk) * TOK * 4 * DH
         ),
-    )(counts, slots, *queries, *key_values, *(x for state in states for x in state), *extras)
-
-
-def project_kernel(scale_ref, lse_ref, top_ref, acc_ref, weight_ref, out_ref):
+    )(
+        counts,
+        slots,
+        *(in_hbm(x) for x in (*queries, *key_values)),
+        *(in_hbm(x) if x.ndim == 4 else x for x in state),
+        *extras,
+    )
+
+
+def project_kernel(
+    scale_ref, place_ref, lse_ref, top_ref, acc_hbm, weight_ref, latent_ref, out_ref, acc_ref, sems
+):
+    copies = [pltpu.make_async_copy(acc_hbm.at[j], acc_ref.at[j], sems.at[j]) for j in range(4)]
+    for copy in copies:
+        copy.start()
     lane = lax.broadcasted_iota(jnp.int32, (ROWS, TCOLS, 128), 2)
     blank = jnp.zeros((1, TCOLS, 128), jnp.float32)
     for j in range(4):
@@ -186,6 +218,7 @@
         peak = jnp.maximum(jnp.maximum(stats[0], stats[1]), jnp.maximum(stats[2], stats[3]))
         total = sum(jnp.exp2(stat - peak) for stat in stats)
         factor = jnp.exp2(top_ref[j] * LOG2_SCALE - peak) / total * scale_ref[0]
+        copies[j].wait()
         mixed = jnp.concatenate(
             [(acc_ref[j, h] * factor[h : h + 1]).astype(jnp.bfloat16) for h in range(2)], 0
         )
@@ -199,52 +232,33 @@
             for half in range(2):
                 cut = window[row, half * 8 : half * 8 + CUT]
                 out_ref[half * 4 + row % 4, row // 4 * 4 + j] = cut.astype(jnp.bfloat16)
-
-
-def project(scale, lse, top, acc, weight):
+    band, zl = place_ref[0], place_ref[1]
+    edge = pltpu.roll(latent_ref[...], 64, 1) * scale_ref[1]
+    lane = lax.broadcasted_iota(jnp.int32, (TCOLS, 128), 1)
+    for target, part in ((band + 1, lane < 32), (band - 1, lane >= 96)):
+
+        @pl.when((target >= 0) & (target < ROWS))
+        def _():
+            sent = jnp.where(part, edge, 0.0)
+            for half in range(2):
+                at = (half * 4 + (target & 3), (target >> 2) * 4 + zl)
+                out_ref[at] = (
+                    out_ref[at].astype(jnp.float32) + sent[half * 8 : half * 8 + CUT]
+                ).astype(jnp.bfloat16)
+
+
+def project(scale, place, lse, top, acc, weight, latent):
     return pl.pallas_call(
         project_kernel,
         out_shape=jax.ShapeDtypeStruct((8, 16, CUT, 128), jnp.bfloat16),
-        in_specs=[SMEM] + [VMEM] * 4,
+        in_specs=[SMEM, SMEM, VMEM, VMEM, HBM, VMEM, VMEM],
         out_specs=VMEM,
+        scratch_shapes=[
+            pltpu.VMEM((4, 2, DH, TOK), jnp.float32),
+            pltpu.SemaphoreType.DMA((4,)),
+        ],
         compiler_params=pltpu.CompilerParams(vmem_limit_bytes=32 * 2**20),
-    )(scale, lse, top, acc, weight)
-
-
-def added_kernel(shares_ref, out_ref):
-    total = shares_ref[0].astype(jnp.float32)
-    for source in range(1, shares_ref.shape[0]):
-        total += shares_ref[source].astype(jnp.float32)
-    out_ref[...] = total.astype(jnp.bfloat16)
-
-
-def added(shares):
-    return pl.pallas_call(
-        added_kernel,
-        out_shape=jax.ShapeDtypeStruct(shares.shape[1:], shares.dtype),
-        in_specs=[VMEM],
-        out_specs=VMEM,
-    )(shares)
-
-
-def denoised_kernel(sigma_ref, shares_ref, latent_ref, current_ref, window_ref):
-    total = shares_ref[0].astype(jnp.float32)
-    for source in range(1, shares_ref.shape[0]):
-        total += shares_ref[source].astype(jnp.float32)
-    window_ref[...] = total
-    current_ref[...] = (latent_ref[...] - sigma_ref[0] * total).astype(jnp.bfloat16)
-
-
-def denoised(sigma, shares, latent):
-    return pl.pallas_call(
-        denoised_kernel,
-        out_shape=(
-            jax.ShapeDtypeStruct(latent.shape, jnp.bfloat16),
-            jax.ShapeDtypeStruct(latent.shape, jnp.float32),
-        ),
-        in_specs=[SMEM, VMEM, VMEM],
-        out_specs=(VMEM, VMEM),
-    )(sigma, shares, latent)
+    )(scale, place, lse, top, in_hbm(acc), weight, latent)
 
 
 def decode_kernel(half_ref, own_ref, last_ref, older_ref, even_ref, odd_ref, bias_ref, gain_ref, out_ref):
@@ -308,44 +322,56 @@
 ):
     cfg, zh, x = lax.axis_index("cfg"), lax.axis_index("zh"), lax.axis_index("x")
     y, zl = lax.axis_index("y"), lax.axis_index("zl")
-    seq, band = ("y", "zl"), ("zh", "x")
+    seq = ("y", "zl")
 
     own = jnp.concatenate([keys[0], values[0]], 1)
-    key_values = [own] + [lax.ppermute(own, "y", ring(d)) for d in (1, 3, 2)]
+    before, after = lax.ppermute(own, "y", ring(1)), lax.ppermute(own, "y", ring(-1))
+    across = [
+        lax.ppermute(before[:, : 2 * DH], "y", ring(1)),
+        lax.ppermute(after[:, 2 * DH :], "y", ring(-1)),
+    ]
+    key_values = [own, before, after] + across
     queries = [query[0]] + [lax.ppermute(query[0], "zl", crossed(m)) for m in (1, 2, 3)]
     block = jnp.stack([((y - d) % SIDE) * SIDE + zl for d in (0, 1, 3, 2)])
     counts = jnp.clip(lengths[0] - block * TOK, 0, TOK).astype(jnp.int32)
     slots = jnp.stack([zl ^ m for m in range(4)]).astype(jnp.int32)
 
-    *near, rows = attend(
-        counts[:3], slots, queries[:2], key_values[:3], extras=(latent.reshape(2, 8, 128),)
-    )
-    far = attend(counts[:3], slots, queries[2:], key_values[:3])
-    above = lax.ppermute(rows[1:2], band, moved(1))
-    below = lax.ppermute(rows[0:1], band, moved(-1))
-    grid = jnp.concatenate([above, rows, below], 0).reshape(4, TCOLS, 2, -1)
-    grid = grid.transpose(1, 0, 2, 3).reshape(TCOLS, 128)
+    rows = latent[0].reshape(2, TCOLS, 32)
+    blank = jnp.zeros((TCOLS, 32), jnp.float32)
+    grid = jnp.concatenate([blank, rows[0], rows[1], blank], 1)
     latent_window = lax.dynamic_slice_in_dim(grid, cfg * 8, CUT, 0)
     even, odd = conv_matrices(conv_weight)
+    bias_row, gain_row = conv_bias.reshape(1, -1), gain.reshape(1, -1)
     part = lax.dynamic_slice_in_dim(head_weight, (zh * SIDE + x) * 2 * DH, 2 * DH, 0)
     weight = jnp.concatenate([part[:, 32:], part, part[:, :32]], 1)
-    scale = jnp.where(cfg == 0, GUIDE, 1.0 - GUIDE).astype(jnp.float32).reshape(1)
-
+    sigma = noise_level(timestep[0], STEPS)
+    scale = jnp.stack(
+        [
+            jnp.where(cfg == 0, GUIDE, 1.0 - GUIDE).astype(jnp.float32),
+            jnp.where(cfg == 0, -1.0 / sigma, 0.0),
+        ]
+    )
+    place = jnp.stack([zh * SIDE + x, zl]).astype(jnp.int32)
+
+    near = attend(counts[:3], slots, queries[:2], key_values[:3])
     lse, top, acc = attend(
-        counts[3:],
+        counts,
         slots,
         queries,
-        key_values[3:],
-        (near, far),
-        (latent_window, even, odd, weight),
+        key_values,
+        near,
+        skip=3,
+        extras=(grid, latent_window, even, odd, weight, bias_row, gain_row, scale, place),
         last=True,
     )
     lse = lax.all_to_all(lse, "zl", 0, 0, tiled=True)
-    shares = project(scale, lse, top, acc, weight)
+    shares = project(scale, place, lse, top, acc, weight, grid)
     shares = lax.all_to_all(shares, ("cfg", "x"), 0, 0, tiled=True)
-    shares = lax.all_to_all(added(shares), ("zh", "zl"), 0, 0, tiled=True)
-    sigma = noise_level(timestep, STEPS)
-    current, window = denoised(sigma, shares, latent_window)
+    shares = jnp.sum(shares.astype(jnp.float32), 0).astype(jnp.bfloat16)
+    shares = lax.all_to_all(shares, ("zh", "zl"), 0, 0, tiled=True)
+    window = jnp.sum(shares.astype(jnp.float32), 0)
+
+    current = (latent_window - sigma * window).astype(jnp.bfloat16)
     last = lax.ppermute(current, seq, moved(1))
     older = lax.ppermute(current, seq, moved(2))
     mine = lax.dynamic_slice_in_dim(window, cfg * 8, TCOLS // 2, 0)[:, 32:96]
@@ -357,8 +383,8 @@
         older,
         even,
         odd,
-        conv_bias.reshape(1, -1),
-        gain.reshape(1, -1),
+        bias_row,
+        gain_row,
     )
     return (velocity, decoded[None])
 

time: 143 us -> 130 us (0.909); the launches traced: 141 us -> 129 us
  local copies, waits for them, and re-layouts: 18.6 us -> 6.24 us
  blocking collectives: 24.8 us -> 27.5 us
    unnamed x42 -> x16, local copies, waits for them, and re-layouts: 13.8 us -> 1.68 us
    all_to_all x0 -> x1, blocking collectives: none -> 10.8 us  [local(): lse = lax.all_to_all(lse, 'zl', 0, 0, tiled=True)]
    all_to_all x1, blocking collectives: 24.8 us -> 16.6 us  [local(): shares = lax.all_to_all(shares, ('cfg', 'x'), 0, 0, tiled=True)]
    all_to_all x2 -> x1, waiting for transfers between devices: 19 us -> 13.9 us  [local(): shares = lax.all_to_all(shares, ('zh', 'zl'), 0, 0, tiled=True)]
    ppermute x1, waiting for transfers between devices: 0.79 us -> 4.48 us  [local(): last = lax.ppermute(current, seq, moved(1))]
    ppermute x5 -> x4, waiting for transfers between devices: 0.01 us -> 3.25 us  [the longest x1 3.25 us: local(): lax.ppermute(own, 'y', ring(-1))]
    pallas_call x5 -> x2, Pallas kernels: 22.6 us -> 19.4 us  [attend(): pl.pallas_call(functools.partial(attention_kernel, nq=nq, nk=nk, skip=ski...]
    pallas_call x1, Pallas kernels: 0.51 us -> 2.89 us  [project(): pl.pallas_call(project_kernel, out_shape=jax.ShapeDtypeStruct((8, 16, CUT...]
  transfers between devices with their start and end apart: 12 -> 10, of which waited for: 4 -> 4; matrix products, arithmetic and copies ran while one was open for 4% -> 5% of each run, Pallas kernels for 9% -> 6%
where the time goes in v3:
time: 130 us; the launch traced here: 129 us
  starting transfers between devices  45.2 us (35%)
  blocking collectives  27.5 us (21%)
  Pallas kernels  23.5 us (18%)
  waiting for transfers between devices  22.1 us (17%)
  local copies, waits for them, and re-layouts  6.24 us (5%)
  between operations  2.45 us (2%)
  other arithmetic  2.3 us (2%)
    pallas_call x2, Pallas kernels, attend(): pl.pallas_call(functools.partial(attention_kernel, nq=nq, nk=nk, skip=ski...  19.4 us
    all_to_all x1, blocking collectives, local(): shares = lax.all_to_all(shares, ('cfg', 'x'), 0, 0, tiled=True)  16.6 us
    all_to_all x1, waiting for transfers between devices, local(): shares = lax.all_to_all(shares, ('zh', 'zl'), 0, 0, tiled=True)  13.9 us
    all_to_all x1, starting transfers between devices, local(): shares = lax.all_to_all(shares, ('zh', 'zl'), 0, 0, tiled=True)  12.5 us
    ppermute x3, starting transfers between devices, local(): lax.ppermute(query[0], 'zl', crossed(m))  11.1 us
    all_to_all x1, blocking collectives, local(): lse = lax.all_to_all(lse, 'zl', 0, 0, tiled=True)  10.8 us
    ppermute x1, starting transfers between devices, local(): lax.ppermute(own, 'y', ring(1))  5.96 us
    ppermute x1, starting transfers between devices, local(): lax.ppermute(before[:, :2 * DH], 'y', ring(1))  5.13 us
  transfers between devices with their start and end apart: 10, of which 4 were waited for; matrix products, arithmetic and copies ran while one was open for 5% of the time, Pallas kernels for 6%

profile of v3, /device:TPU:24, one launch (start us, length us, event | category | flops | bytes accessed | tf_op | source)
XLA Modules:
  0.0 129.3 jit_solution(18360411656075010278)
XLA Ops:
  0.6 0.0 copy-start
  0.6 6.7 %collective-permute-start.2 = (bf16[512,256]{1,0:T(8,128)(2,1)}, bf16[512,256]{1,0:T(8,128)(2,1)S(1)}, u32[]{:S(2)}, u32[]{:S(2)}) collective-permute-start(bf16[512,256]{1,0:T(8,128)(2,1)} %bitcast.47), channel_id=1, source_target_pairs={{0,3},{1,2},{2,1},{3,0},{4,7},{5,6},{6,5},{7,4},{8,11},{9,10},{10,... | collective-permute-start | bytes 786440 | tf_op jit(solution)/shard_map/ppermute | solution.py:334
  7.3 1.9 %collective-permute-start.1 = (bf16[512,256]{1,0:T(8,128)(2,1)}, bf16[512,256]{1,0:T(8,128)(2,1)}, u32[]{:S(2)}, u32[]{:S(2)}) collective-permute-start(bf16[512,256]{1,0:T(8,128)(2,1)} %bitcast.48), channel_id=1, source_target_pairs={{0,2},{1,3},{2,0},{3,1},{4,6},{5,7},{6,4},{7,5},{8,10},{9,11},{10,... | collective-permute-start | bytes 786440 | tf_op jit(solution)/shard_map/ppermute | solution.py:334
  9.3 2.5 %collective-permute-start = (bf16[512,256]{1,0:T(8,128)(2,1)}, bf16[512,256]{1,0:T(8,128)(2,1)}, u32[]{:S(2)}, u32[]{:S(2)}) collective-permute-start(bf16[512,256]{1,0:T(8,128)(2,1)} %bitcast.49), channel_id=1, source_target_pairs={{0,1},{1,0},{2,3},{3,2},{4,5},{5,4},{6,7},{7,6},{8,9},{9,8},{10,11... | collective-permute-start | bytes 786440 | tf_op jit(solution)/shard_map/ppermute | solution.py:334
  11.8 1.1 pad_maximum_fusion.refs_2_.refs_4_
  12.8 2.7 %collective-permute-start.4 = (bf16[512,512]{1,0:T(8,128)(2,1)S(1)}, bf16[512,512]{1,0:T(8,128)(2,1)}, u32[]{:S(2)}, u32[]{:S(2)}) collective-permute-start(bf16[512,512]{1,0:T(8,128)(2,1)S(1)} %pad_maximum_fusion.refs_2_.refs_4_), channel_id=1, source_target_pairs={{0,12},{4,0},{8,4},{12,8},{1,13},{5,1},{9,5},{13,9},{2,14},{6,2},{... | collective-permute-start | bytes 1572872 | tf_op jit(solution)/shard_map/ppermute | solution.py:328
  15.5 6.0 %collective-permute-start.3 = (bf16[512,512]{1,0:T(8,128)(2,1)S(1)}, bf16[512,512]{1,0:T(8,128)(2,1)}, u32[]{:S(2)}, u32[]{:S(2)}) collective-permute-start(bf16[512,512]{1,0:T(8,128)(2,1)S(1)} %pad_maximum_fusion.refs_2_.refs_4_), channel_id=1, source_target_pairs={{0,4},{4,8},{8,12},{12,0},{1,5},{5,9},{9,13},{13,1},{2,6},{6,10},{... | collective-permute-start | bytes 1572872 | tf_op jit(solution)/shard_map/ppermute | solution.py:328
  22.2 0.7 fusion.4
  22.9 0.1 copy.25
  23.0 0.1 squeeze.26
  23.1 0.1 copy.32
  23.2 0.1 copy.26
  23.3 0.1 squeeze.27
  23.4 1.0 pad.6
  24.4 0.1 fusion.2
  24.5 0.1 pad_maximum_fusion.2.refs_12_.latent_ref
  24.6 0.1 pad_add_fusion.1
  24.7 0.1 fusion.3
  24.8 0.1 pad_add_fusion.refs_20_.place_ref
  25.6 0.1 copy.28
  25.7 0.1 copy.27
  25.8 0.1 pad_maximum_fusion.1.refs_16_.weight_ref
  25.9 3.2 %collective-permute-done.4.refs_4_.refs_6_ = bf16[512,512]{1,0:T(8,128)(2,1)} collective-permute-done((bf16[512,512]{1,0:T(8,128)(2,1)S(1)}, bf16[512,512]{1,0:T(8,128)(2,1)}, u32[]{:S(2)}, u32[]{:S(2)}) %collective-permute-start.4) | collective-permute-done | bytes 524320 | tf_op jit(solution)/shard_map/ppermute | solution.py:328
  29.2 1.0 slice.35
  30.1 1.9 %collective-permute-start.6 = (bf16[512,256]{1,0:T(8,128)(2,1)S(1)}, bf16[512,256]{1,0:T(8,128)(2,1)S(1)}, u32[]{:S(2)}, u32[]{:S(2)}) collective-permute-start(bf16[512,256]{1,0:T(8,128)(2,1)S(1)} %slice.35), channel_id=1, source_target_pairs={{0,12},{4,0},{8,4},{12,8},{1,13},{5,1},{9,5},{13,9},{2,14},{6,2},{... | collective-permute-start | bytes 786440 | tf_op jit(solution)/shard_map/ppermute | solution.py:331
  32.1 0.0 collective-permute-done.3.refs_3_.refs_5_
  32.1 1.0 slice.34
  33.0 5.1 %collective-permute-start.5 = (bf16[512,256]{1,0:T(8,128)(2,1)S(1)}, bf16[512,256]{1,0:T(8,128)(2,1)S(1)}, u32[]{:S(2)}, u32[]{:S(2)}) collective-permute-start(bf16[512,256]{1,0:T(8,128)(2,1)S(1)} %slice.34), channel_id=1, source_target_pairs={{0,4},{4,8},{8,12},{12,0},{1,5},{5,9},{9,13},{13,1},{2,6},{6,10},{... | collective-permute-start | bytes 786440 | tf_op jit(solution)/shard_map/ppermute | solution.py:330
  38.2 0.1 pad_maximum_fusion.3.refs_19_.scale_ref
  38.3 7.7 %shard_map.113 = (f32[2,2,512]{2,1,0:T(2,128)S(1)}, f32[2,2,512]{2,1,0:T(2,128)S(1)}, f32[2,2,128,512]{3,2,1,0:T(8,128)}) custom-call(s32[3]{0:T(128)S(1)} %bitcast.40, s32[4]{0:T(128)S(1)} %get-tuple-element.24.slot_ref, bf16[512,256]{1,0:T(8,128)(2,1)} %bitcast.50, bf16[512,256]{1,0:T(8,128)(2,1)} %collective-permute-done.refs_1_, ...), custom_call_target="tpu_custom_call" | custom-call | flops 1610612736 | bytes 2097152 | tf_op jit(solution)/shard_map/pallas_call | solution.py:184
  46.1 0.7 copy-done.4
  46.7 0.1 copy-done.5
  46.8 0.1 copy-done.6
  46.9 11.7 %shard_map.114 = (f32[4,4,2,512]{3,2,1,0:T(2,128)S(1)}, f32[4,2,512]{2,1,0:T(2,128)S(1)}, f32[4,2,128,512]{3,2,1,0:T(8,128)}) custom-call(s32[4]{0:T(128)S(1)} %get-tuple-element.25.count_ref, s32[4]{0:T(128)S(1)} %get-tuple-element.24.slot_ref, bf16[512,256]{1,0:T(8,128)(2,1)} %bitcast.51, bf16[512,256]{1,0:T(8,128)(2,1)} %collective-permute-done.refs_1_, ...), custom_call_target="tpu_custom_call" | custom-call | flops 2684354560 | bytes 3145728 | tf_op jit(solution)/shard_map/pallas_call | solution.py:184
  58.7 10.8 %all_to_all.15.lse_ref = f32[4,4,2,512]{3,2,1,0:T(2,128)S(1)} all-to-all(f32[4,4,2,512]{3,2,1,0:T(2,128)S(1)} %get-tuple-element.11), channel_id=1, replica_groups=mesh['cfg'=2,'zh'=4,'x'=4,'y'=4,'zl'=4] {'zl'}, dimensions={0} | all-to-all | bytes 131072 | tf_op jit(solution)/shard_map/all_to_all | solution.py:367
  69.5 2.9 %shard_map.115 = bf16[8,16,24,128]{3,2,1,0:T(8,128)(2,1)S(1)} custom-call(f32[2]{0:T(128)S(1)} %pad_maximum_fusion.3.refs_19_.scale_ref, s32[2]{0:T(128)S(1)} %pad_add_fusion.refs_20_.place_ref, f32[4,4,2,512]{3,2,1,0:T(2,128)S(1)} %all_to_all.15.lse_ref, f32[4,2,512]{2,1,0:T(2,128)S(1)} %get-tuple-element.12.top_ref, ...), custom_call_target="tpu_custom_call" | custom-call | tf_op jit(solution)/shard_map/pallas_call | solution.py:251
  72.4 16.6 %all_to_all.16 = bf16[8,16,24,128]{3,2,1,0:T(8,128)(2,1)S(1)} all-to-all(bf16[8,16,24,128]{3,2,1,0:T(8,128)(2,1)S(1)} %shard_map.115), channel_id=1, replica_groups=mesh['cfg'=2,'zh'=4,'x'=4,'y'=4,'zl'=4] {'cfg','x'}, dimensions={0} | all-to-all | bytes 1572864 | tf_op jit(solution)/shard_map/all_to_all | solution.py:369
  89.0 0.8 reduce_sum.21
  89.8 12.5 %all-to-all-start.2 = ((bf16[16,24,128]{2,1,0:T(8,128)(2,1)}), bf16[16,24,128]{2,1,0:T(8,128)(2,1)S(1)}, u32[]{:S(2)}, u32[]{:S(2)}) async-start(bf16[16,24,128]{2,1,0:T(8,128)(2,1)} %reduce_sum.21), calls=%async_computation.2 | async-start | bytes 196608 | tf_op jit(solution)/shard_map/all_to_all | solution.py:371
  102.4 13.9 %all-to-all-done.2 = bf16[16,24,128]{2,1,0:T(8,128)(2,1)S(1)} async-done(((bf16[16,24,128]{2,1,0:T(8,128)(2,1)}), bf16[16,24,128]{2,1,0:T(8,128)(2,1)S(1)}, u32[]{:S(2)}, u32[]{:S(2)}) %all-to-all-start.2) | async-done | bytes 98336 | tf_op jit(solution)/shard_map/all_to_all | solution.py:371
  116.3 3.6 %collective-permute-start.8 = (bf16[24,128]{1,0:T(8,128)(2,1)S(1)}, bf16[24,128]{1,0:T(8,128)(2,1)S(1)}, u32[]{:S(2)}, u32[]{:S(2)}) collective-permute-start(bf16[24,128]{1,0:T(8,128)(2,1)S(1)} %subtract_convert_fusion.own_ref), channel_id=1, source_target_pairs={{0,2},{1,3},{2,4},{3,5},{4,6},{5,7},{6,8},{7,9},{8,10},{9,11},{10,... | collective-permute-start | bytes 18440 | tf_op jit(solution)/shard_map/ppermute | solution.py:376
  119.9 2.5 %collective-permute-start.7 = (bf16[24,128]{1,0:T(8,128)(2,1)S(1)}, bf16[24,128]{1,0:T(8,128)(2,1)S(1)}, u32[]{:S(2)}, u32[]{:S(2)}) collective-permute-start(bf16[24,128]{1,0:T(8,128)(2,1)S(1)} %subtract_convert_fusion.own_ref), channel_id=1, source_target_pairs={{0,1},{1,2},{2,3},{3,4},{4,5},{5,6},{6,7},{7,8},{8,9},{9,10},{10,1... | collective-permute-start | bytes 18440 | tf_op jit(solution)/shard_map/ppermute | solution.py:375
  122.3 0.1 dynamic-slice
  122.4 0.1 reshape.50
  122.5 0.7 copy.31
  123.2 0.4 collective-permute-done.8.older_ref
  123.6 4.5 %collective-permute-done.7.last_ref = bf16[24,128]{1,0:T(8,128)(2,1)S(1)} collective-permute-done((bf16[24,128]{1,0:T(8,128)(2,1)S(1)}, bf16[24,128]{1,0:T(8,128)(2,1)S(1)}, u32[]{:S(2)}, u32[]{:S(2)}) %collective-permute-start.7) | collective-permute-done | bytes 6176 | tf_op jit(solution)/shard_map/ppermute | solution.py:375
  128.1 1.2 shard_map.116
  (23 shorter events, 0.1 us)
Async XLA Ops:
  0.6 22.4 %copy-start = (bf16[4096,64]{0,1:T(8,128)(2,1)S(1)}, bf16[4096,64]{0,1:T(8,128)(2,1)}, u32[]{:S(2)}) copy-start(bf16[4096,64]{0,1:T(8,128)(2,1)} %param.16) | copy-start | bytes 1572868
  0.6 45.4 %collective-permute-start.2 = (bf16[512,256]{1,0:T(8,128)(2,1)}, bf16[512,256]{1,0:T(8,128)(2,1)S(1)}, u32[]{:S(2)}, u32[]{:S(2)}) collective-permute-start(bf16[512,256]{1,0:T(8,128)(2,1)} %bitcast.47), channel_id=1, source_target_pairs={{0,3},{1,2},{2,1},{3,0},{4,7},{5,6},{6,5},{7,4},{8,11},{9,10},{10,... | collective-permute-start | bytes 786440 | tf_op jit(solution)/shard_map/ppermute | solution.py:334
  7.3 38.7 %collective-permute-start.1 = (bf16[512,256]{1,0:T(8,128)(2,1)}, bf16[512,256]{1,0:T(8,128)(2,1)}, u32[]{:S(2)}, u32[]{:S(2)}) collective-permute-start(bf16[512,256]{1,0:T(8,128)(2,1)} %bitcast.48), channel_id=1, source_target_pairs={{0,2},{1,3},{2,0},{3,1},{4,6},{5,7},{6,4},{7,5},{8,10},{9,11},{10,... | collective-permute-start | bytes 786440 | tf_op jit(solution)/shard_map/ppermute | solution.py:334
  9.3 29.0 %collective-permute-start = (bf16[512,256]{1,0:T(8,128)(2,1)}, bf16[512,256]{1,0:T(8,128)(2,1)}, u32[]{:S(2)}, u32[]{:S(2)}) collective-permute-start(bf16[512,256]{1,0:T(8,128)(2,1)} %bitcast.49), channel_id=1, source_target_pairs={{0,1},{1,0},{2,3},{3,2},{4,5},{5,4},{6,7},{7,6},{8,9},{9,8},{10,11... | collective-permute-start | bytes 786440 | tf_op jit(solution)/shard_map/ppermute | solution.py:334
  11.7 13.8 %copy-start.2 = (f32[384]{0:T(512)S(1)}, f32[384]{0:T(512)}, u32[]{:S(2)}) copy-start(f32[384]{0:T(512)} %param.18) | copy-start | bytes 4612
  11.7 13.8 %copy-start.3 = (f32[384]{0:T(512)S(1)}, f32[384]{0:T(512)}, u32[]{:S(2)}) copy-start(f32[384]{0:T(512)} %param.19) | copy-start | bytes 4612
  12.8 12.8 %copy-start.1 = (bf16[512,512]{1,0:T(8,128)(2,1)}, bf16[512,512]{1,0:T(8,128)(2,1)S(1)}, u32[]{:S(2)}) copy-start(bf16[512,512]{1,0:T(8,128)(2,1)S(1)} %pad_maximum_fusion.refs_2_.refs_4_) | copy-start | bytes 1572868
  12.8 16.3 %collective-permute-start.4 = (bf16[512,512]{1,0:T(8,128)(2,1)S(1)}, bf16[512,512]{1,0:T(8,128)(2,1)}, u32[]{:S(2)}, u32[]{:S(2)}) collective-permute-start(bf16[512,512]{1,0:T(8,128)(2,1)S(1)} %pad_maximum_fusion.refs_2_.refs_4_), channel_id=1, source_target_pairs={{0,12},{4,0},{8,4},{12,8},{1,13},{5,1},{9,5},{13,9},{2,14},{6,2},{... | collective-permute-start | bytes 1572872 | tf_op jit(solution)/shard_map/ppermute | solution.py:328
  15.5 16.6 %collective-permute-start.3 = (bf16[512,512]{1,0:T(8,128)(2,1)S(1)}, bf16[512,512]{1,0:T(8,128)(2,1)}, u32[]{:S(2)}, u32[]{:S(2)}) collective-permute-start(bf16[512,512]{1,0:T(8,128)(2,1)S(1)} %pad_maximum_fusion.refs_2_.refs_4_), channel_id=1, source_target_pairs={{0,4},{4,8},{8,12},{12,0},{1,5},{5,9},{9,13},{13,1},{2,6},{6,10},{... | collective-permute-start | bytes 1572872 | tf_op jit(solution)/shard_map/ppermute | solution.py:328
  30.1 15.9 %collective-permute-start.6 = (bf16[512,256]{1,0:T(8,128)(2,1)S(1)}, bf16[512,256]{1,0:T(8,128)(2,1)S(1)}, u32[]{:S(2)}, u32[]{:S(2)}) collective-permute-start(bf16[512,256]{1,0:T(8,128)(2,1)S(1)} %slice.35), channel_id=1, source_target_pairs={{0,12},{4,0},{8,4},{12,8},{1,13},{5,1},{9,5},{13,9},{2,14},{6,2},{... | collective-permute-start | bytes 786440 | tf_op jit(solution)/shard_map/ppermute | solution.py:331
  33.0 13.0 %collective-permute-start.5 = (bf16[512,256]{1,0:T(8,128)(2,1)S(1)}, bf16[512,256]{1,0:T(8,128)(2,1)S(1)}, u32[]{:S(2)}, u32[]{:S(2)}) collective-permute-start(bf16[512,256]{1,0:T(8,128)(2,1)S(1)} %slice.34), channel_id=1, source_target_pairs={{0,4},{4,8},{8,12},{12,0},{1,5},{5,9},{9,13},{13,1},{2,6},{6,10},{... | collective-permute-start | bytes 786440 | tf_op jit(solution)/shard_map/ppermute | solution.py:330
  46.0 0.7 copy-start.4
  46.0 0.8 copy-start.5
  46.1 0.9 copy-start.6
  89.8 26.5 %all-to-all-start.2 = ((bf16[16,24,128]{2,1,0:T(8,128)(2,1)}), bf16[16,24,128]{2,1,0:T(8,128)(2,1)S(1)}, u32[]{:S(2)}, u32[]{:S(2)}) async-start(bf16[16,24,128]{2,1,0:T(8,128)(2,1)} %reduce_sum.21), calls=%async_computation.2 | async-start | bytes 196608 | tf_op jit(solution)/shard_map/all_to_all | solution.py:371
  116.3 7.3 %collective-permute-start.8 = (bf16[24,128]{1,0:T(8,128)(2,1)S(1)}, bf16[24,128]{1,0:T(8,128)(2,1)S(1)}, u32[]{:S(2)}, u32[]{:S(2)}) collective-permute-start(bf16[24,128]{1,0:T(8,128)(2,1)S(1)} %subtract_convert_fusion.own_ref), channel_id=1, source_target_pairs={{0,2},{1,3},{2,4},{3,5},{4,6},{5,7},{6,8},{7,9},{8,10},{9,11},{10,... | collective-permute-start | bytes 18440 | tf_op jit(solution)/shard_map/ppermute | solution.py:376
  119.9 8.2 %collective-permute-start.7 = (bf16[24,128]{1,0:T(8,128)(2,1)S(1)}, bf16[24,128]{1,0:T(8,128)(2,1)S(1)}, u32[]{:S(2)}, u32[]{:S(2)}) collective-permute-start(bf16[24,128]{1,0:T(8,128)(2,1)S(1)} %subtract_convert_fusion.own_ref), channel_id=1, source_target_pairs={{0,1},{1,2},{2,3},{3,4},{4,5},{5,6},{6,7},{7,8},{8,9},{9,10},{10,1... | collective-permute-start | bytes 18440 | tf_op jit(solution)/shard_map/ppermute | solution.py:375

commit v4 on v3

v4 whole, which is shorter than its diff:
```python
import functools
import math

import jax
import jax.numpy as jnp
from jax import lax
from jax.experimental import pallas as pl
from jax.experimental.pallas import tpu as pltpu
from jax.sharding import Mesh
from jax.sharding import PartitionSpec as P

DH = 128
STEPS = 50
GUIDE = 5.0
SHIFT_FACTOR = 5.0
NEG_FILL = -1e30
EPSILON = 1e-06
SIDE = 4
TOK = 512
ROWS, TCOLS = 16, 32
PATCH = 64
CHUNK = 2 * PATCH + 16
CUT = 24
LOG2_SCALE = math.log2(math.e) / math.sqrt(DH)

VMEM = pl.BlockSpec(memory_space=pltpu.VMEM)
SMEM = pl.BlockSpec(memory_space=pltpu.SMEM)
HBM = pl.BlockSpec(memory_space=pltpu.HBM)
ANY = pl.BlockSpec(memory_space=pl.ANY)


def in_hbm(value):
    return pltpu.with_memory_space_constraint(value, pltpu.HBM)


def noise_level(timestep, total_steps):
    frac = 1.0 - timestep.astype(jnp.float32) / total_steps
    return SHIFT_FACTOR * frac / (1.0 + (SHIFT_FACTOR - 1.0) * frac)


def ring(steps):
    return [(i, (i + steps) % SIDE) for i in range(SIDE)]


def crossed(mask):
    return [(i, i ^ mask) for i in range(SIDE)]


def moved(steps):
    count = SIDE * SIDE
    return [(i, i + steps) for i in range(count) if 0 <= i + steps < count]


def prepare_kernel(keys_ref, values_ref, out_ref, values, turned, sems):
    first = pltpu.make_async_copy(keys_ref, out_ref.at[pl.ds(0, TOK)], sems.at[0])
    second = pltpu.make_async_copy(values_ref, values, sems.at[1])
    first.start()
    second.start()
    second.wait()
    for half in range(2):
        rows = slice(half * 2 * DH, (half + 1) * 2 * DH)
        turned[rows] = jnp.transpose(values[rows])
    third = pltpu.make_async_copy(turned, out_ref.at[pl.ds(TOK, TOK)], sems.at[1])
    third.start()
    first.wait()
    third.wait()


def prepared(keys, values):
    return pl.pallas_call(
        prepare_kernel,
        out_shape=pltpu.HBM((2 * TOK, 2 * DH), jnp.bfloat16),
        in_specs=[HBM] * 2,
        out_specs=HBM,
        scratch_shapes=[pltpu.VMEM((TOK, 2 * DH), jnp.bfloat16)] * 2
        + [pltpu.SemaphoreType.DMA((2,))],
    )(in_hbm(keys), in_hbm(values))


def attention_kernel(count_ref, *refs, nq, whole, split, carry, nx, last):
    refs = list(refs)

    def take(size):
        taken = refs[:size]
        del refs[:size]
        return taken

    nk = whole + split
    q_refs, kv_refs = take(nq), take(whole + 2 * split)
    weight_hbm = take(1)[0] if last else None
    if carry:
        top_in, denom_in, acc_in = take(3)
    take(nx)
    if last:
        chunk_refs = take(nq)
        qs, ks, vs, scores, sems, acc_ref, top_ref, denom, weight_ref = refs
    else:
        top_ref, denom, acc_out = take(3)
        qs, ks, vs, scores, sems, acc_ref = refs

    sem = iter(range(64))

    def copied(source, target):
        copy = pltpu.make_async_copy(source, target, sems.at[next(sem)])
        copy.start()
        return copy

    arriving = []
    for b in range(nk):
        if b < whole:
            keys, values = kv_refs[b].at[pl.ds(0, TOK)], kv_refs[b].at[pl.ds(TOK, TOK)]
        else:
            keys, values = kv_refs[whole], kv_refs[whole + 1]
        group = [copied(keys, ks.at[b])]
        for half in range(2):
            for h in range(2):
                group.append(
                    copied(
                        values.at[pl.ds(half * 2 * DH + h * DH, DH)],
                        vs.at[b, h, pl.ds(0, DH), pl.ds(half * 2 * DH, 2 * DH)],
                    )
                )
        if b == 0:
            group += [copied(q_refs[j], qs.at[j]) for j in range(nq)]
            if carry:
                group.append(copied(acc_in, acc_ref))
        arriving.append(group)
    if last:
        arriving[0].append(copied(weight_hbm, weight_ref))
    if carry:
        top_ref[...] = top_in[...]
        denom[...] = denom_in[...]
    else:
        top_ref[...] = jnp.full((nq, 2, TOK), NEG_FILL, jnp.float32)
        denom[...] = jnp.zeros((nq, 2, TOK), jnp.float32)
        acc_ref[...] = jnp.zeros((nq, 2, DH, TOK), jnp.float32)
    for b in range(nk):
        for h in range(2):
            vs[b, h, DH:] = jnp.ones((16, TOK), jnp.bfloat16)
    for copy in arriving[0]:
        copy.wait()

    def scored(j, b, h):
        return lax.dot_general(
            ks[b, :, h * DH : (h + 1) * DH],
            qs[j, :, h * DH : (h + 1) * DH],
            (((1,), (1,)), ((), ())),
            preferred_element_type=jnp.float32,
        )

    def folded(j, b, h, score, masked):
        if masked:
            valid = lax.broadcasted_iota(jnp.int32, (TOK, TOK), 0) < count_ref[b]
            score = jnp.where(valid, score, NEG_FILL)
        old = top_ref[j, h : h + 1]
        new = jnp.maximum(old, jnp.max(score, axis=0, keepdims=True))
        weights = jnp.exp2((score - new) * LOG2_SCALE)
        if masked:
            weights = jnp.where(valid, weights, 0.0)
        factor = jnp.exp2((old - new) * LOG2_SCALE)
        top_ref[j, h : h + 1] = new
        mixed = jnp.dot(vs[b, h], weights.astype(jnp.bfloat16), preferred_element_type=jnp.float32)
        denom[j, h : h + 1] = denom[j, h : h + 1] * factor + mixed[DH : DH + 1]
        acc_ref[j, h] = acc_ref[j, h] * factor + mixed[:DH]

    total = nq * nk

    def step(t, _):
        j, b = lax.div(t, nk), lax.rem(t, nk)
        later = jnp.minimum(t + 1, total - 1)
        next_j, next_b = lax.div(later, nk), lax.rem(later, nk)
        count = count_ref[b]
        for needed in range(1, nk):

            @pl.when(t == needed - 1)
            def _():
                for copy in arriving[needed]:
                    copy.wait()

        def update(masked):
            scores[1] = scored(j, b, 1)
            folded(j, b, 0, scores[0], masked)
            scores[0] = scored(next_j, next_b, 0)
            folded(j, b, 1, scores[1], masked)

        @pl.when(count >= TOK)
        def _():
            update(False)

        @pl.when((count > 0) & (count < TOK))
        def _():
            update(True)

        @pl.when(count <= 0)
        def _():
            scores[0] = scored(next_j, next_b, 0)

        return 0

    scores[0] = scored(0, 0, 0)
    lax.fori_loop(0, total, step, 0)
    if not last:
        copy = pltpu.make_async_copy(acc_ref, acc_out, sems.at[0])
        copy.start()
        copy.wait()
        return
    for j in range(nq):
        parts, rows = [], []
        for h in range(2):
            mixed = (acc_ref[j, h] * (1.0 / denom[j, h : h + 1])).astype(jnp.bfloat16)
            parts.append(jnp.dot(weight_ref[h], mixed, preferred_element_type=jnp.float32))
            stat = top_ref[j, h : h + 1] * LOG2_SCALE + jnp.log2(denom[j, h : h + 1])
            for _ in range(3):
                piece = stat.astype(jnp.bfloat16).astype(jnp.float32)
                rows.append(piece)
                stat = stat - piece
        blank = jnp.zeros((CHUNK - 2 * PATCH - 6, TOK), jnp.float32)
        chunk_refs[j][...] = jnp.concatenate(parts + rows + [blank], 0).astype(jnp.bfloat16)


def attend(counts, queries, blocks, pair=(), weight=None, state=(), extras=()):
    f32, bf16 = jnp.float32, jnp.bfloat16
    nq, whole, split, last = len(queries), len(blocks), len(pair) // 2, weight is not None
    nk = whole + split
    stat = jax.ShapeDtypeStruct((nq, 2, TOK), f32)
    chunk = jax.ShapeDtypeStruct((CHUNK, TOK), bf16)
    acc = pltpu.HBM((nq, 2, DH, TOK), f32)
    scratch = [
        pltpu.VMEM((nq, TOK, 2 * DH), bf16),
        pltpu.VMEM((nk, TOK, 2 * DH), bf16),
        pltpu.VMEM((nk, 2, DH + 16, TOK), bf16),
        pltpu.VMEM((2, TOK, TOK), f32),
        pltpu.SemaphoreType.DMA((5 * nk + nq + 2,)),
        pltpu.VMEM((nq, 2, DH, TOK), f32),
    ]
    if last:
        scratch += [pltpu.VMEM((nq, 2, TOK), f32)] * 2 + [pltpu.VMEM((2, PATCH, DH), bf16)]
    work = nq * nk * 2 * TOK * TOK
    return pl.pallas_call(
        functools.partial(
            attention_kernel,
            nq=nq,
            whole=whole,
            split=split,
            carry=bool(state),
            nx=len(extras),
            last=last,
        ),
        out_shape=(chunk,) * nq if last else (stat, stat, acc),
        in_specs=[SMEM]
        + [HBM] * (nq + whole + len(pair) + last)
        + ([VMEM, VMEM, HBM] if state else [])
        + [ANY] * len(extras),
        out_specs=(VMEM,) * nq if last else (VMEM, VMEM, HBM),
        scratch_shapes=scratch,
        compiler_params=pltpu.CompilerParams(vmem_limit_bytes=24 * 2**20),
        cost_estimate=pl.CostEstimate(
            flops=work * DH * 4, transcendentals=work, bytes_accessed=(nq + 2 * nk) * TOK * 4 * DH
        ),
    )(
        counts,
        *(in_hbm(x) for x in (*queries, *blocks, *pair)),
        *((in_hbm(weight),) if last else ()),
        *(in_hbm(x) if x.ndim == 4 else x for x in state),
        *extras,
    )


def combine_kernel(scale_ref, place_ref, *refs):
    chunk_refs, (latent_ref, out_ref) = refs[:4], refs[4:]
    stats = []
    for h in range(2):
        base = 2 * PATCH + 3 * h
        pieces = [ref[2 * PATCH :].astype(jnp.float32) for ref in chunk_refs]
        at = base - 2 * PATCH
        stats.append([x[at : at + 1] + x[at + 1 : at + 2] + x[at + 2 : at + 3] for x in pieces])
    values = jnp.zeros((PATCH, TOK), jnp.float32)
    for h in range(2):
        peak = jnp.maximum(
            jnp.maximum(stats[h][0], stats[h][1]), jnp.maximum(stats[h][2], stats[h][3])
        )
        shares = [jnp.exp2(stat - peak) for stat in stats[h]]
        norm = scale_ref[0] / (shares[0] + shares[1] + shares[2] + shares[3])
        for ref, share in zip(chunk_refs, shares):
            values += ref[h * PATCH : (h + 1) * PATCH].astype(jnp.float32) * (share * norm)
    values = jnp.transpose(jnp.concatenate([values[32:], values, values[:32]], 0))
    values = values.reshape(ROWS, TCOLS, 128)
    lane = lax.broadcasted_iota(jnp.int32, (ROWS, TCOLS, 128), 2)
    blank = jnp.zeros((1, TCOLS, 128), jnp.float32)
    above = jnp.concatenate([blank, values[:-1]], 0)
    below = jnp.concatenate([values[1:], blank], 0)
    window = jnp.where(lane < 32, above, jnp.where(lane < 96, values, below))
    for row in range(ROWS):
        for half in range(2):
            cut = window[row, half * 8 : half * 8 + CUT]
            out_ref[half * ROWS + row] = cut.astype(jnp.bfloat16)
    band = place_ref[0]
    edge = pltpu.roll(latent_ref[...], 64, 1) * scale_ref[1]
    lane = lax.broadcasted_iota(jnp.int32, (TCOLS, 128), 1)
    for target, part in ((band + 1, lane < 32), (band - 1, lane >= 96)):

        @pl.when((target >= 0) & (target < ROWS))
        def _():
            sent = jnp.where(part, edge, 0.0)
            for half in range(2):
                at = half * ROWS + target
                out_ref[at] = (
                    out_ref[at].astype(jnp.float32) + sent[half * 8 : half * 8 + CUT]
                ).astype(jnp.bfloat16)


def combine(scale, place, chunks, latent):
    return pl.pallas_call(
        combine_kernel,
        out_shape=jax.ShapeDtypeStruct((2 * ROWS, CUT, 128), jnp.bfloat16),
        in_specs=[SMEM, SMEM] + [VMEM] * 5,
        out_specs=VMEM,
        compiler_params=pltpu.CompilerParams(vmem_limit_bytes=16 * 2**20),
    )(scale, place, *chunks, latent)


def decode_kernel(half_ref, own_ref, last_ref, older_ref, even_ref, odd_ref, bias_ref, gain_ref, out_ref):
    left = half_ref[0] == 0
    blank = jnp.zeros((1, 128), jnp.float32)
    even, odd = [], []
    for ref in (older_ref, last_ref, own_ref):
        block = ref[...].astype(jnp.float32)
        here = jnp.where(left, block[0:16], block[8:24])
        before = jnp.where(left, jnp.concatenate([blank, block[0:15]], 0), block[7:23])
        after = jnp.where(left, block[1:17], jnp.concatenate([block[9:24], blank], 0))
        rows = [
            jnp.concatenate([x, pltpu.roll(x, 96, 1)], 0).astype(jnp.bfloat16)
            for x in (before, here, after)
        ]
        even += rows[0:2]
        odd += rows[1:3]
    finished = []
    for parts, weight_ref in ((even, even_ref), (odd, odd_ref)):
        features = (
            jnp.dot(
                jnp.concatenate(parts, 1), weight_ref[...], preferred_element_type=jnp.float32
            )
            + bias_ref[...]
        )
        power = jnp.mean(features * features, axis=1, keepdims=True)
        scaled = features * lax.rsqrt(power + EPSILON) * gain_ref[...]
        finished.append((scaled / (1.0 + jnp.exp(-scaled))).astype(jnp.bfloat16))
    target = lax.broadcasted_iota(jnp.int32, (32, 32), 0)
    source = lax.broadcasted_iota(jnp.int32, (32, 32), 1)
    order = ((target & 1) * 16 + (target >> 1) == source).astype(jnp.float32).astype(jnp.bfloat16)
    for row in range(2):
        both = jnp.concatenate([x[row * 16 : row * 16 + 16] for x in finished], 0)
        out_ref[row] = jnp.dot(order, both, preferred_element_type=jnp.float32).astype(jnp.bfloat16)


def decode(half, own, last, older, even, odd, bias, gain):
    chans = bias.shape[1]
    return pl.pallas_call(
        decode_kernel,
        out_shape=jax.ShapeDtypeStruct((2, 32, chans), jnp.bfloat16),
        in_specs=[SMEM] + [VMEM] * 7,
        out_specs=VMEM,
        compiler_params=pltpu.CompilerParams(vmem_limit_bytes=32 * 2**20),
    )(half, own, last, older, even, odd, bias, gain)


def conv_matrices(conv_weight):
    taps, _, _, chans, outs = conv_weight.shape
    padded = jnp.pad(conv_weight, ((0, 0), (0, 1), (0, 0), (0, 0), (0, 0)))
    blank = jnp.zeros((taps, 4, 1, chans, outs), conv_weight.dtype)
    both = []
    for parts in ([blank, padded], [padded, blank]):
        spread = jnp.concatenate(parts, 2).reshape(taps, 4, 2, 2, chans, outs)
        both.append(spread.transpose(0, 2, 1, 3, 4, 5).reshape(taps * 16 * chans, outs))
    return both


def local(
    query, keys, values, lengths, timestep, latent, head_weight, conv_weight, conv_bias, gain
):
    cfg, zh, x = lax.axis_index("cfg"), lax.axis_index("zh"), lax.axis_index("x")
    y, zl = lax.axis_index("y"), lax.axis_index("zl")
    seq = ("y", "zl")

    own = prepared(keys[0], values[0])
    before, after = lax.ppermute(own, "y", ring(1)), lax.ppermute(own, "y", ring(-1))
    pair = [
        lax.ppermute(before[:TOK], "y", ring(1)),
        lax.ppermute(after[TOK:], "y", ring(-1)),
    ]
    blocks = [own, before, after]
    queries = [query[0]] + [lax.ppermute(query[0], "zl", crossed(m)) for m in (1, 2, 3)]
    block = jnp.stack([((y - d) % SIDE) * SIDE + zl for d in (0, 1, 3, 2)])
    counts = jnp.clip(lengths[0] - block * TOK, 0, TOK).astype(jnp.int32)

    rows = latent[0].reshape(2, TCOLS, 32)
    blank = jnp.zeros((TCOLS, 32), jnp.float32)
    grid = jnp.concatenate([blank, rows[0], rows[1], blank], 1)
    latent_window = lax.dynamic_slice_in_dim(grid, cfg * 8, CUT, 0)
    even, odd = conv_matrices(conv_weight)
    bias_row, gain_row = conv_bias.reshape(1, -1), gain.reshape(1, -1)
    part = lax.dynamic_slice_in_dim(head_weight, (zh * SIDE + x) * 2 * DH, 2 * DH, 0)
    weight = part.T.reshape(PATCH, 2, DH).transpose(1, 0, 2)
    sigma = noise_level(timestep[0], STEPS)
    scale = jnp.stack(
        [
            jnp.where(cfg == 0, GUIDE, 1.0 - GUIDE).astype(jnp.float32),
            jnp.where(cfg == 0, -1.0 / sigma, 0.0),
        ]
    )
    place = jnp.stack([zh * SIDE + x, zl]).astype(jnp.int32)

    near = attend(counts[:3], queries[:2], blocks)
    constants = (grid, latent_window, even, odd, bias_row, gain_row)
    (third,) = attend(counts, queries[3:], blocks, pair, weight, extras=constants)
    (second,) = attend(counts, queries[2:3], blocks, pair, weight, extras=(third,))
    mine, first = attend(counts[3:], queries[:2], [], pair, weight, near, (second,))
    chunks = [mine] + [
        lax.ppermute(chunk, "zl", crossed(m)) for m, chunk in ((3, third), (2, second), (1, first))
    ]
    shares = combine(scale, place, chunks, grid)
    shares = lax.all_to_all(shares, ("cfg", "zh", "x"), 0, 0, tiled=True)
    window = jnp.sum(shares.astype(jnp.float32), 0)

    current = (latent_window - sigma * window).astype(jnp.bfloat16)
    last = lax.ppermute(current, seq, moved(1))
    older = lax.ppermute(current, seq, moved(2))
    cells = lax.dynamic_slice_in_dim(window, cfg * 8, TCOLS // 2, 0)[:, 32:96]
    velocity = cells.reshape(TCOLS // 2, 2, 2, -1).transpose(1, 0, 2, 3).reshape(1, 2, TCOLS, -1)
    decoded = decode(
        cfg.astype(jnp.int32).reshape(1),
        current,
        last,
        older,
        even,
        odd,
        bias_row,
        gain_row,
    )
    return (velocity, decoded[None])


def solution(mesh):
    split = Mesh(
        mesh.devices.reshape(2, SIDE, SIDE, SIDE, SIDE), ("cfg", "zh", "x", "y", "zl")
    )
    seq, band = ("y", "zl"), ("zh", "x")
    tokens = P("cfg", seq, band)
    return jax.shard_map(
        local,
        mesh=split,
        in_specs=(
            tokens,
            tokens,
            tokens,
            P(),
            P(),
            P(seq, band, None, None),
            P(),
            P(),
            P(),
            P(),
        ),
        out_specs=(P(seq, band, "cfg", None), P(seq, band, "cfg", None)),
        check_vma=False,
    )
```

time: 130 us -> 131 us (level)
  blocking collectives: 27.5 us -> 0 us
  Pallas kernels: 23.5 us -> 35.5 us
  starting transfers between devices: 45.2 us -> 56.8 us
  waiting for transfers between devices: 22.1 us -> 26.4 us
  local copies, waits for them, and re-layouts: 6.24 us -> 8.66 us
  other arithmetic: 2.3 us -> 0.37 us
    all_to_all x2 -> x0, blocking collectives: 27.5 us -> none  [the longest x1 16.6 us: local(): shares = lax.all_to_all(shares, ('cfg', 'x'), 0, 0, tiled=True)]
    pallas_call x3 -> x6, Pallas kernels: 22.3 us -> 34.3 us  [the longest x4 23.8 us: attend(): pl.pallas_call(functools.partial(attention_kernel, nq=nq, whole=whole, sp...]
    ppermute x2 -> x5, starting transfers between devices: 7.05 us -> 16.6 us  [the longest x3 9.57 us: local(): lax.ppermute(chunk, 'zl', crossed(m))]
    all_to_all x1, waiting for transfers between devices: 13.9 us -> 19.1 us  [local(): shares = lax.all_to_all(shares, ('cfg', 'zh', 'x'), 0, 0, tiled=True)]
    ppermute x1, waiting for transfers between devices: 4.48 us -> 0.01 us  [local(): last = lax.ppermute(current, seq, moved(1))]
    ppermute x1, waiting for transfers between devices: 0.41 us -> 4.32 us  [local(): older = lax.ppermute(current, seq, moved(2))]
    ppermute x1, waiting for transfers between devices: 3.25 us -> 0.01 us  [local(): lax.ppermute(own, 'y', ring(-1))]
    ppermute x2 -> x5, waiting for transfers between devices: 0.01 us -> 2.96 us  [the longest x3 2.96 us: local(): lax.ppermute(chunk, 'zl', crossed(m))]
  transfers between devices with their start and end apart: 10 -> 13, of which waited for: 4 -> 3; matrix products, arithmetic and copies ran while one was open for 5% -> 4% of each run, Pallas kernels for 6% -> 18%
where the time goes in v4:
time: 131 us; the launch traced here: 130 us
  starting transfers between devices  56.8 us (43%)
  Pallas kernels  35.5 us (27%)
  waiting for transfers between devices  26.4 us (20%)
  local copies, waits for them, and re-layouts  8.66 us (7%)
  between operations  2.42 us (2%)
    pallas_call x4, Pallas kernels, attend(): pl.pallas_call(functools.partial(attention_kernel, nq=nq, whole=whole, sp...  23.8 us
    all_to_all x1, waiting for transfers between devices, local(): shares = lax.all_to_all(shares, ('cfg', 'zh', 'x'), 0, 0, tiled=True)  19.1 us
    all_to_all x1, starting transfers between devices, local(): shares = lax.all_to_all(shares, ('cfg', 'zh', 'x'), 0, 0, tiled=True)  13.2 us
    ppermute x3, starting transfers between devices, local(): lax.ppermute(query[0], 'zl', crossed(m))  10.1 us
    ppermute x3, starting transfers between devices, local(): lax.ppermute(chunk, 'zl', crossed(m))  9.57 us
    pallas_call x1, Pallas kernels, prepared(): pl.pallas_call(prepare_kernel, out_shape=pltpu.HBM((2 * TOK, 2 * DH), jnp...  9.06 us
    ppermute x1, starting transfers between devices, local(): lax.ppermute(own, 'y', ring(1))  7.64 us
    ppermute x1, starting transfers between devices, local(): last = lax.ppermute(current, seq, moved(1))  5.32 us
  transfers between devices with their start and end apart: 13, of which 3 were waited for; matrix products, arithmetic and copies ran while one was open for 4% of the time, Pallas kernels for 18%

profile of v4, /device:TPU:24, one launch (start us, length us, event | category | flops | bytes accessed | tf_op | source)
XLA Modules:
  0.0 130.2 jit_solution(16841081025910476894)
XLA Ops:
  0.6 0.0 copy-start
  0.7 9.1 %shard_map.113.refs_2_.refs_1_ = bf16[1024,256]{1,0:T(8,128)(2,1)} custom-call(bf16[512,256]{1,0:T(8,128)(2,1)} %bitcast.53, bf16[512,256]{1,0:T(8,128)(2,1)} %bitcast.54), custom_call_target="tpu_custom_call" | custom-call | tf_op jit(solution)/shard_map/pallas_call | solution.py:70
  9.7 7.6 %collective-permute-start.1 = (bf16[1024,256]{1,0:T(8,128)(2,1)}, bf16[1024,256]{1,0:T(8,128)(2,1)S(1)}, u32[]{:S(2)}, u32[]{:S(2)}) collective-permute-start(bf16[1024,256]{1,0:T(8,128)(2,1)} %shard_map.113.refs_2_.refs_1_), channel_id=1, source_target_pairs={{0,4},{4,8},{8,12},{12,0},{1,5},{5,9},{9,13},{13,1},{2,6},{6,10},{... | collective-permute-start | bytes 1572872 | tf_op jit(solution)/shard_map/ppermute | solution.py:386
  17.4 1.9 %collective-permute-start.3 = (bf16[1024,256]{1,0:T(8,128)(2,1)}, bf16[1024,256]{1,0:T(8,128)(2,1)}, u32[]{:S(2)}, u32[]{:S(2)}) collective-permute-start(bf16[1024,256]{1,0:T(8,128)(2,1)} %shard_map.113.refs_2_.refs_1_), channel_id=1, source_target_pairs={{0,12},{4,0},{8,4},{12,8},{1,13},{5,1},{9,5},{13,9},{2,14},{6,2},{... | collective-permute-start | bytes 1572872 | tf_op jit(solution)/shard_map/ppermute | solution.py:386
  19.3 3.0 %collective-permute-start.6 = (bf16[512,256]{1,0:T(8,128)(2,1)S(1)}, bf16[512,256]{1,0:T(8,128)(2,1)}, u32[]{:S(2)}, u32[]{:S(2)}) collective-permute-start(bf16[512,256]{1,0:T(8,128)(2,1)S(1)} %bitcast.50), channel_id=1, source_target_pairs={{0,3},{1,2},{2,1},{3,0},{4,7},{5,6},{6,5},{7,4},{8,11},{9,10},{10,... | collective-permute-start | bytes 786440 | tf_op jit(solution)/shard_map/ppermute | solution.py:392
  22.3 1.9 %collective-permute-start.5 = (bf16[512,256]{1,0:T(8,128)(2,1)S(1)}, bf16[512,256]{1,0:T(8,128)(2,1)}, u32[]{:S(2)}, u32[]{:S(2)}) collective-permute-start(bf16[512,256]{1,0:T(8,128)(2,1)S(1)} %bitcast.51), channel_id=1, source_target_pairs={{0,2},{1,3},{2,0},{3,1},{4,6},{5,7},{6,4},{7,5},{8,10},{9,11},{10,... | collective-permute-start | bytes 786440 | tf_op jit(solution)/shard_map/ppermute | solution.py:392
  24.2 5.2 %collective-permute-start = (bf16[512,256]{1,0:T(8,128)(2,1)S(1)}, bf16[512,256]{1,0:T(8,128)(2,1)S(1)}, u32[]{:S(2)}, u32[]{:S(2)}) collective-permute-start(bf16[512,256]{1,0:T(8,128)(2,1)S(1)} %bitcast.52), channel_id=1, source_target_pairs={{0,1},{1,0},{2,3},{3,2},{4,5},{5,4},{6,7},{7,6},{8,9},{9,8},{10,11... | collective-permute-start | bytes 786440 | tf_op jit(solution)/shard_map/ppermute | solution.py:392
  29.5 0.1 copy.18
  29.6 0.1 squeeze.26
  29.7 0.1 copy.19
  29.7 0.1 squeeze.27
  29.8 0.1 pad_maximum_fusion.refs_7_.refs_4_
  29.9 0.6 bitcast_bitcast_fusion.refs_6_.refs_4_
  31.3 0.2 fusion.2
  31.4 0.8 copy-done.6
  32.2 0.7 slice.30
  32.9 5.1 %collective-permute-start.2 = (bf16[512,256]{1,0:T(8,128)(2,1)}, bf16[512,256]{1,0:T(8,128)(2,1)S(1)}, u32[]{:S(2)}, u32[]{:S(2)}) collective-permute-start(bf16[512,256]{1,0:T(8,128)(2,1)} %slice.30), channel_id=1, source_target_pairs={{0,4},{4,8},{8,12},{12,0},{1,5},{5,9},{9,13},{13,1},{2,6},{6,10},{... | collective-permute-start | bytes 786440 | tf_op jit(solution)/shard_map/ppermute | solution.py:388
  38.1 1.7 %slice.31 = bf16[512,256]{1,0:T(8,128)(2,1)} slice(bf16[1024,256]{1,0:T(8,128)(2,1)} %collective-permute-done.3.refs_4_.refs_3_), slice={[512:1024], [0:256]} | slice | bytes 524288 | tf_op jit(solution)/shard_map/slice | solution.py:389
  39.7 1.9 %collective-permute-start.4 = (bf16[512,256]{1,0:T(8,128)(2,1)}, bf16[512,256]{1,0:T(8,128)(2,1)S(1)}, u32[]{:S(2)}, u32[]{:S(2)}) collective-permute-start(bf16[512,256]{1,0:T(8,128)(2,1)} %slice.31), channel_id=1, source_target_pairs={{0,12},{4,0},{8,4},{12,8},{1,13},{5,1},{9,5},{13,9},{2,14},{6,2},{... | collective-permute-start | bytes 786440 | tf_op jit(solution)/shard_map/ppermute | solution.py:389
  41.6 0.1 fusion.1.count_ref
  41.7 0.1 copy.20
  41.8 0.1 copy.21
  41.9 0.6 copy-done.8
  42.5 0.7 copy-done.9
  43.2 0.6 slice.23.count_ref
  44.5 0.7 copy-done.3
  45.2 7.9 %shard_map.114 = (f32[2,2,512]{2,1,0:T(2,128)S(1)}, f32[2,2,512]{2,1,0:T(2,128)S(1)}, f32[2,2,128,512]{3,2,1,0:T(8,128)}) custom-call(s32[3]{0:T(128)S(1)} %bitcast.45, bf16[512,256]{1,0:T(8,128)(2,1)} %bitcast.48, bf16[512,256]{1,0:T(8,128)(2,1)} %copy-done.3, bf16[1024,256]{1,0:T(8,128)(2,1)} %shard_map.113.refs_2_.refs_1_, bf16[1024,256]{1,0:T(8,128)(2,1)} %copy-done.6, ...), custom_call_target="tpu_custom_call" | custom-call | flops 1610612736 | bytes 2097152 | tf_op jit(solution)/shard_map/pallas_call | solution.py:239
  53.2 0.7 copy-done.4
  53.8 0.1 copy-done.5
  53.9 5.8 %shard_map.115.refs_7_ = bf16[144,512]{1,0:T(8,128)(2,1)S(1)} custom-call(s32[4]{0:T(128)S(1)} %fusion.1.count_ref, bf16[512,256]{1,0:T(8,128)(2,1)} %collective-permute-done.6.refs_0_, bf16[1024,256]{1,0:T(8,128)(2,1)} %shard_map.113.refs_2_.refs_1_, bf16[1024,256]{1,0:T(8,128)(2,1)} %copy-done.6, bf16[1024,256]{1,0:T(8,128)(2,1)} %collective-permute-done.3.refs_4_.refs_3_, ...), custom_call_target="tpu_custom_call" | custom-call | flops 1073741824 | bytes 2359296 | tf_op jit(solution)/shard_map/pallas_call | solution.py:239
  59.8 1.9 %collective-permute-start.7 = (bf16[144,512]{1,0:T(8,128)(2,1)S(1)}, bf16[144,512]{1,0:T(8,128)(2,1)S(1)}, u32[]{:S(2)}, u32[]{:S(2)}) collective-permute-start(bf16[144,512]{1,0:T(8,128)(2,1)S(1)} %shard_map.115.refs_7_), channel_id=1, source_target_pairs={{0,3},{1,2},{2,1},{3,0},{4,7},{5,6},{6,5},{7,4},{8,11},{9,10},{10,... | collective-permute-start | bytes 442376 | tf_op jit(solution)/shard_map/ppermute | solution.py:419
  61.7 5.8 %shard_map.116.refs_8_ = bf16[144,512]{1,0:T(8,128)(2,1)S(1)} custom-call(s32[4]{0:T(128)S(1)} %fusion.1.count_ref, bf16[512,256]{1,0:T(8,128)(2,1)} %collective-permute-done.5.refs_0_, bf16[1024,256]{1,0:T(8,128)(2,1)} %shard_map.113.refs_2_.refs_1_, bf16[1024,256]{1,0:T(8,128)(2,1)} %copy-done.6, bf16[1024,256]{1,0:T(8,128)(2,1)} %collective-permute-done.3.refs_4_.refs_3_, ...), custom_call_target="tpu_custom_call" | custom-call | flops 1073741824 | bytes 2359296 | tf_op jit(solution)/shard_map/pallas_call | solution.py:239
  67.5 1.9 %collective-permute-start.8 = (bf16[144,512]{1,0:T(8,128)(2,1)S(1)}, bf16[144,512]{1,0:T(8,128)(2,1)S(1)}, u32[]{:S(2)}, u32[]{:S(2)}) collective-permute-start(bf16[144,512]{1,0:T(8,128)(2,1)S(1)} %shard_map.116.refs_8_), channel_id=1, source_target_pairs={{0,2},{1,3},{2,0},{3,1},{4,6},{5,7},{6,4},{7,5},{8,10},{9,11},{10,... | collective-permute-start | bytes 442376 | tf_op jit(solution)/shard_map/ppermute | solution.py:419
  69.5 4.2 %shard_map.117 = (bf16[144,512]{1,0:T(8,128)(2,1)S(1)}, bf16[144,512]{1,0:T(8,128)(2,1)S(1)}) custom-call(s32[1]{0:T(128)} %slice.23.count_ref, bf16[512,256]{1,0:T(8,128)(2,1)} %bitcast.49, bf16[512,256]{1,0:T(8,128)(2,1)} %copy-done.3, bf16[512,256]{1,0:T(8,128)(2,1)} %copy-done.4, bf16[512,256]{1,0:T(8,128)(2,1)} %copy-done.5, ...), custom_call_target="tpu_custom_call" | custom-call | flops 536870912 | bytes 1048576 | tf_op jit(solution)/shard_map/pallas_call | solution.py:239
  73.7 5.7 %collective-permute-start.9 = (bf16[144,512]{1,0:T(8,128)(2,1)S(1)}, bf16[144,512]{1,0:T(8,128)(2,1)S(1)}, u32[]{:S(2)}, u32[]{:S(2)}) collective-permute-start(bf16[144,512]{1,0:T(8,128)(2,1)S(1)} %get-tuple-element.11), channel_id=1, source_target_pairs={{0,1},{1,0},{2,3},{3,2},{4,5},{5,4},{6,7},{7,6},{8,9},{9,8},{10,11... | collective-permute-start | bytes 442376 | tf_op jit(solution)/shard_map/ppermute | solution.py:419
  79.5 0.1 pad_maximum_fusion.1.scale_ref
  79.5 0.1 pad_add_fusion.place_ref
  79.6 3.0 %collective-permute-done.9.refs_3_ = bf16[144,512]{1,0:T(8,128)(2,1)S(1)} collective-permute-done((bf16[144,512]{1,0:T(8,128)(2,1)S(1)}, bf16[144,512]{1,0:T(8,128)(2,1)S(1)}, u32[]{:S(2)}, u32[]{:S(2)}) %collective-permute-start.9) | collective-permute-done | bytes 147488 | tf_op jit(solution)/shard_map/ppermute | solution.py:419
  82.6 1.5 %shard_map.118 = bf16[32,24,128]{2,1,0:T(8,128)(2,1)} custom-call(f32[2]{0:T(128)S(1)} %pad_maximum_fusion.1.scale_ref, s32[2]{0:T(128)S(1)} %pad_add_fusion.place_ref, bf16[144,512]{1,0:T(8,128)(2,1)S(1)} %get-tuple-element.10.refs_0_, bf16[144,512]{1,0:T(8,128)(2,1)S(1)} %collective-permute-done.7.refs_1_, ...), custom_call_target="tpu_custom_call" | custom-call | tf_op jit(solution)/shard_map/pallas_call | solution.py:313
  84.0 13.2 %all-to-all-start = ((bf16[32,24,128]{2,1,0:T(8,128)(2,1)}), bf16[32,24,128]{2,1,0:T(8,128)(2,1)S(1)}, u32[]{:S(2)}, u32[]{:S(2)}) async-start(bf16[32,24,128]{2,1,0:T(8,128)(2,1)} %shard_map.118), calls=%async_computation | async-start | bytes 393216 | tf_op jit(solution)/shard_map/all_to_all | solution.py:422
  97.2 19.1 %all-to-all-done = bf16[32,24,128]{2,1,0:T(8,128)(2,1)S(1)} async-done(((bf16[32,24,128]{2,1,0:T(8,128)(2,1)}), bf16[32,24,128]{2,1,0:T(8,128)(2,1)S(1)}, u32[]{:S(2)}, u32[]{:S(2)}) %all-to-all-start) | async-done | bytes 196640 | tf_op jit(solution)/shard_map/all_to_all | solution.py:422
  116.4 5.3 %collective-permute-start.10 = (bf16[24,128]{1,0:T(8,128)(2,1)S(1)}, bf16[24,128]{1,0:T(8,128)(2,1)S(1)}, u32[]{:S(2)}, u32[]{:S(2)}) collective-permute-start(bf16[24,128]{1,0:T(8,128)(2,1)S(1)} %subtract_convert_fusion.own_ref), channel_id=1, source_target_pairs={{0,1},{1,2},{2,3},{3,4},{4,5},{5,6},{6,7},{7,8},{8,9},{9,10},{10,1... | collective-permute-start | bytes 18440 | tf_op jit(solution)/shard_map/ppermute | solution.py:426
  121.7 2.1 %collective-permute-start.11 = (bf16[24,128]{1,0:T(8,128)(2,1)S(1)}, bf16[24,128]{1,0:T(8,128)(2,1)S(1)}, u32[]{:S(2)}, u32[]{:S(2)}) collective-permute-start(bf16[24,128]{1,0:T(8,128)(2,1)S(1)} %subtract_convert_fusion.own_ref), channel_id=1, source_target_pairs={{0,2},{1,3},{2,4},{3,5},{4,6},{5,7},{6,8},{7,9},{8,10},{9,11},{10,... | collective-permute-start | bytes 18440 | tf_op jit(solution)/shard_map/ppermute | solution.py:427
  123.8 0.1 dynamic-slice
  123.9 0.1 reshape.54
  124.0 0.7 copy.23
  124.7 4.3 %collective-permute-done.11.older_ref = bf16[24,128]{1,0:T(8,128)(2,1)S(1)} collective-permute-done((bf16[24,128]{1,0:T(8,128)(2,1)S(1)}, bf16[24,128]{1,0:T(8,128)(2,1)S(1)}, u32[]{:S(2)}, u32[]{:S(2)}) %collective-permute-start.11) | collective-permute-done | bytes 6176 | tf_op jit(solution)/shard_map/ppermute | solution.py:427
  129.0 1.2 shard_map.119
  (32 shorter events, 0.2 us)
Async XLA Ops:
  0.6 29.3 %copy-start = (bf16[4096,64]{0,1:T(8,128)(2,1)S(1)}, bf16[4096,64]{0,1:T(8,128)(2,1)}, u32[]{:S(2)}) copy-start(bf16[4096,64]{0,1:T(8,128)(2,1)} %param.16) | copy-start | bytes 1572868
  0.6 18.7 %copy-start.2 = (bf16[1,512,256]{2,1,0:T(8,128)(2,1)S(1)}, bf16[1,512,256]{2,1,0:T(8,128)(2,1)}, u32[]{:S(2)}) copy-start(bf16[1,512,256]{2,1,0:T(8,128)(2,1)} %param.10) | copy-start | bytes 786436
  0.7 28.8 %copy-start.7 = (f32[1,2,64,16]{2,3,1,0:T(8,128)S(1)}, f32[1,2,64,16]{2,3,1,0:T(8,128)}, u32[]{:S(2)}) copy-start(f32[1,2,64,16]{2,3,1,0:T(8,128)} %param.15) | copy-start | bytes 24580
  9.7 21.5 %copy-start.1 = (bf16[3,3,3,16,384]{4,3,2,1,0:T(8,128)(2,1)S(1)}, bf16[3,3,3,16,384]{4,3,2,1,0:T(8,128)(2,1)}, u32[]{:S(2)}) copy-start(bf16[3,3,3,16,384]{4,3,2,1,0:T(8,128)(2,1)} %param.17) | copy-start | bytes 995332
  9.7 21.7 %collective-permute-start.1 = (bf16[1024,256]{1,0:T(8,128)(2,1)}, bf16[1024,256]{1,0:T(8,128)(2,1)S(1)}, u32[]{:S(2)}, u32[]{:S(2)}) collective-permute-start(bf16[1024,256]{1,0:T(8,128)(2,1)} %shard_map.113.refs_2_.refs_1_), channel_id=1, source_target_pairs={{0,4},{4,8},{8,12},{12,0},{1,5},{5,9},{9,13},{13,1},{2,6},{6,10},{... | collective-permute-start | bytes 1572872 | tf_op jit(solution)/shard_map/ppermute | solution.py:386
  17.4 20.7 %collective-permute-start.3 = (bf16[1024,256]{1,0:T(8,128)(2,1)}, bf16[1024,256]{1,0:T(8,128)(2,1)}, u32[]{:S(2)}, u32[]{:S(2)}) collective-permute-start(bf16[1024,256]{1,0:T(8,128)(2,1)} %shard_map.113.refs_2_.refs_1_), channel_id=1, source_target_pairs={{0,12},{4,0},{8,4},{12,8},{1,13},{5,1},{9,5},{13,9},{2,14},{6,2},{... | collective-permute-start | bytes 1572872 | tf_op jit(solution)/shard_map/ppermute | solution.py:386
  19.3 33.8 %collective-permute-start.6 = (bf16[512,256]{1,0:T(8,128)(2,1)S(1)}, bf16[512,256]{1,0:T(8,128)(2,1)}, u32[]{:S(2)}, u32[]{:S(2)}) collective-permute-start(bf16[512,256]{1,0:T(8,128)(2,1)S(1)} %bitcast.50), channel_id=1, source_target_pairs={{0,3},{1,2},{2,1},{3,0},{4,7},{5,6},{6,5},{7,4},{8,11},{9,10},{10,... | collective-permute-start | bytes 786440 | tf_op jit(solution)/shard_map/ppermute | solution.py:392
  22.3 39.4 %collective-permute-start.5 = (bf16[512,256]{1,0:T(8,128)(2,1)S(1)}, bf16[512,256]{1,0:T(8,128)(2,1)}, u32[]{:S(2)}, u32[]{:S(2)}) collective-permute-start(bf16[512,256]{1,0:T(8,128)(2,1)S(1)} %bitcast.51), channel_id=1, source_target_pairs={{0,2},{1,3},{2,0},{3,1},{4,6},{5,7},{6,4},{7,5},{8,10},{9,11},{10,... | collective-permute-start | bytes 786440 | tf_op jit(solution)/shard_map/ppermute | solution.py:392
  24.2 20.3 %collective-permute-start = (bf16[512,256]{1,0:T(8,128)(2,1)S(1)}, bf16[512,256]{1,0:T(8,128)(2,1)S(1)}, u32[]{:S(2)}, u32[]{:S(2)}) collective-permute-start(bf16[512,256]{1,0:T(8,128)(2,1)S(1)} %bitcast.52), channel_id=1, source_target_pairs={{0,1},{1,0},{2,3},{3,2},{4,5},{5,4},{6,7},{7,6},{8,9},{9,8},{10,11... | collective-permute-start | bytes 786440 | tf_op jit(solution)/shard_map/ppermute | solution.py:392
  31.4 0.8 copy-start.6
  32.9 20.2 %collective-permute-start.2 = (bf16[512,256]{1,0:T(8,128)(2,1)}, bf16[512,256]{1,0:T(8,128)(2,1)S(1)}, u32[]{:S(2)}, u32[]{:S(2)}) collective-permute-start(bf16[512,256]{1,0:T(8,128)(2,1)} %slice.30), channel_id=1, source_target_pairs={{0,4},{4,8},{8,12},{12,0},{1,5},{5,9},{9,13},{13,1},{2,6},{6,10},{... | collective-permute-start | bytes 786440 | tf_op jit(solution)/shard_map/ppermute | solution.py:388
  39.7 13.4 %collective-permute-start.4 = (bf16[512,256]{1,0:T(8,128)(2,1)}, bf16[512,256]{1,0:T(8,128)(2,1)S(1)}, u32[]{:S(2)}, u32[]{:S(2)}) collective-permute-start(bf16[512,256]{1,0:T(8,128)(2,1)} %slice.31), channel_id=1, source_target_pairs={{0,12},{4,0},{8,4},{12,8},{1,13},{5,1},{9,5},{13,9},{2,14},{6,2},{... | collective-permute-start | bytes 786440 | tf_op jit(solution)/shard_map/ppermute | solution.py:389
  41.8 0.7 copy-start.8
  42.5 0.7 copy-start.9
  44.5 0.7 copy-start.3
  53.1 0.7 copy-start.4
  53.2 0.8 copy-start.5
  59.8 22.8 %collective-permute-start.7 = (bf16[144,512]{1,0:T(8,128)(2,1)S(1)}, bf16[144,512]{1,0:T(8,128)(2,1)S(1)}, u32[]{:S(2)}, u32[]{:S(2)}) collective-permute-start(bf16[144,512]{1,0:T(8,128)(2,1)S(1)} %shard_map.115.refs_7_), channel_id=1, source_target_pairs={{0,3},{1,2},{2,1},{3,0},{4,7},{5,6},{6,5},{7,4},{8,11},{9,10},{10,... | collective-permute-start | bytes 442376 | tf_op jit(solution)/shard_map/ppermute | solution.py:419
  67.5 15.0 %collective-permute-start.8 = (bf16[144,512]{1,0:T(8,128)(2,1)S(1)}, bf16[144,512]{1,0:T(8,128)(2,1)S(1)}, u32[]{:S(2)}, u32[]{:S(2)}) collective-permute-start(bf16[144,512]{1,0:T(8,128)(2,1)S(1)} %shard_map.116.refs_8_), channel_id=1, source_target_pairs={{0,2},{1,3},{2,0},{3,1},{4,6},{5,7},{6,4},{7,5},{8,10},{9,11},{10,... | collective-permute-start | bytes 442376 | tf_op jit(solution)/shard_map/ppermute | solution.py:419
  73.7 8.8 %collective-permute-start.9 = (bf16[144,512]{1,0:T(8,128)(2,1)S(1)}, bf16[144,512]{1,0:T(8,128)(2,1)S(1)}, u32[]{:S(2)}, u32[]{:S(2)}) collective-permute-start(bf16[144,512]{1,0:T(8,128)(2,1)S(1)} %get-tuple-element.11), channel_id=1, source_target_pairs={{0,1},{1,0},{2,3},{3,2},{4,5},{5,4},{6,7},{7,6},{8,9},{9,8},{10,11... | collective-permute-start | bytes 442376 | tf_op jit(solution)/shard_map/ppermute | solution.py:419
  84.0 32.3 %all-to-all-start = ((bf16[32,24,128]{2,1,0:T(8,128)(2,1)}), bf16[32,24,128]{2,1,0:T(8,128)(2,1)S(1)}, u32[]{:S(2)}, u32[]{:S(2)}) async-start(bf16[32,24,128]{2,1,0:T(8,128)(2,1)} %shard_map.118), calls=%async_computation | async-start | bytes 393216 | tf_op jit(solution)/shard_map/all_to_all | solution.py:422
  116.4 8.3 %collective-permute-start.10 = (bf16[24,128]{1,0:T(8,128)(2,1)S(1)}, bf16[24,128]{1,0:T(8,128)(2,1)S(1)}, u32[]{:S(2)}, u32[]{:S(2)}) collective-permute-start(bf16[24,128]{1,0:T(8,128)(2,1)S(1)} %subtract_convert_fusion.own_ref), channel_id=1, source_target_pairs={{0,1},{1,2},{2,3},{3,4},{4,5},{5,6},{6,7},{7,8},{8,9},{9,10},{10,1... | collective-permute-start | bytes 18440 | tf_op jit(solution)/shard_map/ppermute | solution.py:426
  121.7 7.3 %collective-permute-start.11 = (bf16[24,128]{1,0:T(8,128)(2,1)S(1)}, bf16[24,128]{1,0:T(8,128)(2,1)S(1)}, u32[]{:S(2)}, u32[]{:S(2)}) collective-permute-start(bf16[24,128]{1,0:T(8,128)(2,1)S(1)} %subtract_convert_fusion.own_ref), channel_id=1, source_target_pairs={{0,2},{1,3},{2,4},{3,5},{4,6},{5,7},{6,8},{7,9},{8,10},{9,11},{10,... | collective-permute-start | bytes 18440 | tf_op jit(solution)/shard_map/ppermute | solution.py:427

commit v5 on v4

--- a/solution.py
+++ b/solution.py
@@ -51,18 +51,18 @@
     return [(i, i + steps) for i in range(count) if 0 <= i + steps < count]
 
 
-def prepare_kernel(keys_ref, values_ref, out_ref, values, turned, sems):
-    first = pltpu.make_async_copy(keys_ref, out_ref.at[pl.ds(0, TOK)], sems.at[0])
+def prepare_kernel(keys_ref, values_ref, out_ref, values, both, sems):
+    first = pltpu.make_async_copy(keys_ref, both.at[pl.ds(0, TOK)], sems.at[0])
     second = pltpu.make_async_copy(values_ref, values, sems.at[1])
     first.start()
     second.start()
     second.wait()
     for half in range(2):
-        rows = slice(half * 2 * DH, (half + 1) * 2 * DH)
-        turned[rows] = jnp.transpose(values[rows])
-    third = pltpu.make_async_copy(turned, out_ref.at[pl.ds(TOK, TOK)], sems.at[1])
+        at = half * 2 * DH
+        both[TOK + at : TOK + at + 2 * DH] = jnp.transpose(values[at : at + 2 * DH])
+    first.wait()
+    third = pltpu.make_async_copy(both, out_ref, sems.at[0])
     third.start()
-    first.wait()
     third.wait()
 
 
@@ -72,12 +72,15 @@
         out_shape=pltpu.HBM((2 * TOK, 2 * DH), jnp.bfloat16),
         in_specs=[HBM] * 2,
         out_specs=HBM,
-        scratch_shapes=[pltpu.VMEM((TOK, 2 * DH), jnp.bfloat16)] * 2
-        + [pltpu.SemaphoreType.DMA((2,))],
+        scratch_shapes=[
+            pltpu.VMEM((TOK, 2 * DH), jnp.bfloat16),
+            pltpu.VMEM((2 * TOK, 2 * DH), jnp.bfloat16),
+            pltpu.SemaphoreType.DMA((2,)),
+        ],
     )(in_hbm(keys), in_hbm(values))
 
 
-def attention_kernel(count_ref, *refs, nq, whole, split, carry, nx, last):
+def attention_kernel(count_ref, *refs, nq, nk, start, carry, nx, last):
     refs = list(refs)
 
     def take(size):
@@ -85,8 +88,7 @@
         del refs[:size]
         return taken
 
-    nk = whole + split
-    q_refs, kv_refs = take(nq), take(whole + 2 * split)
+    q_refs, kv_refs = take(nq), take(nk)
     weight_hbm = take(1)[0] if last else None
     if carry:
         top_in, denom_in, acc_in = take(3)
@@ -107,10 +109,7 @@
 
     arriving = []
     for b in range(nk):
-        if b < whole:
-            keys, values = kv_refs[b].at[pl.ds(0, TOK)], kv_refs[b].at[pl.ds(TOK, TOK)]
-        else:
-            keys, values = kv_refs[whole], kv_refs[whole + 1]
+        keys, values = kv_refs[b].at[pl.ds(0, TOK)], kv_refs[b].at[pl.ds(TOK, TOK)]
         group = [copied(keys, ks.at[b])]
         for half in range(2):
             for h in range(2):
@@ -150,7 +149,7 @@
 
     def folded(j, b, h, score, masked):
         if masked:
-            valid = lax.broadcasted_iota(jnp.int32, (TOK, TOK), 0) < count_ref[b]
+            valid = lax.broadcasted_iota(jnp.int32, (TOK, TOK), 0) < count_ref[start + b]
             score = jnp.where(valid, score, NEG_FILL)
         old = top_ref[j, h : h + 1]
         new = jnp.maximum(old, jnp.max(score, axis=0, keepdims=True))
@@ -169,7 +168,7 @@
         j, b = lax.div(t, nk), lax.rem(t, nk)
         later = jnp.minimum(t + 1, total - 1)
         next_j, next_b = lax.div(later, nk), lax.rem(later, nk)
-        count = count_ref[b]
+        count = count_ref[start + b]
         for needed in range(1, nk):
 
             @pl.when(t == needed - 1)
@@ -218,10 +217,9 @@
         chunk_refs[j][...] = jnp.concatenate(parts + rows + [blank], 0).astype(jnp.bfloat16)
 
 
-def attend(counts, queries, blocks, pair=(), weight=None, state=(), extras=()):
+def attend(counts, queries, blocks, start=0, weight=None, state=(), extras=()):
     f32, bf16 = jnp.float32, jnp.bfloat16
-    nq, whole, split, last = len(queries), len(blocks), len(pair) // 2, weight is not None
-    nk = whole + split
+    nq, nk, last = len(queries), len(blocks), weight is not None
     stat = jax.ShapeDtypeStruct((nq, 2, TOK), f32)
     chunk = jax.ShapeDtypeStruct((CHUNK, TOK), bf16)
     acc = pltpu.HBM((nq, 2, DH, TOK), f32)
@@ -240,15 +238,15 @@
         functools.partial(
             attention_kernel,
             nq=nq,
-            whole=whole,
-            split=split,
+            nk=nk,
+            start=start,
             carry=bool(state),
             nx=len(extras),
             last=last,
         ),
         out_shape=(chunk,) * nq if last else (stat, stat, acc),
         in_specs=[SMEM]
-        + [HBM] * (nq + whole + len(pair) + last)
+        + [HBM] * (nq + nk + last)
         + ([VMEM, VMEM, HBM] if state else [])
         + [ANY] * len(extras),
         out_specs=(VMEM,) * nq if last else (VMEM, VMEM, HBM),
@@ -259,7 +257,7 @@
         ),
     )(
         counts,
-        *(in_hbm(x) for x in (*queries, *blocks, *pair)),
+        *(in_hbm(x) for x in (*queries, *blocks)),
         *((in_hbm(weight),) if last else ()),
         *(in_hbm(x) if x.ndim == 4 else x for x in state),
         *extras,
@@ -383,12 +381,7 @@
     seq = ("y", "zl")
 
     own = prepared(keys[0], values[0])
-    before, after = lax.ppermute(own, "y", ring(1)), lax.ppermute(own, "y", ring(-1))
-    pair = [
-        lax.ppermute(before[:TOK], "y", ring(1)),
-        lax.ppermute(after[TOK:], "y", ring(-1)),
-    ]
-    blocks = [own, before, after]
+    blocks = [own] + [lax.ppermute(own, "y", ring(d)) for d in (1, 3, 2)]
     queries = [query[0]] + [lax.ppermute(query[0], "zl", crossed(m)) for m in (1, 2, 3)]
     block = jnp.stack([((y - d) % SIDE) * SIDE + zl for d in (0, 1, 3, 2)])
     counts = jnp.clip(lengths[0] - block * TOK, 0, TOK).astype(jnp.int32)
@@ -410,11 +403,10 @@
     )
     place = jnp.stack([zh * SIDE + x, zl]).astype(jnp.int32)
 
-    near = attend(counts[:3], queries[:2], blocks)
-    constants = (grid, latent_window, even, odd, bias_row, gain_row)
-    (third,) = attend(counts, queries[3:], blocks, pair, weight, extras=constants)
-    (second,) = attend(counts, queries[2:3], blocks, pair, weight, extras=(third,))
-    mine, first = attend(counts[3:], queries[:2], [], pair, weight, near, (second,))
+    near = attend(counts, queries[:2], blocks[:3])
+    (third,) = attend(counts, queries[3:], blocks, weight=weight, extras=near[:1])
+    (second,) = attend(counts, queries[2:3], blocks, weight=weight, extras=(third,))
+    mine, first = attend(counts, queries[:2], blocks[3:], 3, weight, near, (second,))
     chunks = [mine] + [
         lax.ppermute(chunk, "zl", crossed(m)) for m, chunk in ((3, third), (2, second), (1, first))
     ]

time: 131 us -> 126 us (0.962)
  waiting for transfers between devices: 26.4 us -> 34.6 us
  Pallas kernels: 35.5 us -> 28.5 us
  starting transfers between devices: 56.8 us -> 53.8 us
  local copies, waits for them, and re-layouts: 8.66 us -> 5.84 us
    pallas_call x1, Pallas kernels: 9.06 us -> 2.06 us  [prepared(): pl.pallas_call(prepare_kernel, out_shape=pltpu.HBM((2 * TOK, 2 * DH), jnp...]
    ppermute x4 -> x3, waiting for transfers between devices: 0.01 us -> 5.3 us  [local(): blocks = [own] + [lax.ppermute(own, 'y', ring(d)) for d in (1, 3, 2)]]
    ppermute x1, waiting for transfers between devices: 4.32 us -> 0.01 us  [local(): older = lax.ppermute(current, seq, moved(2))]
    ppermute x1, waiting for transfers between devices: 0.01 us -> 3.83 us  [local(): last = lax.ppermute(current, seq, moved(1))]
    ppermute x4 -> x3, starting transfers between devices: 16.6 us -> 12.8 us  [local(): blocks = [own] + [lax.ppermute(own, 'y', ring(d)) for d in (1, 3, 2)]]
    all_to_all x1, starting transfers between devices: 13.2 us -> 16.9 us  [local(): shares = lax.all_to_all(shares, ('cfg', 'zh', 'x'), 0, 0, tiled=True)]
    ppermute x1, starting transfers between devices: 2.11 us -> 5.55 us  [local(): older = lax.ppermute(current, seq, moved(2))]
    ppermute x1, starting transfers between devices: 5.32 us -> 1.92 us  [local(): last = lax.ppermute(current, seq, moved(1))]
  transfers between devices with their start and end apart: 13 -> 12, of which waited for: 3 -> 5; matrix products, arithmetic and copies ran while one was open for 4% -> 2% of each run, Pallas kernels for 18% -> 19%
where the time goes in v5:
time: 126 us; the launch traced here: 125 us
  starting transfers between devices  53.8 us (43%)
  waiting for transfers between devices  34.6 us (27%)
  Pallas kernels  28.5 us (23%)
  local copies, waits for them, and re-layouts  5.84 us (5%)
  between operations  2.36 us (2%)
    pallas_call x4, Pallas kernels, attend(): pl.pallas_call(functools.partial(attention_kernel, nq=nq, nk=nk, start=st...  23.8 us
    all_to_all x1, waiting for transfers between devices, local(): shares = lax.all_to_all(shares, ('cfg', 'zh', 'x'), 0, 0, tiled=True)  19 us
    all_to_all x1, starting transfers between devices, local(): shares = lax.all_to_all(shares, ('cfg', 'zh', 'x'), 0, 0, tiled=True)  16.9 us
    ppermute x3, starting transfers between devices, local(): blocks = [own] + [lax.ppermute(own, 'y', ring(d)) for d in (1, 3, 2)]  12.8 us
    ppermute x3, starting transfers between devices, local(): lax.ppermute(chunk, 'zl', crossed(m))  9.54 us
    ppermute x3, starting transfers between devices, local(): lax.ppermute(query[0], 'zl', crossed(m))  7.11 us
    ppermute x1, starting transfers between devices, local(): older = lax.ppermute(current, seq, moved(2))  5.55 us
    ppermute x3, waiting for transfers between devices, local(): blocks = [own] + [lax.ppermute(own, 'y', ring(d)) for d in (1, 3, 2)]  5.3 us
  transfers between devices with their start and end apart: 12, of which 5 were waited for; matrix products, arithmetic and copies ran while one was open for 2% of the time, Pallas kernels for 19%

profile of v5, /device:TPU:24, one launch (start us, length us, event | category | flops | bytes accessed | tf_op | source)
XLA Modules:
  0.0 125.4 jit_solution(3683177091710151815)
XLA Ops:
  0.6 0.0 copy-start
  0.6 0.0 copy-start.3
  0.7 2.1 %shard_map.113.refs_2_.refs_1_ = bf16[1024,256]{1,0:T(8,128)(2,1)} custom-call(bf16[512,256]{1,0:T(8,128)(2,1)} %bitcast.49, bf16[512,256]{1,0:T(8,128)(2,1)} %bitcast.50), custom_call_target="tpu_custom_call" | custom-call | tf_op jit(solution)/shard_map/pallas_call | solution.py:70
  2.7 7.5 %collective-permute-start.2 = (bf16[1024,256]{1,0:T(8,128)(2,1)}, bf16[1024,256]{1,0:T(8,128)(2,1)S(1)}, u32[]{:S(2)}, u32[]{:S(2)}) collective-permute-start(bf16[1024,256]{1,0:T(8,128)(2,1)} %shard_map.113.refs_2_.refs_1_), channel_id=1, source_target_pairs={{0,4},{4,8},{8,12},{12,0},{1,5},{5,9},{9,13},{13,1},{2,6},{6,10},{... | collective-permute-start | bytes 1572872 | tf_op jit(solution)/shard_map/ppermute | solution.py:384
  10.2 1.9 %collective-permute-start.3 = (bf16[1024,256]{1,0:T(8,128)(2,1)}, bf16[1024,256]{1,0:T(8,128)(2,1)S(1)}, u32[]{:S(2)}, u32[]{:S(2)}) collective-permute-start(bf16[1024,256]{1,0:T(8,128)(2,1)} %shard_map.113.refs_2_.refs_1_), channel_id=1, source_target_pairs={{0,12},{4,0},{8,4},{12,8},{1,13},{5,1},{9,5},{13,9},{2,14},{6,2},{... | collective-permute-start | bytes 1572872 | tf_op jit(solution)/shard_map/ppermute | solution.py:384
  12.2 3.4 %collective-permute-start.1 = (bf16[1024,256]{1,0:T(8,128)(2,1)}, bf16[1024,256]{1,0:T(8,128)(2,1)S(1)}, u32[]{:S(2)}, u32[]{:S(2)}) collective-permute-start(bf16[1024,256]{1,0:T(8,128)(2,1)} %shard_map.113.refs_2_.refs_1_), channel_id=1, source_target_pairs={{0,8},{4,12},{8,0},{12,4},{1,9},{5,13},{9,1},{13,5},{2,10},{6,14},... | collective-permute-start | bytes 1572872 | tf_op jit(solution)/shard_map/ppermute | solution.py:384
  15.5 1.9 %collective-permute-start = (bf16[512,256]{1,0:T(8,128)(2,1)S(1)}, bf16[512,256]{1,0:T(8,128)(2,1)S(1)}, u32[]{:S(2)}, u32[]{:S(2)}) collective-permute-start(bf16[512,256]{1,0:T(8,128)(2,1)S(1)} %bitcast.46), channel_id=1, source_target_pairs={{0,1},{1,0},{2,3},{3,2},{4,5},{5,4},{6,7},{7,6},{8,9},{9,8},{10,11... | collective-permute-start | bytes 786440 | tf_op jit(solution)/shard_map/ppermute | solution.py:385
  17.5 2.8 %collective-permute-start.5 = (bf16[512,256]{1,0:T(8,128)(2,1)S(1)}, bf16[512,256]{1,0:T(8,128)(2,1)S(1)}, u32[]{:S(2)}, u32[]{:S(2)}) collective-permute-start(bf16[512,256]{1,0:T(8,128)(2,1)S(1)} %bitcast.47), channel_id=1, source_target_pairs={{0,3},{1,2},{2,1},{3,0},{4,7},{5,6},{6,5},{7,4},{8,11},{9,10},{10,... | collective-permute-start | bytes 786440 | tf_op jit(solution)/shard_map/ppermute | solution.py:385
  21.0 0.6 bitcast_bitcast_fusion.refs_5_.refs_3_
  21.7 0.1 pad_maximum_fusion.1.scale_ref
  22.4 0.1 copy-done.5
  22.5 3.2 %collective-permute-done.refs_1_ = bf16[512,256]{1,0:T(8,128)(2,1)S(1)} collective-permute-done((bf16[512,256]{1,0:T(8,128)(2,1)S(1)}, bf16[512,256]{1,0:T(8,128)(2,1)S(1)}, u32[]{:S(2)}, u32[]{:S(2)}) %collective-permute-start) | collective-permute-done | bytes 262176 | tf_op jit(solution)/shard_map/ppermute | solution.py:385
  25.7 2.4 %collective-permute-start.4 = (bf16[512,256]{1,0:T(8,128)(2,1)S(1)}, bf16[512,256]{1,0:T(8,128)(2,1)S(1)}, u32[]{:S(2)}, u32[]{:S(2)}) collective-permute-start(bf16[512,256]{1,0:T(8,128)(2,1)S(1)} %bitcast.48), channel_id=1, source_target_pairs={{0,2},{1,3},{2,0},{3,1},{4,6},{5,7},{6,4},{7,5},{8,10},{9,11},{10,... | collective-permute-start | bytes 786440 | tf_op jit(solution)/shard_map/ppermute | solution.py:385
  28.1 0.1 fusion.1.count_ref
  28.1 5.3 %collective-permute-done.3.refs_4_.refs_3_ = bf16[1024,256]{1,0:T(8,128)(2,1)S(1)} collective-permute-done((bf16[1024,256]{1,0:T(8,128)(2,1)}, bf16[1024,256]{1,0:T(8,128)(2,1)S(1)}, u32[]{:S(2)}, u32[]{:S(2)}) %collective-permute-start.3) | collective-permute-done | bytes 524320 | tf_op jit(solution)/shard_map/ppermute | solution.py:384
  33.5 0.8 copy-done.9
  34.2 7.9 %shard_map.114 = (f32[2,2,512]{2,1,0:T(2,128)S(1)}, f32[2,2,512]{2,1,0:T(2,128)S(1)}, f32[2,2,128,512]{3,2,1,0:T(8,128)}) custom-call(s32[4]{0:T(128)S(1)} %fusion.1.count_ref, bf16[512,256]{1,0:T(8,128)(2,1)} %bitcast.44, bf16[512,256]{1,0:T(8,128)(2,1)} %copy-done.4, bf16[1024,256]{1,0:T(8,128)(2,1)} %shard_map.113.refs_2_.refs_1_, ...), custom_call_target="tpu_custom_call" | custom-call | flops 1610612736 | bytes 2097152 | tf_op jit(solution)/shard_map/pallas_call | solution.py:237
  42.2 0.7 copy-done.10
  42.9 0.2 copy-done.1
  43.1 5.8 %shard_map.115.refs_6_ = bf16[144,512]{1,0:T(8,128)(2,1)S(1)} custom-call(s32[4]{0:T(128)S(1)} %fusion.1.count_ref, bf16[512,256]{1,0:T(8,128)(2,1)} %copy-done.10, bf16[1024,256]{1,0:T(8,128)(2,1)} %shard_map.113.refs_2_.refs_1_, bf16[1024,256]{1,0:T(8,128)(2,1)} %copy-done.8, bf16[1024,256]{1,0:T(8,128)(2,1)} %copy-done.9, bf16[1024,256]{1,0:T(8,128)(2,1)} %copy-done.1, ...), custom_call_target="tpu_custom_call" | custom-call | flops 1073741824 | bytes 2359296 | tf_op jit(solution)/shard_map/pallas_call | solution.py:237
  48.9 4.3 %collective-permute-start.6 = (bf16[144,512]{1,0:T(8,128)(2,1)S(1)}, bf16[144,512]{1,0:T(8,128)(2,1)S(1)}, u32[]{:S(2)}, u32[]{:S(2)}) collective-permute-start(bf16[144,512]{1,0:T(8,128)(2,1)S(1)} %shard_map.115.refs_6_), channel_id=1, source_target_pairs={{0,3},{1,2},{2,1},{3,0},{4,7},{5,6},{6,5},{7,4},{8,11},{9,10},{10,... | collective-permute-start | bytes 442376 | tf_op jit(solution)/shard_map/ppermute | solution.py:411
  53.3 0.7 copy-done.11
  54.0 5.8 %shard_map.116.refs_7_ = bf16[144,512]{1,0:T(8,128)(2,1)S(1)} custom-call(s32[4]{0:T(128)S(1)} %fusion.1.count_ref, bf16[512,256]{1,0:T(8,128)(2,1)} %copy-done.11, bf16[1024,256]{1,0:T(8,128)(2,1)} %shard_map.113.refs_2_.refs_1_, bf16[1024,256]{1,0:T(8,128)(2,1)} %copy-done.8, bf16[1024,256]{1,0:T(8,128)(2,1)} %copy-done.9, bf16[1024,256]{1,0:T(8,128)(2,1)} %copy-done.1, ...), custom_call_target="tpu_custom_call" | custom-call | flops 1073741824 | bytes 2359296 | tf_op jit(solution)/shard_map/pallas_call | solution.py:237
  59.8 1.9 %collective-permute-start.7 = (bf16[144,512]{1,0:T(8,128)(2,1)S(1)}, bf16[144,512]{1,0:T(8,128)(2,1)S(1)}, u32[]{:S(2)}, u32[]{:S(2)}) collective-permute-start(bf16[144,512]{1,0:T(8,128)(2,1)S(1)} %shard_map.116.refs_7_), channel_id=1, source_target_pairs={{0,2},{1,3},{2,0},{3,1},{4,6},{5,7},{6,4},{7,5},{8,10},{9,11},{10,... | collective-permute-start | bytes 442376 | tf_op jit(solution)/shard_map/ppermute | solution.py:411
  61.7 4.2 %shard_map.117 = (bf16[144,512]{1,0:T(8,128)(2,1)S(1)}, bf16[144,512]{1,0:T(8,128)(2,1)S(1)}) custom-call(s32[4]{0:T(128)S(1)} %fusion.1.count_ref, bf16[512,256]{1,0:T(8,128)(2,1)} %bitcast.45, bf16[512,256]{1,0:T(8,128)(2,1)} %copy-done.4, bf16[1024,256]{1,0:T(8,128)(2,1)} %copy-done.1, bf16[2,64,128]{2,1,0:T(8,128)(2,1)} %bitcast_bitcast_fusion.refs_5_.refs_3_, ...), custom_call_target="tpu_custom_call" | custom-call | flops 536870912 | bytes 1048576 | tf_op jit(solution)/shard_map/pallas_call | solution.py:237
  65.9 3.3 %collective-permute-start.8 = (bf16[144,512]{1,0:T(8,128)(2,1)S(1)}, bf16[144,512]{1,0:T(8,128)(2,1)S(1)}, u32[]{:S(2)}, u32[]{:S(2)}) collective-permute-start(bf16[144,512]{1,0:T(8,128)(2,1)S(1)} %get-tuple-element.11), channel_id=1, source_target_pairs={{0,1},{1,0},{2,3},{3,2},{4,5},{5,4},{6,7},{7,6},{8,9},{9,8},{10,11... | collective-permute-start | bytes 442376 | tf_op jit(solution)/shard_map/ppermute | solution.py:411
  69.2 0.1 pad_add_fusion.place_ref
  69.3 0.1 copy.18
  69.4 0.1 squeeze.26
  69.5 0.1 copy.19
  69.6 0.1 squeeze.27
  69.6 0.1 pad_maximum_fusion.refs_4_
  69.7 3.3 %collective-permute-done.8.refs_3_ = bf16[144,512]{1,0:T(8,128)(2,1)S(1)} collective-permute-done((bf16[144,512]{1,0:T(8,128)(2,1)S(1)}, bf16[144,512]{1,0:T(8,128)(2,1)S(1)}, u32[]{:S(2)}, u32[]{:S(2)}) %collective-permute-start.8) | collective-permute-done | bytes 147488 | tf_op jit(solution)/shard_map/ppermute | solution.py:411
  73.0 1.5 %shard_map.118 = bf16[32,24,128]{2,1,0:T(8,128)(2,1)} custom-call(f32[2]{0:T(128)S(1)} %pad_maximum_fusion.1.scale_ref, s32[2]{0:T(128)S(1)} %pad_add_fusion.place_ref, bf16[144,512]{1,0:T(8,128)(2,1)S(1)} %get-tuple-element.10.refs_0_, bf16[144,512]{1,0:T(8,128)(2,1)S(1)} %collective-permute-done.6.refs_1_, ...), custom_call_target="tpu_custom_call" | custom-call | tf_op jit(solution)/shard_map/pallas_call | solution.py:311
  74.5 16.9 %all-to-all-start = ((bf16[32,24,128]{2,1,0:T(8,128)(2,1)}), bf16[32,24,128]{2,1,0:T(8,128)(2,1)S(1)}, u32[]{:S(2)}, u32[]{:S(2)}) async-start(bf16[32,24,128]{2,1,0:T(8,128)(2,1)} %shard_map.118), calls=%async_computation | async-start | bytes 393216 | tf_op jit(solution)/shard_map/all_to_all | solution.py:414
  91.4 19.0 %all-to-all-done = bf16[32,24,128]{2,1,0:T(8,128)(2,1)S(1)} async-done(((bf16[32,24,128]{2,1,0:T(8,128)(2,1)}), bf16[32,24,128]{2,1,0:T(8,128)(2,1)S(1)}, u32[]{:S(2)}, u32[]{:S(2)}) %all-to-all-start) | async-done | bytes 196640 | tf_op jit(solution)/shard_map/all_to_all | solution.py:414
  110.5 5.6 %collective-permute-start.10 = (bf16[24,128]{1,0:T(8,128)(2,1)S(1)}, bf16[24,128]{1,0:T(8,128)(2,1)S(1)}, u32[]{:S(2)}, u32[]{:S(2)}) collective-permute-start(bf16[24,128]{1,0:T(8,128)(2,1)S(1)} %subtract_convert_fusion.own_ref), channel_id=1, source_target_pairs={{0,2},{1,3},{2,4},{3,5},{4,6},{5,7},{6,8},{7,9},{8,10},{9,11},{10,... | collective-permute-start | bytes 18440 | tf_op jit(solution)/shard_map/ppermute | solution.py:419
  116.0 1.9 %collective-permute-start.9 = (bf16[24,128]{1,0:T(8,128)(2,1)S(1)}, bf16[24,128]{1,0:T(8,128)(2,1)S(1)}, u32[]{:S(2)}, u32[]{:S(2)}) collective-permute-start(bf16[24,128]{1,0:T(8,128)(2,1)S(1)} %subtract_convert_fusion.own_ref), channel_id=1, source_target_pairs={{0,1},{1,2},{2,3},{3,4},{4,5},{5,6},{6,7},{7,8},{8,9},{9,10},{10,1... | collective-permute-start | bytes 18440 | tf_op jit(solution)/shard_map/ppermute | solution.py:418
  118.0 0.1 fusion.2
  118.1 0.1 copy.21
  118.2 0.1 copy.22
  118.3 0.6 copy-done.6
  118.9 0.7 copy-done.7
  119.5 0.1 dynamic-slice
  119.6 0.1 reshape.48
  119.7 0.7 copy.23
  120.4 3.8 %collective-permute-done.9.last_ref = bf16[24,128]{1,0:T(8,128)(2,1)S(1)} collective-permute-done((bf16[24,128]{1,0:T(8,128)(2,1)S(1)}, bf16[24,128]{1,0:T(8,128)(2,1)S(1)}, u32[]{:S(2)}, u32[]{:S(2)}) %collective-permute-start.9) | collective-permute-done | bytes 6176 | tf_op jit(solution)/shard_map/ppermute | solution.py:418
  124.2 1.2 shard_map.119
  (30 shorter events, 0.2 us)
Async XLA Ops:
  0.6 20.4 %copy-start = (bf16[4096,64]{0,1:T(8,128)(2,1)S(1)}, bf16[4096,64]{0,1:T(8,128)(2,1)}, u32[]{:S(2)}) copy-start(bf16[4096,64]{0,1:T(8,128)(2,1)} %param.16) | copy-start | bytes 1572868
  0.6 14.9 %copy-start.3 = (bf16[1,512,256]{2,1,0:T(8,128)(2,1)S(1)}, bf16[1,512,256]{2,1,0:T(8,128)(2,1)}, u32[]{:S(2)}) copy-start(bf16[1,512,256]{2,1,0:T(8,128)(2,1)} %param.10) | copy-start | bytes 786436
  2.7 25.4 %collective-permute-start.2 = (bf16[1024,256]{1,0:T(8,128)(2,1)}, bf16[1024,256]{1,0:T(8,128)(2,1)S(1)}, u32[]{:S(2)}, u32[]{:S(2)}) collective-permute-start(bf16[1024,256]{1,0:T(8,128)(2,1)} %shard_map.113.refs_2_.refs_1_), channel_id=1, source_target_pairs={{0,4},{4,8},{8,12},{12,0},{1,5},{5,9},{9,13},{13,1},{2,6},{6,10},{... | collective-permute-start | bytes 1572872 | tf_op jit(solution)/shard_map/ppermute | solution.py:384
  10.2 23.2 %collective-permute-start.3 = (bf16[1024,256]{1,0:T(8,128)(2,1)}, bf16[1024,256]{1,0:T(8,128)(2,1)S(1)}, u32[]{:S(2)}, u32[]{:S(2)}) collective-permute-start(bf16[1024,256]{1,0:T(8,128)(2,1)} %shard_map.113.refs_2_.refs_1_), channel_id=1, source_target_pairs={{0,12},{4,0},{8,4},{12,8},{1,13},{5,1},{9,5},{13,9},{2,14},{6,2},{... | collective-permute-start | bytes 1572872 | tf_op jit(solution)/shard_map/ppermute | solution.py:384
  12.2 30.1 %collective-permute-start.1 = (bf16[1024,256]{1,0:T(8,128)(2,1)}, bf16[1024,256]{1,0:T(8,128)(2,1)S(1)}, u32[]{:S(2)}, u32[]{:S(2)}) collective-permute-start(bf16[1024,256]{1,0:T(8,128)(2,1)} %shard_map.113.refs_2_.refs_1_), channel_id=1, source_target_pairs={{0,8},{4,12},{8,0},{12,4},{1,9},{5,13},{9,1},{13,5},{2,10},{6,14},... | collective-permute-start | bytes 1572872 | tf_op jit(solution)/shard_map/ppermute | solution.py:384
  15.5 10.1 %collective-permute-start = (bf16[512,256]{1,0:T(8,128)(2,1)S(1)}, bf16[512,256]{1,0:T(8,128)(2,1)S(1)}, u32[]{:S(2)}, u32[]{:S(2)}) collective-permute-start(bf16[512,256]{1,0:T(8,128)(2,1)S(1)} %bitcast.46), channel_id=1, source_target_pairs={{0,1},{1,0},{2,3},{3,2},{4,5},{5,4},{6,7},{7,6},{8,9},{9,8},{10,11... | collective-permute-start | bytes 786440 | tf_op jit(solution)/shard_map/ppermute | solution.py:385
  17.5 24.7 %collective-permute-start.5 = (bf16[512,256]{1,0:T(8,128)(2,1)S(1)}, bf16[512,256]{1,0:T(8,128)(2,1)S(1)}, u32[]{:S(2)}, u32[]{:S(2)}) collective-permute-start(bf16[512,256]{1,0:T(8,128)(2,1)S(1)} %bitcast.47), channel_id=1, source_target_pairs={{0,3},{1,2},{2,1},{3,0},{4,7},{5,6},{6,5},{7,4},{8,11},{9,10},{10,... | collective-permute-start | bytes 786440 | tf_op jit(solution)/shard_map/ppermute | solution.py:385
  21.7 0.7 copy-start.5
  25.7 7.8 %copy-start.4 = (bf16[512,256]{1,0:T(8,128)(2,1)}, bf16[512,256]{1,0:T(8,128)(2,1)S(1)}, u32[]{:S(2)}) copy-start(bf16[512,256]{1,0:T(8,128)(2,1)S(1)} %collective-permute-done.refs_1_) | copy-start | bytes 786436
  25.7 27.6 %collective-permute-start.4 = (bf16[512,256]{1,0:T(8,128)(2,1)S(1)}, bf16[512,256]{1,0:T(8,128)(2,1)S(1)}, u32[]{:S(2)}, u32[]{:S(2)}) collective-permute-start(bf16[512,256]{1,0:T(8,128)(2,1)S(1)} %bitcast.48), channel_id=1, source_target_pairs={{0,2},{1,3},{2,0},{3,1},{4,6},{5,7},{6,4},{7,5},{8,10},{9,11},{10,... | collective-permute-start | bytes 786440 | tf_op jit(solution)/shard_map/ppermute | solution.py:385
  28.1 5.3 %copy-start.8 = (bf16[1024,256]{1,0:T(8,128)(2,1)}, bf16[1024,256]{1,0:T(8,128)(2,1)S(1)}, u32[]{:S(2)}) copy-start(bf16[1024,256]{1,0:T(8,128)(2,1)S(1)} %collective-permute-done.2.refs_3_.refs_2_) | copy-start | bytes 1572868
  33.4 0.8 copy-start.9
  42.2 0.7 copy-start.10
  42.2 0.9 copy-start.1
  48.9 24.1 %collective-permute-start.6 = (bf16[144,512]{1,0:T(8,128)(2,1)S(1)}, bf16[144,512]{1,0:T(8,128)(2,1)S(1)}, u32[]{:S(2)}, u32[]{:S(2)}) collective-permute-start(bf16[144,512]{1,0:T(8,128)(2,1)S(1)} %shard_map.115.refs_6_), channel_id=1, source_target_pairs={{0,3},{1,2},{2,1},{3,0},{4,7},{5,6},{6,5},{7,4},{8,11},{9,10},{10,... | collective-permute-start | bytes 442376 | tf_op jit(solution)/shard_map/ppermute | solution.py:411
  53.2 0.7 copy-start.11
  59.8 13.2 %collective-permute-start.7 = (bf16[144,512]{1,0:T(8,128)(2,1)S(1)}, bf16[144,512]{1,0:T(8,128)(2,1)S(1)}, u32[]{:S(2)}, u32[]{:S(2)}) collective-permute-start(bf16[144,512]{1,0:T(8,128)(2,1)S(1)} %shard_map.116.refs_7_), channel_id=1, source_target_pairs={{0,2},{1,3},{2,0},{3,1},{4,6},{5,7},{6,4},{7,5},{8,10},{9,11},{10,... | collective-permute-start | bytes 442376 | tf_op jit(solution)/shard_map/ppermute | solution.py:411
  65.9 7.0 %collective-permute-start.8 = (bf16[144,512]{1,0:T(8,128)(2,1)S(1)}, bf16[144,512]{1,0:T(8,128)(2,1)S(1)}, u32[]{:S(2)}, u32[]{:S(2)}) collective-permute-start(bf16[144,512]{1,0:T(8,128)(2,1)S(1)} %get-tuple-element.11), channel_id=1, source_target_pairs={{0,1},{1,0},{2,3},{3,2},{4,5},{5,4},{6,7},{7,6},{8,9},{9,8},{10,11... | collective-permute-start | bytes 442376 | tf_op jit(solution)/shard_map/ppermute | solution.py:411
  74.5 16.9 %copy-start.2 = (bf16[3,3,3,16,384]{4,3,2,1,0:T(8,128)(2,1)S(1)}, bf16[3,3,3,16,384]{4,3,2,1,0:T(8,128)(2,1)}, u32[]{:S(2)}) copy-start(bf16[3,3,3,16,384]{4,3,2,1,0:T(8,128)(2,1)} %param.17) | copy-start | bytes 995332
  74.5 35.9 %all-to-all-start = ((bf16[32,24,128]{2,1,0:T(8,128)(2,1)}), bf16[32,24,128]{2,1,0:T(8,128)(2,1)S(1)}, u32[]{:S(2)}, u32[]{:S(2)}) async-start(bf16[32,24,128]{2,1,0:T(8,128)(2,1)} %shard_map.118), calls=%async_computation | async-start | bytes 393216 | tf_op jit(solution)/shard_map/all_to_all | solution.py:414
  110.5 9.9 %collective-permute-start.10 = (bf16[24,128]{1,0:T(8,128)(2,1)S(1)}, bf16[24,128]{1,0:T(8,128)(2,1)S(1)}, u32[]{:S(2)}, u32[]{:S(2)}) collective-permute-start(bf16[24,128]{1,0:T(8,128)(2,1)S(1)} %subtract_convert_fusion.own_ref), channel_id=1, source_target_pairs={{0,2},{1,3},{2,4},{3,5},{4,6},{5,7},{6,8},{7,9},{8,10},{9,11},{10,... | collective-permute-start | bytes 18440 | tf_op jit(solution)/shard_map/ppermute | solution.py:419
  116.0 8.2 %collective-permute-start.9 = (bf16[24,128]{1,0:T(8,128)(2,1)S(1)}, bf16[24,128]{1,0:T(8,128)(2,1)S(1)}, u32[]{:S(2)}, u32[]{:S(2)}) collective-permute-start(bf16[24,128]{1,0:T(8,128)(2,1)S(1)} %subtract_convert_fusion.own_ref), channel_id=1, source_target_pairs={{0,1},{1,2},{2,3},{3,4},{4,5},{5,6},{6,7},{7,8},{8,9},{9,10},{10,1... | collective-permute-start | bytes 18440 | tf_op jit(solution)/shard_map/ppermute | solution.py:418
  118.2 0.7 copy-start.6
  118.9 0.7 copy-start.7

commit v6 on v5

--- a/solution.py
+++ b/solution.py
@@ -266,6 +266,7 @@
 
 def combine_kernel(scale_ref, place_ref, *refs):
     chunk_refs, (latent_ref, out_ref) = refs[:4], refs[4:]
+    zh = place_ref[0]
     stats = []
     for h in range(2):
         base = 2 * PATCH + 3 * h
@@ -291,8 +292,8 @@
     for row in range(ROWS):
         for half in range(2):
             cut = window[row, half * 8 : half * 8 + CUT]
-            out_ref[half * ROWS + row] = cut.astype(jnp.bfloat16)
-    band = place_ref[0]
+            out_ref[half * SIDE + row % SIDE, (row // SIDE) ^ zh] = cut.astype(jnp.bfloat16)
+    band = zh * SIDE + place_ref[1]
     edge = pltpu.roll(latent_ref[...], 64, 1) * scale_ref[1]
     lane = lax.broadcasted_iota(jnp.int32, (TCOLS, 128), 1)
     for target, part in ((band + 1, lane < 32), (band - 1, lane >= 96)):
@@ -301,7 +302,7 @@
         def _():
             sent = jnp.where(part, edge, 0.0)
             for half in range(2):
-                at = half * ROWS + target
+                at = (half * SIDE + (target & 3), (target >> 2) ^ zh)
                 out_ref[at] = (
                     out_ref[at].astype(jnp.float32) + sent[half * 8 : half * 8 + CUT]
                 ).astype(jnp.bfloat16)
@@ -310,7 +311,7 @@
 def combine(scale, place, chunks, latent):
     return pl.pallas_call(
         combine_kernel,
-        out_shape=jax.ShapeDtypeStruct((2 * ROWS, CUT, 128), jnp.bfloat16),
+        out_shape=jax.ShapeDtypeStruct((2 * SIDE, SIDE, CUT, 128), jnp.bfloat16),
         in_specs=[SMEM, SMEM] + [VMEM] * 5,
         out_specs=VMEM,
         compiler_params=pltpu.CompilerParams(vmem_limit_bytes=16 * 2**20),
@@ -401,18 +402,21 @@
             jnp.where(cfg == 0, -1.0 / sigma, 0.0),
         ]
     )
-    place = jnp.stack([zh * SIDE + x, zl]).astype(jnp.int32)
-
-    near = attend(counts, queries[:2], blocks[:3])
+    place = jnp.stack([zh, x]).astype(jnp.int32)
+
+    near = attend(counts, queries[:1], blocks[:3])
     (third,) = attend(counts, queries[3:], blocks, weight=weight, extras=near[:1])
-    (second,) = attend(counts, queries[2:3], blocks, weight=weight, extras=(third,))
-    mine, first = attend(counts, queries[:2], blocks[3:], 3, weight, near, (second,))
+    second, first = attend(counts, queries[2:0:-1], blocks, weight=weight, extras=(third,))
+    (mine,) = attend(counts, queries[:1], blocks[3:], 3, weight, near, (second, first))
     chunks = [mine] + [
         lax.ppermute(chunk, "zl", crossed(m)) for m, chunk in ((3, third), (2, second), (1, first))
     ]
     shares = combine(scale, place, chunks, grid)
-    shares = lax.all_to_all(shares, ("cfg", "zh", "x"), 0, 0, tiled=True)
-    window = jnp.sum(shares.astype(jnp.float32), 0)
+    shares = lax.all_to_all(shares, ("cfg", "x"), 0, 0, tiled=True)
+    shares = jnp.sum(shares.astype(jnp.float32), 0)
+    other = lax.ppermute(shares[1:3], "zh", crossed(1))
+    passed = lax.ppermute(shares[3] + other[1], "zh", crossed(3))
+    window = shares[0] + other[0] + passed
 
     current = (latent_window - sigma * window).astype(jnp.bfloat16)
     last = lax.ppermute(current, seq, moved(1))

time: 126 us -> 117 us (0.929)
  waiting for transfers between devices: 34.6 us -> 11.7 us
  blocking collectives: 0 us -> 10.5 us
  starting transfers between devices: 53.8 us -> 57.5 us
  Pallas kernels: 28.5 us -> 26.8 us
    all_to_all x1 -> x0, waiting for transfers between devices: 19 us -> none  [local(): shares = lax.all_to_all(shares, ('cfg', 'zh', 'x'), 0, 0, tiled=True)]
    ppermute x0 -> x2, starting transfers between devices: none -> 18.5 us  [the longest x1 9.4 us: local(): passed = lax.ppermute(shares[3] + other[1], 'zh', crossed(3))]
    all_to_all x1 -> x0, starting transfers between devices: 16.9 us -> none  [local(): shares = lax.all_to_all(shares, ('cfg', 'zh', 'x'), 0, 0, tiled=True)]
    all_to_all x0 -> x1, blocking collectives: none -> 10.5 us  [local(): shares = lax.all_to_all(shares, ('cfg', 'x'), 0, 0, tiled=True)]
    ppermute x1, waiting for transfers between devices: 3.83 us -> 0.01 us  [local(): last = lax.ppermute(current, seq, moved(1))]
    ppermute x0 -> x2, waiting for transfers between devices: none -> 3.35 us  [the longest x1 1.79 us: local(): other = lax.ppermute(shares[1:3], 'zh', crossed(1))]
    ppermute x3, waiting for transfers between devices: 3.22 us -> 0.01 us  [local(): lax.ppermute(query[0], 'zl', crossed(m))]
    ppermute x3, starting transfers between devices: 7.11 us -> 10.1 us  [local(): lax.ppermute(query[0], 'zl', crossed(m))]
  transfers between devices with their start and end apart: 12 -> 13, of which waited for: 5 -> 6; matrix products, arithmetic and copies ran while one was open for 2% -> 2% of each run, Pallas kernels for 19% -> 20%
where the time goes in v6:
time: 117 us; the launch traced here: 116 us
  starting transfers between devices  57.5 us (49%)
  Pallas kernels  26.8 us (23%)
  waiting for transfers between devices  11.7 us (10%)
  blocking collectives  10.5 us (9%)
  local copies, waits for them, and re-layouts  6.56 us (6%)
  between operations  2.44 us (2%)
    pallas_call x4, Pallas kernels, attend(): pl.pallas_call(functools.partial(attention_kernel, nq=nq, nk=nk, start=st...  22.8 us
    ppermute x3, starting transfers between devices, local(): blocks = [own] + [lax.ppermute(own, 'y', ring(d)) for d in (1, 3, 2)]  12.8 us
    all_to_all x1, blocking collectives, local(): shares = lax.all_to_all(shares, ('cfg', 'x'), 0, 0, tiled=True)  10.5 us
    ppermute x3, starting transfers between devices, local(): lax.ppermute(query[0], 'zl', crossed(m))  10.1 us
    ppermute x1, starting transfers between devices, local(): passed = lax.ppermute(shares[3] + other[1], 'zh', crossed(3))  9.4 us
    ppermute x3, starting transfers between devices, local(): lax.ppermute(chunk, 'zl', crossed(m))  9.27 us
    ppermute x1, starting transfers between devices, local(): other = lax.ppermute(shares[1:3], 'zh', crossed(1))  9.12 us
    ppermute x3, waiting for transfers between devices, local(): blocks = [own] + [lax.ppermute(own, 'y', ring(d)) for d in (1, 3, 2)]  5.45 us
  transfers between devices with their start and end apart: 13, of which 6 were waited for; matrix products, arithmetic and copies ran while one was open for 2% of the time, Pallas kernels for 20%

profile of v6, /device:TPU:24, one launch (start us, length us, event | category | flops | bytes accessed | tf_op | source)
XLA Modules:
  0.0 115.9 jit_solution(14408352323463115081)
XLA Ops:
  0.7 2.0 %shard_map.113.refs_1_.refs_2_ = bf16[1024,256]{1,0:T(8,128)(2,1)} custom-call(bf16[512,256]{1,0:T(8,128)(2,1)} %bitcast.51, bf16[512,256]{1,0:T(8,128)(2,1)} %bitcast.52), custom_call_target="tpu_custom_call" | custom-call | tf_op jit(solution)/shard_map/pallas_call | solution.py:70
  2.7 7.5 %collective-permute-start.1 = (bf16[1024,256]{1,0:T(8,128)(2,1)}, bf16[1024,256]{1,0:T(8,128)(2,1)S(1)}, u32[]{:S(2)}, u32[]{:S(2)}) collective-permute-start(bf16[1024,256]{1,0:T(8,128)(2,1)} %shard_map.113.refs_1_.refs_2_), channel_id=1, source_target_pairs={{0,4},{4,8},{8,12},{12,0},{1,5},{5,9},{9,13},{13,1},{2,6},{6,10},{... | collective-permute-start | bytes 1572872 | tf_op jit(solution)/shard_map/ppermute | solution.py:385
  10.2 1.9 %collective-permute-start.2 = (bf16[1024,256]{1,0:T(8,128)(2,1)}, bf16[1024,256]{1,0:T(8,128)(2,1)S(1)}, u32[]{:S(2)}, u32[]{:S(2)}) collective-permute-start(bf16[1024,256]{1,0:T(8,128)(2,1)} %shard_map.113.refs_1_.refs_2_), channel_id=1, source_target_pairs={{0,12},{4,0},{8,4},{12,8},{1,13},{5,1},{9,5},{13,9},{2,14},{6,2},{... | collective-permute-start | bytes 1572872 | tf_op jit(solution)/shard_map/ppermute | solution.py:385
  12.2 3.4 %collective-permute-start = (bf16[1024,256]{1,0:T(8,128)(2,1)}, bf16[1024,256]{1,0:T(8,128)(2,1)S(1)}, u32[]{:S(2)}, u32[]{:S(2)}) collective-permute-start(bf16[1024,256]{1,0:T(8,128)(2,1)} %shard_map.113.refs_1_.refs_2_), channel_id=1, source_target_pairs={{0,8},{4,12},{8,0},{12,4},{1,9},{5,13},{9,1},{13,5},{2,10},{6,14},... | collective-permute-start | bytes 1572872 | tf_op jit(solution)/shard_map/ppermute | solution.py:385
  15.5 2.7 %collective-permute-start.5 = (bf16[512,256]{1,0:T(8,128)(2,1)S(1)}, bf16[512,256]{1,0:T(8,128)(2,1)S(1)}, u32[]{:S(2)}, u32[]{:S(2)}) collective-permute-start(bf16[512,256]{1,0:T(8,128)(2,1)S(1)} %bitcast.55), channel_id=1, source_target_pairs={{0,3},{1,2},{2,1},{3,0},{4,7},{5,6},{6,5},{7,4},{8,11},{9,10},{10,... | collective-permute-start | bytes 786440 | tf_op jit(solution)/shard_map/ppermute | solution.py:386
  18.3 1.9 %collective-permute-start.3 = (bf16[512,256]{1,0:T(8,128)(2,1)S(1)}, bf16[512,256]{1,0:T(8,128)(2,1)S(1)}, u32[]{:S(2)}, u32[]{:S(2)}) collective-permute-start(bf16[512,256]{1,0:T(8,128)(2,1)S(1)} %bitcast.56), channel_id=1, source_target_pairs={{0,2},{1,3},{2,0},{3,1},{4,6},{5,7},{6,4},{7,5},{8,10},{9,11},{10,... | collective-permute-start | bytes 786440 | tf_op jit(solution)/shard_map/ppermute | solution.py:386
  21.6 0.6 bitcast_bitcast_fusion.refs_5_.refs_6_.refs_2_
  22.3 0.1 copy-done.4
  22.4 0.1 pad_maximum_fusion.1.scale_ref
  22.4 5.5 %collective-permute-start.4 = (bf16[512,256]{1,0:T(8,128)(2,1)S(1)}, bf16[512,256]{1,0:T(8,128)(2,1)S(1)}, u32[]{:S(2)}, u32[]{:S(2)}) collective-permute-start(bf16[512,256]{1,0:T(8,128)(2,1)S(1)} %bitcast.57), channel_id=1, source_target_pairs={{0,1},{1,0},{2,3},{3,2},{4,5},{5,4},{6,7},{7,6},{8,9},{9,8},{10,11... | collective-permute-start | bytes 786440 | tf_op jit(solution)/shard_map/ppermute | solution.py:386
  27.9 0.1 fusion.4.count_ref
  28.0 5.4 %collective-permute-done.2.refs_3_.refs_4_ = bf16[1024,256]{1,0:T(8,128)(2,1)S(1)} collective-permute-done((bf16[1024,256]{1,0:T(8,128)(2,1)}, bf16[1024,256]{1,0:T(8,128)(2,1)S(1)}, u32[]{:S(2)}, u32[]{:S(2)}) %collective-permute-start.2) | collective-permute-done | bytes 524320 | tf_op jit(solution)/shard_map/ppermute | solution.py:385
  33.4 0.8 copy-done.8
  34.2 5.2 %shard_map.114 = (f32[1,2,512]{2,1,0:T(2,128)S(1)}, f32[1,2,512]{2,1,0:T(2,128)S(1)}, f32[1,2,128,512]{3,2,1,0:T(8,128)}) custom-call(s32[4]{0:T(128)S(1)} %fusion.4.count_ref, bf16[512,256]{1,0:T(8,128)(2,1)} %bitcast.53, bf16[1024,256]{1,0:T(8,128)(2,1)} %shard_map.113.refs_1_.refs_2_, bf16[1024,256]{1,0:T(8,128)(2,1)} %copy-done.7, ...), custom_call_target="tpu_custom_call" | custom-call | flops 805306368 | bytes 1835008 | tf_op jit(solution)/shard_map/pallas_call | solution.py:237
  39.5 0.7 copy-done.10
  40.1 0.2 copy-done.1
  40.3 5.7 %shard_map.115.refs_7_ = bf16[144,512]{1,0:T(8,128)(2,1)S(1)} custom-call(s32[4]{0:T(128)S(1)} %fusion.4.count_ref, bf16[512,256]{1,0:T(8,128)(2,1)} %copy-done.10, bf16[1024,256]{1,0:T(8,128)(2,1)} %shard_map.113.refs_1_.refs_2_, bf16[1024,256]{1,0:T(8,128)(2,1)} %copy-done.7, bf16[1024,256]{1,0:T(8,128)(2,1)} %copy-done.8, bf16[1024,256]{1,0:T(8,128)(2,1)} %copy-done.1, ...), custom_call_target="tpu_custom_call" | custom-call | flops 1073741824 | bytes 2359296 | tf_op jit(solution)/shard_map/pallas_call | solution.py:237
  46.0 5.1 %collective-permute-start.6 = (bf16[144,512]{1,0:T(8,128)(2,1)S(1)}, bf16[144,512]{1,0:T(8,128)(2,1)S(1)}, u32[]{:S(2)}, u32[]{:S(2)}) collective-permute-start(bf16[144,512]{1,0:T(8,128)(2,1)S(1)} %shard_map.115.refs_7_), channel_id=1, source_target_pairs={{0,3},{1,2},{2,1},{3,0},{4,7},{5,6},{6,5},{7,4},{8,11},{9,10},{10,... | collective-permute-start | bytes 442376 | tf_op jit(solution)/shard_map/ppermute | solution.py:412
  51.2 0.7 copy-done.9
  51.9 0.7 copy-done.11
  52.6 8.8 %shard_map.116 = (bf16[144,512]{1,0:T(8,128)(2,1)S(1)}, bf16[144,512]{1,0:T(8,128)(2,1)S(1)}) custom-call(s32[4]{0:T(128)S(1)} %fusion.4.count_ref, bf16[512,256]{1,0:T(8,128)(2,1)} %copy-done.9, bf16[512,256]{1,0:T(8,128)(2,1)} %copy-done.11, bf16[1024,256]{1,0:T(8,128)(2,1)} %shard_map.113.refs_1_.refs_2_, bf16[1024,256]{1,0:T(8,128)(2,1)} %copy-done.7, ...), custom_call_target="tpu_custom_call" | custom-call | flops 2147483648 | bytes 2621440 | tf_op jit(solution)/shard_map/pallas_call | solution.py:237
  61.4 1.9 %collective-permute-start.7 = (bf16[144,512]{1,0:T(8,128)(2,1)S(1)}, bf16[144,512]{1,0:T(8,128)(2,1)S(1)}, u32[]{:S(2)}, u32[]{:S(2)}) collective-permute-start(bf16[144,512]{1,0:T(8,128)(2,1)S(1)} %get-tuple-element.10.refs_6_), channel_id=1, source_target_pairs={{0,2},{1,3},{2,0},{3,1},{4,6},{5,7},{6,4},{7,5},{8,10},{9,11},{10,... | collective-permute-start | bytes 442376 | tf_op jit(solution)/shard_map/ppermute | solution.py:412
  63.3 2.2 %collective-permute-start.8 = (bf16[144,512]{1,0:T(8,128)(2,1)S(1)}, bf16[144,512]{1,0:T(8,128)(2,1)S(1)}, u32[]{:S(2)}, u32[]{:S(2)}) collective-permute-start(bf16[144,512]{1,0:T(8,128)(2,1)S(1)} %get-tuple-element.11.refs_7_), channel_id=1, source_target_pairs={{0,1},{1,0},{2,3},{3,2},{4,5},{5,4},{6,7},{7,6},{8,9},{9,8},{10,11... | collective-permute-start | bytes 442376 | tf_op jit(solution)/shard_map/ppermute | solution.py:412
  65.5 0.1 pad_add_fusion.place_ref
  65.6 0.1 copy.18
  65.7 0.1 squeeze.30
  65.8 0.1 copy.19
  65.8 0.1 squeeze.31
  65.9 0.1 pad_maximum_fusion.refs_4_
  66.0 3.2 %shard_map.117.refs_0_ = bf16[144,512]{1,0:T(8,128)(2,1)S(1)} custom-call(s32[4]{0:T(128)S(1)} %fusion.4.count_ref, bf16[512,256]{1,0:T(8,128)(2,1)} %bitcast.54, bf16[1024,256]{1,0:T(8,128)(2,1)} %copy-done.1, bf16[2,64,128]{2,1,0:T(8,128)(2,1)} %bitcast_bitcast_fusion.refs_5_.refs_6_.refs_2_, f32[1,2,512]{2,1,0:T(2,128)S(1)} %get-tuple-element.7.refs_6_.refs_3_, ...), custom_call_target="tpu_custom_call" | custom-call | flops 268435456 | bytes 786432 | tf_op jit(solution)/shard_map/pallas_call | solution.py:237
  69.2 1.6 %collective-permute-done.7.refs_2_ = bf16[144,512]{1,0:T(8,128)(2,1)S(1)} collective-permute-done((bf16[144,512]{1,0:T(8,128)(2,1)S(1)}, bf16[144,512]{1,0:T(8,128)(2,1)S(1)}, u32[]{:S(2)}, u32[]{:S(2)}) %collective-permute-start.7) | collective-permute-done | bytes 147488 | tf_op jit(solution)/shard_map/ppermute | solution.py:412
  70.7 1.1 collective-permute-done.8.refs_3_
  71.8 0.8 shard_map.118
  72.6 10.5 %all_to_all.5 = bf16[8,4,24,128]{3,2,1,0:T(8,128)(2,1)S(1)} all-to-all(bf16[8,4,24,128]{3,2,1,0:T(8,128)(2,1)S(1)} %shard_map.118), channel_id=1, replica_groups=mesh['cfg'=2,'zh'=4,'x'=4,'y'=4,'zl'=4] {'cfg','x'}, dimensions={0} | all-to-all | bytes 393216 | tf_op jit(solution)/shard_map/all_to_all | solution.py:415
  83.2 9.1 %collective-permute-start.9 = (f32[2,24,128]{2,1,0:T(8,128)S(1)}, f32[2,24,128]{2,1,0:T(8,128)S(1)}, u32[]{:S(2)}, u32[]{:S(2)}) collective-permute-start(f32[2,24,128]{2,1,0:T(8,128)S(1)} %slice.35), channel_id=1, source_target_pairs={{0,64},{64,0},{128,192},{192,128},{1,65},{65,1},{129,193},{193,129... | collective-permute-start | bytes 73736 | tf_op jit(solution)/shard_map/ppermute | solution.py:417
  92.3 1.8 %collective-permute-done.9 = f32[2,24,128]{2,1,0:T(8,128)S(1)} collective-permute-done((f32[2,24,128]{2,1,0:T(8,128)S(1)}, f32[2,24,128]{2,1,0:T(8,128)S(1)}, u32[]{:S(2)}, u32[]{:S(2)}) %collective-permute-start.9) | collective-permute-done | bytes 24608 | tf_op jit(solution)/shard_map/ppermute | solution.py:417
  94.1 9.4 %collective-permute-start.10 = (f32[24,128]{1,0:T(8,128)S(1)}, f32[24,128]{1,0:T(8,128)S(1)}, u32[]{:S(2)}, u32[]{:S(2)}) collective-permute-start(f32[24,128]{1,0:T(8,128)S(1)} %fusion), channel_id=1, source_target_pairs={{0,192},{64,128},{128,64},{192,0},{1,193},{65,129},{129,65},{193,1... | collective-permute-start | bytes 36872 | tf_op jit(solution)/shard_map/ppermute | solution.py:418
  103.6 1.6 %collective-permute-done.10 = f32[24,128]{1,0:T(8,128)S(1)} collective-permute-done((f32[24,128]{1,0:T(8,128)S(1)}, f32[24,128]{1,0:T(8,128)S(1)}, u32[]{:S(2)}, u32[]{:S(2)}) %collective-permute-start.10) | collective-permute-done | bytes 12320 | tf_op jit(solution)/shard_map/ppermute | solution.py:418
  105.2 2.2 %collective-permute-start.11 = (bf16[24,128]{1,0:T(8,128)(2,1)S(1)}, bf16[24,128]{1,0:T(8,128)(2,1)S(1)}, u32[]{:S(2)}, u32[]{:S(2)}) collective-permute-start(bf16[24,128]{1,0:T(8,128)(2,1)S(1)} %get-tuple-element.14.own_ref), channel_id=1, source_target_pairs={{0,1},{1,2},{2,3},{3,4},{4,5},{5,6},{6,7},{7,8},{8,9},{9,10},{10,1... | collective-permute-start | bytes 18440 | tf_op jit(solution)/shard_map/ppermute | solution.py:422
  107.4 4.6 %collective-permute-start.12 = (bf16[24,128]{1,0:T(8,128)(2,1)S(1)}, bf16[24,128]{1,0:T(8,128)(2,1)S(1)}, u32[]{:S(2)}, u32[]{:S(2)}) collective-permute-start(bf16[24,128]{1,0:T(8,128)(2,1)S(1)} %get-tuple-element.14.own_ref), channel_id=1, source_target_pairs={{0,2},{1,3},{2,4},{3,5},{4,6},{5,7},{6,8},{7,9},{8,10},{9,11},{10,... | collective-permute-start | bytes 18440 | tf_op jit(solution)/shard_map/ppermute | solution.py:423
  112.0 0.1 fusion.6
  112.3 0.6 copy-done.5
  112.9 0.7 copy-done.6
  113.6 0.1 dynamic-slice
  113.7 0.1 reshape.50
  113.8 0.7 copy.23
  114.5 0.2 collective-permute-done.12.older_ref
  114.7 1.2 %shard_map.119 = bf16[2,32,384]{2,1,0:T(8,128)(2,1)} custom-call(s32[1]{0:T(128)} %bitcast.20.half_ref, bf16[24,128]{1,0:T(8,128)(2,1)S(1)} %get-tuple-element.14.own_ref, bf16[24,128]{1,0:T(8,128)(2,1)S(1)} %collective-permute-done.11.last_ref, bf16[24,128]{1,0:T(8,128)(2,1)S(1)} %collective-permute-done.12.older_ref, bf16[768,384]{1,0:T(8,128)(2,1)S(1)} %bitcast.47, ...), custom_call_target="tpu_custom_call" | custom-call | tf_op jit(solution)/shard_map/pallas_call | solution.py:357
  (35 shorter events, 0.3 us)
Async XLA Ops:
  0.6 21.0 %copy-start = (bf16[4096,64]{0,1:T(8,128)(2,1)S(1)}, bf16[4096,64]{0,1:T(8,128)(2,1)}, u32[]{:S(2)}) copy-start(bf16[4096,64]{0,1:T(8,128)(2,1)} %param.16) | copy-start | bytes 1572868
  0.6 14.9 %copy-start.3 = (bf16[1,512,256]{2,1,0:T(8,128)(2,1)S(1)}, bf16[1,512,256]{2,1,0:T(8,128)(2,1)}, u32[]{:S(2)}) copy-start(bf16[1,512,256]{2,1,0:T(8,128)(2,1)} %param.10) | copy-start | bytes 786436
  2.7 19.7 %collective-permute-start.1 = (bf16[1024,256]{1,0:T(8,128)(2,1)}, bf16[1024,256]{1,0:T(8,128)(2,1)S(1)}, u32[]{:S(2)}, u32[]{:S(2)}) collective-permute-start(bf16[1024,256]{1,0:T(8,128)(2,1)} %shard_map.113.refs_1_.refs_2_), channel_id=1, source_target_pairs={{0,4},{4,8},{8,12},{12,0},{1,5},{5,9},{9,13},{13,1},{2,6},{6,10},{... | collective-permute-start | bytes 1572872 | tf_op jit(solution)/shard_map/ppermute | solution.py:385
  10.2 23.2 %collective-permute-start.2 = (bf16[1024,256]{1,0:T(8,128)(2,1)}, bf16[1024,256]{1,0:T(8,128)(2,1)S(1)}, u32[]{:S(2)}, u32[]{:S(2)}) collective-permute-start(bf16[1024,256]{1,0:T(8,128)(2,1)} %shard_map.113.refs_1_.refs_2_), channel_id=1, source_target_pairs={{0,12},{4,0},{8,4},{12,8},{1,13},{5,1},{9,5},{13,9},{2,14},{6,2},{... | collective-permute-start | bytes 1572872 | tf_op jit(solution)/shard_map/ppermute | solution.py:385
  12.2 27.3 %collective-permute-start = (bf16[1024,256]{1,0:T(8,128)(2,1)}, bf16[1024,256]{1,0:T(8,128)(2,1)S(1)}, u32[]{:S(2)}, u32[]{:S(2)}) collective-permute-start(bf16[1024,256]{1,0:T(8,128)(2,1)} %shard_map.113.refs_1_.refs_2_), channel_id=1, source_target_pairs={{0,8},{4,12},{8,0},{12,4},{1,9},{5,13},{9,1},{13,5},{2,10},{6,14},... | collective-permute-start | bytes 1572872 | tf_op jit(solution)/shard_map/ppermute | solution.py:385
  15.5 23.9 %collective-permute-start.5 = (bf16[512,256]{1,0:T(8,128)(2,1)S(1)}, bf16[512,256]{1,0:T(8,128)(2,1)S(1)}, u32[]{:S(2)}, u32[]{:S(2)}) collective-permute-start(bf16[512,256]{1,0:T(8,128)(2,1)S(1)} %bitcast.55), channel_id=1, source_target_pairs={{0,3},{1,2},{2,1},{3,0},{4,7},{5,6},{6,5},{7,4},{8,11},{9,10},{10,... | collective-permute-start | bytes 786440 | tf_op jit(solution)/shard_map/ppermute | solution.py:386
  18.3 32.9 %collective-permute-start.3 = (bf16[512,256]{1,0:T(8,128)(2,1)S(1)}, bf16[512,256]{1,0:T(8,128)(2,1)S(1)}, u32[]{:S(2)}, u32[]{:S(2)}) collective-permute-start(bf16[512,256]{1,0:T(8,128)(2,1)S(1)} %bitcast.56), channel_id=1, source_target_pairs={{0,2},{1,3},{2,0},{3,1},{4,6},{5,7},{6,4},{7,5},{8,10},{9,11},{10,... | collective-permute-start | bytes 786440 | tf_op jit(solution)/shard_map/ppermute | solution.py:386
  21.6 0.7 copy-start.4
  22.4 11.0 %copy-start.7 = (bf16[1024,256]{1,0:T(8,128)(2,1)}, bf16[1024,256]{1,0:T(8,128)(2,1)S(1)}, u32[]{:S(2)}) copy-start(bf16[1024,256]{1,0:T(8,128)(2,1)S(1)} %collective-permute-done.1.refs_2_.refs_3_) | copy-start | bytes 1572868
  22.4 28.7 %collective-permute-start.4 = (bf16[512,256]{1,0:T(8,128)(2,1)S(1)}, bf16[512,256]{1,0:T(8,128)(2,1)S(1)}, u32[]{:S(2)}, u32[]{:S(2)}) collective-permute-start(bf16[512,256]{1,0:T(8,128)(2,1)S(1)} %bitcast.57), channel_id=1, source_target_pairs={{0,1},{1,0},{2,3},{3,2},{4,5},{5,4},{6,7},{7,6},{8,9},{9,8},{10,11... | collective-permute-start | bytes 786440 | tf_op jit(solution)/shard_map/ppermute | solution.py:386
  33.4 0.8 copy-start.8
  39.4 0.7 copy-start.10
  39.4 0.9 copy-start.1
  46.0 25.8 %collective-permute-start.6 = (bf16[144,512]{1,0:T(8,128)(2,1)S(1)}, bf16[144,512]{1,0:T(8,128)(2,1)S(1)}, u32[]{:S(2)}, u32[]{:S(2)}) collective-permute-start(bf16[144,512]{1,0:T(8,128)(2,1)S(1)} %shard_map.115.refs_7_), channel_id=1, source_target_pairs={{0,3},{1,2},{2,1},{3,0},{4,7},{5,6},{6,5},{7,4},{8,11},{9,10},{10,... | collective-permute-start | bytes 442376 | tf_op jit(solution)/shard_map/ppermute | solution.py:412
  51.1 0.7 copy-start.9
  51.9 0.7 copy-start.11
  61.4 9.3 %collective-permute-start.7 = (bf16[144,512]{1,0:T(8,128)(2,1)S(1)}, bf16[144,512]{1,0:T(8,128)(2,1)S(1)}, u32[]{:S(2)}, u32[]{:S(2)}) collective-permute-start(bf16[144,512]{1,0:T(8,128)(2,1)S(1)} %get-tuple-element.10.refs_6_), channel_id=1, source_target_pairs={{0,2},{1,3},{2,0},{3,1},{4,6},{5,7},{6,4},{7,5},{8,10},{9,11},{10,... | collective-permute-start | bytes 442376 | tf_op jit(solution)/shard_map/ppermute | solution.py:412
  63.3 8.5 %collective-permute-start.8 = (bf16[144,512]{1,0:T(8,128)(2,1)S(1)}, bf16[144,512]{1,0:T(8,128)(2,1)S(1)}, u32[]{:S(2)}, u32[]{:S(2)}) collective-permute-start(bf16[144,512]{1,0:T(8,128)(2,1)S(1)} %get-tuple-element.11.refs_7_), channel_id=1, source_target_pairs={{0,1},{1,0},{2,3},{3,2},{4,5},{5,4},{6,7},{7,6},{8,9},{9,8},{10,11... | collective-permute-start | bytes 442376 | tf_op jit(solution)/shard_map/ppermute | solution.py:412
  72.6 30.9 %copy-start.2 = (bf16[3,3,3,16,384]{4,3,2,1,0:T(8,128)(2,1)S(1)}, bf16[3,3,3,16,384]{4,3,2,1,0:T(8,128)(2,1)}, u32[]{:S(2)}) copy-start(bf16[3,3,3,16,384]{4,3,2,1,0:T(8,128)(2,1)} %param.17) | copy-start | bytes 995332
  83.2 10.9 %collective-permute-start.9 = (f32[2,24,128]{2,1,0:T(8,128)S(1)}, f32[2,24,128]{2,1,0:T(8,128)S(1)}, u32[]{:S(2)}, u32[]{:S(2)}) collective-permute-start(f32[2,24,128]{2,1,0:T(8,128)S(1)} %slice.35), channel_id=1, source_target_pairs={{0,64},{64,0},{128,192},{192,128},{1,65},{65,1},{129,193},{193,129... | collective-permute-start | bytes 73736 | tf_op jit(solution)/shard_map/ppermute | solution.py:417
  94.1 11.1 %collective-permute-start.10 = (f32[24,128]{1,0:T(8,128)S(1)}, f32[24,128]{1,0:T(8,128)S(1)}, u32[]{:S(2)}, u32[]{:S(2)}) collective-permute-start(f32[24,128]{1,0:T(8,128)S(1)} %fusion), channel_id=1, source_target_pairs={{0,192},{64,128},{128,64},{192,0},{1,193},{65,129},{129,65},{193,1... | collective-permute-start | bytes 36872 | tf_op jit(solution)/shard_map/ppermute | solution.py:418
  105.2 9.3 %collective-permute-start.11 = (bf16[24,128]{1,0:T(8,128)(2,1)S(1)}, bf16[24,128]{1,0:T(8,128)(2,1)S(1)}, u32[]{:S(2)}, u32[]{:S(2)}) collective-permute-start(bf16[24,128]{1,0:T(8,128)(2,1)S(1)} %get-tuple-element.14.own_ref), channel_id=1, source_target_pairs={{0,1},{1,2},{2,3},{3,4},{4,5},{5,6},{6,7},{7,8},{8,9},{9,10},{10,1... | collective-permute-start | bytes 18440 | tf_op jit(solution)/shard_map/ppermute | solution.py:422
  107.4 7.3 %collective-permute-start.12 = (bf16[24,128]{1,0:T(8,128)(2,1)S(1)}, bf16[24,128]{1,0:T(8,128)(2,1)S(1)}, u32[]{:S(2)}, u32[]{:S(2)}) collective-permute-start(bf16[24,128]{1,0:T(8,128)(2,1)S(1)} %get-tuple-element.14.own_ref), channel_id=1, source_target_pairs={{0,2},{1,3},{2,4},{3,5},{4,6},{5,7},{6,8},{7,9},{8,10},{9,11},{10,... | collective-permute-start | bytes 18440 | tf_op jit(solution)/shard_map/ppermute | solution.py:423
  112.2 0.7 copy-start.5
  112.9 0.7 copy-start.6

commit v7 on v6

--- a/solution.py
+++ b/solution.py
@@ -80,7 +80,7 @@
     )(in_hbm(keys), in_hbm(values))
 
 
-def attention_kernel(count_ref, *refs, nq, nk, start, carry, nx, last):
+def attention_kernel(count_ref, *refs, nq, nk, nx):
     refs = list(refs)
 
     def take(size):
@@ -89,16 +89,9 @@
         return taken
 
     q_refs, kv_refs = take(nq), take(nk)
-    weight_hbm = take(1)[0] if last else None
-    if carry:
-        top_in, denom_in, acc_in = take(3)
-    take(nx)
-    if last:
-        chunk_refs = take(nq)
-        qs, ks, vs, scores, sems, acc_ref, top_ref, denom, weight_ref = refs
-    else:
-        top_ref, denom, acc_out = take(3)
-        qs, ks, vs, scores, sems, acc_ref = refs
+    weight_hbm = take(1 + nx)[0]
+    chunk_refs = take(nq)
+    qs, ks, vs, scores, sems, acc_ref, top_ref, denom, weight_ref = refs
 
     sem = iter(range(64))
 
@@ -121,18 +114,11 @@
                 )
         if b == 0:
             group += [copied(q_refs[j], qs.at[j]) for j in range(nq)]
-            if carry:
-                group.append(copied(acc_in, acc_ref))
         arriving.append(group)
-    if last:
-        arriving[0].append(copied(weight_hbm, weight_ref))
-    if carry:
-        top_ref[...] = top_in[...]
-        denom[...] = denom_in[...]
-    else:
-        top_ref[...] = jnp.full((nq, 2, TOK), NEG_FILL, jnp.float32)
-        denom[...] = jnp.zeros((nq, 2, TOK), jnp.float32)
-        acc_ref[...] = jnp.zeros((nq, 2, DH, TOK), jnp.float32)
+    arriving[0].append(copied(weight_hbm, weight_ref))
+    top_ref[...] = jnp.full((nq, 2, TOK), NEG_FILL, jnp.float32)
+    denom[...] = jnp.zeros((nq, 2, TOK), jnp.float32)
+    acc_ref[...] = jnp.zeros((nq, 2, DH, TOK), jnp.float32)
     for b in range(nk):
         for h in range(2):
             vs[b, h, DH:] = jnp.ones((16, TOK), jnp.bfloat16)
@@ -149,7 +135,7 @@
 
     def folded(j, b, h, score, masked):
         if masked:
-            valid = lax.broadcasted_iota(jnp.int32, (TOK, TOK), 0) < count_ref[start + b]
+            valid = lax.broadcasted_iota(jnp.int32, (TOK, TOK), 0) < count_ref[b]
             score = jnp.where(valid, score, NEG_FILL)
         old = top_ref[j, h : h + 1]
         new = jnp.maximum(old, jnp.max(score, axis=0, keepdims=True))
@@ -168,7 +154,7 @@
         j, b = lax.div(t, nk), lax.rem(t, nk)
         later = jnp.minimum(t + 1, total - 1)
         next_j, next_b = lax.div(later, nk), lax.rem(later, nk)
-        count = count_ref[start + b]
+        count = count_ref[b]
         for needed in range(1, nk):
 
             @pl.when(t == needed - 1)
@@ -198,11 +184,6 @@
 
     scores[0] = scored(0, 0, 0)
     lax.fori_loop(0, total, step, 0)
-    if not last:
-        copy = pltpu.make_async_copy(acc_ref, acc_out, sems.at[0])
-        copy.start()
-        copy.wait()
-        return
     for j in range(nq):
         parts, rows = [], []
         for h in range(2):
@@ -217,56 +198,35 @@
         chunk_refs[j][...] = jnp.concatenate(parts + rows + [blank], 0).astype(jnp.bfloat16)
 
 
-def attend(counts, queries, blocks, start=0, weight=None, state=(), extras=()):
+def attend(counts, queries, blocks, weight, extras=()):
     f32, bf16 = jnp.float32, jnp.bfloat16
-    nq, nk, last = len(queries), len(blocks), weight is not None
-    stat = jax.ShapeDtypeStruct((nq, 2, TOK), f32)
-    chunk = jax.ShapeDtypeStruct((CHUNK, TOK), bf16)
-    acc = pltpu.HBM((nq, 2, DH, TOK), f32)
-    scratch = [
-        pltpu.VMEM((nq, TOK, 2 * DH), bf16),
-        pltpu.VMEM((nk, TOK, 2 * DH), bf16),
-        pltpu.VMEM((nk, 2, DH + 16, TOK), bf16),
-        pltpu.VMEM((2, TOK, TOK), f32),
-        pltpu.SemaphoreType.DMA((5 * nk + nq + 2,)),
-        pltpu.VMEM((nq, 2, DH, TOK), f32),
-    ]
-    if last:
-        scratch += [pltpu.VMEM((nq, 2, TOK), f32)] * 2 + [pltpu.VMEM((2, PATCH, DH), bf16)]
+    nq, nk = len(queries), len(blocks)
     work = nq * nk * 2 * TOK * TOK
     return pl.pallas_call(
-        functools.partial(
-            attention_kernel,
-            nq=nq,
-            nk=nk,
-            start=start,
-            carry=bool(state),
-            nx=len(extras),
-            last=last,
-        ),
-        out_shape=(chunk,) * nq if last else (stat, stat, acc),
-        in_specs=[SMEM]
-        + [HBM] * (nq + nk + last)
-        + ([VMEM, VMEM, HBM] if state else [])
-        + [ANY] * len(extras),
-        out_specs=(VMEM,) * nq if last else (VMEM, VMEM, HBM),
-        scratch_shapes=scratch,
+        functools.partial(attention_kernel, nq=nq, nk=nk, nx=len(extras)),
+        out_shape=(jax.ShapeDtypeStruct((CHUNK, TOK), bf16),) * nq,
+        in_specs=[SMEM] + [HBM] * (nq + nk + 1) + [ANY] * len(extras),
+        out_specs=(VMEM,) * nq,
+        scratch_shapes=[
+            pltpu.VMEM((nq, TOK, 2 * DH), bf16),
+            pltpu.VMEM((nk, TOK, 2 * DH), bf16),
+            pltpu.VMEM((nk, 2, DH + 16, TOK), bf16),
+            pltpu.VMEM((2, TOK, TOK), f32),
+            pltpu.SemaphoreType.DMA((5 * nk + nq + 1,)),
+            pltpu.VMEM((nq, 2, DH, TOK), f32),
+            pltpu.VMEM((nq, 2, TOK), f32),
+            pltpu.VMEM((nq, 2, TOK), f32),
+            pltpu.VMEM((2, PATCH, DH), bf16),
+        ],
         compiler_params=pltpu.CompilerParams(vmem_limit_bytes=24 * 2**20),
         cost_estimate=pl.CostEstimate(
             flops=work * DH * 4, transcendentals=work, bytes_accessed=(nq + 2 * nk) * TOK * 4 * DH
         ),
-    )(
-        counts,
-        *(in_hbm(x) for x in (*queries, *blocks)),
-        *((in_hbm(weight),) if last else ()),
-        *(in_hbm(x) if x.ndim == 4 else x for x in state),
-        *extras,
-    )
+    )(counts, *(in_hbm(x) for x in (*queries, *blocks, weight)), *extras)
 
 
 def combine_kernel(scale_ref, place_ref, *refs):
     chunk_refs, (latent_ref, out_ref) = refs[:4], refs[4:]
-    zh = place_ref[0]
     stats = []
     for h in range(2):
         base = 2 * PATCH + 3 * h
@@ -292,8 +252,8 @@
     for row in range(ROWS):
         for half in range(2):
             cut = window[row, half * 8 : half * 8 + CUT]
-            out_ref[half * SIDE + row % SIDE, (row // SIDE) ^ zh] = cut.astype(jnp.bfloat16)
-    band = zh * SIDE + place_ref[1]
+            out_ref[half * SIDE + row % SIDE, row // SIDE] = cut.astype(jnp.bfloat16)
+    band = place_ref[0]
     edge = pltpu.roll(latent_ref[...], 64, 1) * scale_ref[1]
     lane = lax.broadcasted_iota(jnp.int32, (TCOLS, 128), 1)
     for target, part in ((band + 1, lane < 32), (band - 1, lane >= 96)):
@@ -302,7 +262,7 @@
         def _():
             sent = jnp.where(part, edge, 0.0)
             for half in range(2):
-                at = (half * SIDE + (target & 3), (target >> 2) ^ zh)
+                at = (half * SIDE + (target & 3), target >> 2)
                 out_ref[at] = (
                     out_ref[at].astype(jnp.float32) + sent[half * 8 : half * 8 + CUT]
                 ).astype(jnp.bfloat16)
@@ -402,21 +362,18 @@
             jnp.where(cfg == 0, -1.0 / sigma, 0.0),
         ]
     )
-    place = jnp.stack([zh, x]).astype(jnp.int32)
-
-    near = attend(counts, queries[:1], blocks[:3])
-    (third,) = attend(counts, queries[3:], blocks, weight=weight, extras=near[:1])
-    second, first = attend(counts, queries[2:0:-1], blocks, weight=weight, extras=(third,))
-    (mine,) = attend(counts, queries[:1], blocks[3:], 3, weight, near, (second, first))
+    place = (zh * SIDE + x).astype(jnp.int32).reshape(1)
+
+    third, second, first = attend(counts, queries[3:0:-1], blocks, weight)
+    (mine,) = attend(counts, queries[:1], blocks, weight, extras=(third,))
     chunks = [mine] + [
         lax.ppermute(chunk, "zl", crossed(m)) for m, chunk in ((3, third), (2, second), (1, first))
     ]
     shares = combine(scale, place, chunks, grid)
     shares = lax.all_to_all(shares, ("cfg", "x"), 0, 0, tiled=True)
     shares = jnp.sum(shares.astype(jnp.float32), 0)
-    other = lax.ppermute(shares[1:3], "zh", crossed(1))
-    passed = lax.ppermute(shares[3] + other[1], "zh", crossed(3))
-    window = shares[0] + other[0] + passed
+    shares = lax.all_to_all(shares, "zh", 0, 0, tiled=True)
+    window = jnp.sum(shares, 0)
 
     current = (latent_window - sigma * window).astype(jnp.bfloat16)
     last = lax.ppermute(current, seq, moved(1))

time: 117 us -> 119 us (1.017)
  waiting for transfers between devices: 11.7 us -> 25.7 us
  Pallas kernels: 26.8 us -> 21.6 us
  starting transfers between devices: 57.5 us -> 52.4 us
  local copies, waits for them, and re-layouts: 6.56 us -> 5.04 us
    ppermute x2 -> x0, starting transfers between devices: 18.5 us -> none  [the longest x1 9.4 us: local(): passed = lax.ppermute(shares[3] + other[1], 'zh', crossed(3))]
    all_to_all x0 -> x1, waiting for transfers between devices: none -> 12.8 us  [local(): shares = lax.all_to_all(shares, 'zh', 0, 0, tiled=True)]
    all_to_all x0 -> x1, starting transfers between devices: none -> 12.4 us  [local(): shares = lax.all_to_all(shares, 'zh', 0, 0, tiled=True)]
    ppermute x3, waiting for transfers between devices: 0.01 us -> 6.77 us  [local(): lax.ppermute(query[0], 'zl', crossed(m))]
    pallas_call x4 -> x2, Pallas kernels: 22.8 us -> 17.6 us  [attend(): pl.pallas_call(functools.partial(attention_kernel, nq=nq, nk=nk, nx=len(e...]
    ppermute x3, starting transfers between devices: 10.1 us -> 14.1 us  [local(): lax.ppermute(query[0], 'zl', crossed(m))]
    ppermute x3, starting transfers between devices: 12.8 us -> 8.98 us  [local(): blocks = [own] + [lax.ppermute(own, 'y', ring(d)) for d in (1, 3, 2)]]
    ppermute x2 -> x0, waiting for transfers between devices: 3.35 us -> none  [the longest x1 1.79 us: local(): other = lax.ppermute(shares[1:3], 'zh', crossed(1))]
  transfers between devices with their start and end apart: 13 -> 12, of which waited for: 6 -> 5; matrix products, arithmetic and copies ran while one was open for 2% -> 2% of each run, Pallas kernels for 20% -> 7%
where the time goes in v7:
time: 119 us; the launch traced here: 118 us
  starting transfers between devices  52.4 us (44%)
  waiting for transfers between devices  25.7 us (22%)
  Pallas kernels  21.6 us (18%)
  blocking collectives  10.5 us (9%)
  local copies, waits for them, and re-layouts  5.04 us (4%)
  between operations  2.42 us (2%)
    pallas_call x2, Pallas kernels, attend(): pl.pallas_call(functools.partial(attention_kernel, nq=nq, nk=nk, nx=len(e...  17.6 us
    ppermute x3, starting transfers between devices, local(): lax.ppermute(query[0], 'zl', crossed(m))  14.1 us
    all_to_all x1, waiting for transfers between devices, local(): shares = lax.all_to_all(shares, 'zh', 0, 0, tiled=True)  12.8 us
    all_to_all x1, starting transfers between devices, local(): shares = lax.all_to_all(shares, 'zh', 0, 0, tiled=True)  12.4 us
    all_to_all x1, blocking collectives, local(): shares = lax.all_to_all(shares, ('cfg', 'x'), 0, 0, tiled=True)  10.5 us
    ppermute x3, starting transfers between devices, local(): lax.ppermute(chunk, 'zl', crossed(m))  10.1 us
    ppermute x3, starting transfers between devices, local(): blocks = [own] + [lax.ppermute(own, 'y', ring(d)) for d in (1, 3, 2)]  8.98 us
    ppermute x3, waiting for transfers between devices, local(): lax.ppermute(query[0], 'zl', crossed(m))  6.77 us
  transfers between devices with their start and end apart: 12, of which 5 were waited for; matrix products, arithmetic and copies ran while one was open for 2% of the time, Pallas kernels for 7%

profile of v7, /device:TPU:24, one launch (start us, length us, event | category | flops | bytes accessed | tf_op | source)
XLA Modules:
  0.0 118.5 jit_solution(17480972258377050311)
XLA Ops:
  0.6 0.0 copy-start
  0.6 6.7 %collective-permute-start.3 = (bf16[512,256]{1,0:T(8,128)(2,1)}, bf16[512,256]{1,0:T(8,128)(2,1)S(1)}, u32[]{:S(2)}, u32[]{:S(2)}) collective-permute-start(bf16[512,256]{1,0:T(8,128)(2,1)} %bitcast.47), channel_id=1, source_target_pairs={{0,3},{1,2},{2,1},{3,0},{4,7},{5,6},{6,5},{7,4},{8,11},{9,10},{10,... | collective-permute-start | bytes 786440 | tf_op jit(solution)/shard_map/ppermute | solution.py:346
  7.3 0.0 copy-start.8
  7.3 2.0 %shard_map.113.refs_3_.refs_1_ = bf16[1024,256]{1,0:T(8,128)(2,1)} custom-call(bf16[512,256]{1,0:T(8,128)(2,1)} %bitcast.43, bf16[512,256]{1,0:T(8,128)(2,1)} %bitcast.44), custom_call_target="tpu_custom_call" | custom-call | tf_op jit(solution)/shard_map/pallas_call | solution.py:70
  9.4 2.9 %collective-permute-start = (bf16[1024,256]{1,0:T(8,128)(2,1)}, bf16[1024,256]{1,0:T(8,128)(2,1)S(1)}, u32[]{:S(2)}, u32[]{:S(2)}) collective-permute-start(bf16[1024,256]{1,0:T(8,128)(2,1)} %shard_map.113.refs_3_.refs_1_), channel_id=1, source_target_pairs={{0,4},{4,8},{8,12},{12,0},{1,5},{5,9},{9,13},{13,1},{2,6},{6,10},{... | collective-permute-start | bytes 1572872 | tf_op jit(solution)/shard_map/ppermute | solution.py:345
  12.3 3.0 %collective-permute-start.1 = (bf16[1024,256]{1,0:T(8,128)(2,1)}, bf16[1024,256]{1,0:T(8,128)(2,1)S(1)}, u32[]{:S(2)}, u32[]{:S(2)}) collective-permute-start(bf16[1024,256]{1,0:T(8,128)(2,1)} %shard_map.113.refs_3_.refs_1_), channel_id=1, source_target_pairs={{0,12},{4,0},{8,4},{12,8},{1,13},{5,1},{9,5},{13,9},{2,14},{6,2},{... | collective-permute-start | bytes 1572872 | tf_op jit(solution)/shard_map/ppermute | solution.py:345
  15.2 3.1 %collective-permute-start.2 = (bf16[1024,256]{1,0:T(8,128)(2,1)}, bf16[1024,256]{1,0:T(8,128)(2,1)S(1)}, u32[]{:S(2)}, u32[]{:S(2)}) collective-permute-start(bf16[1024,256]{1,0:T(8,128)(2,1)} %shard_map.113.refs_3_.refs_1_), channel_id=1, source_target_pairs={{0,8},{4,12},{8,0},{12,4},{1,9},{5,13},{9,1},{13,5},{2,10},{6,14},... | collective-permute-start | bytes 1572872 | tf_op jit(solution)/shard_map/ppermute | solution.py:345
  18.4 1.9 %collective-permute-start.4 = (bf16[512,256]{1,0:T(8,128)(2,1)S(1)}, bf16[512,256]{1,0:T(8,128)(2,1)S(1)}, u32[]{:S(2)}, u32[]{:S(2)}) collective-permute-start(bf16[512,256]{1,0:T(8,128)(2,1)S(1)} %bitcast.49), channel_id=1, source_target_pairs={{0,2},{1,3},{2,0},{3,1},{4,6},{5,7},{6,4},{7,5},{8,10},{9,11},{10,... | collective-permute-start | bytes 786440 | tf_op jit(solution)/shard_map/ppermute | solution.py:346
  20.3 0.0 copy-start.2
  21.0 0.0 copy-done.2
  21.1 5.5 %collective-permute-start.5 = (bf16[512,256]{1,0:T(8,128)(2,1)S(1)}, bf16[512,256]{1,0:T(8,128)(2,1)S(1)}, u32[]{:S(2)}, u32[]{:S(2)}) collective-permute-start(bf16[512,256]{1,0:T(8,128)(2,1)S(1)} %bitcast.50), channel_id=1, source_target_pairs={{0,1},{1,0},{2,3},{3,2},{4,5},{5,4},{6,7},{7,6},{8,9},{9,8},{10,11... | collective-permute-start | bytes 786440 | tf_op jit(solution)/shard_map/ppermute | solution.py:346
  26.5 0.1 fusion.1.count_ref
  27.3 0.1 copy.25
  27.4 0.1 squeeze.26
  27.5 0.1 copy.26
  27.5 0.1 squeeze.27
  27.7 0.1 pad_maximum_fusion.refs_4_
  27.8 0.6 bitcast_bitcast_fusion.refs_7_.refs_5_
  28.4 4.1 %collective-permute-done.4.refs_1_ = bf16[512,256]{1,0:T(8,128)(2,1)S(1)} collective-permute-done((bf16[512,256]{1,0:T(8,128)(2,1)S(1)}, bf16[512,256]{1,0:T(8,128)(2,1)S(1)}, u32[]{:S(2)}, u32[]{:S(2)}) %collective-permute-start.4) | collective-permute-done | bytes 262176 | tf_op jit(solution)/shard_map/ppermute | solution.py:346
  32.5 2.7 %collective-permute-done.5.refs_2_ = bf16[512,256]{1,0:T(8,128)(2,1)S(1)} collective-permute-done((bf16[512,256]{1,0:T(8,128)(2,1)S(1)}, bf16[512,256]{1,0:T(8,128)(2,1)S(1)}, u32[]{:S(2)}, u32[]{:S(2)}) %collective-permute-start.5) | collective-permute-done | bytes 262176 | tf_op jit(solution)/shard_map/ppermute | solution.py:346
  35.2 4.0 %collective-permute-done.1.refs_5_.refs_3_ = bf16[1024,256]{1,0:T(8,128)(2,1)S(1)} collective-permute-done((bf16[1024,256]{1,0:T(8,128)(2,1)}, bf16[1024,256]{1,0:T(8,128)(2,1)S(1)}, u32[]{:S(2)}, u32[]{:S(2)}) %collective-permute-start.1) | collective-permute-done | bytes 524320 | tf_op jit(solution)/shard_map/ppermute | solution.py:345
  39.3 0.8 copy-done.6
  40.0 0.8 copy-done.7
  40.8 11.9 %shard_map.114 = (bf16[144,512]{1,0:T(8,128)(2,1)S(1)}, bf16[144,512]{1,0:T(8,128)(2,1)S(1)}, bf16[144,512]{1,0:T(8,128)(2,1)S(1)}) custom-call(s32[4]{0:T(128)S(1)} %fusion.1.count_ref, bf16[512,256]{1,0:T(8,128)(2,1)} %copy-done.9, bf16[512,256]{1,0:T(8,128)(2,1)} %copy-done.10, bf16[512,256]{1,0:T(8,128)(2,1)} %copy-done.11, ...), custom_call_target="tpu_custom_call" | custom-call | flops 3221225472 | bytes 2883584 | tf_op jit(solution)/shard_map/pallas_call | solution.py:205
  52.7 2.9 %collective-permute-start.6 = (bf16[144,512]{1,0:T(8,128)(2,1)S(1)}, bf16[144,512]{1,0:T(8,128)(2,1)S(1)}, u32[]{:S(2)}, u32[]{:S(2)}) collective-permute-start(bf16[144,512]{1,0:T(8,128)(2,1)S(1)} %get-tuple-element.5.refs_6_), channel_id=1, source_target_pairs={{0,3},{1,2},{2,1},{3,0},{4,7},{5,6},{6,5},{7,4},{8,11},{9,10},{10,... | collective-permute-start | bytes 442376 | tf_op jit(solution)/shard_map/ppermute | solution.py:370
  55.6 1.9 %collective-permute-start.7 = (bf16[144,512]{1,0:T(8,128)(2,1)S(1)}, bf16[144,512]{1,0:T(8,128)(2,1)S(1)}, u32[]{:S(2)}, u32[]{:S(2)}) collective-permute-start(bf16[144,512]{1,0:T(8,128)(2,1)S(1)} %get-tuple-element.6), channel_id=1, source_target_pairs={{0,2},{1,3},{2,0},{3,1},{4,6},{5,7},{6,4},{7,5},{8,10},{9,11},{10,... | collective-permute-start | bytes 442376 | tf_op jit(solution)/shard_map/ppermute | solution.py:370
  57.5 5.3 %collective-permute-start.8 = (bf16[144,512]{1,0:T(8,128)(2,1)S(1)}, bf16[144,512]{1,0:T(8,128)(2,1)S(1)}, u32[]{:S(2)}, u32[]{:S(2)}) collective-permute-start(bf16[144,512]{1,0:T(8,128)(2,1)S(1)} %get-tuple-element.7), channel_id=1, source_target_pairs={{0,1},{1,0},{2,3},{3,2},{4,5},{5,4},{6,7},{7,6},{8,9},{9,8},{10,11... | collective-permute-start | bytes 442376 | tf_op jit(solution)/shard_map/ppermute | solution.py:370
  62.8 0.1 pad_maximum_fusion.1.scale_ref
  62.9 5.7 %shard_map.115.refs_0_ = bf16[144,512]{1,0:T(8,128)(2,1)S(1)} custom-call(s32[4]{0:T(128)S(1)} %fusion.1.count_ref, bf16[512,256]{1,0:T(8,128)(2,1)} %bitcast.48, bf16[1024,256]{1,0:T(8,128)(2,1)} %shard_map.113.refs_3_.refs_1_, bf16[1024,256]{1,0:T(8,128)(2,1)} %copy-done.5, bf16[1024,256]{1,0:T(8,128)(2,1)} %copy-done.6, bf16[1024,256]{1,0:T(8,128)(2,1)} %copy-done.7, ...), custom_call_target="tpu_custom_call" | custom-call | flops 1073741824 | bytes 2359296 | tf_op jit(solution)/shard_map/pallas_call | solution.py:205
  68.6 0.8 shard_map.116
  69.4 0.0 copy-start.1
  69.5 10.5 %all_to_all.10 = bf16[8,4,24,128]{3,2,1,0:T(8,128)(2,1)S(1)} all-to-all(bf16[8,4,24,128]{3,2,1,0:T(8,128)(2,1)S(1)} %shard_map.116), channel_id=1, replica_groups=mesh['cfg'=2,'zh'=4,'x'=4,'y'=4,'zl'=4] {'cfg','x'}, dimensions={0} | all-to-all | bytes 393216 | tf_op jit(solution)/shard_map/all_to_all | solution.py:373
  80.0 0.6 convert_reduce_fusion
  80.6 12.4 %all-to-all-start.1 = ((f32[4,24,128]{2,1,0:T(8,128)}), f32[4,24,128]{2,1,0:T(8,128)S(1)}, u32[]{:S(2)}, u32[]{:S(2)}) async-start(f32[4,24,128]{2,1,0:T(8,128)} %convert_reduce_fusion), calls=%async_computation.1 | async-start | bytes 98304 | tf_op jit(solution)/shard_map/all_to_all | solution.py:375
  93.1 12.8 %all-to-all-done.1 = f32[4,24,128]{2,1,0:T(8,128)S(1)} async-done(((f32[4,24,128]{2,1,0:T(8,128)}), f32[4,24,128]{2,1,0:T(8,128)S(1)}, u32[]{:S(2)}, u32[]{:S(2)}) %all-to-all-start.1) | async-done | bytes 49184 | tf_op jit(solution)/shard_map/all_to_all | solution.py:375
  105.9 3.2 %collective-permute-start.10 = (bf16[24,128]{1,0:T(8,128)(2,1)S(1)}, bf16[24,128]{1,0:T(8,128)(2,1)S(1)}, u32[]{:S(2)}, u32[]{:S(2)}) collective-permute-start(bf16[24,128]{1,0:T(8,128)(2,1)S(1)} %subtract_convert_fusion.own_ref), channel_id=1, source_target_pairs={{0,2},{1,3},{2,4},{3,5},{4,6},{5,7},{6,8},{7,9},{8,10},{9,11},{10,... | collective-permute-start | bytes 18440 | tf_op jit(solution)/shard_map/ppermute | solution.py:380
  109.1 3.7 %collective-permute-start.9 = (bf16[24,128]{1,0:T(8,128)(2,1)S(1)}, bf16[24,128]{1,0:T(8,128)(2,1)S(1)}, u32[]{:S(2)}, u32[]{:S(2)}) collective-permute-start(bf16[24,128]{1,0:T(8,128)(2,1)S(1)} %subtract_convert_fusion.own_ref), channel_id=1, source_target_pairs={{0,1},{1,2},{2,3},{3,4},{4,5},{5,6},{6,7},{7,8},{8,9},{9,10},{10,1... | collective-permute-start | bytes 18440 | tf_op jit(solution)/shard_map/ppermute | solution.py:379
  112.8 0.1 fusion.2
  112.9 0.1 copy.28
  113.0 0.0 copy-start.3
  113.0 0.1 copy.29
  113.1 0.6 copy-done.3
  113.7 0.7 copy-done.4
  114.3 0.1 dynamic-slice
  114.4 0.1 reshape.52
  114.5 0.7 copy.30
  115.2 2.1 %collective-permute-done.9.last_ref = bf16[24,128]{1,0:T(8,128)(2,1)S(1)} collective-permute-done((bf16[24,128]{1,0:T(8,128)(2,1)S(1)}, bf16[24,128]{1,0:T(8,128)(2,1)S(1)}, u32[]{:S(2)}, u32[]{:S(2)}) %collective-permute-start.9) | collective-permute-done | bytes 6176 | tf_op jit(solution)/shard_map/ppermute | solution.py:379
  117.3 1.2 %shard_map.117 = bf16[2,32,384]{2,1,0:T(8,128)(2,1)} custom-call(s32[1]{0:T(128)} %bitcast.17.half_ref, bf16[24,128]{1,0:T(8,128)(2,1)S(1)} %subtract_convert_fusion.own_ref, bf16[24,128]{1,0:T(8,128)(2,1)S(1)} %collective-permute-done.9.last_ref, bf16[24,128]{1,0:T(8,128)(2,1)S(1)} %collective-permute-done.10.older_ref, bf16[768,384]{1,0:T(8,128)(2,1)S(1)} %bitcast.39, ...), custom_call_target="tpu_custom_call" | custom-call | tf_op jit(solution)/shard_map/pallas_call | solution.py:317
  (29 shorter events, 0.1 us)
Async XLA Ops:
  0.6 27.1 %copy-start = (bf16[4096,64]{0,1:T(8,128)(2,1)S(1)}, bf16[4096,64]{0,1:T(8,128)(2,1)}, u32[]{:S(2)}) copy-start(bf16[4096,64]{0,1:T(8,128)(2,1)} %param.16) | copy-start | bytes 1572868
  0.6 20.4 %collective-permute-start.3 = (bf16[512,256]{1,0:T(8,128)(2,1)}, bf16[512,256]{1,0:T(8,128)(2,1)S(1)}, u32[]{:S(2)}, u32[]{:S(2)}) collective-permute-start(bf16[512,256]{1,0:T(8,128)(2,1)} %bitcast.47), channel_id=1, source_target_pairs={{0,3},{1,2},{2,1},{3,0},{4,7},{5,6},{6,5},{7,4},{8,11},{9,10},{10,... | collective-permute-start | bytes 786440 | tf_op jit(solution)/shard_map/ppermute | solution.py:346
  7.3 11.0 %copy-start.8 = (bf16[1,512,256]{2,1,0:T(8,128)(2,1)S(1)}, bf16[1,512,256]{2,1,0:T(8,128)(2,1)}, u32[]{:S(2)}) copy-start(bf16[1,512,256]{2,1,0:T(8,128)(2,1)} %param.10) | copy-start | bytes 786436
  9.4 25.8 %collective-permute-start = (bf16[1024,256]{1,0:T(8,128)(2,1)}, bf16[1024,256]{1,0:T(8,128)(2,1)S(1)}, u32[]{:S(2)}, u32[]{:S(2)}) collective-permute-start(bf16[1024,256]{1,0:T(8,128)(2,1)} %shard_map.113.refs_3_.refs_1_), channel_id=1, source_target_pairs={{0,4},{4,8},{8,12},{12,0},{1,5},{5,9},{9,13},{13,1},{2,6},{6,10},{... | collective-permute-start | bytes 1572872 | tf_op jit(solution)/shard_map/ppermute | solution.py:345
  12.3 27.0 %collective-permute-start.1 = (bf16[1024,256]{1,0:T(8,128)(2,1)}, bf16[1024,256]{1,0:T(8,128)(2,1)S(1)}, u32[]{:S(2)}, u32[]{:S(2)}) collective-permute-start(bf16[1024,256]{1,0:T(8,128)(2,1)} %shard_map.113.refs_3_.refs_1_), channel_id=1, source_target_pairs={{0,12},{4,0},{8,4},{12,8},{1,13},{5,1},{9,5},{13,9},{2,14},{6,2},{... | collective-permute-start | bytes 1572872 | tf_op jit(solution)/shard_map/ppermute | solution.py:345
  15.2 24.0 %collective-permute-start.2 = (bf16[1024,256]{1,0:T(8,128)(2,1)}, bf16[1024,256]{1,0:T(8,128)(2,1)S(1)}, u32[]{:S(2)}, u32[]{:S(2)}) collective-permute-start(bf16[1024,256]{1,0:T(8,128)(2,1)} %shard_map.113.refs_3_.refs_1_), channel_id=1, source_target_pairs={{0,8},{4,12},{8,0},{12,4},{1,9},{5,13},{9,1},{13,5},{2,10},{6,14},... | collective-permute-start | bytes 1572872 | tf_op jit(solution)/shard_map/ppermute | solution.py:345
  18.4 14.1 %collective-permute-start.4 = (bf16[512,256]{1,0:T(8,128)(2,1)S(1)}, bf16[512,256]{1,0:T(8,128)(2,1)S(1)}, u32[]{:S(2)}, u32[]{:S(2)}) collective-permute-start(bf16[512,256]{1,0:T(8,128)(2,1)S(1)} %bitcast.49), channel_id=1, source_target_pairs={{0,2},{1,3},{2,0},{3,1},{4,6},{5,7},{6,4},{7,5},{8,10},{9,11},{10,... | collective-permute-start | bytes 786440 | tf_op jit(solution)/shard_map/ppermute | solution.py:346
  20.3 0.7 copy-start.2
  21.1 18.1 %copy-start.9 = (bf16[512,256]{1,0:T(8,128)(2,1)}, bf16[512,256]{1,0:T(8,128)(2,1)S(1)}, u32[]{:S(2)}) copy-start(bf16[512,256]{1,0:T(8,128)(2,1)S(1)} %collective-permute-done.3.refs_0_) | copy-start | bytes 786436
  21.1 14.1 %collective-permute-start.5 = (bf16[512,256]{1,0:T(8,128)(2,1)S(1)}, bf16[512,256]{1,0:T(8,128)(2,1)S(1)}, u32[]{:S(2)}, u32[]{:S(2)}) collective-permute-start(bf16[512,256]{1,0:T(8,128)(2,1)S(1)} %bitcast.50), channel_id=1, source_target_pairs={{0,1},{1,0},{2,3},{3,2},{4,5},{5,4},{6,7},{7,6},{8,9},{9,8},{10,11... | collective-permute-start | bytes 786440 | tf_op jit(solution)/shard_map/ppermute | solution.py:346
  32.5 6.8 %copy-start.10 = (bf16[512,256]{1,0:T(8,128)(2,1)}, bf16[512,256]{1,0:T(8,128)(2,1)S(1)}, u32[]{:S(2)}) copy-start(bf16[512,256]{1,0:T(8,128)(2,1)S(1)} %collective-permute-done.4.refs_1_) | copy-start | bytes 786436
  35.2 4.1 %copy-start.11 = (bf16[512,256]{1,0:T(8,128)(2,1)}, bf16[512,256]{1,0:T(8,128)(2,1)S(1)}, u32[]{:S(2)}) copy-start(bf16[512,256]{1,0:T(8,128)(2,1)S(1)} %collective-permute-done.5.refs_2_) | copy-start | bytes 786436
  35.2 4.1 %copy-start.5 = (bf16[1024,256]{1,0:T(8,128)(2,1)}, bf16[1024,256]{1,0:T(8,128)(2,1)S(1)}, u32[]{:S(2)}) copy-start(bf16[1024,256]{1,0:T(8,128)(2,1)S(1)} %collective-permute-done.refs_4_.refs_2_) | copy-start | bytes 1572868
  39.2 0.8 copy-start.6
  40.0 0.8 copy-start.7
  52.7 15.9 %collective-permute-start.6 = (bf16[144,512]{1,0:T(8,128)(2,1)S(1)}, bf16[144,512]{1,0:T(8,128)(2,1)S(1)}, u32[]{:S(2)}, u32[]{:S(2)}) collective-permute-start(bf16[144,512]{1,0:T(8,128)(2,1)S(1)} %get-tuple-element.5.refs_6_), channel_id=1, source_target_pairs={{0,3},{1,2},{2,1},{3,0},{4,7},{5,6},{6,5},{7,4},{8,11},{9,10},{10,... | collective-permute-start | bytes 442376 | tf_op jit(solution)/shard_map/ppermute | solution.py:370
  55.6 13.0 %collective-permute-start.7 = (bf16[144,512]{1,0:T(8,128)(2,1)S(1)}, bf16[144,512]{1,0:T(8,128)(2,1)S(1)}, u32[]{:S(2)}, u32[]{:S(2)}) collective-permute-start(bf16[144,512]{1,0:T(8,128)(2,1)S(1)} %get-tuple-element.6), channel_id=1, source_target_pairs={{0,2},{1,3},{2,0},{3,1},{4,6},{5,7},{6,4},{7,5},{8,10},{9,11},{10,... | collective-permute-start | bytes 442376 | tf_op jit(solution)/shard_map/ppermute | solution.py:370
  57.5 11.1 %collective-permute-start.8 = (bf16[144,512]{1,0:T(8,128)(2,1)S(1)}, bf16[144,512]{1,0:T(8,128)(2,1)S(1)}, u32[]{:S(2)}, u32[]{:S(2)}) collective-permute-start(bf16[144,512]{1,0:T(8,128)(2,1)S(1)} %get-tuple-element.7), channel_id=1, source_target_pairs={{0,1},{1,0},{2,3},{3,2},{4,5},{5,4},{6,7},{7,6},{8,9},{9,8},{10,11... | collective-permute-start | bytes 442376 | tf_op jit(solution)/shard_map/ppermute | solution.py:370
  69.4 23.6 %copy-start.1 = (bf16[3,3,3,16,384]{4,3,2,1,0:T(8,128)(2,1)S(1)}, bf16[3,3,3,16,384]{4,3,2,1,0:T(8,128)(2,1)}, u32[]{:S(2)}) copy-start(bf16[3,3,3,16,384]{4,3,2,1,0:T(8,128)(2,1)} %param.17) | copy-start | bytes 995332
  80.6 25.3 %all-to-all-start.1 = ((f32[4,24,128]{2,1,0:T(8,128)}), f32[4,24,128]{2,1,0:T(8,128)S(1)}, u32[]{:S(2)}, u32[]{:S(2)}) async-start(f32[4,24,128]{2,1,0:T(8,128)} %convert_reduce_fusion), calls=%async_computation.1 | async-start | bytes 98304 | tf_op jit(solution)/shard_map/all_to_all | solution.py:375
  105.9 9.3 %collective-permute-start.10 = (bf16[24,128]{1,0:T(8,128)(2,1)S(1)}, bf16[24,128]{1,0:T(8,128)(2,1)S(1)}, u32[]{:S(2)}, u32[]{:S(2)}) collective-permute-start(bf16[24,128]{1,0:T(8,128)(2,1)S(1)} %subtract_convert_fusion.own_ref), channel_id=1, source_target_pairs={{0,2},{1,3},{2,4},{3,5},{4,6},{5,7},{6,8},{7,9},{8,10},{9,11},{10,... | collective-permute-start | bytes 18440 | tf_op jit(solution)/shard_map/ppermute | solution.py:380
  109.1 8.2 %collective-permute-start.9 = (bf16[24,128]{1,0:T(8,128)(2,1)S(1)}, bf16[24,128]{1,0:T(8,128)(2,1)S(1)}, u32[]{:S(2)}, u32[]{:S(2)}) collective-permute-start(bf16[24,128]{1,0:T(8,128)(2,1)S(1)} %subtract_convert_fusion.own_ref), channel_id=1, source_target_pairs={{0,1},{1,2},{2,3},{3,4},{4,5},{5,6},{6,7},{7,8},{8,9},{9,10},{10,1... | collective-permute-start | bytes 18440 | tf_op jit(solution)/shard_map/ppermute | solution.py:379
  113.0 0.7 copy-start.3
  113.7 0.7 copy-start.4

commit v8 on v7

--- a/solution.py
+++ b/solution.py
@@ -20,7 +20,6 @@
 ROWS, TCOLS = 16, 32
 PATCH = 64
 CHUNK = 2 * PATCH + 16
-CUT = 24
 LOG2_SCALE = math.log2(math.e) / math.sqrt(DH)
 
 VMEM = pl.BlockSpec(memory_space=pltpu.VMEM)
@@ -249,10 +248,7 @@
     above = jnp.concatenate([blank, values[:-1]], 0)
     below = jnp.concatenate([values[1:], blank], 0)
     window = jnp.where(lane < 32, above, jnp.where(lane < 96, values, below))
-    for row in range(ROWS):
-        for half in range(2):
-            cut = window[row, half * 8 : half * 8 + CUT]
-            out_ref[half * SIDE + row % SIDE, row // SIDE] = cut.astype(jnp.bfloat16)
+    out_ref[...] = window.astype(jnp.bfloat16)
     band = place_ref[0]
     edge = pltpu.roll(latent_ref[...], 64, 1) * scale_ref[1]
     lane = lax.broadcasted_iota(jnp.int32, (TCOLS, 128), 1)
@@ -261,17 +257,13 @@
         @pl.when((target >= 0) & (target < ROWS))
         def _():
             sent = jnp.where(part, edge, 0.0)
-            for half in range(2):
-                at = (half * SIDE + (target & 3), target >> 2)
-                out_ref[at] = (
-                    out_ref[at].astype(jnp.float32) + sent[half * 8 : half * 8 + CUT]
-                ).astype(jnp.bfloat16)
+            out_ref[target] = (out_ref[target].astype(jnp.float32) + sent).astype(jnp.bfloat16)
 
 
 def combine(scale, place, chunks, latent):
     return pl.pallas_call(
         combine_kernel,
-        out_shape=jax.ShapeDtypeStruct((2 * SIDE, SIDE, CUT, 128), jnp.bfloat16),
+        out_shape=jax.ShapeDtypeStruct((ROWS, TCOLS, 128), jnp.bfloat16),
         in_specs=[SMEM, SMEM] + [VMEM] * 5,
         out_specs=VMEM,
         compiler_params=pltpu.CompilerParams(vmem_limit_bytes=16 * 2**20),
@@ -284,9 +276,9 @@
     even, odd = [], []
     for ref in (older_ref, last_ref, own_ref):
         block = ref[...].astype(jnp.float32)
-        here = jnp.where(left, block[0:16], block[8:24])
-        before = jnp.where(left, jnp.concatenate([blank, block[0:15]], 0), block[7:23])
-        after = jnp.where(left, block[1:17], jnp.concatenate([block[9:24], blank], 0))
+        here = jnp.where(left, block[0:16], block[16:32])
+        before = jnp.where(left, jnp.concatenate([blank, block[0:15]], 0), block[15:31])
+        after = jnp.where(left, block[1:17], jnp.concatenate([block[17:32], blank], 0))
         rows = [
             jnp.concatenate([x, pltpu.roll(x, 96, 1)], 0).astype(jnp.bfloat16)
             for x in (before, here, after)
@@ -350,7 +342,6 @@
     rows = latent[0].reshape(2, TCOLS, 32)
     blank = jnp.zeros((TCOLS, 32), jnp.float32)
     grid = jnp.concatenate([blank, rows[0], rows[1], blank], 1)
-    latent_window = lax.dynamic_slice_in_dim(grid, cfg * 8, CUT, 0)
     even, odd = conv_matrices(conv_weight)
     bias_row, gain_row = conv_bias.reshape(1, -1), gain.reshape(1, -1)
     part = lax.dynamic_slice_in_dim(head_weight, (zh * SIDE + x) * 2 * DH, 2 * DH, 0)
@@ -370,15 +361,13 @@
         lax.ppermute(chunk, "zl", crossed(m)) for m, chunk in ((3, third), (2, second), (1, first))
     ]
     shares = combine(scale, place, chunks, grid)
-    shares = lax.all_to_all(shares, ("cfg", "x"), 0, 0, tiled=True)
-    shares = jnp.sum(shares.astype(jnp.float32), 0)
-    shares = lax.all_to_all(shares, "zh", 0, 0, tiled=True)
-    window = jnp.sum(shares, 0)
-
-    current = (latent_window - sigma * window).astype(jnp.bfloat16)
+    shares = lax.all_to_all(shares, ("zh", "x"), 0, 0, tiled=True)
+    window = lax.psum(jnp.sum(shares.astype(jnp.float32), 0), "cfg")
+
+    current = (grid - sigma * window).astype(jnp.bfloat16)
     last = lax.ppermute(current, seq, moved(1))
     older = lax.ppermute(current, seq, moved(2))
-    cells = lax.dynamic_slice_in_dim(window, cfg * 8, TCOLS // 2, 0)[:, 32:96]
+    cells = lax.dynamic_slice_in_dim(window, cfg * (TCOLS // 2), TCOLS // 2, 0)[:, 32:96]
     velocity = cells.reshape(TCOLS // 2, 2, 2, -1).transpose(1, 0, 2, 3).reshape(1, 2, TCOLS, -1)
     decoded = decode(
         cfg.astype(jnp.int32).reshape(1),

time: 119 us -> 117 us (0.983)
  blocking collectives: 10.5 us -> 3.36 us
  waiting for transfers between devices: 25.7 us -> 28.4 us
    all_to_all x1 -> x0, blocking collectives: 10.5 us -> none  [local(): shares = lax.all_to_all(shares, ('cfg', 'x'), 0, 0, tiled=True)]
    psum x0 -> x1, blocking collectives: none -> 3.36 us  [local(): window = lax.psum(jnp.sum(shares.astype(jnp.float32), 0), 'cfg')]
    all_to_all x1, starting transfers between devices: 12.4 us -> 15 us  [local(): shares = lax.all_to_all(shares, ('zh', 'x'), 0, 0, tiled=True)]
    all_to_all x1, waiting for transfers between devices: 12.8 us -> 15.1 us  [local(): shares = lax.all_to_all(shares, ('zh', 'x'), 0, 0, tiled=True)]
    ppermute x1, starting transfers between devices: 3.17 us -> 1.92 us  [local(): older = lax.ppermute(current, seq, moved(2))]
where the time goes in v8:
time: 117 us; the launch traced here: 116 us
  starting transfers between devices  53.4 us (46%)
  waiting for transfers between devices  28.4 us (24%)
  Pallas kernels  22.7 us (19%)
  local copies, waits for them, and re-layouts  5.05 us (4%)
  blocking collectives  3.36 us (3%)
  between operations  2.41 us (2%)
    pallas_call x2, Pallas kernels, attend(): pl.pallas_call(functools.partial(attention_kernel, nq=nq, nk=nk, nx=len(e...  18.1 us
    all_to_all x1, waiting for transfers between devices, local(): shares = lax.all_to_all(shares, ('zh', 'x'), 0, 0, tiled=True)  15.1 us
    all_to_all x1, starting transfers between devices, local(): shares = lax.all_to_all(shares, ('zh', 'x'), 0, 0, tiled=True)  15 us
    ppermute x3, starting transfers between devices, local(): lax.ppermute(query[0], 'zl', crossed(m))  14.1 us
    ppermute x3, starting transfers between devices, local(): lax.ppermute(chunk, 'zl', crossed(m))  10.1 us
    ppermute x3, starting transfers between devices, local(): blocks = [own] + [lax.ppermute(own, 'y', ring(d)) for d in (1, 3, 2)]  8.98 us
    ppermute x3, waiting for transfers between devices, local(): lax.ppermute(query[0], 'zl', crossed(m))  6.77 us
    ppermute x3, waiting for transfers between devices, local(): blocks = [own] + [lax.ppermute(own, 'y', ring(d)) for d in (1, 3, 2)]  4.05 us
  transfers between devices with their start and end apart: 12, of which 5 were waited for; matrix products, arithmetic and copies ran while one was open for 2% of the time, Pallas kernels for 7%

profile of v8, /device:TPU:24, one launch (start us, length us, event | category | flops | bytes accessed | tf_op | source)
XLA Modules:
  0.0 115.6 jit_solution(14545734932341749283)
XLA Ops:
  0.6 0.0 copy-start
  0.6 6.7 %collective-permute-start.3 = (bf16[512,256]{1,0:T(8,128)(2,1)}, bf16[512,256]{1,0:T(8,128)(2,1)S(1)}, u32[]{:S(2)}, u32[]{:S(2)}) collective-permute-start(bf16[512,256]{1,0:T(8,128)(2,1)} %bitcast.47), channel_id=1, source_target_pairs={{0,3},{1,2},{2,1},{3,0},{4,7},{5,6},{6,5},{7,4},{8,11},{9,10},{10,... | collective-permute-start | bytes 786440 | tf_op jit(solution)/shard_map/ppermute | solution.py:338
  7.3 0.0 copy-start.8
  7.3 2.0 %shard_map.113.refs_3_.refs_1_ = bf16[1024,256]{1,0:T(8,128)(2,1)} custom-call(bf16[512,256]{1,0:T(8,128)(2,1)} %bitcast.43, bf16[512,256]{1,0:T(8,128)(2,1)} %bitcast.44), custom_call_target="tpu_custom_call" | custom-call | tf_op jit(solution)/shard_map/pallas_call | solution.py:69
  9.4 2.9 %collective-permute-start = (bf16[1024,256]{1,0:T(8,128)(2,1)}, bf16[1024,256]{1,0:T(8,128)(2,1)S(1)}, u32[]{:S(2)}, u32[]{:S(2)}) collective-permute-start(bf16[1024,256]{1,0:T(8,128)(2,1)} %shard_map.113.refs_3_.refs_1_), channel_id=1, source_target_pairs={{0,4},{4,8},{8,12},{12,0},{1,5},{5,9},{9,13},{13,1},{2,6},{6,10},{... | collective-permute-start | bytes 1572872 | tf_op jit(solution)/shard_map/ppermute | solution.py:337
  12.3 3.0 %collective-permute-start.1 = (bf16[1024,256]{1,0:T(8,128)(2,1)}, bf16[1024,256]{1,0:T(8,128)(2,1)S(1)}, u32[]{:S(2)}, u32[]{:S(2)}) collective-permute-start(bf16[1024,256]{1,0:T(8,128)(2,1)} %shard_map.113.refs_3_.refs_1_), channel_id=1, source_target_pairs={{0,12},{4,0},{8,4},{12,8},{1,13},{5,1},{9,5},{13,9},{2,14},{6,2},{... | collective-permute-start | bytes 1572872 | tf_op jit(solution)/shard_map/ppermute | solution.py:337
  15.2 3.1 %collective-permute-start.2 = (bf16[1024,256]{1,0:T(8,128)(2,1)}, bf16[1024,256]{1,0:T(8,128)(2,1)S(1)}, u32[]{:S(2)}, u32[]{:S(2)}) collective-permute-start(bf16[1024,256]{1,0:T(8,128)(2,1)} %shard_map.113.refs_3_.refs_1_), channel_id=1, source_target_pairs={{0,8},{4,12},{8,0},{12,4},{1,9},{5,13},{9,1},{13,5},{2,10},{6,14},... | collective-permute-start | bytes 1572872 | tf_op jit(solution)/shard_map/ppermute | solution.py:337
  18.4 1.9 %collective-permute-start.4 = (bf16[512,256]{1,0:T(8,128)(2,1)S(1)}, bf16[512,256]{1,0:T(8,128)(2,1)S(1)}, u32[]{:S(2)}, u32[]{:S(2)}) collective-permute-start(bf16[512,256]{1,0:T(8,128)(2,1)S(1)} %bitcast.49), channel_id=1, source_target_pairs={{0,2},{1,3},{2,0},{3,1},{4,6},{5,7},{6,4},{7,5},{8,10},{9,11},{10,... | collective-permute-start | bytes 786440 | tf_op jit(solution)/shard_map/ppermute | solution.py:338
  20.3 0.0 copy-start.2
  21.0 0.0 copy-done.2
  21.1 5.5 %collective-permute-start.5 = (bf16[512,256]{1,0:T(8,128)(2,1)S(1)}, bf16[512,256]{1,0:T(8,128)(2,1)S(1)}, u32[]{:S(2)}, u32[]{:S(2)}) collective-permute-start(bf16[512,256]{1,0:T(8,128)(2,1)S(1)} %bitcast.50), channel_id=1, source_target_pairs={{0,1},{1,0},{2,3},{3,2},{4,5},{5,4},{6,7},{7,6},{8,9},{9,8},{10,11... | collective-permute-start | bytes 786440 | tf_op jit(solution)/shard_map/ppermute | solution.py:338
  26.5 0.1 fusion.1.count_ref
  27.3 0.1 copy.18
  27.4 0.1 squeeze.26
  27.5 0.1 copy.19
  27.5 0.1 squeeze.27
  27.7 0.1 pad_maximum_fusion.refs_4_
  27.8 0.6 bitcast_bitcast_fusion.refs_7_.refs_5_
  28.4 4.1 %collective-permute-done.4.refs_1_ = bf16[512,256]{1,0:T(8,128)(2,1)S(1)} collective-permute-done((bf16[512,256]{1,0:T(8,128)(2,1)S(1)}, bf16[512,256]{1,0:T(8,128)(2,1)S(1)}, u32[]{:S(2)}, u32[]{:S(2)}) %collective-permute-start.4) | collective-permute-done | bytes 262176 | tf_op jit(solution)/shard_map/ppermute | solution.py:338
  32.5 2.7 %collective-permute-done.5.refs_2_ = bf16[512,256]{1,0:T(8,128)(2,1)S(1)} collective-permute-done((bf16[512,256]{1,0:T(8,128)(2,1)S(1)}, bf16[512,256]{1,0:T(8,128)(2,1)S(1)}, u32[]{:S(2)}, u32[]{:S(2)}) %collective-permute-start.5) | collective-permute-done | bytes 262176 | tf_op jit(solution)/shard_map/ppermute | solution.py:338
  35.2 4.0 %collective-permute-done.1.refs_5_.refs_3_ = bf16[1024,256]{1,0:T(8,128)(2,1)S(1)} collective-permute-done((bf16[1024,256]{1,0:T(8,128)(2,1)}, bf16[1024,256]{1,0:T(8,128)(2,1)S(1)}, u32[]{:S(2)}, u32[]{:S(2)}) %collective-permute-start.1) | collective-permute-done | bytes 524320 | tf_op jit(solution)/shard_map/ppermute | solution.py:337
  39.3 0.8 copy-done.6
  40.0 0.8 copy-done.7
  40.8 12.3 %shard_map.114 = (bf16[144,512]{1,0:T(8,128)(2,1)S(1)}, bf16[144,512]{1,0:T(8,128)(2,1)S(1)}, bf16[144,512]{1,0:T(8,128)(2,1)S(1)}) custom-call(s32[4]{0:T(128)S(1)} %fusion.1.count_ref, bf16[512,256]{1,0:T(8,128)(2,1)} %copy-done.9, bf16[512,256]{1,0:T(8,128)(2,1)} %copy-done.10, bf16[512,256]{1,0:T(8,128)(2,1)} %copy-done.11, ...), custom_call_target="tpu_custom_call" | custom-call | flops 3221225472 | bytes 2883584 | tf_op jit(solution)/shard_map/pallas_call | solution.py:204
  53.1 1.9 %collective-permute-start.6 = (bf16[144,512]{1,0:T(8,128)(2,1)S(1)}, bf16[144,512]{1,0:T(8,128)(2,1)S(1)}, u32[]{:S(2)}, u32[]{:S(2)}) collective-permute-start(bf16[144,512]{1,0:T(8,128)(2,1)S(1)} %get-tuple-element.5.refs_6_), channel_id=1, source_target_pairs={{0,3},{1,2},{2,1},{3,0},{4,7},{5,6},{6,5},{7,4},{8,11},{9,10},{10,... | collective-permute-start | bytes 442376 | tf_op jit(solution)/shard_map/ppermute | solution.py:361
  55.0 1.9 %collective-permute-start.7 = (bf16[144,512]{1,0:T(8,128)(2,1)S(1)}, bf16[144,512]{1,0:T(8,128)(2,1)S(1)}, u32[]{:S(2)}, u32[]{:S(2)}) collective-permute-start(bf16[144,512]{1,0:T(8,128)(2,1)S(1)} %get-tuple-element.6), channel_id=1, source_target_pairs={{0,2},{1,3},{2,0},{3,1},{4,6},{5,7},{6,4},{7,5},{8,10},{9,11},{10,... | collective-permute-start | bytes 442376 | tf_op jit(solution)/shard_map/ppermute | solution.py:361
  57.0 6.3 %collective-permute-start.8 = (bf16[144,512]{1,0:T(8,128)(2,1)S(1)}, bf16[144,512]{1,0:T(8,128)(2,1)S(1)}, u32[]{:S(2)}, u32[]{:S(2)}) collective-permute-start(bf16[144,512]{1,0:T(8,128)(2,1)S(1)} %get-tuple-element.7), channel_id=1, source_target_pairs={{0,1},{1,0},{2,3},{3,2},{4,5},{5,4},{6,7},{7,6},{8,9},{9,8},{10,11... | collective-permute-start | bytes 442376 | tf_op jit(solution)/shard_map/ppermute | solution.py:361
  63.2 0.1 pad_maximum_fusion.1.scale_ref
  63.3 5.8 %shard_map.115.refs_0_ = bf16[144,512]{1,0:T(8,128)(2,1)S(1)} custom-call(s32[4]{0:T(128)S(1)} %fusion.1.count_ref, bf16[512,256]{1,0:T(8,128)(2,1)} %bitcast.48, bf16[1024,256]{1,0:T(8,128)(2,1)} %shard_map.113.refs_3_.refs_1_, bf16[1024,256]{1,0:T(8,128)(2,1)} %copy-done.5, bf16[1024,256]{1,0:T(8,128)(2,1)} %copy-done.6, bf16[1024,256]{1,0:T(8,128)(2,1)} %copy-done.7, ...), custom_call_target="tpu_custom_call" | custom-call | flops 1073741824 | bytes 2359296 | tf_op jit(solution)/shard_map/pallas_call | solution.py:204
  69.2 0.0 copy-start.1
  69.2 1.4 %shard_map.116 = bf16[16,32,128]{2,1,0:T(8,128)(2,1)} custom-call(f32[2]{0:T(128)S(1)} %pad_maximum_fusion.1.scale_ref, s32[1]{0:T(128)} %bitcast.4.place_ref, bf16[144,512]{1,0:T(8,128)(2,1)S(1)} %shard_map.115.refs_0_, bf16[144,512]{1,0:T(8,128)(2,1)S(1)} %collective-permute-done.6.refs_1_, bf16[144,512]{1,0:T(8,128)(2,1)S(1)} %collective-permute-done.7.refs_2_, ...), custom_call_target="tpu_custom_call" | custom-call | tf_op jit(solution)/shard_map/pallas_call | solution.py:264
  70.6 15.0 %all-to-all-start = ((bf16[16,32,128]{2,1,0:T(8,128)(2,1)}), bf16[16,32,128]{2,1,0:T(8,128)(2,1)S(1)}, u32[]{:S(2)}, u32[]{:S(2)}) async-start(bf16[16,32,128]{2,1,0:T(8,128)(2,1)} %shard_map.116), calls=%async_computation | async-start | bytes 262144 | tf_op jit(solution)/shard_map/all_to_all | solution.py:364
  85.7 15.1 %all-to-all-done = bf16[16,32,128]{2,1,0:T(8,128)(2,1)S(1)} async-done(((bf16[16,32,128]{2,1,0:T(8,128)(2,1)}), bf16[16,32,128]{2,1,0:T(8,128)(2,1)S(1)}, u32[]{:S(2)}, u32[]{:S(2)}) %all-to-all-start) | async-done | bytes 131104 | tf_op jit(solution)/shard_map/all_to_all | solution.py:364
  100.8 3.4 %psum.7 = f32[32,128]{1,0:T(8,128)S(1)} all-reduce(f32[32,128]{1,0:T(8,128)S(1)} %convert_reduce_fusion), channel_id=1, replica_groups=mesh['cfg'=2,'zh'=4,'x'=4,'y'=4,'zl'=4] {'cfg'}, use_global_device_ids=true, to_apply=%region_1.2 | all-reduce | flops 4096 | bytes 32768 | tf_op jit(solution)/shard_map/psum | solution.py:365
  104.2 0.1 subtract_convert_fusion.own_ref
  104.3 1.9 %collective-permute-start.10 = (bf16[32,128]{1,0:T(8,128)(2,1)S(1)}, bf16[32,128]{1,0:T(8,128)(2,1)S(1)}, u32[]{:S(2)}, u32[]{:S(2)}) collective-permute-start(bf16[32,128]{1,0:T(8,128)(2,1)S(1)} %subtract_convert_fusion.own_ref), channel_id=1, source_target_pairs={{0,2},{1,3},{2,4},{3,5},{4,6},{5,7},{6,8},{7,9},{8,10},{9,11},{10,... | collective-permute-start | bytes 24584 | tf_op jit(solution)/shard_map/ppermute | solution.py:369
  106.2 3.3 %collective-permute-start.9 = (bf16[32,128]{1,0:T(8,128)(2,1)S(1)}, bf16[32,128]{1,0:T(8,128)(2,1)S(1)}, u32[]{:S(2)}, u32[]{:S(2)}) collective-permute-start(bf16[32,128]{1,0:T(8,128)(2,1)S(1)} %subtract_convert_fusion.own_ref), channel_id=1, source_target_pairs={{0,1},{1,2},{2,3},{3,4},{4,5},{5,6},{6,7},{7,8},{8,9},{9,10},{10,1... | collective-permute-start | bytes 24584 | tf_op jit(solution)/shard_map/ppermute | solution.py:368
  109.6 0.1 fusion.2
  109.7 0.1 copy.21
  109.8 0.0 copy-start.3
  109.8 0.1 copy.22
  109.9 0.6 copy-done.3
  110.5 0.7 copy-done.4
  111.1 0.1 dynamic-slice
  111.2 0.1 reshape.52
  111.3 0.7 copy.23
  112.0 2.4 %collective-permute-done.9.last_ref = bf16[32,128]{1,0:T(8,128)(2,1)S(1)} collective-permute-done((bf16[32,128]{1,0:T(8,128)(2,1)S(1)}, bf16[32,128]{1,0:T(8,128)(2,1)S(1)}, u32[]{:S(2)}, u32[]{:S(2)}) %collective-permute-start.9) | collective-permute-done | bytes 8224 | tf_op jit(solution)/shard_map/ppermute | solution.py:368
  114.4 1.2 %shard_map.117 = bf16[2,32,384]{2,1,0:T(8,128)(2,1)} custom-call(s32[1]{0:T(128)} %bitcast.17.half_ref, bf16[32,128]{1,0:T(8,128)(2,1)S(1)} %subtract_convert_fusion.own_ref, bf16[32,128]{1,0:T(8,128)(2,1)S(1)} %collective-permute-done.9.last_ref, bf16[32,128]{1,0:T(8,128)(2,1)S(1)} %collective-permute-done.10.older_ref, bf16[768,384]{1,0:T(8,128)(2,1)S(1)} %bitcast.39, ...), custom_call_target="tpu_custom_call" | custom-call | tf_op jit(solution)/shard_map/pallas_call | solution.py:309
  (28 shorter events, 0.1 us)
Async XLA Ops:
  0.6 27.1 %copy-start = (bf16[4096,64]{0,1:T(8,128)(2,1)S(1)}, bf16[4096,64]{0,1:T(8,128)(2,1)}, u32[]{:S(2)}) copy-start(bf16[4096,64]{0,1:T(8,128)(2,1)} %param.16) | copy-start | bytes 1572868
  0.6 20.4 %collective-permute-start.3 = (bf16[512,256]{1,0:T(8,128)(2,1)}, bf16[512,256]{1,0:T(8,128)(2,1)S(1)}, u32[]{:S(2)}, u32[]{:S(2)}) collective-permute-start(bf16[512,256]{1,0:T(8,128)(2,1)} %bitcast.47), channel_id=1, source_target_pairs={{0,3},{1,2},{2,1},{3,0},{4,7},{5,6},{6,5},{7,4},{8,11},{9,10},{10,... | collective-permute-start | bytes 786440 | tf_op jit(solution)/shard_map/ppermute | solution.py:338
  7.3 11.0 %copy-start.8 = (bf16[1,512,256]{2,1,0:T(8,128)(2,1)S(1)}, bf16[1,512,256]{2,1,0:T(8,128)(2,1)}, u32[]{:S(2)}) copy-start(bf16[1,512,256]{2,1,0:T(8,128)(2,1)} %param.10) | copy-start | bytes 786436
  9.4 25.8 %collective-permute-start = (bf16[1024,256]{1,0:T(8,128)(2,1)}, bf16[1024,256]{1,0:T(8,128)(2,1)S(1)}, u32[]{:S(2)}, u32[]{:S(2)}) collective-permute-start(bf16[1024,256]{1,0:T(8,128)(2,1)} %shard_map.113.refs_3_.refs_1_), channel_id=1, source_target_pairs={{0,4},{4,8},{8,12},{12,0},{1,5},{5,9},{9,13},{13,1},{2,6},{6,10},{... | collective-permute-start | bytes 1572872 | tf_op jit(solution)/shard_map/ppermute | solution.py:337
  12.3 27.0 %collective-permute-start.1 = (bf16[1024,256]{1,0:T(8,128)(2,1)}, bf16[1024,256]{1,0:T(8,128)(2,1)S(1)}, u32[]{:S(2)}, u32[]{:S(2)}) collective-permute-start(bf16[1024,256]{1,0:T(8,128)(2,1)} %shard_map.113.refs_3_.refs_1_), channel_id=1, source_target_pairs={{0,12},{4,0},{8,4},{12,8},{1,13},{5,1},{9,5},{13,9},{2,14},{6,2},{... | collective-permute-start | bytes 1572872 | tf_op jit(solution)/shard_map/ppermute | solution.py:337
  15.2 24.0 %collective-permute-start.2 = (bf16[1024,256]{1,0:T(8,128)(2,1)}, bf16[1024,256]{1,0:T(8,128)(2,1)S(1)}, u32[]{:S(2)}, u32[]{:S(2)}) collective-permute-start(bf16[1024,256]{1,0:T(8,128)(2,1)} %shard_map.113.refs_3_.refs_1_), channel_id=1, source_target_pairs={{0,8},{4,12},{8,0},{12,4},{1,9},{5,13},{9,1},{13,5},{2,10},{6,14},... | collective-permute-start | bytes 1572872 | tf_op jit(solution)/shard_map/ppermute | solution.py:337
  18.4 14.1 %collective-permute-start.4 = (bf16[512,256]{1,0:T(8,128)(2,1)S(1)}, bf16[512,256]{1,0:T(8,128)(2,1)S(1)}, u32[]{:S(2)}, u32[]{:S(2)}) collective-permute-start(bf16[512,256]{1,0:T(8,128)(2,1)S(1)} %bitcast.49), channel_id=1, source_target_pairs={{0,2},{1,3},{2,0},{3,1},{4,6},{5,7},{6,4},{7,5},{8,10},{9,11},{10,... | collective-permute-start | bytes 786440 | tf_op jit(solution)/shard_map/ppermute | solution.py:338
  20.3 0.7 copy-start.2
  21.1 18.1 %copy-start.9 = (bf16[512,256]{1,0:T(8,128)(2,1)}, bf16[512,256]{1,0:T(8,128)(2,1)S(1)}, u32[]{:S(2)}) copy-start(bf16[512,256]{1,0:T(8,128)(2,1)S(1)} %collective-permute-done.3.refs_0_) | copy-start | bytes 786436
  21.1 14.1 %collective-permute-start.5 = (bf16[512,256]{1,0:T(8,128)(2,1)S(1)}, bf16[512,256]{1,0:T(8,128)(2,1)S(1)}, u32[]{:S(2)}, u32[]{:S(2)}) collective-permute-start(bf16[512,256]{1,0:T(8,128)(2,1)S(1)} %bitcast.50), channel_id=1, source_target_pairs={{0,1},{1,0},{2,3},{3,2},{4,5},{5,4},{6,7},{7,6},{8,9},{9,8},{10,11... | collective-permute-start | bytes 786440 | tf_op jit(solution)/shard_map/ppermute | solution.py:338
  32.5 6.8 %copy-start.10 = (bf16[512,256]{1,0:T(8,128)(2,1)}, bf16[512,256]{1,0:T(8,128)(2,1)S(1)}, u32[]{:S(2)}) copy-start(bf16[512,256]{1,0:T(8,128)(2,1)S(1)} %collective-permute-done.4.refs_1_) | copy-start | bytes 786436
  35.2 4.1 %copy-start.11 = (bf16[512,256]{1,0:T(8,128)(2,1)}, bf16[512,256]{1,0:T(8,128)(2,1)S(1)}, u32[]{:S(2)}) copy-start(bf16[512,256]{1,0:T(8,128)(2,1)S(1)} %collective-permute-done.5.refs_2_) | copy-start | bytes 786436
  35.2 4.1 %copy-start.5 = (bf16[1024,256]{1,0:T(8,128)(2,1)}, bf16[1024,256]{1,0:T(8,128)(2,1)S(1)}, u32[]{:S(2)}) copy-start(bf16[1024,256]{1,0:T(8,128)(2,1)S(1)} %collective-permute-done.refs_4_.refs_2_) | copy-start | bytes 1572868
  39.2 0.8 copy-start.6
  40.0 0.8 copy-start.7
  53.1 16.1 %collective-permute-start.6 = (bf16[144,512]{1,0:T(8,128)(2,1)S(1)}, bf16[144,512]{1,0:T(8,128)(2,1)S(1)}, u32[]{:S(2)}, u32[]{:S(2)}) collective-permute-start(bf16[144,512]{1,0:T(8,128)(2,1)S(1)} %get-tuple-element.5.refs_6_), channel_id=1, source_target_pairs={{0,3},{1,2},{2,1},{3,0},{4,7},{5,6},{6,5},{7,4},{8,11},{9,10},{10,... | collective-permute-start | bytes 442376 | tf_op jit(solution)/shard_map/ppermute | solution.py:361
  55.0 14.1 %collective-permute-start.7 = (bf16[144,512]{1,0:T(8,128)(2,1)S(1)}, bf16[144,512]{1,0:T(8,128)(2,1)S(1)}, u32[]{:S(2)}, u32[]{:S(2)}) collective-permute-start(bf16[144,512]{1,0:T(8,128)(2,1)S(1)} %get-tuple-element.6), channel_id=1, source_target_pairs={{0,2},{1,3},{2,0},{3,1},{4,6},{5,7},{6,4},{7,5},{8,10},{9,11},{10,... | collective-permute-start | bytes 442376 | tf_op jit(solution)/shard_map/ppermute | solution.py:361
  57.0 12.2 %collective-permute-start.8 = (bf16[144,512]{1,0:T(8,128)(2,1)S(1)}, bf16[144,512]{1,0:T(8,128)(2,1)S(1)}, u32[]{:S(2)}, u32[]{:S(2)}) collective-permute-start(bf16[144,512]{1,0:T(8,128)(2,1)S(1)} %get-tuple-element.7), channel_id=1, source_target_pairs={{0,1},{1,0},{2,3},{3,2},{4,5},{5,4},{6,7},{7,6},{8,9},{9,8},{10,11... | collective-permute-start | bytes 442376 | tf_op jit(solution)/shard_map/ppermute | solution.py:361
  69.2 16.5 %copy-start.1 = (bf16[3,3,3,16,384]{4,3,2,1,0:T(8,128)(2,1)S(1)}, bf16[3,3,3,16,384]{4,3,2,1,0:T(8,128)(2,1)}, u32[]{:S(2)}) copy-start(bf16[3,3,3,16,384]{4,3,2,1,0:T(8,128)(2,1)} %param.17) | copy-start | bytes 995332
  70.6 30.2 %all-to-all-start = ((bf16[16,32,128]{2,1,0:T(8,128)(2,1)}), bf16[16,32,128]{2,1,0:T(8,128)(2,1)S(1)}, u32[]{:S(2)}, u32[]{:S(2)}) async-start(bf16[16,32,128]{2,1,0:T(8,128)(2,1)} %shard_map.116), calls=%async_computation | async-start | bytes 262144 | tf_op jit(solution)/shard_map/all_to_all | solution.py:364
  104.3 7.7 %collective-permute-start.10 = (bf16[32,128]{1,0:T(8,128)(2,1)S(1)}, bf16[32,128]{1,0:T(8,128)(2,1)S(1)}, u32[]{:S(2)}, u32[]{:S(2)}) collective-permute-start(bf16[32,128]{1,0:T(8,128)(2,1)S(1)} %subtract_convert_fusion.own_ref), channel_id=1, source_target_pairs={{0,2},{1,3},{2,4},{3,5},{4,6},{5,7},{6,8},{7,9},{8,10},{9,11},{10,... | collective-permute-start | bytes 24584 | tf_op jit(solution)/shard_map/ppermute | solution.py:369
  106.2 8.2 %collective-permute-start.9 = (bf16[32,128]{1,0:T(8,128)(2,1)S(1)}, bf16[32,128]{1,0:T(8,128)(2,1)S(1)}, u32[]{:S(2)}, u32[]{:S(2)}) collective-permute-start(bf16[32,128]{1,0:T(8,128)(2,1)S(1)} %subtract_convert_fusion.own_ref), channel_id=1, source_target_pairs={{0,1},{1,2},{2,3},{3,4},{4,5},{5,6},{6,7},{7,8},{8,9},{9,10},{10,1... | collective-permute-start | bytes 24584 | tf_op jit(solution)/shard_map/ppermute | solution.py:368
  109.8 0.7 copy-start.3
  110.5 0.7 copy-start.4

commit v9 on v8

--- a/solution.py
+++ b/solution.py
@@ -204,7 +204,7 @@
     return pl.pallas_call(
         functools.partial(attention_kernel, nq=nq, nk=nk, nx=len(extras)),
         out_shape=(jax.ShapeDtypeStruct((CHUNK, TOK), bf16),) * nq,
-        in_specs=[SMEM] + [HBM] * (nq + nk + 1) + [ANY] * len(extras),
+        in_specs=[SMEM] + [ANY] * (nq + nk + 1 + len(extras)),
         out_specs=(VMEM,) * nq,
         scratch_shapes=[
             pltpu.VMEM((nq, TOK, 2 * DH), bf16),
@@ -221,7 +221,7 @@
         cost_estimate=pl.CostEstimate(
             flops=work * DH * 4, transcendentals=work, bytes_accessed=(nq + 2 * nk) * TOK * 4 * DH
         ),
-    )(counts, *(in_hbm(x) for x in (*queries, *blocks, weight)), *extras)
+    )(counts, *queries, *blocks, weight, *extras)
 
 
 def combine_kernel(scale_ref, place_ref, *refs):
@@ -248,7 +248,8 @@
     above = jnp.concatenate([blank, values[:-1]], 0)
     below = jnp.concatenate([values[1:], blank], 0)
     window = jnp.where(lane < 32, above, jnp.where(lane < 96, values, below))
-    out_ref[...] = window.astype(jnp.bfloat16)
+    for row in range(ROWS):
+        out_ref[row] = window[row].astype(jnp.bfloat16)
     band = place_ref[0]
     edge = pltpu.roll(latent_ref[...], 64, 1) * scale_ref[1]
     lane = lax.broadcasted_iota(jnp.int32, (TCOLS, 128), 1)
@@ -270,7 +271,30 @@
     )(scale, place, *chunks, latent)
 
 
-def decode_kernel(half_ref, own_ref, last_ref, older_ref, even_ref, odd_ref, bias_ref, gain_ref, out_ref):
+def decode_kernel(
+    half_ref,
+    own_ref,
+    last_ref,
+    older_ref,
+    even_hbm,
+    odd_hbm,
+    bias_hbm,
+    gain_hbm,
+    out_ref,
+    even_ref,
+    odd_ref,
+    bias_ref,
+    gain_ref,
+    sems,
+):
+    copies = [
+        pltpu.make_async_copy(even_hbm, even_ref, sems.at[0]),
+        pltpu.make_async_copy(odd_hbm, odd_ref, sems.at[1]),
+        pltpu.make_async_copy(bias_hbm, bias_ref.at[0], sems.at[2]),
+        pltpu.make_async_copy(gain_hbm, gain_ref.at[0], sems.at[3]),
+    ]
+    for copy in copies:
+        copy.start()
     left = half_ref[0] == 0
     blank = jnp.zeros((1, 128), jnp.float32)
     even, odd = [], []
@@ -285,6 +309,8 @@
         ]
         even += rows[0:2]
         odd += rows[1:3]
+    for copy in copies:
+        copy.wait()
     finished = []
     for parts, weight_ref in ((even, even_ref), (odd, odd_ref)):
         features = (
@@ -305,12 +331,19 @@
 
 
 def decode(half, own, last, older, even, odd, bias, gain):
-    chans = bias.shape[1]
+    chans = bias.shape[0]
     return pl.pallas_call(
         decode_kernel,
         out_shape=jax.ShapeDtypeStruct((2, 32, chans), jnp.bfloat16),
-        in_specs=[SMEM] + [VMEM] * 7,
+        in_specs=[SMEM] + [VMEM] * 3 + [ANY] * 4,
         out_specs=VMEM,
+        scratch_shapes=[
+            pltpu.VMEM(even.shape, even.dtype),
+            pltpu.VMEM(odd.shape, odd.dtype),
+            pltpu.VMEM((1, chans), jnp.float32),
+            pltpu.VMEM((1, chans), jnp.float32),
+            pltpu.SemaphoreType.DMA((4,)),
+        ],
         compiler_params=pltpu.CompilerParams(vmem_limit_bytes=32 * 2**20),
     )(half, own, last, older, even, odd, bias, gain)
 
@@ -343,7 +376,6 @@
     blank = jnp.zeros((TCOLS, 32), jnp.float32)
     grid = jnp.concatenate([blank, rows[0], rows[1], blank], 1)
     even, odd = conv_matrices(conv_weight)
-    bias_row, gain_row = conv_bias.reshape(1, -1), gain.reshape(1, -1)
     part = lax.dynamic_slice_in_dim(head_weight, (zh * SIDE + x) * 2 * DH, 2 * DH, 0)
     weight = part.T.reshape(PATCH, 2, DH).transpose(1, 0, 2)
     sigma = noise_level(timestep[0], STEPS)
@@ -356,7 +388,7 @@
     place = (zh * SIDE + x).astype(jnp.int32).reshape(1)
 
     third, second, first = attend(counts, queries[3:0:-1], blocks, weight)
-    (mine,) = attend(counts, queries[:1], blocks, weight, extras=(third,))
+    (mine,) = attend(counts, queries[:1], blocks, weight, extras=(third, even, odd))
     chunks = [mine] + [
         lax.ppermute(chunk, "zl", crossed(m)) for m, chunk in ((3, third), (2, second), (1, first))
     ]
@@ -376,8 +408,8 @@
         older,
         even,
         odd,
-        bias_row,
-        gain_row,
+        conv_bias,
+        gain,
     )
     return (velocity, decoded[None])
 

time: 117 us -> 123 us (1.051)
  starting transfers between devices: 53.4 us -> 61.2 us
  Pallas kernels: 22.7 us -> 20.6 us
    ppermute x3, waiting for transfers between devices: 4.05 us -> 0.01 us  [local(): blocks = [own] + [lax.ppermute(own, 'y', ring(d)) for d in (1, 3, 2)]]
    ppermute x3, starting transfers between devices: 8.98 us -> 12.9 us  [local(): blocks = [own] + [lax.ppermute(own, 'y', ring(d)) for d in (1, 3, 2)]]
    ppermute x3, waiting for transfers between devices: 6.77 us -> 9.56 us  [local(): lax.ppermute(query[0], 'zl', crossed(m))]
    pallas_call x2, Pallas kernels: 18.1 us -> 15.6 us  [attend(): pl.pallas_call(functools.partial(attention_kernel, nq=nq, nk=nk, nx=len(e...]
    unnamed x25 -> x17, local copies, waits for them, and re-layouts: 3.6 us -> 1.59 us
    all_to_all x1, starting transfers between devices: 15 us -> 16.6 us  [local(): shares = lax.all_to_all(shares, ('zh', 'x'), 0, 0, tiled=True)]
    ppermute x3, starting transfers between devices: 14.1 us -> 15.5 us  [local(): lax.ppermute(query[0], 'zl', crossed(m))]
    concatenate x1, local copies, waits for them, and re-layouts: 0.13 us -> 1.37 us  [conv_matrices(): spread = jnp.concatenate(parts, 2).reshape(taps, 4, 2, 2, chans, outs)]
  transfers between devices with their start and end apart: 12 -> 12, of which waited for: 5 -> 6; matrix products, arithmetic and copies ran while one was open for 2% -> 3% of each run, Pallas kernels for 7% -> 4%
where the time goes in v9:
time: 123 us; the launch traced here: 122 us
  starting transfers between devices  61.2 us (50%)
  waiting for transfers between devices  29.5 us (24%)
  Pallas kernels  20.6 us (17%)
  local copies, waits for them, and re-layouts  4.42 us (4%)
  blocking collectives  3.36 us (3%)
  between operations  2.42 us (2%)
    all_to_all x1, starting transfers between devices, local(): shares = lax.all_to_all(shares, ('zh', 'x'), 0, 0, tiled=True)  16.6 us
    pallas_call x2, Pallas kernels, attend(): pl.pallas_call(functools.partial(attention_kernel, nq=nq, nk=nk, nx=len(e...  15.6 us
    ppermute x3, starting transfers between devices, local(): lax.ppermute(query[0], 'zl', crossed(m))  15.5 us
    all_to_all x1, waiting for transfers between devices, local(): shares = lax.all_to_all(shares, ('zh', 'x'), 0, 0, tiled=True)  15.5 us
    ppermute x3, starting transfers between devices, local(): blocks = [own] + [lax.ppermute(own, 'y', ring(d)) for d in (1, 3, 2)]  12.9 us
    ppermute x3, starting transfers between devices, local(): lax.ppermute(chunk, 'zl', crossed(m))  10.1 us
    ppermute x3, waiting for transfers between devices, local(): lax.ppermute(query[0], 'zl', crossed(m))  9.56 us
    ppermute x1, starting transfers between devices, local(): last = lax.ppermute(current, seq, moved(1))  3.76 us
  transfers between devices with their start and end apart: 12, of which 6 were waited for; matrix products, arithmetic and copies ran while one was open for 3% of the time, Pallas kernels for 4%

profile of v9, /device:TPU:24, one launch (start us, length us, event | category | flops | bytes accessed | tf_op | source)
XLA Modules:
  0.0 121.8 jit_solution(9669625950385118532)
XLA Ops:
  0.6 0.0 copy-start
  0.6 0.0 copy-start.4
  0.7 2.0 %shard_map.113.refs_3_.refs_1_ = bf16[1024,256]{1,0:T(8,128)(2,1)} custom-call(bf16[512,256]{1,0:T(8,128)(2,1)} %bitcast.49, bf16[512,256]{1,0:T(8,128)(2,1)} %bitcast.50), custom_call_target="tpu_custom_call" | custom-call | tf_op jit(solution)/shard_map/pallas_call | solution.py:69
  2.7 0.0 copy-start.6
  2.7 7.6 %collective-permute-start = (bf16[1024,256]{1,0:T(8,128)(2,1)}, bf16[1024,256]{1,0:T(8,128)(2,1)S(1)}, u32[]{:S(2)}, u32[]{:S(2)}) collective-permute-start(bf16[1024,256]{1,0:T(8,128)(2,1)} %shard_map.113.refs_3_.refs_1_), channel_id=1, source_target_pairs={{0,4},{4,8},{8,12},{12,0},{1,5},{5,9},{9,13},{13,1},{2,6},{6,10},{... | collective-permute-start | bytes 1572872 | tf_op jit(solution)/shard_map/ppermute | solution.py:370
  10.4 1.9 %collective-permute-start.1 = (bf16[1024,256]{1,0:T(8,128)(2,1)}, bf16[1024,256]{1,0:T(8,128)(2,1)S(1)}, u32[]{:S(2)}, u32[]{:S(2)}) collective-permute-start(bf16[1024,256]{1,0:T(8,128)(2,1)} %shard_map.113.refs_3_.refs_1_), channel_id=1, source_target_pairs={{0,12},{4,0},{8,4},{12,8},{1,13},{5,1},{9,5},{13,9},{2,14},{6,2},{... | collective-permute-start | bytes 1572872 | tf_op jit(solution)/shard_map/ppermute | solution.py:370
  12.3 3.4 %collective-permute-start.2 = (bf16[1024,256]{1,0:T(8,128)(2,1)}, bf16[1024,256]{1,0:T(8,128)(2,1)S(1)}, u32[]{:S(2)}, u32[]{:S(2)}) collective-permute-start(bf16[1024,256]{1,0:T(8,128)(2,1)} %shard_map.113.refs_3_.refs_1_), channel_id=1, source_target_pairs={{0,8},{4,12},{8,0},{12,4},{1,9},{5,13},{9,1},{13,5},{2,10},{6,14},... | collective-permute-start | bytes 1572872 | tf_op jit(solution)/shard_map/ppermute | solution.py:370
  15.7 2.7 %collective-permute-start.3 = (bf16[512,256]{1,0:T(8,128)(2,1)S(1)}, bf16[512,256]{1,0:T(8,128)(2,1)S(1)}, u32[]{:S(2)}, u32[]{:S(2)}) collective-permute-start(bf16[512,256]{1,0:T(8,128)(2,1)S(1)} %bitcast.43), channel_id=1, source_target_pairs={{0,3},{1,2},{2,1},{3,0},{4,7},{5,6},{6,5},{7,4},{8,11},{9,10},{10,... | collective-permute-start | bytes 786440 | tf_op jit(solution)/shard_map/ppermute | solution.py:371
  18.4 1.9 %collective-permute-start.4 = (bf16[512,256]{1,0:T(8,128)(2,1)S(1)}, bf16[512,256]{1,0:T(8,128)(2,1)S(1)}, u32[]{:S(2)}, u32[]{:S(2)}) collective-permute-start(bf16[512,256]{1,0:T(8,128)(2,1)S(1)} %bitcast.44), channel_id=1, source_target_pairs={{0,2},{1,3},{2,0},{3,1},{4,6},{5,7},{6,4},{7,5},{8,10},{9,11},{10,... | collective-permute-start | bytes 786440 | tf_op jit(solution)/shard_map/ppermute | solution.py:371
  21.1 0.1 copy.20
  21.2 0.1 squeeze.26
  21.2 0.1 copy.21
  21.3 0.1 squeeze.27
  21.4 0.1 pad_maximum_fusion.refs_4_
  21.5 5.4 %collective-permute-done.3.refs_0_ = bf16[512,256]{1,0:T(8,128)(2,1)S(1)} collective-permute-done((bf16[512,256]{1,0:T(8,128)(2,1)S(1)}, bf16[512,256]{1,0:T(8,128)(2,1)S(1)}, u32[]{:S(2)}, u32[]{:S(2)}) %collective-permute-start.3) | collective-permute-done | bytes 262176 | tf_op jit(solution)/shard_map/ppermute | solution.py:371
  26.8 10.9 %collective-permute-start.5 = (bf16[512,256]{1,0:T(8,128)(2,1)S(1)}, bf16[512,256]{1,0:T(8,128)(2,1)S(1)}, u32[]{:S(2)}, u32[]{:S(2)}) collective-permute-start(bf16[512,256]{1,0:T(8,128)(2,1)S(1)} %bitcast.45), channel_id=1, source_target_pairs={{0,1},{1,0},{2,3},{3,2},{4,5},{5,4},{6,7},{7,6},{8,9},{9,8},{10,11... | collective-permute-start | bytes 786440 | tf_op jit(solution)/shard_map/ppermute | solution.py:371
  37.7 0.1 fusion.1.count_ref
  38.5 0.8 pad.6
  39.4 1.4 %fusion.2 = (bf16[3,4,4,16,384]{4,3,2,1,0:T(8,128)(2,1)S(1)}, bf16[3,4,4,16,384]{4,3,2,1,0:T(8,128)(2,1)S(1)}) fusion(bf16[3,4,3,16,384]{4,3,2,1,0:T(8,128)(2,1)} %pad.6), kind=kLoop, calls=%fused_computation.9 | loop fusion | bytes 1622016 | tf_op jit(solution)/shard_map/concatenate | solution.py:357
  40.8 4.2 %collective-permute-done.5.refs_2_ = bf16[512,256]{1,0:T(8,128)(2,1)S(1)} collective-permute-done((bf16[512,256]{1,0:T(8,128)(2,1)S(1)}, bf16[512,256]{1,0:T(8,128)(2,1)S(1)}, u32[]{:S(2)}, u32[]{:S(2)}) %collective-permute-start.5) | collective-permute-done | bytes 262176 | tf_op jit(solution)/shard_map/ppermute | solution.py:371
  45.0 11.0 %shard_map.114 = (bf16[144,512]{1,0:T(8,128)(2,1)S(1)}, bf16[144,512]{1,0:T(8,128)(2,1)S(1)}, bf16[144,512]{1,0:T(8,128)(2,1)S(1)}) custom-call(s32[4]{0:T(128)S(1)} %fusion.1.count_ref, bf16[512,256]{1,0:T(8,128)(2,1)S(1)} %collective-permute-done.3.refs_0_, bf16[512,256]{1,0:T(8,128)(2,1)S(1)} %collective-permute-done.4.refs_1_, ...), custom_call_target="tpu_custom_call" | custom-call | flops 3221225472 | bytes 2883584 | tf_op jit(solution)/shard_map/pallas_call | solution.py:204
  56.0 2.6 %collective-permute-start.6 = (bf16[144,512]{1,0:T(8,128)(2,1)S(1)}, bf16[144,512]{1,0:T(8,128)(2,1)S(1)}, u32[]{:S(2)}, u32[]{:S(2)}) collective-permute-start(bf16[144,512]{1,0:T(8,128)(2,1)S(1)} %get-tuple-element.5.refs_6_), channel_id=1, source_target_pairs={{0,3},{1,2},{2,1},{3,0},{4,7},{5,6},{6,5},{7,4},{8,11},{9,10},{10,... | collective-permute-start | bytes 442376 | tf_op jit(solution)/shard_map/ppermute | solution.py:393
  58.6 1.9 %collective-permute-start.7 = (bf16[144,512]{1,0:T(8,128)(2,1)S(1)}, bf16[144,512]{1,0:T(8,128)(2,1)S(1)}, u32[]{:S(2)}, u32[]{:S(2)}) collective-permute-start(bf16[144,512]{1,0:T(8,128)(2,1)S(1)} %get-tuple-element.6), channel_id=1, source_target_pairs={{0,2},{1,3},{2,0},{3,1},{4,6},{5,7},{6,4},{7,5},{8,10},{9,11},{10,... | collective-permute-start | bytes 442376 | tf_op jit(solution)/shard_map/ppermute | solution.py:393
  60.5 5.6 %collective-permute-start.8 = (bf16[144,512]{1,0:T(8,128)(2,1)S(1)}, bf16[144,512]{1,0:T(8,128)(2,1)S(1)}, u32[]{:S(2)}, u32[]{:S(2)}) collective-permute-start(bf16[144,512]{1,0:T(8,128)(2,1)S(1)} %get-tuple-element.7), channel_id=1, source_target_pairs={{0,1},{1,0},{2,3},{3,2},{4,5},{5,4},{6,7},{7,6},{8,9},{9,8},{10,11... | collective-permute-start | bytes 442376 | tf_op jit(solution)/shard_map/ppermute | solution.py:393
  66.2 0.1 pad_maximum_fusion.1.scale_ref
  66.3 0.1 copy.18
  66.3 0.0 copy-start.5
  66.3 0.1 copy.19
  66.4 0.9 copy-done.5
  67.3 4.6 %shard_map.115.refs_0_ = bf16[144,512]{1,0:T(8,128)(2,1)S(1)} custom-call(s32[4]{0:T(128)S(1)} %fusion.1.count_ref, bf16[512,256]{1,0:T(8,128)(2,1)S(1)} %bitcast.46, bf16[1024,256]{1,0:T(8,128)(2,1)S(1)} %copy-done.1, bf16[1024,256]{1,0:T(8,128)(2,1)S(1)} %collective-permute-done.refs_4_.refs_2_, ...), custom_call_target="tpu_custom_call" | custom-call | flops 1073741824 | bytes 2359296 | tf_op jit(solution)/shard_map/pallas_call | solution.py:204
  71.9 0.0 collective-permute-done.6.refs_1_
  71.9 0.0 collective-permute-done.7.refs_2_
  71.9 0.8 collective-permute-done.8.refs_3_
  72.7 1.5 %shard_map.116 = bf16[16,32,128]{2,1,0:T(8,128)(2,1)} custom-call(f32[2]{0:T(128)S(1)} %pad_maximum_fusion.1.scale_ref, s32[1]{0:T(128)} %bitcast.4.place_ref, bf16[144,512]{1,0:T(8,128)(2,1)S(1)} %shard_map.115.refs_0_, bf16[144,512]{1,0:T(8,128)(2,1)S(1)} %collective-permute-done.6.refs_1_, bf16[144,512]{1,0:T(8,128)(2,1)S(1)} %collective-permute-done.7.refs_2_, ...), custom_call_target="tpu_custom_call" | custom-call | tf_op jit(solution)/shard_map/pallas_call | solution.py:265
  74.2 16.6 %all-to-all-start = ((bf16[16,32,128]{2,1,0:T(8,128)(2,1)}), bf16[16,32,128]{2,1,0:T(8,128)(2,1)S(1)}, u32[]{:S(2)}, u32[]{:S(2)}) async-start(bf16[16,32,128]{2,1,0:T(8,128)(2,1)} %shard_map.116), calls=%async_computation | async-start | bytes 262144 | tf_op jit(solution)/shard_map/all_to_all | solution.py:396
  90.8 15.5 %all-to-all-done = bf16[16,32,128]{2,1,0:T(8,128)(2,1)S(1)} async-done(((bf16[16,32,128]{2,1,0:T(8,128)(2,1)}), bf16[16,32,128]{2,1,0:T(8,128)(2,1)S(1)}, u32[]{:S(2)}, u32[]{:S(2)}) %all-to-all-start) | async-done | bytes 131104 | tf_op jit(solution)/shard_map/all_to_all | solution.py:396
  106.3 3.4 %psum.7 = f32[32,128]{1,0:T(8,128)S(1)} all-reduce(f32[32,128]{1,0:T(8,128)S(1)} %convert_reduce_fusion), channel_id=1, replica_groups=mesh['cfg'=2,'zh'=4,'x'=4,'y'=4,'zl'=4] {'cfg'}, use_global_device_ids=true, to_apply=%region_1.2 | all-reduce | flops 4096 | bytes 32768 | tf_op jit(solution)/shard_map/psum | solution.py:397
  109.7 0.1 subtract_convert_fusion.own_ref
  109.8 2.3 %collective-permute-start.10 = (bf16[32,128]{1,0:T(8,128)(2,1)S(1)}, bf16[32,128]{1,0:T(8,128)(2,1)S(1)}, u32[]{:S(2)}, u32[]{:S(2)}) collective-permute-start(bf16[32,128]{1,0:T(8,128)(2,1)S(1)} %subtract_convert_fusion.own_ref), channel_id=1, source_target_pairs={{0,2},{1,3},{2,4},{3,5},{4,6},{5,7},{6,8},{7,9},{8,10},{9,11},{10,... | collective-permute-start | bytes 24584 | tf_op jit(solution)/shard_map/ppermute | solution.py:401
  112.1 3.8 %collective-permute-start.9 = (bf16[32,128]{1,0:T(8,128)(2,1)S(1)}, bf16[32,128]{1,0:T(8,128)(2,1)S(1)}, u32[]{:S(2)}, u32[]{:S(2)}) collective-permute-start(bf16[32,128]{1,0:T(8,128)(2,1)S(1)} %subtract_convert_fusion.own_ref), channel_id=1, source_target_pairs={{0,1},{1,2},{2,3},{3,4},{4,5},{5,6},{6,7},{7,8},{8,9},{9,10},{10,1... | collective-permute-start | bytes 24584 | tf_op jit(solution)/shard_map/ppermute | solution.py:400
  115.9 0.1 dynamic-slice
  115.9 0.1 reshape.50
  116.1 0.0 copy-start.2
  116.1 0.0 copy-start.3
  116.1 0.7 copy.23
  116.8 0.3 collective-permute-done.10.older_ref
  117.1 3.2 %collective-permute-done.9.last_ref = bf16[32,128]{1,0:T(8,128)(2,1)S(1)} collective-permute-done((bf16[32,128]{1,0:T(8,128)(2,1)S(1)}, bf16[32,128]{1,0:T(8,128)(2,1)S(1)}, u32[]{:S(2)}, u32[]{:S(2)}) %collective-permute-start.9) | collective-permute-done | bytes 8224 | tf_op jit(solution)/shard_map/ppermute | solution.py:400
  120.3 1.5 %shard_map.117 = bf16[2,32,384]{2,1,0:T(8,128)(2,1)} custom-call(s32[1]{0:T(128)} %bitcast.23.half_ref, bf16[32,128]{1,0:T(8,128)(2,1)S(1)} %subtract_convert_fusion.own_ref, bf16[32,128]{1,0:T(8,128)(2,1)S(1)} %collective-permute-done.9.last_ref, bf16[32,128]{1,0:T(8,128)(2,1)S(1)} %collective-permute-done.10.older_ref, bf16[768,384]{1,0:T(8,128)(2,1)S(1)} %bitcast.40, ...), custom_call_target="tpu_custom_call" | custom-call | tf_op jit(solution)/shard_map/pallas_call | solution.py:335
  (18 shorter events, 0.1 us)
Async XLA Ops:
  0.6 38.7 %copy-start = (bf16[4096,64]{0,1:T(8,128)(2,1)S(1)}, bf16[4096,64]{0,1:T(8,128)(2,1)}, u32[]{:S(2)}) copy-start(bf16[4096,64]{0,1:T(8,128)(2,1)} %param.16) | copy-start | bytes 1572868
  0.6 15.0 %copy-start.4 = (bf16[1,512,256]{2,1,0:T(8,128)(2,1)S(1)}, bf16[1,512,256]{2,1,0:T(8,128)(2,1)}, u32[]{:S(2)}) copy-start(bf16[1,512,256]{2,1,0:T(8,128)(2,1)} %param.10) | copy-start | bytes 786436
  0.7 19.7 %copy-start.7 = (f32[1,2,64,16]{2,3,1,0:T(8,128)S(1)}, f32[1,2,64,16]{2,3,1,0:T(8,128)}, u32[]{:S(2)}) copy-start(f32[1,2,64,16]{2,3,1,0:T(8,128)} %param.15) | copy-start | bytes 24580
  2.7 35.8 %copy-start.6 = (bf16[3,3,3,16,384]{4,3,2,1,0:T(8,128)(2,1)S(1)}, bf16[3,3,3,16,384]{4,3,2,1,0:T(8,128)(2,1)}, u32[]{:S(2)}) copy-start(bf16[3,3,3,16,384]{4,3,2,1,0:T(8,128)(2,1)} %param.17) | copy-start | bytes 995332
  2.7 42.3 %collective-permute-start = (bf16[1024,256]{1,0:T(8,128)(2,1)}, bf16[1024,256]{1,0:T(8,128)(2,1)S(1)}, u32[]{:S(2)}, u32[]{:S(2)}) collective-permute-start(bf16[1024,256]{1,0:T(8,128)(2,1)} %shard_map.113.refs_3_.refs_1_), channel_id=1, source_target_pairs={{0,4},{4,8},{8,12},{12,0},{1,5},{5,9},{9,13},{13,1},{2,6},{6,10},{... | collective-permute-start | bytes 1572872 | tf_op jit(solution)/shard_map/ppermute | solution.py:370
  10.4 34.6 %collective-permute-start.1 = (bf16[1024,256]{1,0:T(8,128)(2,1)}, bf16[1024,256]{1,0:T(8,128)(2,1)S(1)}, u32[]{:S(2)}, u32[]{:S(2)}) collective-permute-start(bf16[1024,256]{1,0:T(8,128)(2,1)} %shard_map.113.refs_3_.refs_1_), channel_id=1, source_target_pairs={{0,12},{4,0},{8,4},{12,8},{1,13},{5,1},{9,5},{13,9},{2,14},{6,2},{... | collective-permute-start | bytes 1572872 | tf_op jit(solution)/shard_map/ppermute | solution.py:370
  12.3 32.7 %collective-permute-start.2 = (bf16[1024,256]{1,0:T(8,128)(2,1)}, bf16[1024,256]{1,0:T(8,128)(2,1)S(1)}, u32[]{:S(2)}, u32[]{:S(2)}) collective-permute-start(bf16[1024,256]{1,0:T(8,128)(2,1)} %shard_map.113.refs_3_.refs_1_), channel_id=1, source_target_pairs={{0,8},{4,12},{8,0},{12,4},{1,9},{5,13},{9,1},{13,5},{2,10},{6,14},... | collective-permute-start | bytes 1572872 | tf_op jit(solution)/shard_map/ppermute | solution.py:370
  15.7 11.2 %collective-permute-start.3 = (bf16[512,256]{1,0:T(8,128)(2,1)S(1)}, bf16[512,256]{1,0:T(8,128)(2,1)S(1)}, u32[]{:S(2)}, u32[]{:S(2)}) collective-permute-start(bf16[512,256]{1,0:T(8,128)(2,1)S(1)} %bitcast.43), channel_id=1, source_target_pairs={{0,3},{1,2},{2,1},{3,0},{4,7},{5,6},{6,5},{7,4},{8,11},{9,10},{10,... | collective-permute-start | bytes 786440 | tf_op jit(solution)/shard_map/ppermute | solution.py:371
  18.4 22.4 %collective-permute-start.4 = (bf16[512,256]{1,0:T(8,128)(2,1)S(1)}, bf16[512,256]{1,0:T(8,128)(2,1)S(1)}, u32[]{:S(2)}, u32[]{:S(2)}) collective-permute-start(bf16[512,256]{1,0:T(8,128)(2,1)S(1)} %bitcast.44), channel_id=1, source_target_pairs={{0,2},{1,3},{2,0},{3,1},{4,6},{5,7},{6,4},{7,5},{8,10},{9,11},{10,... | collective-permute-start | bytes 786440 | tf_op jit(solution)/shard_map/ppermute | solution.py:371
  26.8 18.1 %collective-permute-start.5 = (bf16[512,256]{1,0:T(8,128)(2,1)S(1)}, bf16[512,256]{1,0:T(8,128)(2,1)S(1)}, u32[]{:S(2)}, u32[]{:S(2)}) collective-permute-start(bf16[512,256]{1,0:T(8,128)(2,1)S(1)} %bitcast.45), channel_id=1, source_target_pairs={{0,1},{1,0},{2,3},{3,2},{4,5},{5,4},{6,7},{7,6},{8,9},{9,8},{10,11... | collective-permute-start | bytes 786440 | tf_op jit(solution)/shard_map/ppermute | solution.py:371
  39.4 5.6 %copy-start.1 = (bf16[1024,256]{1,0:T(8,128)(2,1)S(1)}, bf16[1024,256]{1,0:T(8,128)(2,1)}, u32[]{:S(2)}) copy-start(bf16[1024,256]{1,0:T(8,128)(2,1)} %shard_map.113.refs_3_.refs_1_) | copy-start | bytes 1572868
  56.0 15.8 %collective-permute-start.6 = (bf16[144,512]{1,0:T(8,128)(2,1)S(1)}, bf16[144,512]{1,0:T(8,128)(2,1)S(1)}, u32[]{:S(2)}, u32[]{:S(2)}) collective-permute-start(bf16[144,512]{1,0:T(8,128)(2,1)S(1)} %get-tuple-element.5.refs_6_), channel_id=1, source_target_pairs={{0,3},{1,2},{2,1},{3,0},{4,7},{5,6},{6,5},{7,4},{8,11},{9,10},{10,... | collective-permute-start | bytes 442376 | tf_op jit(solution)/shard_map/ppermute | solution.py:393
  58.6 13.3 %collective-permute-start.7 = (bf16[144,512]{1,0:T(8,128)(2,1)S(1)}, bf16[144,512]{1,0:T(8,128)(2,1)S(1)}, u32[]{:S(2)}, u32[]{:S(2)}) collective-permute-start(bf16[144,512]{1,0:T(8,128)(2,1)S(1)} %get-tuple-element.6), channel_id=1, source_target_pairs={{0,2},{1,3},{2,0},{3,1},{4,6},{5,7},{6,4},{7,5},{8,10},{9,11},{10,... | collective-permute-start | bytes 442376 | tf_op jit(solution)/shard_map/ppermute | solution.py:393
  60.5 12.2 %collective-permute-start.8 = (bf16[144,512]{1,0:T(8,128)(2,1)S(1)}, bf16[144,512]{1,0:T(8,128)(2,1)S(1)}, u32[]{:S(2)}, u32[]{:S(2)}) collective-permute-start(bf16[144,512]{1,0:T(8,128)(2,1)S(1)} %get-tuple-element.7), channel_id=1, source_target_pairs={{0,1},{1,0},{2,3},{3,2},{4,5},{5,4},{6,7},{7,6},{8,9},{9,8},{10,11... | collective-permute-start | bytes 442376 | tf_op jit(solution)/shard_map/ppermute | solution.py:393
  66.3 1.0 copy-start.5
  74.2 32.1 %all-to-all-start = ((bf16[16,32,128]{2,1,0:T(8,128)(2,1)}), bf16[16,32,128]{2,1,0:T(8,128)(2,1)S(1)}, u32[]{:S(2)}, u32[]{:S(2)}) async-start(bf16[16,32,128]{2,1,0:T(8,128)(2,1)} %shard_map.116), calls=%async_computation | async-start | bytes 262144 | tf_op jit(solution)/shard_map/all_to_all | solution.py:396
  109.8 7.3 %collective-permute-start.10 = (bf16[32,128]{1,0:T(8,128)(2,1)S(1)}, bf16[32,128]{1,0:T(8,128)(2,1)S(1)}, u32[]{:S(2)}, u32[]{:S(2)}) collective-permute-start(bf16[32,128]{1,0:T(8,128)(2,1)S(1)} %subtract_convert_fusion.own_ref), channel_id=1, source_target_pairs={{0,2},{1,3},{2,4},{3,5},{4,6},{5,7},{6,8},{7,9},{8,10},{9,11},{10,... | collective-permute-start | bytes 24584 | tf_op jit(solution)/shard_map/ppermute | solution.py:401
  112.1 8.2 %collective-permute-start.9 = (bf16[32,128]{1,0:T(8,128)(2,1)S(1)}, bf16[32,128]{1,0:T(8,128)(2,1)S(1)}, u32[]{:S(2)}, u32[]{:S(2)}) collective-permute-start(bf16[32,128]{1,0:T(8,128)(2,1)S(1)} %subtract_convert_fusion.own_ref), channel_id=1, source_target_pairs={{0,1},{1,2},{2,3},{3,4},{4,5},{5,6},{6,7},{7,8},{8,9},{9,10},{10,1... | collective-permute-start | bytes 24584 | tf_op jit(solution)/shard_map/ppermute | solution.py:400
  116.1 4.3 %copy-start.2 = (f32[384]{0:T(512)S(1)}, f32[384]{0:T(512)}, u32[]{:S(2)}) copy-start(f32[384]{0:T(512)} %bias_hbm.1) | copy-start | bytes 4612
  116.1 4.3 %copy-start.3 = (f32[384]{0:T(512)S(1)}, f32[384]{0:T(512)}, u32[]{:S(2)}) copy-start(f32[384]{0:T(512)} %gain_hbm.1) | copy-start | bytes 4612

commit v10 on v9

--- a/solution.py
+++ b/solution.py
@@ -276,22 +276,18 @@
     own_ref,
     last_ref,
     older_ref,
-    even_hbm,
-    odd_hbm,
+    even_ref,
+    odd_ref,
     bias_hbm,
     gain_hbm,
     out_ref,
-    even_ref,
-    odd_ref,
     bias_ref,
     gain_ref,
     sems,
 ):
     copies = [
-        pltpu.make_async_copy(even_hbm, even_ref, sems.at[0]),
-        pltpu.make_async_copy(odd_hbm, odd_ref, sems.at[1]),
-        pltpu.make_async_copy(bias_hbm, bias_ref.at[0], sems.at[2]),
-        pltpu.make_async_copy(gain_hbm, gain_ref.at[0], sems.at[3]),
+        pltpu.make_async_copy(bias_hbm, bias_ref.at[0], sems.at[0]),
+        pltpu.make_async_copy(gain_hbm, gain_ref.at[0], sems.at[1]),
     ]
     for copy in copies:
         copy.start()
@@ -335,17 +331,15 @@
     return pl.pallas_call(
         decode_kernel,
         out_shape=jax.ShapeDtypeStruct((2, 32, chans), jnp.bfloat16),
-        in_specs=[SMEM] + [VMEM] * 3 + [ANY] * 4,
+        in_specs=[SMEM] + [VMEM] * 5 + [HBM] * 2,
         out_specs=VMEM,
         scratch_shapes=[
-            pltpu.VMEM(even.shape, even.dtype),
-            pltpu.VMEM(odd.shape, odd.dtype),
             pltpu.VMEM((1, chans), jnp.float32),
             pltpu.VMEM((1, chans), jnp.float32),
-            pltpu.SemaphoreType.DMA((4,)),
+            pltpu.SemaphoreType.DMA((2,)),
         ],
         compiler_params=pltpu.CompilerParams(vmem_limit_bytes=32 * 2**20),
-    )(half, own, last, older, even, odd, bias, gain)
+    )(half, own, last, older, even, odd, in_hbm(bias), in_hbm(gain))
 
 
 def conv_matrices(conv_weight):
@@ -388,7 +382,7 @@
     place = (zh * SIDE + x).astype(jnp.int32).reshape(1)
 
     third, second, first = attend(counts, queries[3:0:-1], blocks, weight)
-    (mine,) = attend(counts, queries[:1], blocks, weight, extras=(third, even, odd))
+    (mine,) = attend(counts, queries[:1], blocks, weight, extras=(third,))
     chunks = [mine] + [
         lax.ppermute(chunk, "zl", crossed(m)) for m, chunk in ((3, third), (2, second), (1, first))
     ]

time: 123 us -> 116 us (0.943)
  starting transfers between devices: 61.2 us -> 54.5 us
  local copies, waits for them, and re-layouts: 4.42 us -> 1.53 us
  waiting for transfers between devices: 29.5 us -> 30.8 us
    ppermute x3, waiting for transfers between devices: 0.01 us -> 3.95 us  [local(): blocks = [own] + [lax.ppermute(own, 'y', ring(d)) for d in (1, 3, 2)]]
    ppermute x3, starting transfers between devices: 12.9 us -> 9.12 us  [local(): blocks = [own] + [lax.ppermute(own, 'y', ring(d)) for d in (1, 3, 2)]]
    ppermute x3, waiting for transfers between devices: 9.56 us -> 7.51 us  [local(): lax.ppermute(query[0], 'zl', crossed(m))]
    all_to_all x1, starting transfers between devices: 16.6 us -> 14.9 us  [local(): shares = lax.all_to_all(shares, ('zh', 'x'), 0, 0, tiled=True)]
    ppermute x3, starting transfers between devices: 15.5 us -> 14.1 us  [local(): lax.ppermute(query[0], 'zl', crossed(m))]
    concatenate x1, local copies, waits for them, and re-layouts: 1.37 us -> 0.13 us  [conv_matrices(): spread = jnp.concatenate(parts, 2).reshape(taps, 4, 2, 2, chans, outs)]
  transfers between devices with their start and end apart: 12 -> 12, of which waited for: 6 -> 7; matrix products, arithmetic and copies ran while one was open for 3% -> 2% of each run, Pallas kernels for 4% -> 6%
where the time goes in v10:
time: 116 us; the launch traced here: 114 us
  starting transfers between devices  54.5 us (47%)
  waiting for transfers between devices  30.8 us (27%)
  Pallas kernels  21 us (18%)
  blocking collectives  3.36 us (3%)
  between operations  2.39 us (2%)
  local copies, waits for them, and re-layouts  1.53 us (1%)
    pallas_call x2, Pallas kernels, attend(): pl.pallas_call(functools.partial(attention_kernel, nq=nq, nk=nk, nx=len(e...  15.7 us
    all_to_all x1, waiting for transfers between devices, local(): shares = lax.all_to_all(shares, ('zh', 'x'), 0, 0, tiled=True)  15.1 us
    all_to_all x1, starting transfers between devices, local(): shares = lax.all_to_all(shares, ('zh', 'x'), 0, 0, tiled=True)  14.9 us
    ppermute x3, starting transfers between devices, local(): lax.ppermute(query[0], 'zl', crossed(m))  14.1 us
    ppermute x3, starting transfers between devices, local(): lax.ppermute(chunk, 'zl', crossed(m))  10.1 us
    ppermute x3, starting transfers between devices, local(): blocks = [own] + [lax.ppermute(own, 'y', ring(d)) for d in (1, 3, 2)]  9.12 us
    ppermute x3, waiting for transfers between devices, local(): lax.ppermute(query[0], 'zl', crossed(m))  7.51 us
    ppermute x3, waiting for transfers between devices, local(): blocks = [own] + [lax.ppermute(own, 'y', ring(d)) for d in (1, 3, 2)]  3.95 us
  transfers between devices with their start and end apart: 12, of which 7 were waited for; matrix products, arithmetic and copies ran while one was open for 2% of the time, Pallas kernels for 6%

profile of v10, /device:TPU:24, one launch (start us, length us, event | category | flops | bytes accessed | tf_op | source)
XLA Modules:
  0.0 113.9 jit_solution(5533447786482138842)
XLA Ops:
  0.6 0.0 copy-start
  0.6 6.7 %collective-permute-start.3 = (bf16[512,256]{1,0:T(8,128)(2,1)}, bf16[512,256]{1,0:T(8,128)(2,1)S(1)}, u32[]{:S(2)}, u32[]{:S(2)}) collective-permute-start(bf16[512,256]{1,0:T(8,128)(2,1)} %bitcast.41), channel_id=1, source_target_pairs={{0,3},{1,2},{2,1},{3,0},{4,7},{5,6},{6,5},{7,4},{8,11},{9,10},{10,... | collective-permute-start | bytes 786440 | tf_op jit(solution)/shard_map/ppermute | solution.py:365
  7.3 0.0 copy-start.2
  7.3 0.0 copy-start.4
  7.3 2.0 %shard_map.113.refs_3_.refs_1_ = bf16[1024,256]{1,0:T(8,128)(2,1)} custom-call(bf16[512,256]{1,0:T(8,128)(2,1)} %bitcast.47, bf16[512,256]{1,0:T(8,128)(2,1)} %bitcast.48), custom_call_target="tpu_custom_call" | custom-call | tf_op jit(solution)/shard_map/pallas_call | solution.py:69
  9.4 3.0 %collective-permute-start = (bf16[1024,256]{1,0:T(8,128)(2,1)}, bf16[1024,256]{1,0:T(8,128)(2,1)S(1)}, u32[]{:S(2)}, u32[]{:S(2)}) collective-permute-start(bf16[1024,256]{1,0:T(8,128)(2,1)} %shard_map.113.refs_3_.refs_1_), channel_id=1, source_target_pairs={{0,4},{4,8},{8,12},{12,0},{1,5},{5,9},{9,13},{13,1},{2,6},{6,10},{... | collective-permute-start | bytes 1572872 | tf_op jit(solution)/shard_map/ppermute | solution.py:364
  12.4 3.0 %collective-permute-start.1 = (bf16[1024,256]{1,0:T(8,128)(2,1)}, bf16[1024,256]{1,0:T(8,128)(2,1)S(1)}, u32[]{:S(2)}, u32[]{:S(2)}) collective-permute-start(bf16[1024,256]{1,0:T(8,128)(2,1)} %shard_map.113.refs_3_.refs_1_), channel_id=1, source_target_pairs={{0,12},{4,0},{8,4},{12,8},{1,13},{5,1},{9,5},{13,9},{2,14},{6,2},{... | collective-permute-start | bytes 1572872 | tf_op jit(solution)/shard_map/ppermute | solution.py:364
  15.3 3.1 %collective-permute-start.2 = (bf16[1024,256]{1,0:T(8,128)(2,1)}, bf16[1024,256]{1,0:T(8,128)(2,1)S(1)}, u32[]{:S(2)}, u32[]{:S(2)}) collective-permute-start(bf16[1024,256]{1,0:T(8,128)(2,1)} %shard_map.113.refs_3_.refs_1_), channel_id=1, source_target_pairs={{0,8},{4,12},{8,0},{12,4},{1,9},{5,13},{9,1},{13,5},{2,10},{6,14},... | collective-permute-start | bytes 1572872 | tf_op jit(solution)/shard_map/ppermute | solution.py:364
  18.5 0.0 copy-done.2
  18.5 1.9 %collective-permute-start.4 = (bf16[512,256]{1,0:T(8,128)(2,1)S(1)}, bf16[512,256]{1,0:T(8,128)(2,1)S(1)}, u32[]{:S(2)}, u32[]{:S(2)}) collective-permute-start(bf16[512,256]{1,0:T(8,128)(2,1)S(1)} %bitcast.42), channel_id=1, source_target_pairs={{0,2},{1,3},{2,0},{3,1},{4,6},{5,7},{6,4},{7,5},{8,10},{9,11},{10,... | collective-permute-start | bytes 786440 | tf_op jit(solution)/shard_map/ppermute | solution.py:365
  21.2 0.0 collective-permute-done.3.refs_0_
  21.2 5.5 %collective-permute-start.5 = (bf16[512,256]{1,0:T(8,128)(2,1)S(1)}, bf16[512,256]{1,0:T(8,128)(2,1)}, u32[]{:S(2)}, u32[]{:S(2)}) collective-permute-start(bf16[512,256]{1,0:T(8,128)(2,1)S(1)} %bitcast.43), channel_id=1, source_target_pairs={{0,1},{1,0},{2,3},{3,2},{4,5},{5,4},{6,7},{7,6},{8,9},{9,8},{10,11... | collective-permute-start | bytes 786440 | tf_op jit(solution)/shard_map/ppermute | solution.py:365
  26.7 0.1 fusion.1.count_ref
  27.4 0.1 copy.18
  27.5 0.1 squeeze.26
  27.6 0.1 copy.19
  27.6 0.1 squeeze.27
  27.8 0.1 pad_maximum_fusion.refs_4_
  27.9 4.7 %collective-permute-done.4.refs_1_ = bf16[512,256]{1,0:T(8,128)(2,1)S(1)} collective-permute-done((bf16[512,256]{1,0:T(8,128)(2,1)S(1)}, bf16[512,256]{1,0:T(8,128)(2,1)S(1)}, u32[]{:S(2)}, u32[]{:S(2)}) %collective-permute-start.4) | collective-permute-done | bytes 262176 | tf_op jit(solution)/shard_map/ppermute | solution.py:365
  32.6 2.8 %collective-permute-done.5.refs_2_ = bf16[512,256]{1,0:T(8,128)(2,1)} collective-permute-done((bf16[512,256]{1,0:T(8,128)(2,1)S(1)}, bf16[512,256]{1,0:T(8,128)(2,1)}, u32[]{:S(2)}, u32[]{:S(2)}) %collective-permute-start.5) | collective-permute-done | bytes 262176 | tf_op jit(solution)/shard_map/ppermute | solution.py:365
  35.4 0.0 collective-permute-done.refs_4_.refs_2_
  35.4 3.9 %collective-permute-done.1.refs_5_.refs_3_ = bf16[1024,256]{1,0:T(8,128)(2,1)S(1)} collective-permute-done((bf16[1024,256]{1,0:T(8,128)(2,1)}, bf16[1024,256]{1,0:T(8,128)(2,1)S(1)}, u32[]{:S(2)}, u32[]{:S(2)}) %collective-permute-start.1) | collective-permute-done | bytes 524320 | tf_op jit(solution)/shard_map/ppermute | solution.py:364
  39.3 0.0 collective-permute-done.2.refs_6_.refs_4_
  39.4 11.2 %shard_map.114 = (bf16[144,512]{1,0:T(8,128)(2,1)S(1)}, bf16[144,512]{1,0:T(8,128)(2,1)S(1)}, bf16[144,512]{1,0:T(8,128)(2,1)S(1)}) custom-call(s32[4]{0:T(128)S(1)} %fusion.1.count_ref, bf16[512,256]{1,0:T(8,128)(2,1)S(1)} %collective-permute-done.3.refs_0_, bf16[512,256]{1,0:T(8,128)(2,1)S(1)} %collective-permute-done.4.refs_1_, ...), custom_call_target="tpu_custom_call" | custom-call | flops 3221225472 | bytes 2883584 | tf_op jit(solution)/shard_map/pallas_call | solution.py:204
  50.6 1.9 %collective-permute-start.6 = (bf16[144,512]{1,0:T(8,128)(2,1)S(1)}, bf16[144,512]{1,0:T(8,128)(2,1)S(1)}, u32[]{:S(2)}, u32[]{:S(2)}) collective-permute-start(bf16[144,512]{1,0:T(8,128)(2,1)S(1)} %get-tuple-element.5.refs_6_), channel_id=1, source_target_pairs={{0,3},{1,2},{2,1},{3,0},{4,7},{5,6},{6,5},{7,4},{8,11},{9,10},{10,... | collective-permute-start | bytes 442376 | tf_op jit(solution)/shard_map/ppermute | solution.py:387
  52.5 2.6 %collective-permute-start.7 = (bf16[144,512]{1,0:T(8,128)(2,1)S(1)}, bf16[144,512]{1,0:T(8,128)(2,1)S(1)}, u32[]{:S(2)}, u32[]{:S(2)}) collective-permute-start(bf16[144,512]{1,0:T(8,128)(2,1)S(1)} %get-tuple-element.6), channel_id=1, source_target_pairs={{0,2},{1,3},{2,0},{3,1},{4,6},{5,7},{6,4},{7,5},{8,10},{9,11},{10,... | collective-permute-start | bytes 442376 | tf_op jit(solution)/shard_map/ppermute | solution.py:387
  55.1 5.6 %collective-permute-start.8 = (bf16[144,512]{1,0:T(8,128)(2,1)S(1)}, bf16[144,512]{1,0:T(8,128)(2,1)S(1)}, u32[]{:S(2)}, u32[]{:S(2)}) collective-permute-start(bf16[144,512]{1,0:T(8,128)(2,1)S(1)} %get-tuple-element.7), channel_id=1, source_target_pairs={{0,1},{1,0},{2,3},{3,2},{4,5},{5,4},{6,7},{7,6},{8,9},{9,8},{10,11... | collective-permute-start | bytes 442376 | tf_op jit(solution)/shard_map/ppermute | solution.py:387
  60.7 0.1 pad_maximum_fusion.1.scale_ref
  60.8 4.5 %shard_map.115.refs_0_ = bf16[144,512]{1,0:T(8,128)(2,1)S(1)} custom-call(s32[4]{0:T(128)S(1)} %fusion.1.count_ref, bf16[512,256]{1,0:T(8,128)(2,1)S(1)} %bitcast.44, bf16[1024,256]{1,0:T(8,128)(2,1)S(1)} %copy-done.1, bf16[1024,256]{1,0:T(8,128)(2,1)S(1)} %collective-permute-done.refs_4_.refs_2_, ...), custom_call_target="tpu_custom_call" | custom-call | flops 1073741824 | bytes 2359296 | tf_op jit(solution)/shard_map/pallas_call | solution.py:204
  65.3 0.0 collective-permute-done.6.refs_1_
  65.3 0.6 collective-permute-done.7.refs_2_
  65.9 0.4 collective-permute-done.8.refs_3_
  66.3 1.4 %shard_map.116 = bf16[16,32,128]{2,1,0:T(8,128)(2,1)} custom-call(f32[2]{0:T(128)S(1)} %pad_maximum_fusion.1.scale_ref, s32[1]{0:T(128)} %bitcast.4.place_ref, bf16[144,512]{1,0:T(8,128)(2,1)S(1)} %shard_map.115.refs_0_, bf16[144,512]{1,0:T(8,128)(2,1)S(1)} %collective-permute-done.6.refs_1_, bf16[144,512]{1,0:T(8,128)(2,1)S(1)} %collective-permute-done.7.refs_2_, ...), custom_call_target="tpu_custom_call" | custom-call | tf_op jit(solution)/shard_map/pallas_call | solution.py:265
  67.7 14.9 %all-to-all-start = ((bf16[16,32,128]{2,1,0:T(8,128)(2,1)}), bf16[16,32,128]{2,1,0:T(8,128)(2,1)S(1)}, u32[]{:S(2)}, u32[]{:S(2)}) async-start(bf16[16,32,128]{2,1,0:T(8,128)(2,1)} %shard_map.116), calls=%async_computation | async-start | bytes 262144 | tf_op jit(solution)/shard_map/all_to_all | solution.py:390
  82.8 15.1 %all-to-all-done = bf16[16,32,128]{2,1,0:T(8,128)(2,1)S(1)} async-done(((bf16[16,32,128]{2,1,0:T(8,128)(2,1)}), bf16[16,32,128]{2,1,0:T(8,128)(2,1)S(1)}, u32[]{:S(2)}, u32[]{:S(2)}) %all-to-all-start) | async-done | bytes 131104 | tf_op jit(solution)/shard_map/all_to_all | solution.py:390
  97.9 3.4 %psum.7 = f32[32,128]{1,0:T(8,128)S(1)} all-reduce(f32[32,128]{1,0:T(8,128)S(1)} %convert_reduce_fusion), channel_id=1, replica_groups=mesh['cfg'=2,'zh'=4,'x'=4,'y'=4,'zl'=4] {'cfg'}, use_global_device_ids=true, to_apply=%region_1.2 | all-reduce | flops 4096 | bytes 32768 | tf_op jit(solution)/shard_map/psum | solution.py:391
  101.3 0.1 subtract_convert_fusion.own_ref
  101.3 2.5 %collective-permute-start.10 = (bf16[32,128]{1,0:T(8,128)(2,1)S(1)}, bf16[32,128]{1,0:T(8,128)(2,1)S(1)}, u32[]{:S(2)}, u32[]{:S(2)}) collective-permute-start(bf16[32,128]{1,0:T(8,128)(2,1)S(1)} %subtract_convert_fusion.own_ref), channel_id=1, source_target_pairs={{0,2},{1,3},{2,4},{3,5},{4,6},{5,7},{6,8},{7,9},{8,10},{9,11},{10,... | collective-permute-start | bytes 24584 | tf_op jit(solution)/shard_map/ppermute | solution.py:395
  103.9 3.8 %collective-permute-start.9 = (bf16[32,128]{1,0:T(8,128)(2,1)S(1)}, bf16[32,128]{1,0:T(8,128)(2,1)S(1)}, u32[]{:S(2)}, u32[]{:S(2)}) collective-permute-start(bf16[32,128]{1,0:T(8,128)(2,1)S(1)} %subtract_convert_fusion.own_ref), channel_id=1, source_target_pairs={{0,1},{1,2},{2,3},{3,4},{4,5},{5,6},{6,7},{7,8},{8,9},{9,10},{10,1... | collective-permute-start | bytes 24584 | tf_op jit(solution)/shard_map/ppermute | solution.py:394
  107.6 0.1 fusion.2
  107.8 0.1 copy.21
  107.8 0.1 copy.22
  107.9 0.1 dynamic-slice
  108.0 0.1 reshape.46
  108.1 0.7 copy.23
  108.8 0.0 collective-permute-done.10.older_ref
  108.8 3.3 %collective-permute-done.9.last_ref = bf16[32,128]{1,0:T(8,128)(2,1)S(1)} collective-permute-done((bf16[32,128]{1,0:T(8,128)(2,1)S(1)}, bf16[32,128]{1,0:T(8,128)(2,1)S(1)}, u32[]{:S(2)}, u32[]{:S(2)}) %collective-permute-start.9) | collective-permute-done | bytes 8224 | tf_op jit(solution)/shard_map/ppermute | solution.py:394
  112.1 1.8 %shard_map.117 = bf16[2,32,384]{2,1,0:T(8,128)(2,1)} custom-call(s32[1]{0:T(128)} %bitcast.17.half_ref, bf16[32,128]{1,0:T(8,128)(2,1)S(1)} %subtract_convert_fusion.own_ref, bf16[32,128]{1,0:T(8,128)(2,1)S(1)} %collective-permute-done.9.last_ref, bf16[32,128]{1,0:T(8,128)(2,1)S(1)} %collective-permute-done.10.older_ref, bf16[768,384]{1,0:T(8,128)(2,1)S(1)} %bitcast.39, ...), custom_call_target="tpu_custom_call" | custom-call | tf_op jit(solution)/shard_map/pallas_call | solution.py:331
  (12 shorter events, 0.1 us)
Async XLA Ops:
  0.6 27.2 %copy-start = (bf16[4096,64]{0,1:T(8,128)(2,1)S(1)}, bf16[4096,64]{0,1:T(8,128)(2,1)}, u32[]{:S(2)}) copy-start(bf16[4096,64]{0,1:T(8,128)(2,1)} %param.16) | copy-start | bytes 1572868
  0.6 20.5 %collective-permute-start.3 = (bf16[512,256]{1,0:T(8,128)(2,1)}, bf16[512,256]{1,0:T(8,128)(2,1)S(1)}, u32[]{:S(2)}, u32[]{:S(2)}) collective-permute-start(bf16[512,256]{1,0:T(8,128)(2,1)} %bitcast.41), channel_id=1, source_target_pairs={{0,3},{1,2},{2,1},{3,0},{4,7},{5,6},{6,5},{7,4},{8,11},{9,10},{10,... | collective-permute-start | bytes 786440 | tf_op jit(solution)/shard_map/ppermute | solution.py:365
  7.3 11.2 %copy-start.2 = (bf16[1,512,256]{2,1,0:T(8,128)(2,1)S(1)}, bf16[1,512,256]{2,1,0:T(8,128)(2,1)}, u32[]{:S(2)}) copy-start(bf16[1,512,256]{2,1,0:T(8,128)(2,1)} %param.10) | copy-start | bytes 786436
  7.3 13.8 %copy-start.4 = (f32[1,2,64,16]{2,3,1,0:T(8,128)S(1)}, f32[1,2,64,16]{2,3,1,0:T(8,128)}, u32[]{:S(2)}) copy-start(f32[1,2,64,16]{2,3,1,0:T(8,128)} %param.15) | copy-start | bytes 24580
  9.3 30.0 %copy-start.1 = (bf16[1024,256]{1,0:T(8,128)(2,1)S(1)}, bf16[1024,256]{1,0:T(8,128)(2,1)}, u32[]{:S(2)}) copy-start(bf16[1024,256]{1,0:T(8,128)(2,1)} %shard_map.113.refs_3_.refs_1_) | copy-start | bytes 1572868
  9.4 26.0 %collective-permute-start = (bf16[1024,256]{1,0:T(8,128)(2,1)}, bf16[1024,256]{1,0:T(8,128)(2,1)S(1)}, u32[]{:S(2)}, u32[]{:S(2)}) collective-permute-start(bf16[1024,256]{1,0:T(8,128)(2,1)} %shard_map.113.refs_3_.refs_1_), channel_id=1, source_target_pairs={{0,4},{4,8},{8,12},{12,0},{1,5},{5,9},{9,13},{13,1},{2,6},{6,10},{... | collective-permute-start | bytes 1572872 | tf_op jit(solution)/shard_map/ppermute | solution.py:364
  12.4 27.0 %collective-permute-start.1 = (bf16[1024,256]{1,0:T(8,128)(2,1)}, bf16[1024,256]{1,0:T(8,128)(2,1)S(1)}, u32[]{:S(2)}, u32[]{:S(2)}) collective-permute-start(bf16[1024,256]{1,0:T(8,128)(2,1)} %shard_map.113.refs_3_.refs_1_), channel_id=1, source_target_pairs={{0,12},{4,0},{8,4},{12,8},{1,13},{5,1},{9,5},{13,9},{2,14},{6,2},{... | collective-permute-start | bytes 1572872 | tf_op jit(solution)/shard_map/ppermute | solution.py:364
  15.3 24.0 %collective-permute-start.2 = (bf16[1024,256]{1,0:T(8,128)(2,1)}, bf16[1024,256]{1,0:T(8,128)(2,1)S(1)}, u32[]{:S(2)}, u32[]{:S(2)}) collective-permute-start(bf16[1024,256]{1,0:T(8,128)(2,1)} %shard_map.113.refs_3_.refs_1_), channel_id=1, source_target_pairs={{0,8},{4,12},{8,0},{12,4},{1,9},{5,13},{9,1},{13,5},{2,10},{6,14},... | collective-permute-start | bytes 1572872 | tf_op jit(solution)/shard_map/ppermute | solution.py:364
  18.5 14.1 %collective-permute-start.4 = (bf16[512,256]{1,0:T(8,128)(2,1)S(1)}, bf16[512,256]{1,0:T(8,128)(2,1)S(1)}, u32[]{:S(2)}, u32[]{:S(2)}) collective-permute-start(bf16[512,256]{1,0:T(8,128)(2,1)S(1)} %bitcast.42), channel_id=1, source_target_pairs={{0,2},{1,3},{2,0},{3,1},{4,6},{5,7},{6,4},{7,5},{8,10},{9,11},{10,... | collective-permute-start | bytes 786440 | tf_op jit(solution)/shard_map/ppermute | solution.py:365
  21.2 14.2 %collective-permute-start.5 = (bf16[512,256]{1,0:T(8,128)(2,1)S(1)}, bf16[512,256]{1,0:T(8,128)(2,1)}, u32[]{:S(2)}, u32[]{:S(2)}) collective-permute-start(bf16[512,256]{1,0:T(8,128)(2,1)S(1)} %bitcast.43), channel_id=1, source_target_pairs={{0,1},{1,0},{2,3},{3,2},{4,5},{5,4},{6,7},{7,6},{8,9},{9,8},{10,11... | collective-permute-start | bytes 786440 | tf_op jit(solution)/shard_map/ppermute | solution.py:365
  50.6 14.7 %collective-permute-start.6 = (bf16[144,512]{1,0:T(8,128)(2,1)S(1)}, bf16[144,512]{1,0:T(8,128)(2,1)S(1)}, u32[]{:S(2)}, u32[]{:S(2)}) collective-permute-start(bf16[144,512]{1,0:T(8,128)(2,1)S(1)} %get-tuple-element.5.refs_6_), channel_id=1, source_target_pairs={{0,3},{1,2},{2,1},{3,0},{4,7},{5,6},{6,5},{7,4},{8,11},{9,10},{10,... | collective-permute-start | bytes 442376 | tf_op jit(solution)/shard_map/ppermute | solution.py:387
  52.5 13.3 %collective-permute-start.7 = (bf16[144,512]{1,0:T(8,128)(2,1)S(1)}, bf16[144,512]{1,0:T(8,128)(2,1)S(1)}, u32[]{:S(2)}, u32[]{:S(2)}) collective-permute-start(bf16[144,512]{1,0:T(8,128)(2,1)S(1)} %get-tuple-element.6), channel_id=1, source_target_pairs={{0,2},{1,3},{2,0},{3,1},{4,6},{5,7},{6,4},{7,5},{8,10},{9,11},{10,... | collective-permute-start | bytes 442376 | tf_op jit(solution)/shard_map/ppermute | solution.py:387
  55.1 11.2 %collective-permute-start.8 = (bf16[144,512]{1,0:T(8,128)(2,1)S(1)}, bf16[144,512]{1,0:T(8,128)(2,1)S(1)}, u32[]{:S(2)}, u32[]{:S(2)}) collective-permute-start(bf16[144,512]{1,0:T(8,128)(2,1)S(1)} %get-tuple-element.7), channel_id=1, source_target_pairs={{0,1},{1,0},{2,3},{3,2},{4,5},{5,4},{6,7},{7,6},{8,9},{9,8},{10,11... | collective-permute-start | bytes 442376 | tf_op jit(solution)/shard_map/ppermute | solution.py:387
  66.3 16.4 %copy-start.3 = (bf16[3,3,3,16,384]{4,3,2,1,0:T(8,128)(2,1)S(1)}, bf16[3,3,3,16,384]{4,3,2,1,0:T(8,128)(2,1)}, u32[]{:S(2)}) copy-start(bf16[3,3,3,16,384]{4,3,2,1,0:T(8,128)(2,1)} %param.17) | copy-start | bytes 995332
  67.7 30.1 %all-to-all-start = ((bf16[16,32,128]{2,1,0:T(8,128)(2,1)}), bf16[16,32,128]{2,1,0:T(8,128)(2,1)S(1)}, u32[]{:S(2)}, u32[]{:S(2)}) async-start(bf16[16,32,128]{2,1,0:T(8,128)(2,1)} %shard_map.116), calls=%async_computation | async-start | bytes 262144 | tf_op jit(solution)/shard_map/all_to_all | solution.py:390
  101.3 7.5 %collective-permute-start.10 = (bf16[32,128]{1,0:T(8,128)(2,1)S(1)}, bf16[32,128]{1,0:T(8,128)(2,1)S(1)}, u32[]{:S(2)}, u32[]{:S(2)}) collective-permute-start(bf16[32,128]{1,0:T(8,128)(2,1)S(1)} %subtract_convert_fusion.own_ref), channel_id=1, source_target_pairs={{0,2},{1,3},{2,4},{3,5},{4,6},{5,7},{6,8},{7,9},{8,10},{9,11},{10,... | collective-permute-start | bytes 24584 | tf_op jit(solution)/shard_map/ppermute | solution.py:395
  103.9 8.2 %collective-permute-start.9 = (bf16[32,128]{1,0:T(8,128)(2,1)S(1)}, bf16[32,128]{1,0:T(8,128)(2,1)S(1)}, u32[]{:S(2)}, u32[]{:S(2)}) collective-permute-start(bf16[32,128]{1,0:T(8,128)(2,1)S(1)} %subtract_convert_fusion.own_ref), channel_id=1, source_target_pairs={{0,1},{1,2},{2,3},{3,4},{4,5},{5,6},{6,7},{7,8},{8,9},{9,10},{10,1... | collective-permute-start | bytes 24584 | tf_op jit(solution)/shard_map/ppermute | solution.py:394

commit v11 on v10

--- a/solution.py
+++ b/solution.py
@@ -276,16 +276,19 @@
     own_ref,
     last_ref,
     older_ref,
-    even_ref,
-    odd_ref,
+    taps_hbm,
     bias_hbm,
     gain_hbm,
     out_ref,
+    taps_ref,
+    even_ref,
+    odd_ref,
     bias_ref,
     gain_ref,
     sems,
 ):
     copies = [
+        pltpu.make_async_copy(taps_hbm, taps_ref, sems.at[2]),
         pltpu.make_async_copy(bias_hbm, bias_ref.at[0], sems.at[0]),
         pltpu.make_async_copy(gain_hbm, gain_ref.at[0], sems.at[1]),
     ]
@@ -305,8 +308,17 @@
         ]
         even += rows[0:2]
         odd += rows[1:3]
+    even_ref[...] = jnp.zeros(even_ref.shape, jnp.bfloat16)
+    odd_ref[...] = jnp.zeros(odd_ref.shape, jnp.bfloat16)
     for copy in copies:
         copy.wait()
+    for a in range(3):
+        for u in range(3):
+            for v in range(3):
+                tap = taps_ref[a * 9 + u * 3 + v]
+                for ref, place in ((even_ref, v + 1), (odd_ref, v)):
+                    at = a * 256 + place // 2 * 128 + u * 32 + place % 2 * 16
+                    ref[at : at + 16] = tap
     finished = []
     for parts, weight_ref in ((even, even_ref), (odd, odd_ref)):
         features = (
@@ -326,31 +338,23 @@
         out_ref[row] = jnp.dot(order, both, preferred_element_type=jnp.float32).astype(jnp.bfloat16)
 
 
-def decode(half, own, last, older, even, odd, bias, gain):
+def decode(half, own, last, older, taps, bias, gain):
     chans = bias.shape[0]
     return pl.pallas_call(
         decode_kernel,
         out_shape=jax.ShapeDtypeStruct((2, 32, chans), jnp.bfloat16),
-        in_specs=[SMEM] + [VMEM] * 5 + [HBM] * 2,
+        in_specs=[SMEM] + [VMEM] * 3 + [HBM] * 3,
         out_specs=VMEM,
         scratch_shapes=[
+            pltpu.VMEM(taps.shape, taps.dtype),
+            pltpu.VMEM((768, chans), taps.dtype),
+            pltpu.VMEM((768, chans), taps.dtype),
             pltpu.VMEM((1, chans), jnp.float32),
             pltpu.VMEM((1, chans), jnp.float32),
-            pltpu.SemaphoreType.DMA((2,)),
+            pltpu.SemaphoreType.DMA((3,)),
         ],
         compiler_params=pltpu.CompilerParams(vmem_limit_bytes=32 * 2**20),
-    )(half, own, last, older, even, odd, in_hbm(bias), in_hbm(gain))
-
-
-def conv_matrices(conv_weight):
-    taps, _, _, chans, outs = conv_weight.shape
-    padded = jnp.pad(conv_weight, ((0, 0), (0, 1), (0, 0), (0, 0), (0, 0)))
-    blank = jnp.zeros((taps, 4, 1, chans, outs), conv_weight.dtype)
-    both = []
-    for parts in ([blank, padded], [padded, blank]):
-        spread = jnp.concatenate(parts, 2).reshape(taps, 4, 2, 2, chans, outs)
-        both.append(spread.transpose(0, 2, 1, 3, 4, 5).reshape(taps * 16 * chans, outs))
-    return both
+    )(half, own, last, older, in_hbm(taps), in_hbm(bias), in_hbm(gain))
 
 
 def local(
@@ -369,7 +373,6 @@
     rows = latent[0].reshape(2, TCOLS, 32)
     blank = jnp.zeros((TCOLS, 32), jnp.float32)
     grid = jnp.concatenate([blank, rows[0], rows[1], blank], 1)
-    even, odd = conv_matrices(conv_weight)
     part = lax.dynamic_slice_in_dim(head_weight, (zh * SIDE + x) * 2 * DH, 2 * DH, 0)
     weight = part.T.reshape(PATCH, 2, DH).transpose(1, 0, 2)
     sigma = noise_level(timestep[0], STEPS)
@@ -377,6 +380,7 @@
         [
             jnp.where(cfg == 0, GUIDE, 1.0 - GUIDE).astype(jnp.float32),
             jnp.where(cfg == 0, -1.0 / sigma, 0.0),
+            sigma,
         ]
     )
     place = (zh * SIDE + x).astype(jnp.int32).reshape(1)
@@ -400,8 +404,7 @@
         current,
         last,
         older,
-        even,
-        odd,
+        conv_weight.reshape(27, *conv_weight.shape[3:]),
         conv_bias,
         gain,
     )

time: 116 us -> 115 us (level)
  blocking collectives: 3.36 us -> 33.3 us
  waiting for transfers between devices: 30.8 us -> 15.7 us
  starting transfers between devices: 54.5 us -> 39.8 us
    all_to_all x0 -> x1, blocking collectives: none -> 30 us  [local(): shares = lax.all_to_all(shares, ('zh', 'x'), 0, 0, tiled=True)]
    all_to_all x1 -> x0, waiting for transfers between devices: 15.1 us -> none  [local(): shares = lax.all_to_all(shares, ('zh', 'x'), 0, 0, tiled=True)]
    all_to_all x1 -> x0, starting transfers between devices: 14.9 us -> none  [local(): shares = lax.all_to_all(shares, ('zh', 'x'), 0, 0, tiled=True)]
  transfers between devices with their start and end apart: 12 -> 11, of which waited for: 7 -> 6; matrix products, arithmetic and copies ran while one was open for 2% -> 1% of each run, Pallas kernels for 6% -> 6%
where the time goes in v11:
time: 115 us; the launch traced here: 113 us
  starting transfers between devices  39.8 us (35%)
  blocking collectives  33.3 us (29%)
  Pallas kernels  20.6 us (18%)
  waiting for transfers between devices  15.7 us (14%)
  between operations  2.32 us (2%)
  local copies, waits for them, and re-layouts  1.22 us (1%)
    all_to_all x1, blocking collectives, local(): shares = lax.all_to_all(shares, ('zh', 'x'), 0, 0, tiled=True)  30 us
    pallas_call x2, Pallas kernels, attend(): pl.pallas_call(functools.partial(attention_kernel, nq=nq, nk=nk, nx=len(e...  15.7 us
    ppermute x3, starting transfers between devices, local(): lax.ppermute(query[0], 'zl', crossed(m))  14.1 us
    ppermute x3, starting transfers between devices, local(): lax.ppermute(chunk, 'zl', crossed(m))  10.1 us
    ppermute x3, starting transfers between devices, local(): blocks = [own] + [lax.ppermute(own, 'y', ring(d)) for d in (1, 3, 2)]  9.12 us
    ppermute x3, waiting for transfers between devices, local(): lax.ppermute(query[0], 'zl', crossed(m))  7.49 us
    ppermute x1, starting transfers between devices, local(): last = lax.ppermute(current, seq, moved(1))  4.04 us
    ppermute x3, waiting for transfers between devices, local(): blocks = [own] + [lax.ppermute(own, 'y', ring(d)) for d in (1, 3, 2)]  3.95 us
  transfers between devices with their start and end apart: 11, of which 6 were waited for; matrix products, arithmetic and copies ran while one was open for 1% of the time, Pallas kernels for 6%

profile of v11, /device:TPU:24, one launch (start us, length us, event | category | flops | bytes accessed | tf_op | source)
XLA Modules:
  0.0 113.4 jit_solution(12724234399886529736)
XLA Ops:
  0.6 0.0 copy-start
  0.6 6.7 %collective-permute-start.3 = (bf16[512,256]{1,0:T(8,128)(2,1)}, bf16[512,256]{1,0:T(8,128)(2,1)S(1)}, u32[]{:S(2)}, u32[]{:S(2)}) collective-permute-start(bf16[512,256]{1,0:T(8,128)(2,1)} %bitcast.33), channel_id=1, source_target_pairs={{0,3},{1,2},{2,1},{3,0},{4,7},{5,6},{6,5},{7,4},{8,11},{9,10},{10,... | collective-permute-start | bytes 786440 | tf_op jit(solution)/shard_map/ppermute | solution.py:369
  7.3 0.0 copy-start.2
  7.3 0.0 copy-start.3
  7.3 2.0 %shard_map.113.refs_3_.refs_1_ = bf16[1024,256]{1,0:T(8,128)(2,1)} custom-call(bf16[512,256]{1,0:T(8,128)(2,1)} %bitcast.38, bf16[512,256]{1,0:T(8,128)(2,1)} %bitcast.39), custom_call_target="tpu_custom_call" | custom-call | tf_op jit(solution)/shard_map/pallas_call | solution.py:69
  9.3 0.0 copy-start.1
  9.4 3.0 %collective-permute-start = (bf16[1024,256]{1,0:T(8,128)(2,1)}, bf16[1024,256]{1,0:T(8,128)(2,1)S(1)}, u32[]{:S(2)}, u32[]{:S(2)}) collective-permute-start(bf16[1024,256]{1,0:T(8,128)(2,1)} %shard_map.113.refs_3_.refs_1_), channel_id=1, source_target_pairs={{0,4},{4,8},{8,12},{12,0},{1,5},{5,9},{9,13},{13,1},{2,6},{6,10},{... | collective-permute-start | bytes 1572872 | tf_op jit(solution)/shard_map/ppermute | solution.py:368
  12.4 3.0 %collective-permute-start.1 = (bf16[1024,256]{1,0:T(8,128)(2,1)}, bf16[1024,256]{1,0:T(8,128)(2,1)S(1)}, u32[]{:S(2)}, u32[]{:S(2)}) collective-permute-start(bf16[1024,256]{1,0:T(8,128)(2,1)} %shard_map.113.refs_3_.refs_1_), channel_id=1, source_target_pairs={{0,12},{4,0},{8,4},{12,8},{1,13},{5,1},{9,5},{13,9},{2,14},{6,2},{... | collective-permute-start | bytes 1572872 | tf_op jit(solution)/shard_map/ppermute | solution.py:368
  15.3 3.1 %collective-permute-start.2 = (bf16[1024,256]{1,0:T(8,128)(2,1)}, bf16[1024,256]{1,0:T(8,128)(2,1)S(1)}, u32[]{:S(2)}, u32[]{:S(2)}) collective-permute-start(bf16[1024,256]{1,0:T(8,128)(2,1)} %shard_map.113.refs_3_.refs_1_), channel_id=1, source_target_pairs={{0,8},{4,12},{8,0},{12,4},{1,9},{5,13},{9,1},{13,5},{2,10},{6,14},... | collective-permute-start | bytes 1572872 | tf_op jit(solution)/shard_map/ppermute | solution.py:368
  18.5 0.0 copy-done.2
  18.5 1.9 %collective-permute-start.4 = (bf16[512,256]{1,0:T(8,128)(2,1)S(1)}, bf16[512,256]{1,0:T(8,128)(2,1)S(1)}, u32[]{:S(2)}, u32[]{:S(2)}) collective-permute-start(bf16[512,256]{1,0:T(8,128)(2,1)S(1)} %bitcast.34), channel_id=1, source_target_pairs={{0,2},{1,3},{2,0},{3,1},{4,6},{5,7},{6,4},{7,5},{8,10},{9,11},{10,... | collective-permute-start | bytes 786440 | tf_op jit(solution)/shard_map/ppermute | solution.py:369
  21.1 0.0 copy-done.3
  21.2 0.0 collective-permute-done.3.refs_0_
  21.2 5.5 %collective-permute-start.5 = (bf16[512,256]{1,0:T(8,128)(2,1)S(1)}, bf16[512,256]{1,0:T(8,128)(2,1)}, u32[]{:S(2)}, u32[]{:S(2)}) collective-permute-start(bf16[512,256]{1,0:T(8,128)(2,1)S(1)} %bitcast.35), channel_id=1, source_target_pairs={{0,1},{1,0},{2,3},{3,2},{4,5},{5,4},{6,7},{7,6},{8,9},{9,8},{10,11... | collective-permute-start | bytes 786440 | tf_op jit(solution)/shard_map/ppermute | solution.py:369
  26.7 0.1 fusion.1.count_ref
  27.5 0.1 copy.16
  27.6 0.1 squeeze.26
  27.6 0.1 copy.17
  27.7 0.1 squeeze.27
  27.8 0.1 pad_maximum_fusion.refs_4_
  27.9 0.0 copy-done
  27.9 4.7 %collective-permute-done.4.refs_1_ = bf16[512,256]{1,0:T(8,128)(2,1)S(1)} collective-permute-done((bf16[512,256]{1,0:T(8,128)(2,1)S(1)}, bf16[512,256]{1,0:T(8,128)(2,1)S(1)}, u32[]{:S(2)}, u32[]{:S(2)}) %collective-permute-start.4) | collective-permute-done | bytes 262176 | tf_op jit(solution)/shard_map/ppermute | solution.py:369
  32.6 2.8 %collective-permute-done.5.refs_2_ = bf16[512,256]{1,0:T(8,128)(2,1)} collective-permute-done((bf16[512,256]{1,0:T(8,128)(2,1)S(1)}, bf16[512,256]{1,0:T(8,128)(2,1)}, u32[]{:S(2)}, u32[]{:S(2)}) %collective-permute-start.5) | collective-permute-done | bytes 262176 | tf_op jit(solution)/shard_map/ppermute | solution.py:369
  35.4 0.0 collective-permute-done.refs_4_.refs_2_
  35.4 3.9 %collective-permute-done.1.refs_5_.refs_3_ = bf16[1024,256]{1,0:T(8,128)(2,1)S(1)} collective-permute-done((bf16[1024,256]{1,0:T(8,128)(2,1)}, bf16[1024,256]{1,0:T(8,128)(2,1)S(1)}, u32[]{:S(2)}, u32[]{:S(2)}) %collective-permute-start.1) | collective-permute-done | bytes 524320 | tf_op jit(solution)/shard_map/ppermute | solution.py:368
  39.3 0.0 collective-permute-done.2.refs_6_.refs_4_
  39.3 0.0 copy-done.1
  39.4 11.2 %shard_map.114 = (bf16[144,512]{1,0:T(8,128)(2,1)S(1)}, bf16[144,512]{1,0:T(8,128)(2,1)S(1)}, bf16[144,512]{1,0:T(8,128)(2,1)S(1)}) custom-call(s32[4]{0:T(128)S(1)} %fusion.1.count_ref, bf16[512,256]{1,0:T(8,128)(2,1)S(1)} %collective-permute-done.3.refs_0_, bf16[512,256]{1,0:T(8,128)(2,1)S(1)} %collective-permute-done.4.refs_1_, ...), custom_call_target="tpu_custom_call" | custom-call | flops 3221225472 | bytes 2883584 | tf_op jit(solution)/shard_map/pallas_call | solution.py:204
  50.6 1.9 %collective-permute-start.6 = (bf16[144,512]{1,0:T(8,128)(2,1)S(1)}, bf16[144,512]{1,0:T(8,128)(2,1)S(1)}, u32[]{:S(2)}, u32[]{:S(2)}) collective-permute-start(bf16[144,512]{1,0:T(8,128)(2,1)S(1)} %get-tuple-element.5.refs_6_), channel_id=1, source_target_pairs={{0,3},{1,2},{2,1},{3,0},{4,7},{5,6},{6,5},{7,4},{8,11},{9,10},{10,... | collective-permute-start | bytes 442376 | tf_op jit(solution)/shard_map/ppermute | solution.py:391
  52.5 3.0 %collective-permute-start.7 = (bf16[144,512]{1,0:T(8,128)(2,1)S(1)}, bf16[144,512]{1,0:T(8,128)(2,1)S(1)}, u32[]{:S(2)}, u32[]{:S(2)}) collective-permute-start(bf16[144,512]{1,0:T(8,128)(2,1)S(1)} %get-tuple-element.6), channel_id=1, source_target_pairs={{0,2},{1,3},{2,0},{3,1},{4,6},{5,7},{6,4},{7,5},{8,10},{9,11},{10,... | collective-permute-start | bytes 442376 | tf_op jit(solution)/shard_map/ppermute | solution.py:391
  55.5 5.2 %collective-permute-start.8 = (bf16[144,512]{1,0:T(8,128)(2,1)S(1)}, bf16[144,512]{1,0:T(8,128)(2,1)S(1)}, u32[]{:S(2)}, u32[]{:S(2)}) collective-permute-start(bf16[144,512]{1,0:T(8,128)(2,1)S(1)} %get-tuple-element.7), channel_id=1, source_target_pairs={{0,1},{1,0},{2,3},{3,2},{4,5},{5,4},{6,7},{7,6},{8,9},{9,8},{10,11... | collective-permute-start | bytes 442376 | tf_op jit(solution)/shard_map/ppermute | solution.py:391
  60.7 0.1 pad_maximum_fusion.1.scale_ref
  60.8 4.5 %shard_map.115.refs_0_ = bf16[144,512]{1,0:T(8,128)(2,1)S(1)} custom-call(s32[4]{0:T(128)S(1)} %fusion.1.count_ref, bf16[512,256]{1,0:T(8,128)(2,1)S(1)} %bitcast.36, bf16[1024,256]{1,0:T(8,128)(2,1)S(1)} %copy-done.1, bf16[1024,256]{1,0:T(8,128)(2,1)S(1)} %collective-permute-done.refs_4_.refs_2_, ...), custom_call_target="tpu_custom_call" | custom-call | flops 1073741824 | bytes 2359296 | tf_op jit(solution)/shard_map/pallas_call | solution.py:204
  65.3 0.0 collective-permute-done.6.refs_1_
  65.3 0.9 collective-permute-done.7.refs_2_
  66.2 0.1 collective-permute-done.8.refs_3_
  66.3 0.8 shard_map.116
  67.1 30.0 %all_to_all.5 = bf16[16,32,128]{2,1,0:T(8,128)(2,1)S(1)} all-to-all(bf16[16,32,128]{2,1,0:T(8,128)(2,1)S(1)} %shard_map.116), channel_id=1, replica_groups=mesh['cfg'=2,'zh'=4,'x'=4,'y'=4,'zl'=4] {'zh','x'}, dimensions={0} | all-to-all | bytes 262144 | tf_op jit(solution)/shard_map/all_to_all | solution.py:394
  97.0 3.4 %psum.7 = f32[32,128]{1,0:T(8,128)S(1)} all-reduce(f32[32,128]{1,0:T(8,128)S(1)} %convert_reduce_fusion), channel_id=1, replica_groups=mesh['cfg'=2,'zh'=4,'x'=4,'y'=4,'zl'=4] {'cfg'}, use_global_device_ids=true, to_apply=%region_1.2 | all-reduce | flops 4096 | bytes 32768 | tf_op jit(solution)/shard_map/psum | solution.py:395
  100.4 0.1 subtract_convert_fusion.own_ref
  100.5 2.5 %collective-permute-start.10 = (bf16[32,128]{1,0:T(8,128)(2,1)S(1)}, bf16[32,128]{1,0:T(8,128)(2,1)S(1)}, u32[]{:S(2)}, u32[]{:S(2)}) collective-permute-start(bf16[32,128]{1,0:T(8,128)(2,1)S(1)} %subtract_convert_fusion.own_ref), channel_id=1, source_target_pairs={{0,2},{1,3},{2,4},{3,5},{4,6},{5,7},{6,8},{7,9},{8,10},{9,11},{10,... | collective-permute-start | bytes 24584 | tf_op jit(solution)/shard_map/ppermute | solution.py:399
  103.0 4.0 %collective-permute-start.9 = (bf16[32,128]{1,0:T(8,128)(2,1)S(1)}, bf16[32,128]{1,0:T(8,128)(2,1)S(1)}, u32[]{:S(2)}, u32[]{:S(2)}) collective-permute-start(bf16[32,128]{1,0:T(8,128)(2,1)S(1)} %subtract_convert_fusion.own_ref), channel_id=1, source_target_pairs={{0,1},{1,2},{2,3},{3,4},{4,5},{5,6},{6,7},{7,8},{8,9},{9,10},{10,1... | collective-permute-start | bytes 24584 | tf_op jit(solution)/shard_map/ppermute | solution.py:398
  107.0 0.1 dynamic-slice
  107.1 0.1 reshape.37
  107.2 0.7 copy.19
  107.9 0.0 collective-permute-done.10.older_ref
  107.9 3.3 %collective-permute-done.9.last_ref = bf16[32,128]{1,0:T(8,128)(2,1)S(1)} collective-permute-done((bf16[32,128]{1,0:T(8,128)(2,1)S(1)}, bf16[32,128]{1,0:T(8,128)(2,1)S(1)}, u32[]{:S(2)}, u32[]{:S(2)}) %collective-permute-start.9) | collective-permute-done | bytes 8224 | tf_op jit(solution)/shard_map/ppermute | solution.py:398
  111.2 2.2 %shard_map.117 = bf16[2,32,384]{2,1,0:T(8,128)(2,1)} custom-call(s32[1]{0:T(128)} %bitcast.18.half_ref, bf16[32,128]{1,0:T(8,128)(2,1)S(1)} %subtract_convert_fusion.own_ref, bf16[32,128]{1,0:T(8,128)(2,1)S(1)} %collective-permute-done.9.last_ref, bf16[32,128]{1,0:T(8,128)(2,1)S(1)} %collective-permute-done.10.older_ref, bf16[27,16,384]{2,1,0:T(8,128)(2,1)} %bitcast.37, ...), custom_call_target="tpu_custom_call" | custom-call | tf_op jit(solution)/shard_map/pallas_call | solution.py:343
  (5 shorter events, 0.1 us)
Async XLA Ops:
  0.6 27.2 %copy-start = (bf16[4096,64]{0,1:T(8,128)(2,1)S(1)}, bf16[4096,64]{0,1:T(8,128)(2,1)}, u32[]{:S(2)}) copy-start(bf16[4096,64]{0,1:T(8,128)(2,1)} %param.16) | copy-start | bytes 1572868
  0.6 20.5 %collective-permute-start.3 = (bf16[512,256]{1,0:T(8,128)(2,1)}, bf16[512,256]{1,0:T(8,128)(2,1)S(1)}, u32[]{:S(2)}, u32[]{:S(2)}) collective-permute-start(bf16[512,256]{1,0:T(8,128)(2,1)} %bitcast.33), channel_id=1, source_target_pairs={{0,3},{1,2},{2,1},{3,0},{4,7},{5,6},{6,5},{7,4},{8,11},{9,10},{10,... | collective-permute-start | bytes 786440 | tf_op jit(solution)/shard_map/ppermute | solution.py:369
  7.3 11.2 %copy-start.2 = (bf16[1,512,256]{2,1,0:T(8,128)(2,1)S(1)}, bf16[1,512,256]{2,1,0:T(8,128)(2,1)}, u32[]{:S(2)}) copy-start(bf16[1,512,256]{2,1,0:T(8,128)(2,1)} %param.10) | copy-start | bytes 786436
  7.3 13.8 %copy-start.3 = (f32[1,2,64,16]{2,3,1,0:T(8,128)S(1)}, f32[1,2,64,16]{2,3,1,0:T(8,128)}, u32[]{:S(2)}) copy-start(f32[1,2,64,16]{2,3,1,0:T(8,128)} %param.15) | copy-start | bytes 24580
  9.3 30.0 %copy-start.1 = (bf16[1024,256]{1,0:T(8,128)(2,1)S(1)}, bf16[1024,256]{1,0:T(8,128)(2,1)}, u32[]{:S(2)}) copy-start(bf16[1024,256]{1,0:T(8,128)(2,1)} %shard_map.113.refs_3_.refs_1_) | copy-start | bytes 1572868
  9.4 26.0 %collective-permute-start = (bf16[1024,256]{1,0:T(8,128)(2,1)}, bf16[1024,256]{1,0:T(8,128)(2,1)S(1)}, u32[]{:S(2)}, u32[]{:S(2)}) collective-permute-start(bf16[1024,256]{1,0:T(8,128)(2,1)} %shard_map.113.refs_3_.refs_1_), channel_id=1, source_target_pairs={{0,4},{4,8},{8,12},{12,0},{1,5},{5,9},{9,13},{13,1},{2,6},{6,10},{... | collective-permute-start | bytes 1572872 | tf_op jit(solution)/shard_map/ppermute | solution.py:368
  12.4 27.0 %collective-permute-start.1 = (bf16[1024,256]{1,0:T(8,128)(2,1)}, bf16[1024,256]{1,0:T(8,128)(2,1)S(1)}, u32[]{:S(2)}, u32[]{:S(2)}) collective-permute-start(bf16[1024,256]{1,0:T(8,128)(2,1)} %shard_map.113.refs_3_.refs_1_), channel_id=1, source_target_pairs={{0,12},{4,0},{8,4},{12,8},{1,13},{5,1},{9,5},{13,9},{2,14},{6,2},{... | collective-permute-start | bytes 1572872 | tf_op jit(solution)/shard_map/ppermute | solution.py:368
  15.3 24.0 %collective-permute-start.2 = (bf16[1024,256]{1,0:T(8,128)(2,1)}, bf16[1024,256]{1,0:T(8,128)(2,1)S(1)}, u32[]{:S(2)}, u32[]{:S(2)}) collective-permute-start(bf16[1024,256]{1,0:T(8,128)(2,1)} %shard_map.113.refs_3_.refs_1_), channel_id=1, source_target_pairs={{0,8},{4,12},{8,0},{12,4},{1,9},{5,13},{9,1},{13,5},{2,10},{6,14},... | collective-permute-start | bytes 1572872 | tf_op jit(solution)/shard_map/ppermute | solution.py:368
  18.5 14.1 %collective-permute-start.4 = (bf16[512,256]{1,0:T(8,128)(2,1)S(1)}, bf16[512,256]{1,0:T(8,128)(2,1)S(1)}, u32[]{:S(2)}, u32[]{:S(2)}) collective-permute-start(bf16[512,256]{1,0:T(8,128)(2,1)S(1)} %bitcast.34), channel_id=1, source_target_pairs={{0,2},{1,3},{2,0},{3,1},{4,6},{5,7},{6,4},{7,5},{8,10},{9,11},{10,... | collective-permute-start | bytes 786440 | tf_op jit(solution)/shard_map/ppermute | solution.py:369
  21.2 14.2 %collective-permute-start.5 = (bf16[512,256]{1,0:T(8,128)(2,1)S(1)}, bf16[512,256]{1,0:T(8,128)(2,1)}, u32[]{:S(2)}, u32[]{:S(2)}) collective-permute-start(bf16[512,256]{1,0:T(8,128)(2,1)S(1)} %bitcast.35), channel_id=1, source_target_pairs={{0,1},{1,0},{2,3},{3,2},{4,5},{5,4},{6,7},{7,6},{8,9},{9,8},{10,11... | collective-permute-start | bytes 786440 | tf_op jit(solution)/shard_map/ppermute | solution.py:369
  50.6 14.7 %collective-permute-start.6 = (bf16[144,512]{1,0:T(8,128)(2,1)S(1)}, bf16[144,512]{1,0:T(8,128)(2,1)S(1)}, u32[]{:S(2)}, u32[]{:S(2)}) collective-permute-start(bf16[144,512]{1,0:T(8,128)(2,1)S(1)} %get-tuple-element.5.refs_6_), channel_id=1, source_target_pairs={{0,3},{1,2},{2,1},{3,0},{4,7},{5,6},{6,5},{7,4},{8,11},{9,10},{10,... | collective-permute-start | bytes 442376 | tf_op jit(solution)/shard_map/ppermute | solution.py:391
  52.5 13.7 %collective-permute-start.7 = (bf16[144,512]{1,0:T(8,128)(2,1)S(1)}, bf16[144,512]{1,0:T(8,128)(2,1)S(1)}, u32[]{:S(2)}, u32[]{:S(2)}) collective-permute-start(bf16[144,512]{1,0:T(8,128)(2,1)S(1)} %get-tuple-element.6), channel_id=1, source_target_pairs={{0,2},{1,3},{2,0},{3,1},{4,6},{5,7},{6,4},{7,5},{8,10},{9,11},{10,... | collective-permute-start | bytes 442376 | tf_op jit(solution)/shard_map/ppermute | solution.py:391
  55.5 10.7 %collective-permute-start.8 = (bf16[144,512]{1,0:T(8,128)(2,1)S(1)}, bf16[144,512]{1,0:T(8,128)(2,1)S(1)}, u32[]{:S(2)}, u32[]{:S(2)}) collective-permute-start(bf16[144,512]{1,0:T(8,128)(2,1)S(1)} %get-tuple-element.7), channel_id=1, source_target_pairs={{0,1},{1,0},{2,3},{3,2},{4,5},{5,4},{6,7},{7,6},{8,9},{9,8},{10,11... | collective-permute-start | bytes 442376 | tf_op jit(solution)/shard_map/ppermute | solution.py:391
  100.5 7.4 %collective-permute-start.10 = (bf16[32,128]{1,0:T(8,128)(2,1)S(1)}, bf16[32,128]{1,0:T(8,128)(2,1)S(1)}, u32[]{:S(2)}, u32[]{:S(2)}) collective-permute-start(bf16[32,128]{1,0:T(8,128)(2,1)S(1)} %subtract_convert_fusion.own_ref), channel_id=1, source_target_pairs={{0,2},{1,3},{2,4},{3,5},{4,6},{5,7},{6,8},{7,9},{8,10},{9,11},{10,... | collective-permute-start | bytes 24584 | tf_op jit(solution)/shard_map/ppermute | solution.py:399
  103.0 8.2 %collective-permute-start.9 = (bf16[32,128]{1,0:T(8,128)(2,1)S(1)}, bf16[32,128]{1,0:T(8,128)(2,1)S(1)}, u32[]{:S(2)}, u32[]{:S(2)}) collective-permute-start(bf16[32,128]{1,0:T(8,128)(2,1)S(1)} %subtract_convert_fusion.own_ref), channel_id=1, source_target_pairs={{0,1},{1,2},{2,3},{3,4},{4,5},{5,6},{6,7},{7,8},{8,9},{9,10},{10,1... | collective-permute-start | bytes 24584 | tf_op jit(solution)/shard_map/ppermute | solution.py:398

commit v12 on v8

--- a/solution.py
+++ b/solution.py
@@ -204,7 +204,7 @@
     return pl.pallas_call(
         functools.partial(attention_kernel, nq=nq, nk=nk, nx=len(extras)),
         out_shape=(jax.ShapeDtypeStruct((CHUNK, TOK), bf16),) * nq,
-        in_specs=[SMEM] + [HBM] * (nq + nk + 1) + [ANY] * len(extras),
+        in_specs=[SMEM] + [ANY] * (nq + nk + 1 + len(extras)),
         out_specs=(VMEM,) * nq,
         scratch_shapes=[
             pltpu.VMEM((nq, TOK, 2 * DH), bf16),
@@ -221,7 +221,7 @@
         cost_estimate=pl.CostEstimate(
             flops=work * DH * 4, transcendentals=work, bytes_accessed=(nq + 2 * nk) * TOK * 4 * DH
         ),
-    )(counts, *(in_hbm(x) for x in (*queries, *blocks, weight)), *extras)
+    )(counts, *queries, *blocks, weight, *extras)
 
 
 def combine_kernel(scale_ref, place_ref, *refs):
@@ -248,7 +248,8 @@
     above = jnp.concatenate([blank, values[:-1]], 0)
     below = jnp.concatenate([values[1:], blank], 0)
     window = jnp.where(lane < 32, above, jnp.where(lane < 96, values, below))
-    out_ref[...] = window.astype(jnp.bfloat16)
+    for row in range(ROWS):
+        out_ref[row] = window[row].astype(jnp.bfloat16)
     band = place_ref[0]
     edge = pltpu.roll(latent_ref[...], 64, 1) * scale_ref[1]
     lane = lax.broadcasted_iota(jnp.int32, (TCOLS, 128), 1)
@@ -268,6 +269,41 @@
         out_specs=VMEM,
         compiler_params=pltpu.CompilerParams(vmem_limit_bytes=16 * 2**20),
     )(scale, place, *chunks, latent)
+
+
+def laid_kernel(taps_hbm, bias_hbm, gain_hbm, _, even_ref, odd_ref, bias_ref, gain_ref, taps_ref, sems):
+    copies = [
+        pltpu.make_async_copy(taps_hbm, taps_ref, sems.at[0]),
+        pltpu.make_async_copy(bias_hbm, bias_ref.at[0], sems.at[1]),
+        pltpu.make_async_copy(gain_hbm, gain_ref.at[0], sems.at[2]),
+    ]
+    for copy in copies:
+        copy.start()
+    even_ref[...] = jnp.zeros(even_ref.shape, jnp.bfloat16)
+    odd_ref[...] = jnp.zeros(odd_ref.shape, jnp.bfloat16)
+    for copy in copies:
+        copy.wait()
+    for a in range(3):
+        for u in range(3):
+            for v in range(3):
+                tap = taps_ref[a * 9 + u * 3 + v]
+                for ref, place in ((even_ref, v + 1), (odd_ref, v)):
+                    at = a * 256 + place // 2 * 128 + u * 32 + place % 2 * 16
+                    ref[at : at + 16] = tap
+
+
+def laid(taps, bias, gain, after):
+    chans = taps.shape[-1]
+    matrix = jax.ShapeDtypeStruct((768, chans), jnp.bfloat16)
+    row = jax.ShapeDtypeStruct((1, chans), jnp.float32)
+    return pl.pallas_call(
+        laid_kernel,
+        out_shape=(matrix, matrix, row, row),
+        in_specs=[HBM] * 3 + [ANY],
+        out_specs=(VMEM,) * 4,
+        scratch_shapes=[pltpu.VMEM(taps.shape, taps.dtype), pltpu.SemaphoreType.DMA((3,))],
+        compiler_params=pltpu.CompilerParams(vmem_limit_bytes=16 * 2**20),
+    )(in_hbm(taps), in_hbm(bias), in_hbm(gain), after)
 
 
 def decode_kernel(half_ref, own_ref, last_ref, older_ref, even_ref, odd_ref, bias_ref, gain_ref, out_ref):
@@ -315,17 +351,6 @@
     )(half, own, last, older, even, odd, bias, gain)
 
 
-def conv_matrices(conv_weight):
-    taps, _, _, chans, outs = conv_weight.shape
-    padded = jnp.pad(conv_weight, ((0, 0), (0, 1), (0, 0), (0, 0), (0, 0)))
-    blank = jnp.zeros((taps, 4, 1, chans, outs), conv_weight.dtype)
-    both = []
-    for parts in ([blank, padded], [padded, blank]):
-        spread = jnp.concatenate(parts, 2).reshape(taps, 4, 2, 2, chans, outs)
-        both.append(spread.transpose(0, 2, 1, 3, 4, 5).reshape(taps * 16 * chans, outs))
-    return both
-
-
 def local(
     query, keys, values, lengths, timestep, latent, head_weight, conv_weight, conv_bias, gain
 ):
@@ -342,8 +367,6 @@
     rows = latent[0].reshape(2, TCOLS, 32)
     blank = jnp.zeros((TCOLS, 32), jnp.float32)
     grid = jnp.concatenate([blank, rows[0], rows[1], blank], 1)
-    even, odd = conv_matrices(conv_weight)
-    bias_row, gain_row = conv_bias.reshape(1, -1), gain.reshape(1, -1)
     part = lax.dynamic_slice_in_dim(head_weight, (zh * SIDE + x) * 2 * DH, 2 * DH, 0)
     weight = part.T.reshape(PATCH, 2, DH).transpose(1, 0, 2)
     sigma = noise_level(timestep[0], STEPS)
@@ -351,6 +374,7 @@
         [
             jnp.where(cfg == 0, GUIDE, 1.0 - GUIDE).astype(jnp.float32),
             jnp.where(cfg == 0, -1.0 / sigma, 0.0),
+            sigma,
         ]
     )
     place = (zh * SIDE + x).astype(jnp.int32).reshape(1)
@@ -374,10 +398,7 @@
         current,
         last,
         older,
-        even,
-        odd,
-        bias_row,
-        gain_row,
+        *laid(conv_weight.reshape(27, *conv_weight.shape[3:]), conv_bias, gain, current),
     )
     return (velocity, decoded[None])
 

time: 117 us -> 114 us (0.974)
  blocking collectives: 3.36 us -> 33.9 us
  waiting for transfers between devices: 28.4 us -> 14.6 us
  starting transfers between devices: 53.4 us -> 39.8 us
  local copies, waits for them, and re-layouts: 5.05 us -> 1.22 us
  Pallas kernels: 22.7 us -> 20.7 us
    all_to_all x0 -> x1, blocking collectives: none -> 30.5 us  [local(): shares = lax.all_to_all(shares, ('zh', 'x'), 0, 0, tiled=True)]
    all_to_all x1 -> x0, waiting for transfers between devices: 15.1 us -> none  [local(): shares = lax.all_to_all(shares, ('zh', 'x'), 0, 0, tiled=True)]
    all_to_all x1 -> x0, starting transfers between devices: 15 us -> none  [local(): shares = lax.all_to_all(shares, ('zh', 'x'), 0, 0, tiled=True)]
    unnamed x25 -> x9, local copies, waits for them, and re-layouts: 3.6 us -> 0.7 us
    pallas_call x2, Pallas kernels: 18.1 us -> 15.7 us  [attend(): pl.pallas_call(functools.partial(attention_kernel, nq=nq, nk=nk, nx=len(e...]
  transfers between devices with their start and end apart: 12 -> 11, of which waited for: 5 -> 6; matrix products, arithmetic and copies ran while one was open for 2% -> 1% of each run, Pallas kernels for 7% -> 7%
where the time goes in v12:
time: 114 us; the launch traced here: 113 us
  starting transfers between devices  39.8 us (35%)
  blocking collectives  33.9 us (30%)
  Pallas kernels  20.7 us (18%)
  waiting for transfers between devices  14.6 us (13%)
  between operations  2.34 us (2%)
  local copies, waits for them, and re-layouts  1.22 us (1%)
    all_to_all x1, blocking collectives, local(): shares = lax.all_to_all(shares, ('zh', 'x'), 0, 0, tiled=True)  30.5 us
    pallas_call x2, Pallas kernels, attend(): pl.pallas_call(functools.partial(attention_kernel, nq=nq, nk=nk, nx=len(e...  15.7 us
    ppermute x3, starting transfers between devices, local(): lax.ppermute(query[0], 'zl', crossed(m))  14.1 us
    ppermute x3, starting transfers between devices, local(): lax.ppermute(chunk, 'zl', crossed(m))  10.1 us
    ppermute x3, starting transfers between devices, local(): blocks = [own] + [lax.ppermute(own, 'y', ring(d)) for d in (1, 3, 2)]  9.12 us
    ppermute x3, waiting for transfers between devices, local(): lax.ppermute(query[0], 'zl', crossed(m))  7.49 us
    ppermute x1, starting transfers between devices, local(): last = lax.ppermute(current, seq, moved(1))  4.1 us
    ppermute x3, waiting for transfers between devices, local(): blocks = [own] + [lax.ppermute(own, 'y', ring(d)) for d in (1, 3, 2)]  3.95 us
  transfers between devices with their start and end apart: 11, of which 6 were waited for; matrix products, arithmetic and copies ran while one was open for 1% of the time, Pallas kernels for 7%

profile of v12, /device:TPU:24, one launch (start us, length us, event | category | flops | bytes accessed | tf_op | source)
XLA Modules:
  0.0 112.9 jit_solution(736709268054713616)
XLA Ops:
  0.6 0.0 copy-start
  0.6 6.7 %collective-permute-start.3 = (bf16[512,256]{1,0:T(8,128)(2,1)}, bf16[512,256]{1,0:T(8,128)(2,1)S(1)}, u32[]{:S(2)}, u32[]{:S(2)}) collective-permute-start(bf16[512,256]{1,0:T(8,128)(2,1)} %bitcast.33), channel_id=1, source_target_pairs={{0,3},{1,2},{2,1},{3,0},{4,7},{5,6},{6,5},{7,4},{8,11},{9,10},{10,... | collective-permute-start | bytes 786440 | tf_op jit(solution)/shard_map/ppermute | solution.py:363
  7.3 0.0 copy-start.2
  7.3 0.0 copy-start.3
  7.3 2.0 %shard_map.113.refs_3_.refs_1_ = bf16[1024,256]{1,0:T(8,128)(2,1)} custom-call(bf16[512,256]{1,0:T(8,128)(2,1)} %bitcast.38, bf16[512,256]{1,0:T(8,128)(2,1)} %bitcast.39), custom_call_target="tpu_custom_call" | custom-call | tf_op jit(solution)/shard_map/pallas_call | solution.py:69
  9.4 0.0 copy-start.1
  9.4 3.0 %collective-permute-start = (bf16[1024,256]{1,0:T(8,128)(2,1)}, bf16[1024,256]{1,0:T(8,128)(2,1)S(1)}, u32[]{:S(2)}, u32[]{:S(2)}) collective-permute-start(bf16[1024,256]{1,0:T(8,128)(2,1)} %shard_map.113.refs_3_.refs_1_), channel_id=1, source_target_pairs={{0,4},{4,8},{8,12},{12,0},{1,5},{5,9},{9,13},{13,1},{2,6},{6,10},{... | collective-permute-start | bytes 1572872 | tf_op jit(solution)/shard_map/ppermute | solution.py:362
  12.4 3.0 %collective-permute-start.1 = (bf16[1024,256]{1,0:T(8,128)(2,1)}, bf16[1024,256]{1,0:T(8,128)(2,1)S(1)}, u32[]{:S(2)}, u32[]{:S(2)}) collective-permute-start(bf16[1024,256]{1,0:T(8,128)(2,1)} %shard_map.113.refs_3_.refs_1_), channel_id=1, source_target_pairs={{0,12},{4,0},{8,4},{12,8},{1,13},{5,1},{9,5},{13,9},{2,14},{6,2},{... | collective-permute-start | bytes 1572872 | tf_op jit(solution)/shard_map/ppermute | solution.py:362
  15.4 3.1 %collective-permute-start.2 = (bf16[1024,256]{1,0:T(8,128)(2,1)}, bf16[1024,256]{1,0:T(8,128)(2,1)S(1)}, u32[]{:S(2)}, u32[]{:S(2)}) collective-permute-start(bf16[1024,256]{1,0:T(8,128)(2,1)} %shard_map.113.refs_3_.refs_1_), channel_id=1, source_target_pairs={{0,8},{4,12},{8,0},{12,4},{1,9},{5,13},{9,1},{13,5},{2,10},{6,14},... | collective-permute-start | bytes 1572872 | tf_op jit(solution)/shard_map/ppermute | solution.py:362
  18.5 0.0 copy-done.2
  18.5 1.9 %collective-permute-start.4 = (bf16[512,256]{1,0:T(8,128)(2,1)S(1)}, bf16[512,256]{1,0:T(8,128)(2,1)S(1)}, u32[]{:S(2)}, u32[]{:S(2)}) collective-permute-start(bf16[512,256]{1,0:T(8,128)(2,1)S(1)} %bitcast.34), channel_id=1, source_target_pairs={{0,2},{1,3},{2,0},{3,1},{4,6},{5,7},{6,4},{7,5},{8,10},{9,11},{10,... | collective-permute-start | bytes 786440 | tf_op jit(solution)/shard_map/ppermute | solution.py:363
  21.2 0.0 copy-done.3
  21.2 0.0 collective-permute-done.3.refs_0_
  21.2 5.5 %collective-permute-start.5 = (bf16[512,256]{1,0:T(8,128)(2,1)S(1)}, bf16[512,256]{1,0:T(8,128)(2,1)}, u32[]{:S(2)}, u32[]{:S(2)}) collective-permute-start(bf16[512,256]{1,0:T(8,128)(2,1)S(1)} %bitcast.35), channel_id=1, source_target_pairs={{0,1},{1,0},{2,3},{3,2},{4,5},{5,4},{6,7},{7,6},{8,9},{9,8},{10,11... | collective-permute-start | bytes 786440 | tf_op jit(solution)/shard_map/ppermute | solution.py:363
  26.7 0.1 fusion.1.count_ref
  27.5 0.1 copy.16
  27.6 0.1 squeeze.26
  27.7 0.1 copy.17
  27.7 0.1 squeeze.27
  27.8 0.1 pad_maximum_fusion.refs_4_
  27.9 0.0 copy-done
  27.9 4.7 %collective-permute-done.4.refs_1_ = bf16[512,256]{1,0:T(8,128)(2,1)S(1)} collective-permute-done((bf16[512,256]{1,0:T(8,128)(2,1)S(1)}, bf16[512,256]{1,0:T(8,128)(2,1)S(1)}, u32[]{:S(2)}, u32[]{:S(2)}) %collective-permute-start.4) | collective-permute-done | bytes 262176 | tf_op jit(solution)/shard_map/ppermute | solution.py:363
  32.6 2.8 %collective-permute-done.5.refs_2_ = bf16[512,256]{1,0:T(8,128)(2,1)} collective-permute-done((bf16[512,256]{1,0:T(8,128)(2,1)S(1)}, bf16[512,256]{1,0:T(8,128)(2,1)}, u32[]{:S(2)}, u32[]{:S(2)}) %collective-permute-start.5) | collective-permute-done | bytes 262176 | tf_op jit(solution)/shard_map/ppermute | solution.py:363
  35.4 0.0 collective-permute-done.refs_4_.refs_2_
  35.4 3.9 %collective-permute-done.1.refs_5_.refs_3_ = bf16[1024,256]{1,0:T(8,128)(2,1)S(1)} collective-permute-done((bf16[1024,256]{1,0:T(8,128)(2,1)}, bf16[1024,256]{1,0:T(8,128)(2,1)S(1)}, u32[]{:S(2)}, u32[]{:S(2)}) %collective-permute-start.1) | collective-permute-done | bytes 524320 | tf_op jit(solution)/shard_map/ppermute | solution.py:362
  39.4 0.0 collective-permute-done.2.refs_6_.refs_4_
  39.4 11.2 %shard_map.114 = (bf16[144,512]{1,0:T(8,128)(2,1)S(1)}, bf16[144,512]{1,0:T(8,128)(2,1)S(1)}, bf16[144,512]{1,0:T(8,128)(2,1)S(1)}) custom-call(s32[4]{0:T(128)S(1)} %fusion.1.count_ref, bf16[512,256]{1,0:T(8,128)(2,1)S(1)} %collective-permute-done.3.refs_0_, bf16[512,256]{1,0:T(8,128)(2,1)S(1)} %collective-permute-done.4.refs_1_, ...), custom_call_target="tpu_custom_call" | custom-call | flops 3221225472 | bytes 2883584 | tf_op jit(solution)/shard_map/pallas_call | solution.py:204
  50.6 2.9 %collective-permute-start.6 = (bf16[144,512]{1,0:T(8,128)(2,1)S(1)}, bf16[144,512]{1,0:T(8,128)(2,1)S(1)}, u32[]{:S(2)}, u32[]{:S(2)}) collective-permute-start(bf16[144,512]{1,0:T(8,128)(2,1)S(1)} %get-tuple-element.9.refs_6_), channel_id=1, source_target_pairs={{0,3},{1,2},{2,1},{3,0},{4,7},{5,6},{6,5},{7,4},{8,11},{9,10},{10,... | collective-permute-start | bytes 442376 | tf_op jit(solution)/shard_map/ppermute | solution.py:385
  53.5 1.9 %collective-permute-start.7 = (bf16[144,512]{1,0:T(8,128)(2,1)S(1)}, bf16[144,512]{1,0:T(8,128)(2,1)S(1)}, u32[]{:S(2)}, u32[]{:S(2)}) collective-permute-start(bf16[144,512]{1,0:T(8,128)(2,1)S(1)} %get-tuple-element.10), channel_id=1, source_target_pairs={{0,2},{1,3},{2,0},{3,1},{4,6},{5,7},{6,4},{7,5},{8,10},{9,11},{10,... | collective-permute-start | bytes 442376 | tf_op jit(solution)/shard_map/ppermute | solution.py:385
  55.5 5.3 %collective-permute-start.8 = (bf16[144,512]{1,0:T(8,128)(2,1)S(1)}, bf16[144,512]{1,0:T(8,128)(2,1)S(1)}, u32[]{:S(2)}, u32[]{:S(2)}) collective-permute-start(bf16[144,512]{1,0:T(8,128)(2,1)S(1)} %get-tuple-element.11), channel_id=1, source_target_pairs={{0,1},{1,0},{2,3},{3,2},{4,5},{5,4},{6,7},{7,6},{8,9},{9,8},{10,11... | collective-permute-start | bytes 442376 | tf_op jit(solution)/shard_map/ppermute | solution.py:385
  60.7 0.1 pad_maximum_fusion.1.scale_ref
  60.8 4.5 %shard_map.115.refs_0_ = bf16[144,512]{1,0:T(8,128)(2,1)S(1)} custom-call(s32[4]{0:T(128)S(1)} %fusion.1.count_ref, bf16[512,256]{1,0:T(8,128)(2,1)S(1)} %bitcast.36, bf16[1024,256]{1,0:T(8,128)(2,1)S(1)} %copy-done.1, bf16[1024,256]{1,0:T(8,128)(2,1)S(1)} %collective-permute-done.refs_4_.refs_2_, ...), custom_call_target="tpu_custom_call" | custom-call | flops 1073741824 | bytes 2359296 | tf_op jit(solution)/shard_map/pallas_call | solution.py:204
  65.3 0.0 collective-permute-done.6.refs_1_
  65.3 0.6 collective-permute-done.7.refs_2_
  65.9 0.4 collective-permute-done.8.refs_3_
  66.3 0.8 shard_map.116
  67.1 30.5 %all_to_all.5 = bf16[16,32,128]{2,1,0:T(8,128)(2,1)S(1)} all-to-all(bf16[16,32,128]{2,1,0:T(8,128)(2,1)S(1)} %shard_map.116), channel_id=1, replica_groups=mesh['cfg'=2,'zh'=4,'x'=4,'y'=4,'zl'=4] {'zh','x'}, dimensions={0} | all-to-all | bytes 262144 | tf_op jit(solution)/shard_map/all_to_all | solution.py:388
  97.6 3.4 %psum.7 = f32[32,128]{1,0:T(8,128)S(1)} all-reduce(f32[32,128]{1,0:T(8,128)S(1)} %convert_reduce_fusion), channel_id=1, replica_groups=mesh['cfg'=2,'zh'=4,'x'=4,'y'=4,'zl'=4] {'cfg'}, use_global_device_ids=true, to_apply=%region_1.2 | all-reduce | flops 4096 | bytes 32768 | tf_op jit(solution)/shard_map/psum | solution.py:389
  101.0 0.1 subtract_convert_fusion._.own_ref
  101.0 2.5 %collective-permute-start.10 = (bf16[32,128]{1,0:T(8,128)(2,1)S(1)}, bf16[32,128]{1,0:T(8,128)(2,1)S(1)}, u32[]{:S(2)}, u32[]{:S(2)}) collective-permute-start(bf16[32,128]{1,0:T(8,128)(2,1)S(1)} %subtract_convert_fusion._.own_ref), channel_id=1, source_target_pairs={{0,2},{1,3},{2,4},{3,5},{4,6},{5,7},{6,8},{7,9},{8,10},{9,11},{10,... | collective-permute-start | bytes 24584 | tf_op jit(solution)/shard_map/ppermute | solution.py:393
  103.5 4.1 %collective-permute-start.9 = (bf16[32,128]{1,0:T(8,128)(2,1)S(1)}, bf16[32,128]{1,0:T(8,128)(2,1)S(1)}, u32[]{:S(2)}, u32[]{:S(2)}) collective-permute-start(bf16[32,128]{1,0:T(8,128)(2,1)S(1)} %subtract_convert_fusion._.own_ref), channel_id=1, source_target_pairs={{0,1},{1,2},{2,3},{3,4},{4,5},{5,6},{6,7},{7,8},{8,9},{9,10},{10,1... | collective-permute-start | bytes 24584 | tf_op jit(solution)/shard_map/ppermute | solution.py:392
  107.6 0.1 dynamic-slice
  107.7 0.1 reshape.37
  107.8 0.7 copy.19
  108.5 1.1 shard_map.117
  109.6 0.0 collective-permute-done.10.older_ref
  109.6 2.2 %collective-permute-done.9.last_ref = bf16[32,128]{1,0:T(8,128)(2,1)S(1)} collective-permute-done((bf16[32,128]{1,0:T(8,128)(2,1)S(1)}, bf16[32,128]{1,0:T(8,128)(2,1)S(1)}, u32[]{:S(2)}, u32[]{:S(2)}) %collective-permute-start.9) | collective-permute-done | bytes 8224 | tf_op jit(solution)/shard_map/ppermute | solution.py:392
  111.8 1.2 %shard_map.118 = bf16[2,32,384]{2,1,0:T(8,128)(2,1)} custom-call(s32[1]{0:T(128)} %bitcast.18.half_ref, bf16[32,128]{1,0:T(8,128)(2,1)S(1)} %subtract_convert_fusion._.own_ref, bf16[32,128]{1,0:T(8,128)(2,1)S(1)} %collective-permute-done.9.last_ref, bf16[32,128]{1,0:T(8,128)(2,1)S(1)} %collective-permute-done.10.older_ref, ...), custom_call_target="tpu_custom_call" | custom-call | tf_op jit(solution)/shard_map/pallas_call | solution.py:345
  (6 shorter events, 0.1 us)
Async XLA Ops:
  0.6 27.3 %copy-start = (bf16[4096,64]{0,1:T(8,128)(2,1)S(1)}, bf16[4096,64]{0,1:T(8,128)(2,1)}, u32[]{:S(2)}) copy-start(bf16[4096,64]{0,1:T(8,128)(2,1)} %param.16) | copy-start | bytes 1572868
  0.6 20.5 %collective-permute-start.3 = (bf16[512,256]{1,0:T(8,128)(2,1)}, bf16[512,256]{1,0:T(8,128)(2,1)S(1)}, u32[]{:S(2)}, u32[]{:S(2)}) collective-permute-start(bf16[512,256]{1,0:T(8,128)(2,1)} %bitcast.33), channel_id=1, source_target_pairs={{0,3},{1,2},{2,1},{3,0},{4,7},{5,6},{6,5},{7,4},{8,11},{9,10},{10,... | collective-permute-start | bytes 786440 | tf_op jit(solution)/shard_map/ppermute | solution.py:363
  7.3 11.2 %copy-start.2 = (bf16[1,512,256]{2,1,0:T(8,128)(2,1)S(1)}, bf16[1,512,256]{2,1,0:T(8,128)(2,1)}, u32[]{:S(2)}) copy-start(bf16[1,512,256]{2,1,0:T(8,128)(2,1)} %param.10) | copy-start | bytes 786436
  7.3 13.8 %copy-start.3 = (f32[1,2,64,16]{2,3,1,0:T(8,128)S(1)}, f32[1,2,64,16]{2,3,1,0:T(8,128)}, u32[]{:S(2)}) copy-start(f32[1,2,64,16]{2,3,1,0:T(8,128)} %param.15) | copy-start | bytes 24580
  9.4 30.0 %copy-start.1 = (bf16[1024,256]{1,0:T(8,128)(2,1)S(1)}, bf16[1024,256]{1,0:T(8,128)(2,1)}, u32[]{:S(2)}) copy-start(bf16[1024,256]{1,0:T(8,128)(2,1)} %shard_map.113.refs_3_.refs_1_) | copy-start | bytes 1572868
  9.4 26.0 %collective-permute-start = (bf16[1024,256]{1,0:T(8,128)(2,1)}, bf16[1024,256]{1,0:T(8,128)(2,1)S(1)}, u32[]{:S(2)}, u32[]{:S(2)}) collective-permute-start(bf16[1024,256]{1,0:T(8,128)(2,1)} %shard_map.113.refs_3_.refs_1_), channel_id=1, source_target_pairs={{0,4},{4,8},{8,12},{12,0},{1,5},{5,9},{9,13},{13,1},{2,6},{6,10},{... | collective-permute-start | bytes 1572872 | tf_op jit(solution)/shard_map/ppermute | solution.py:362
  12.4 27.0 %collective-permute-start.1 = (bf16[1024,256]{1,0:T(8,128)(2,1)}, bf16[1024,256]{1,0:T(8,128)(2,1)S(1)}, u32[]{:S(2)}, u32[]{:S(2)}) collective-permute-start(bf16[1024,256]{1,0:T(8,128)(2,1)} %shard_map.113.refs_3_.refs_1_), channel_id=1, source_target_pairs={{0,12},{4,0},{8,4},{12,8},{1,13},{5,1},{9,5},{13,9},{2,14},{6,2},{... | collective-permute-start | bytes 1572872 | tf_op jit(solution)/shard_map/ppermute | solution.py:362
  15.4 24.0 %collective-permute-start.2 = (bf16[1024,256]{1,0:T(8,128)(2,1)}, bf16[1024,256]{1,0:T(8,128)(2,1)S(1)}, u32[]{:S(2)}, u32[]{:S(2)}) collective-permute-start(bf16[1024,256]{1,0:T(8,128)(2,1)} %shard_map.113.refs_3_.refs_1_), channel_id=1, source_target_pairs={{0,8},{4,12},{8,0},{12,4},{1,9},{5,13},{9,1},{13,5},{2,10},{6,14},... | collective-permute-start | bytes 1572872 | tf_op jit(solution)/shard_map/ppermute | solution.py:362
  18.5 14.1 %collective-permute-start.4 = (bf16[512,256]{1,0:T(8,128)(2,1)S(1)}, bf16[512,256]{1,0:T(8,128)(2,1)S(1)}, u32[]{:S(2)}, u32[]{:S(2)}) collective-permute-start(bf16[512,256]{1,0:T(8,128)(2,1)S(1)} %bitcast.34), channel_id=1, source_target_pairs={{0,2},{1,3},{2,0},{3,1},{4,6},{5,7},{6,4},{7,5},{8,10},{9,11},{10,... | collective-permute-start | bytes 786440 | tf_op jit(solution)/shard_map/ppermute | solution.py:363
  21.2 14.2 %collective-permute-start.5 = (bf16[512,256]{1,0:T(8,128)(2,1)S(1)}, bf16[512,256]{1,0:T(8,128)(2,1)}, u32[]{:S(2)}, u32[]{:S(2)}) collective-permute-start(bf16[512,256]{1,0:T(8,128)(2,1)S(1)} %bitcast.35), channel_id=1, source_target_pairs={{0,1},{1,0},{2,3},{3,2},{4,5},{5,4},{6,7},{7,6},{8,9},{9,8},{10,11... | collective-permute-start | bytes 786440 | tf_op jit(solution)/shard_map/ppermute | solution.py:363
  50.6 14.7 %collective-permute-start.6 = (bf16[144,512]{1,0:T(8,128)(2,1)S(1)}, bf16[144,512]{1,0:T(8,128)(2,1)S(1)}, u32[]{:S(2)}, u32[]{:S(2)}) collective-permute-start(bf16[144,512]{1,0:T(8,128)(2,1)S(1)} %get-tuple-element.9.refs_6_), channel_id=1, source_target_pairs={{0,3},{1,2},{2,1},{3,0},{4,7},{5,6},{6,5},{7,4},{8,11},{9,10},{10,... | collective-permute-start | bytes 442376 | tf_op jit(solution)/shard_map/ppermute | solution.py:385
  53.5 12.4 %collective-permute-start.7 = (bf16[144,512]{1,0:T(8,128)(2,1)S(1)}, bf16[144,512]{1,0:T(8,128)(2,1)S(1)}, u32[]{:S(2)}, u32[]{:S(2)}) collective-permute-start(bf16[144,512]{1,0:T(8,128)(2,1)S(1)} %get-tuple-element.10), channel_id=1, source_target_pairs={{0,2},{1,3},{2,0},{3,1},{4,6},{5,7},{6,4},{7,5},{8,10},{9,11},{10,... | collective-permute-start | bytes 442376 | tf_op jit(solution)/shard_map/ppermute | solution.py:385
  55.5 10.8 %collective-permute-start.8 = (bf16[144,512]{1,0:T(8,128)(2,1)S(1)}, bf16[144,512]{1,0:T(8,128)(2,1)S(1)}, u32[]{:S(2)}, u32[]{:S(2)}) collective-permute-start(bf16[144,512]{1,0:T(8,128)(2,1)S(1)} %get-tuple-element.11), channel_id=1, source_target_pairs={{0,1},{1,0},{2,3},{3,2},{4,5},{5,4},{6,7},{7,6},{8,9},{9,8},{10,11... | collective-permute-start | bytes 442376 | tf_op jit(solution)/shard_map/ppermute | solution.py:385
  101.0 8.5 %collective-permute-start.10 = (bf16[32,128]{1,0:T(8,128)(2,1)S(1)}, bf16[32,128]{1,0:T(8,128)(2,1)S(1)}, u32[]{:S(2)}, u32[]{:S(2)}) collective-permute-start(bf16[32,128]{1,0:T(8,128)(2,1)S(1)} %subtract_convert_fusion._.own_ref), channel_id=1, source_target_pairs={{0,2},{1,3},{2,4},{3,5},{4,6},{5,7},{6,8},{7,9},{8,10},{9,11},{10,... | collective-permute-start | bytes 24584 | tf_op jit(solution)/shard_map/ppermute | solution.py:393
  103.5 8.2 %collective-permute-start.9 = (bf16[32,128]{1,0:T(8,128)(2,1)S(1)}, bf16[32,128]{1,0:T(8,128)(2,1)S(1)}, u32[]{:S(2)}, u32[]{:S(2)}) collective-permute-start(bf16[32,128]{1,0:T(8,128)(2,1)S(1)} %subtract_convert_fusion._.own_ref), channel_id=1, source_target_pairs={{0,1},{1,2},{2,3},{3,4},{4,5},{5,6},{6,7},{7,8},{8,9},{9,10},{10,1... | collective-permute-start | bytes 24584 | tf_op jit(solution)/shard_map/ppermute | solution.py:392

commit v13 on v12

--- a/solution.py
+++ b/solution.py
@@ -79,7 +79,7 @@
     )(in_hbm(keys), in_hbm(values))
 
 
-def attention_kernel(count_ref, *refs, nq, nk, nx):
+def attention_kernel(count_ref, *refs, nq, nk, nx, parts, skip, last):
     refs = list(refs)
 
     def take(size):
@@ -88,9 +88,16 @@
         return taken
 
     q_refs, kv_refs = take(nq), take(nk)
-    weight_hbm = take(1 + nx)[0]
-    chunk_refs = take(nq)
-    qs, ks, vs, scores, sems, acc_ref, top_ref, denom, weight_ref = refs
+    weight_hbm = take(1)[0] if last else None
+    if parts:
+        top_in, denom_in, acc_in = take(3)
+    take(nx)
+    if last:
+        chunk_refs = take(nq)
+        qs, ks, vs, scores, sems, acc_ref, top_ref, denom, weight_ref = refs
+    else:
+        top_ref, denom, acc_out = take(3)
+        qs, ks, vs, scores, sems, acc_ref = refs
 
     sem = iter(range(64))
 
@@ -114,10 +121,17 @@
         if b == 0:
             group += [copied(q_refs[j], qs.at[j]) for j in range(nq)]
         arriving.append(group)
-    arriving[0].append(copied(weight_hbm, weight_ref))
-    top_ref[...] = jnp.full((nq, 2, TOK), NEG_FILL, jnp.float32)
-    denom[...] = jnp.zeros((nq, 2, TOK), jnp.float32)
-    acc_ref[...] = jnp.zeros((nq, 2, DH, TOK), jnp.float32)
+    if last:
+        arriving[0].append(copied(weight_hbm, weight_ref))
+    if parts:
+        arriving[0].append(copied(acc_in, acc_ref.at[pl.ds(0, parts)]))
+        top_ref[:parts] = top_in[...]
+        denom[:parts] = denom_in[...]
+        arriving = [[copy for group in arriving for copy in group]] + [[]] * (nk - 1)
+    fresh = nq - parts
+    top_ref[parts:] = jnp.full((fresh, 2, TOK), NEG_FILL, jnp.float32)
+    denom[parts:] = jnp.zeros((fresh, 2, TOK), jnp.float32)
+    acc_ref[parts:] = jnp.zeros((fresh, 2, DH, TOK), jnp.float32)
     for b in range(nk):
         for h in range(2):
             vs[b, h, DH:] = jnp.ones((16, TOK), jnp.bfloat16)
@@ -147,14 +161,22 @@
         denom[j, h : h + 1] = denom[j, h : h + 1] * factor + mixed[DH : DH + 1]
         acc_ref[j, h] = acc_ref[j, h] * factor + mixed[:DH]
 
-    total = nq * nk
+    total = nq * nk - parts * skip
+
+    def tile(t):
+        if not parts:
+            return lax.div(t, nk), lax.rem(t, nk)
+        rest = nk - skip
+        past = t - parts * rest
+        j = jnp.where(past >= 0, parts + lax.div(past, nk), lax.div(t, rest))
+        b = jnp.where(past >= 0, lax.rem(past, nk), skip + lax.rem(t, rest))
+        return j, b
 
     def step(t, _):
-        j, b = lax.div(t, nk), lax.rem(t, nk)
-        later = jnp.minimum(t + 1, total - 1)
-        next_j, next_b = lax.div(later, nk), lax.rem(later, nk)
+        j, b = tile(t)
+        next_j, next_b = tile(jnp.minimum(t + 1, total - 1))
         count = count_ref[b]
-        for needed in range(1, nk):
+        for needed in range(1, nk if not parts else 1):
 
             @pl.when(t == needed - 1)
             def _():
@@ -181,8 +203,13 @@
 
         return 0
 
-    scores[0] = scored(0, 0, 0)
+    scores[0] = scored(0, skip, 0)
     lax.fori_loop(0, total, step, 0)
+    if not last:
+        copy = pltpu.make_async_copy(acc_ref, acc_out, sems.at[0])
+        copy.start()
+        copy.wait()
+        return
     for j in range(nq):
         parts, rows = [], []
         for h in range(2):
@@ -197,31 +224,49 @@
         chunk_refs[j][...] = jnp.concatenate(parts + rows + [blank], 0).astype(jnp.bfloat16)
 
 
-def attend(counts, queries, blocks, weight, extras=()):
+def attend(counts, queries, blocks, weight=None, extras=(), state=(), skip=0):
     f32, bf16 = jnp.float32, jnp.bfloat16
-    nq, nk = len(queries), len(blocks)
-    work = nq * nk * 2 * TOK * TOK
+    nq, nk, last = len(queries), len(blocks), weight is not None
+    parts = state[0].shape[0] if state else 0
+    work = (nq * nk - parts * skip) * 2 * TOK * TOK
+    stat = jax.ShapeDtypeStruct((nq, 2, TOK), f32)
+    chunk = jax.ShapeDtypeStruct((CHUNK, TOK), bf16)
+    ended = [
+        pltpu.VMEM((nq, 2, TOK), f32),
+        pltpu.VMEM((nq, 2, TOK), f32),
+        pltpu.VMEM((2, PATCH, DH), bf16),
+    ]
     return pl.pallas_call(
-        functools.partial(attention_kernel, nq=nq, nk=nk, nx=len(extras)),
-        out_shape=(jax.ShapeDtypeStruct((CHUNK, TOK), bf16),) * nq,
-        in_specs=[SMEM] + [ANY] * (nq + nk + 1 + len(extras)),
-        out_specs=(VMEM,) * nq,
+        functools.partial(
+            attention_kernel, nq=nq, nk=nk, nx=len(extras), parts=parts, skip=skip, last=last
+        ),
+        out_shape=(chunk,) * nq if last else (stat, stat, pltpu.HBM((nq, 2, DH, TOK), f32)),
+        in_specs=[SMEM]
+        + [ANY] * (nq + nk + last)
+        + ([VMEM, VMEM, HBM] if state else [])
+        + [ANY] * len(extras),
+        out_specs=(VMEM,) * nq if last else (VMEM, VMEM, HBM),
         scratch_shapes=[
             pltpu.VMEM((nq, TOK, 2 * DH), bf16),
             pltpu.VMEM((nk, TOK, 2 * DH), bf16),
             pltpu.VMEM((nk, 2, DH + 16, TOK), bf16),
             pltpu.VMEM((2, TOK, TOK), f32),
-            pltpu.SemaphoreType.DMA((5 * nk + nq + 1,)),
+            pltpu.SemaphoreType.DMA((5 * nk + nq + 2,)),
             pltpu.VMEM((nq, 2, DH, TOK), f32),
-            pltpu.VMEM((nq, 2, TOK), f32),
-            pltpu.VMEM((nq, 2, TOK), f32),
-            pltpu.VMEM((2, PATCH, DH), bf16),
-        ],
+        ]
+        + (ended if last else []),
         compiler_params=pltpu.CompilerParams(vmem_limit_bytes=24 * 2**20),
         cost_estimate=pl.CostEstimate(
             flops=work * DH * 4, transcendentals=work, bytes_accessed=(nq + 2 * nk) * TOK * 4 * DH
         ),
-    )(counts, *queries, *blocks, weight, *extras)
+    )(
+        counts,
+        *queries,
+        *blocks,
+        *((weight,) if last else ()),
+        *(in_hbm(x) if x.ndim == 4 else x for x in state),
+        *extras,
+    )
 
 
 def combine_kernel(scale_ref, place_ref, *refs):
@@ -379,7 +424,10 @@
     )
     place = (zh * SIDE + x).astype(jnp.int32).reshape(1)
 
-    third, second, first = attend(counts, queries[3:0:-1], blocks, weight)
+    early = attend(counts, queries[3:1:-1], blocks[:2])
+    third, second, first = attend(
+        counts, queries[3:0:-1], blocks, weight, state=early, skip=2
+    )
     (mine,) = attend(counts, queries[:1], blocks, weight, extras=(third,))
     chunks = [mine] + [
         lax.ppermute(chunk, "zl", crossed(m)) for m, chunk in ((3, third), (2, second), (1, first))

time: 114 us -> 116 us (1.018)
  the two profiles are of different devices: /device:TPU:24 before, /device:TPU:16 now
where the time goes in v13:
time: 116 us; the launch traced here: 115 us
  starting transfers between devices  41.9 us (36%)
  blocking collectives  33.6 us (29%)
  Pallas kernels  23.3 us (20%)
  waiting for transfers between devices  12.8 us (11%)
  between operations  2.34 us (2%)
  local copies, waits for them, and re-layouts  1.22 us (1%)
    all_to_all x1, blocking collectives, local(): shares = lax.all_to_all(shares, ('zh', 'x'), 0, 0, tiled=True)  30.2 us
    pallas_call x3, Pallas kernels, attend(): pl.pallas_call(functools.partial(attention_kernel, nq=nq, nk=nk, nx=len(e...  18.2 us
    ppermute x3, starting transfers between devices, local(): lax.ppermute(query[0], 'zl', crossed(m))  14.9 us
    ppermute x3, starting transfers between devices, local(): blocks = [own] + [lax.ppermute(own, 'y', ring(d)) for d in (1, 3, 2)]  10.2 us
    ppermute x3, starting transfers between devices, local(): lax.ppermute(chunk, 'zl', crossed(m))  10.1 us
    ppermute x3, waiting for transfers between devices, local(): blocks = [own] + [lax.ppermute(own, 'y', ring(d)) for d in (1, 3, 2)]  8.39 us
    ppermute x1, starting transfers between devices, local(): older = lax.ppermute(current, seq, moved(2))  4.86 us
    ppermute x1, waiting for transfers between devices, local(): last = lax.ppermute(current, seq, moved(1))  4.36 us
  transfers between devices with their start and end apart: 11, of which 2 were waited for; matrix products, arithmetic and copies ran while one was open for 1% of the time, Pallas kernels for 11%

profile of v13, /device:TPU:16, one launch (start us, length us, event | category | flops | bytes accessed | tf_op | source)
XLA Modules:
  0.0 115.5 jit_solution(16587101742355326009)
XLA Ops:
  0.6 0.0 copy-start
  0.6 6.7 %collective-permute-start.3 = (bf16[512,256]{1,0:T(8,128)(2,1)}, bf16[512,256]{1,0:T(8,128)(2,1)S(1)}, u32[]{:S(2)}, u32[]{:S(2)}) collective-permute-start(bf16[512,256]{1,0:T(8,128)(2,1)} %bitcast.33), channel_id=1, source_target_pairs={{0,3},{1,2},{2,1},{3,0},{4,7},{5,6},{6,5},{7,4},{8,11},{9,10},{10,... | collective-permute-start | bytes 786440 | tf_op jit(solution)/shard_map/ppermute | solution.py:408
  7.3 1.9 %collective-permute-start.4 = (bf16[512,256]{1,0:T(8,128)(2,1)}, bf16[512,256]{1,0:T(8,128)(2,1)S(1)}, u32[]{:S(2)}, u32[]{:S(2)}) collective-permute-start(bf16[512,256]{1,0:T(8,128)(2,1)} %bitcast.34), channel_id=1, source_target_pairs={{0,2},{1,3},{2,0},{3,1},{4,6},{5,7},{6,4},{7,5},{8,10},{9,11},{10,... | collective-permute-start | bytes 786440 | tf_op jit(solution)/shard_map/ppermute | solution.py:408
  9.2 0.0 copy-start.3
  9.3 0.0 copy-start.2
  9.3 2.0 %shard_map.113.refs_2_.refs_3_.refs_1_ = bf16[1024,256]{1,0:T(8,128)(2,1)} custom-call(bf16[512,256]{1,0:T(8,128)(2,1)} %bitcast.38, bf16[512,256]{1,0:T(8,128)(2,1)} %bitcast.39), custom_call_target="tpu_custom_call" | custom-call | tf_op jit(solution)/shard_map/pallas_call | solution.py:69
  11.3 0.0 copy-start.1
  11.3 3.3 %collective-permute-start = (bf16[1024,256]{1,0:T(8,128)(2,1)}, bf16[1024,256]{1,0:T(8,128)(2,1)S(1)}, u32[]{:S(2)}, u32[]{:S(2)}) collective-permute-start(bf16[1024,256]{1,0:T(8,128)(2,1)} %shard_map.113.refs_2_.refs_3_.refs_1_), channel_id=1, source_target_pairs={{0,4},{4,8},{8,12},{12,0},{1,5},{5,9},{9,13},{13,1},{2,6},{6,10},{... | collective-permute-start | bytes 1572872 | tf_op jit(solution)/shard_map/ppermute | solution.py:407
  14.7 2.7 %collective-permute-start.1 = (bf16[1024,256]{1,0:T(8,128)(2,1)}, bf16[1024,256]{1,0:T(8,128)(2,1)S(1)}, u32[]{:S(2)}, u32[]{:S(2)}) collective-permute-start(bf16[1024,256]{1,0:T(8,128)(2,1)} %shard_map.113.refs_2_.refs_3_.refs_1_), channel_id=1, source_target_pairs={{0,12},{4,0},{8,4},{12,8},{1,13},{5,1},{9,5},{13,9},{2,14},{6,2},{... | collective-permute-start | bytes 1572872 | tf_op jit(solution)/shard_map/ppermute | solution.py:407
  17.3 4.2 %collective-permute-start.2 = (bf16[1024,256]{1,0:T(8,128)(2,1)}, bf16[1024,256]{1,0:T(8,128)(2,1)S(1)}, u32[]{:S(2)}, u32[]{:S(2)}) collective-permute-start(bf16[1024,256]{1,0:T(8,128)(2,1)} %shard_map.113.refs_2_.refs_3_.refs_1_), channel_id=1, source_target_pairs={{0,8},{4,12},{8,0},{12,4},{1,9},{5,13},{9,1},{13,5},{2,10},{6,14},... | collective-permute-start | bytes 1572872 | tf_op jit(solution)/shard_map/ppermute | solution.py:407
  21.5 0.0 copy-done.3
  21.6 0.1 copy.16
  21.6 0.1 squeeze.26
  21.7 0.1 copy.17
  21.8 0.1 squeeze.27
  21.9 0.1 pad_maximum_fusion.refs_4_
  22.6 0.0 collective-permute-done.3.refs_0_
  22.6 0.0 copy-done.2
  22.6 6.3 %collective-permute-start.5 = (bf16[512,256]{1,0:T(8,128)(2,1)S(1)}, bf16[512,256]{1,0:T(8,128)(2,1)}, u32[]{:S(2)}, u32[]{:S(2)}) collective-permute-start(bf16[512,256]{1,0:T(8,128)(2,1)S(1)} %bitcast.35), channel_id=1, source_target_pairs={{0,1},{1,0},{2,3},{3,2},{4,5},{5,4},{6,7},{7,6},{8,9},{9,8},{10,11... | collective-permute-start | bytes 786440 | tf_op jit(solution)/shard_map/ppermute | solution.py:408
  28.9 0.1 fusion.1.count_ref
  29.8 0.0 collective-permute-done.4.refs_1_
  29.8 8.4 %collective-permute-done.refs_3_.refs_4_.refs_2_ = bf16[1024,256]{1,0:T(8,128)(2,1)S(1)} collective-permute-done((bf16[1024,256]{1,0:T(8,128)(2,1)}, bf16[1024,256]{1,0:T(8,128)(2,1)S(1)}, u32[]{:S(2)}, u32[]{:S(2)}) %collective-permute-start) | collective-permute-done | bytes 524320 | tf_op jit(solution)/shard_map/ppermute | solution.py:407
  38.2 5.0 %shard_map.114 = (f32[2,2,512]{2,1,0:T(2,128)S(1)}, f32[2,2,512]{2,1,0:T(2,128)S(1)}, f32[2,2,128,512]{3,2,1,0:T(8,128)}) custom-call(s32[4]{0:T(128)S(1)} %fusion.1.count_ref, bf16[512,256]{1,0:T(8,128)(2,1)S(1)} %collective-permute-done.3.refs_0_, bf16[512,256]{1,0:T(8,128)(2,1)S(1)} %collective-permute-done.4.refs_1_, bf16[1024,256]{1,0:T(8,128)(2,1)S(1)} %copy-done.1, ...), custom_call_target="tpu_custom_call" | custom-call | flops 1073741824 | bytes 1572864 | tf_op jit(solution)/shard_map/pallas_call | solution.py:239
  43.2 0.0 collective-permute-done.5.refs_2_
  43.2 0.0 collective-permute-done.1.refs_5_.refs_3_
  43.2 0.0 collective-permute-done.2.refs_6_.refs_4_
  43.2 8.7 %shard_map.115 = (bf16[144,512]{1,0:T(8,128)(2,1)S(1)}, bf16[144,512]{1,0:T(8,128)(2,1)S(1)}, bf16[144,512]{1,0:T(8,128)(2,1)S(1)}) custom-call(s32[4]{0:T(128)S(1)} %fusion.1.count_ref, bf16[512,256]{1,0:T(8,128)(2,1)S(1)} %collective-permute-done.3.refs_0_, bf16[512,256]{1,0:T(8,128)(2,1)S(1)} %collective-permute-done.4.refs_1_, ...), custom_call_target="tpu_custom_call" | custom-call | flops 2147483648 | bytes 2883584 | tf_op jit(solution)/shard_map/pallas_call | solution.py:239
  52.0 1.9 %collective-permute-start.6 = (bf16[144,512]{1,0:T(8,128)(2,1)S(1)}, bf16[144,512]{1,0:T(8,128)(2,1)S(1)}, u32[]{:S(2)}, u32[]{:S(2)}) collective-permute-start(bf16[144,512]{1,0:T(8,128)(2,1)S(1)} %get-tuple-element.15.refs_6_), channel_id=1, source_target_pairs={{0,3},{1,2},{2,1},{3,0},{4,7},{5,6},{6,5},{7,4},{8,11},{9,10},{10,... | collective-permute-start | bytes 442376 | tf_op jit(solution)/shard_map/ppermute | solution.py:433
  53.9 4.9 %collective-permute-start.7 = (bf16[144,512]{1,0:T(8,128)(2,1)S(1)}, bf16[144,512]{1,0:T(8,128)(2,1)S(1)}, u32[]{:S(2)}, u32[]{:S(2)}) collective-permute-start(bf16[144,512]{1,0:T(8,128)(2,1)S(1)} %get-tuple-element.16), channel_id=1, source_target_pairs={{0,2},{1,3},{2,0},{3,1},{4,6},{5,7},{6,4},{7,5},{8,10},{9,11},{10,... | collective-permute-start | bytes 442376 | tf_op jit(solution)/shard_map/ppermute | solution.py:433
  58.9 3.2 %collective-permute-start.8 = (bf16[144,512]{1,0:T(8,128)(2,1)S(1)}, bf16[144,512]{1,0:T(8,128)(2,1)S(1)}, u32[]{:S(2)}, u32[]{:S(2)}) collective-permute-start(bf16[144,512]{1,0:T(8,128)(2,1)S(1)} %get-tuple-element.17), channel_id=1, source_target_pairs={{0,1},{1,0},{2,3},{3,2},{4,5},{5,4},{6,7},{7,6},{8,9},{9,8},{10,11... | collective-permute-start | bytes 442376 | tf_op jit(solution)/shard_map/ppermute | solution.py:433
  62.1 0.1 pad_maximum_fusion.1.scale_ref
  62.2 4.5 %shard_map.116.refs_0_ = bf16[144,512]{1,0:T(8,128)(2,1)S(1)} custom-call(s32[4]{0:T(128)S(1)} %fusion.1.count_ref, bf16[512,256]{1,0:T(8,128)(2,1)S(1)} %bitcast.36, bf16[1024,256]{1,0:T(8,128)(2,1)S(1)} %copy-done.1, bf16[1024,256]{1,0:T(8,128)(2,1)S(1)} %collective-permute-done.refs_3_.refs_4_.refs_2_, ...), custom_call_target="tpu_custom_call" | custom-call | flops 1073741824 | bytes 2359296 | tf_op jit(solution)/shard_map/pallas_call | solution.py:239
  66.7 0.0 collective-permute-done.6.refs_1_
  66.7 0.0 collective-permute-done.7.refs_2_
  66.7 0.0 collective-permute-done.8.refs_3_
  66.7 0.8 shard_map.117
  67.5 30.2 %all_to_all.5 = bf16[16,32,128]{2,1,0:T(8,128)(2,1)S(1)} all-to-all(bf16[16,32,128]{2,1,0:T(8,128)(2,1)S(1)} %shard_map.117), channel_id=1, replica_groups=mesh['cfg'=2,'zh'=4,'x'=4,'y'=4,'zl'=4] {'zh','x'}, dimensions={0} | all-to-all | bytes 262144 | tf_op jit(solution)/shard_map/all_to_all | solution.py:436
  97.7 3.4 %psum.7 = f32[32,128]{1,0:T(8,128)S(1)} all-reduce(f32[32,128]{1,0:T(8,128)S(1)} %convert_reduce_fusion), channel_id=1, replica_groups=mesh['cfg'=2,'zh'=4,'x'=4,'y'=4,'zl'=4] {'cfg'}, use_global_device_ids=true, to_apply=%region_1.2 | all-reduce | flops 4096 | bytes 32768 | tf_op jit(solution)/shard_map/psum | solution.py:437
  101.1 0.1 subtract_convert_fusion._.own_ref
  101.2 4.9 %collective-permute-start.10 = (bf16[32,128]{1,0:T(8,128)(2,1)S(1)}, bf16[32,128]{1,0:T(8,128)(2,1)S(1)}, u32[]{:S(2)}, u32[]{:S(2)}) collective-permute-start(bf16[32,128]{1,0:T(8,128)(2,1)S(1)} %subtract_convert_fusion._.own_ref), channel_id=1, source_target_pairs={{0,2},{1,3},{2,4},{3,5},{4,6},{5,7},{6,8},{7,9},{8,10},{9,11},{10,... | collective-permute-start | bytes 24584 | tf_op jit(solution)/shard_map/ppermute | solution.py:441
  106.1 1.9 %collective-permute-start.9 = (bf16[32,128]{1,0:T(8,128)(2,1)S(1)}, bf16[32,128]{1,0:T(8,128)(2,1)S(1)}, u32[]{:S(2)}, u32[]{:S(2)}) collective-permute-start(bf16[32,128]{1,0:T(8,128)(2,1)S(1)} %subtract_convert_fusion._.own_ref), channel_id=1, source_target_pairs={{0,1},{1,2},{2,3},{3,4},{4,5},{5,6},{6,7},{7,8},{8,9},{9,10},{10,1... | collective-permute-start | bytes 24584 | tf_op jit(solution)/shard_map/ppermute | solution.py:440
  108.0 0.1 dynamic-slice
  108.1 0.1 reshape.37
  108.2 0.7 copy.19
  108.9 1.1 shard_map.118
  109.9 0.0 collective-permute-done.10.older_ref
  109.9 4.4 %collective-permute-done.9.last_ref = bf16[32,128]{1,0:T(8,128)(2,1)S(1)} collective-permute-done((bf16[32,128]{1,0:T(8,128)(2,1)S(1)}, bf16[32,128]{1,0:T(8,128)(2,1)S(1)}, u32[]{:S(2)}, u32[]{:S(2)}) %collective-permute-start.9) | collective-permute-done | bytes 8224 | tf_op jit(solution)/shard_map/ppermute | solution.py:440
  114.3 1.2 %shard_map.119 = bf16[2,32,384]{2,1,0:T(8,128)(2,1)} custom-call(s32[1]{0:T(128)} %bitcast.18.half_ref, bf16[32,128]{1,0:T(8,128)(2,1)S(1)} %subtract_convert_fusion._.own_ref, bf16[32,128]{1,0:T(8,128)(2,1)S(1)} %collective-permute-done.9.last_ref, bf16[32,128]{1,0:T(8,128)(2,1)S(1)} %collective-permute-done.10.older_ref, ...), custom_call_target="tpu_custom_call" | custom-call | tf_op jit(solution)/shard_map/pallas_call | solution.py:390
  (7 shorter events, 0.1 us)
Async XLA Ops:
  0.6 29.1 %copy-start = (bf16[4096,64]{0,1:T(8,128)(2,1)S(1)}, bf16[4096,64]{0,1:T(8,128)(2,1)}, u32[]{:S(2)}) copy-start(bf16[4096,64]{0,1:T(8,128)(2,1)} %param.16) | copy-start | bytes 1572868
  0.6 22.0 %collective-permute-start.3 = (bf16[512,256]{1,0:T(8,128)(2,1)}, bf16[512,256]{1,0:T(8,128)(2,1)S(1)}, u32[]{:S(2)}, u32[]{:S(2)}) collective-permute-start(bf16[512,256]{1,0:T(8,128)(2,1)} %bitcast.33), channel_id=1, source_target_pairs={{0,3},{1,2},{2,1},{3,0},{4,7},{5,6},{6,5},{7,4},{8,11},{9,10},{10,... | collective-permute-start | bytes 786440 | tf_op jit(solution)/shard_map/ppermute | solution.py:408
  7.3 22.5 %collective-permute-start.4 = (bf16[512,256]{1,0:T(8,128)(2,1)}, bf16[512,256]{1,0:T(8,128)(2,1)S(1)}, u32[]{:S(2)}, u32[]{:S(2)}) collective-permute-start(bf16[512,256]{1,0:T(8,128)(2,1)} %bitcast.34), channel_id=1, source_target_pairs={{0,2},{1,3},{2,0},{3,1},{4,6},{5,7},{6,4},{7,5},{8,10},{9,11},{10,... | collective-permute-start | bytes 786440 | tf_op jit(solution)/shard_map/ppermute | solution.py:408
  9.2 12.3 %copy-start.3 = (f32[1,2,64,16]{2,3,1,0:T(8,128)S(1)}, f32[1,2,64,16]{2,3,1,0:T(8,128)}, u32[]{:S(2)}) copy-start(f32[1,2,64,16]{2,3,1,0:T(8,128)} %param.15) | copy-start | bytes 24580
  9.3 13.4 %copy-start.2 = (bf16[1,512,256]{2,1,0:T(8,128)(2,1)S(1)}, bf16[1,512,256]{2,1,0:T(8,128)(2,1)}, u32[]{:S(2)}) copy-start(bf16[1,512,256]{2,1,0:T(8,128)(2,1)} %param.10) | copy-start | bytes 786436
  11.3 26.9 %copy-start.1 = (bf16[1024,256]{1,0:T(8,128)(2,1)S(1)}, bf16[1024,256]{1,0:T(8,128)(2,1)}, u32[]{:S(2)}) copy-start(bf16[1024,256]{1,0:T(8,128)(2,1)} %shard_map.113.refs_2_.refs_3_.refs_1_) | copy-start | bytes 1572868
  11.3 26.9 %collective-permute-start = (bf16[1024,256]{1,0:T(8,128)(2,1)}, bf16[1024,256]{1,0:T(8,128)(2,1)S(1)}, u32[]{:S(2)}, u32[]{:S(2)}) collective-permute-start(bf16[1024,256]{1,0:T(8,128)(2,1)} %shard_map.113.refs_2_.refs_3_.refs_1_), channel_id=1, source_target_pairs={{0,4},{4,8},{8,12},{12,0},{1,5},{5,9},{9,13},{13,1},{2,6},{6,10},{... | collective-permute-start | bytes 1572872 | tf_op jit(solution)/shard_map/ppermute | solution.py:407
  14.7 28.6 %collective-permute-start.1 = (bf16[1024,256]{1,0:T(8,128)(2,1)}, bf16[1024,256]{1,0:T(8,128)(2,1)S(1)}, u32[]{:S(2)}, u32[]{:S(2)}) collective-permute-start(bf16[1024,256]{1,0:T(8,128)(2,1)} %shard_map.113.refs_2_.refs_3_.refs_1_), channel_id=1, source_target_pairs={{0,12},{4,0},{8,4},{12,8},{1,13},{5,1},{9,5},{13,9},{2,14},{6,2},{... | collective-permute-start | bytes 1572872 | tf_op jit(solution)/shard_map/ppermute | solution.py:407
  17.3 25.9 %collective-permute-start.2 = (bf16[1024,256]{1,0:T(8,128)(2,1)}, bf16[1024,256]{1,0:T(8,128)(2,1)S(1)}, u32[]{:S(2)}, u32[]{:S(2)}) collective-permute-start(bf16[1024,256]{1,0:T(8,128)(2,1)} %shard_map.113.refs_2_.refs_3_.refs_1_), channel_id=1, source_target_pairs={{0,8},{4,12},{8,0},{12,4},{1,9},{5,13},{9,1},{13,5},{2,10},{6,14},... | collective-permute-start | bytes 1572872 | tf_op jit(solution)/shard_map/ppermute | solution.py:407
  22.6 20.6 %collective-permute-start.5 = (bf16[512,256]{1,0:T(8,128)(2,1)S(1)}, bf16[512,256]{1,0:T(8,128)(2,1)}, u32[]{:S(2)}, u32[]{:S(2)}) collective-permute-start(bf16[512,256]{1,0:T(8,128)(2,1)S(1)} %bitcast.35), channel_id=1, source_target_pairs={{0,1},{1,0},{2,3},{3,2},{4,5},{5,4},{6,7},{7,6},{8,9},{9,8},{10,11... | collective-permute-start | bytes 786440 | tf_op jit(solution)/shard_map/ppermute | solution.py:408
  52.0 14.7 %collective-permute-start.6 = (bf16[144,512]{1,0:T(8,128)(2,1)S(1)}, bf16[144,512]{1,0:T(8,128)(2,1)S(1)}, u32[]{:S(2)}, u32[]{:S(2)}) collective-permute-start(bf16[144,512]{1,0:T(8,128)(2,1)S(1)} %get-tuple-element.15.refs_6_), channel_id=1, source_target_pairs={{0,3},{1,2},{2,1},{3,0},{4,7},{5,6},{6,5},{7,4},{8,11},{9,10},{10,... | collective-permute-start | bytes 442376 | tf_op jit(solution)/shard_map/ppermute | solution.py:433
  53.9 12.8 %collective-permute-start.7 = (bf16[144,512]{1,0:T(8,128)(2,1)S(1)}, bf16[144,512]{1,0:T(8,128)(2,1)S(1)}, u32[]{:S(2)}, u32[]{:S(2)}) collective-permute-start(bf16[144,512]{1,0:T(8,128)(2,1)S(1)} %get-tuple-element.16), channel_id=1, source_target_pairs={{0,2},{1,3},{2,0},{3,1},{4,6},{5,7},{6,4},{7,5},{8,10},{9,11},{10,... | collective-permute-start | bytes 442376 | tf_op jit(solution)/shard_map/ppermute | solution.py:433
  58.9 7.8 %collective-permute-start.8 = (bf16[144,512]{1,0:T(8,128)(2,1)S(1)}, bf16[144,512]{1,0:T(8,128)(2,1)S(1)}, u32[]{:S(2)}, u32[]{:S(2)}) collective-permute-start(bf16[144,512]{1,0:T(8,128)(2,1)S(1)} %get-tuple-element.17), channel_id=1, source_target_pairs={{0,1},{1,0},{2,3},{3,2},{4,5},{5,4},{6,7},{7,6},{8,9},{9,8},{10,11... | collective-permute-start | bytes 442376 | tf_op jit(solution)/shard_map/ppermute | solution.py:433
  101.2 8.7 %collective-permute-start.10 = (bf16[32,128]{1,0:T(8,128)(2,1)S(1)}, bf16[32,128]{1,0:T(8,128)(2,1)S(1)}, u32[]{:S(2)}, u32[]{:S(2)}) collective-permute-start(bf16[32,128]{1,0:T(8,128)(2,1)S(1)} %subtract_convert_fusion._.own_ref), channel_id=1, source_target_pairs={{0,2},{1,3},{2,4},{3,5},{4,6},{5,7},{6,8},{7,9},{8,10},{9,11},{10,... | collective-permute-start | bytes 24584 | tf_op jit(solution)/shard_map/ppermute | solution.py:441
  106.1 8.2 %collective-permute-start.9 = (bf16[32,128]{1,0:T(8,128)(2,1)S(1)}, bf16[32,128]{1,0:T(8,128)(2,1)S(1)}, u32[]{:S(2)}, u32[]{:S(2)}) collective-permute-start(bf16[32,128]{1,0:T(8,128)(2,1)S(1)} %subtract_convert_fusion._.own_ref), channel_id=1, source_target_pairs={{0,1},{1,2},{2,3},{3,4},{4,5},{5,6},{6,7},{7,8},{8,9},{9,10},{10,1... | collective-permute-start | bytes 24584 | tf_op jit(solution)/shard_map/ppermute | solution.py:440

commit v14 on v12

--- a/solution.py
+++ b/solution.py
@@ -386,7 +386,8 @@
     ]
     shares = combine(scale, place, chunks, grid)
     shares = lax.all_to_all(shares, ("zh", "x"), 0, 0, tiled=True)
-    window = lax.psum(jnp.sum(shares.astype(jnp.float32), 0), "cfg")
+    window = jnp.sum(shares.astype(jnp.float32), 0)
+    window += lax.ppermute(window, "cfg", [(0, 1), (1, 0)])
 
     current = (grid - sigma * window).astype(jnp.bfloat16)
     last = lax.ppermute(current, seq, moved(1))

time: 114 us -> 113 us (level)
  blocking collectives: 33.9 us -> 30.5 us
  starting transfers between devices: 39.8 us -> 41.8 us
    psum x1 -> x0, blocking collectives: 3.36 us -> none  [local(): window = lax.psum(jnp.sum(shares.astype(jnp.float32), 0), 'cfg')]
    ppermute x1, waiting for transfers between devices: 2.17 us -> 0.01 us  [local(): last = lax.ppermute(current, seq, moved(1))]
    ppermute x0 -> x1, starting transfers between devices: none -> 1.92 us  [local(): window += lax.ppermute(window, 'cfg', [(0, 1), (1, 0)])]
    ppermute x1, starting transfers between devices: 4.1 us -> 2.2 us  [local(): last = lax.ppermute(current, seq, moved(1))]
    ppermute x1, starting transfers between devices: 2.46 us -> 4.36 us  [local(): older = lax.ppermute(current, seq, moved(2))]
    ppermute x0 -> x1, waiting for transfers between devices: none -> 1.15 us  [local(): window += lax.ppermute(window, 'cfg', [(0, 1), (1, 0)])]
  transfers between devices with their start and end apart: 11 -> 12, of which waited for: 6 -> 7; matrix products, arithmetic and copies ran while one was open for 1% -> 1% of each run, Pallas kernels for 7% -> 7%
where the time goes in v14:
time: 113 us; the launch traced here: 111 us
  starting transfers between devices  41.8 us (37%)
  blocking collectives  30.5 us (27%)
  Pallas kernels  20.7 us (18%)
  waiting for transfers between devices  14.6 us (13%)
  between operations  2.35 us (2%)
  local copies, waits for them, and re-layouts  1.22 us (1%)
    all_to_all x1, blocking collectives, local(): shares = lax.all_to_all(shares, ('zh', 'x'), 0, 0, tiled=True)  30.5 us
    pallas_call x2, Pallas kernels, attend(): pl.pallas_call(functools.partial(attention_kernel, nq=nq, nk=nk, nx=len(e...  15.7 us
    ppermute x3, starting transfers between devices, local(): lax.ppermute(query[0], 'zl', crossed(m))  14.1 us
    ppermute x3, starting transfers between devices, local(): lax.ppermute(chunk, 'zl', crossed(m))  10.1 us
    ppermute x3, starting transfers between devices, local(): blocks = [own] + [lax.ppermute(own, 'y', ring(d)) for d in (1, 3, 2)]  9.12 us
    ppermute x3, waiting for transfers between devices, local(): lax.ppermute(query[0], 'zl', crossed(m))  7.49 us
    ppermute x1, starting transfers between devices, local(): older = lax.ppermute(current, seq, moved(2))  4.36 us
    ppermute x3, waiting for transfers between devices, local(): blocks = [own] + [lax.ppermute(own, 'y', ring(d)) for d in (1, 3, 2)]  3.95 us
  transfers between devices with their start and end apart: 12, of which 7 were waited for; matrix products, arithmetic and copies ran while one was open for 1% of the time, Pallas kernels for 7%

profile of v14, /device:TPU:24, one launch (start us, length us, event | category | flops | bytes accessed | tf_op | source)
XLA Modules:
  0.0 111.5 jit_solution(16152363494507813034)
XLA Ops:
  0.6 0.0 copy-start
  0.6 6.7 %collective-permute-start.3 = (bf16[512,256]{1,0:T(8,128)(2,1)}, bf16[512,256]{1,0:T(8,128)(2,1)S(1)}, u32[]{:S(2)}, u32[]{:S(2)}) collective-permute-start(bf16[512,256]{1,0:T(8,128)(2,1)} %bitcast.33), channel_id=1, source_target_pairs={{0,3},{1,2},{2,1},{3,0},{4,7},{5,6},{6,5},{7,4},{8,11},{9,10},{10,... | collective-permute-start | bytes 786440 | tf_op jit(solution)/shard_map/ppermute | solution.py:363
  7.3 0.0 copy-start.2
  7.3 0.0 copy-start.3
  7.3 2.0 %shard_map.113.refs_3_.refs_1_ = bf16[1024,256]{1,0:T(8,128)(2,1)} custom-call(bf16[512,256]{1,0:T(8,128)(2,1)} %bitcast.38, bf16[512,256]{1,0:T(8,128)(2,1)} %bitcast.39), custom_call_target="tpu_custom_call" | custom-call | tf_op jit(solution)/shard_map/pallas_call | solution.py:69
  9.3 0.0 copy-start.1
  9.4 3.0 %collective-permute-start = (bf16[1024,256]{1,0:T(8,128)(2,1)}, bf16[1024,256]{1,0:T(8,128)(2,1)S(1)}, u32[]{:S(2)}, u32[]{:S(2)}) collective-permute-start(bf16[1024,256]{1,0:T(8,128)(2,1)} %shard_map.113.refs_3_.refs_1_), channel_id=1, source_target_pairs={{0,4},{4,8},{8,12},{12,0},{1,5},{5,9},{9,13},{13,1},{2,6},{6,10},{... | collective-permute-start | bytes 1572872 | tf_op jit(solution)/shard_map/ppermute | solution.py:362
  12.4 3.0 %collective-permute-start.1 = (bf16[1024,256]{1,0:T(8,128)(2,1)}, bf16[1024,256]{1,0:T(8,128)(2,1)S(1)}, u32[]{:S(2)}, u32[]{:S(2)}) collective-permute-start(bf16[1024,256]{1,0:T(8,128)(2,1)} %shard_map.113.refs_3_.refs_1_), channel_id=1, source_target_pairs={{0,12},{4,0},{8,4},{12,8},{1,13},{5,1},{9,5},{13,9},{2,14},{6,2},{... | collective-permute-start | bytes 1572872 | tf_op jit(solution)/shard_map/ppermute | solution.py:362
  15.3 3.1 %collective-permute-start.2 = (bf16[1024,256]{1,0:T(8,128)(2,1)}, bf16[1024,256]{1,0:T(8,128)(2,1)S(1)}, u32[]{:S(2)}, u32[]{:S(2)}) collective-permute-start(bf16[1024,256]{1,0:T(8,128)(2,1)} %shard_map.113.refs_3_.refs_1_), channel_id=1, source_target_pairs={{0,8},{4,12},{8,0},{12,4},{1,9},{5,13},{9,1},{13,5},{2,10},{6,14},... | collective-permute-start | bytes 1572872 | tf_op jit(solution)/shard_map/ppermute | solution.py:362
  18.5 0.0 copy-done.2
  18.5 1.9 %collective-permute-start.4 = (bf16[512,256]{1,0:T(8,128)(2,1)S(1)}, bf16[512,256]{1,0:T(8,128)(2,1)S(1)}, u32[]{:S(2)}, u32[]{:S(2)}) collective-permute-start(bf16[512,256]{1,0:T(8,128)(2,1)S(1)} %bitcast.34), channel_id=1, source_target_pairs={{0,2},{1,3},{2,0},{3,1},{4,6},{5,7},{6,4},{7,5},{8,10},{9,11},{10,... | collective-permute-start | bytes 786440 | tf_op jit(solution)/shard_map/ppermute | solution.py:363
  21.1 0.0 copy-done.3
  21.2 0.0 collective-permute-done.3.refs_0_
  21.2 5.5 %collective-permute-start.5 = (bf16[512,256]{1,0:T(8,128)(2,1)S(1)}, bf16[512,256]{1,0:T(8,128)(2,1)}, u32[]{:S(2)}, u32[]{:S(2)}) collective-permute-start(bf16[512,256]{1,0:T(8,128)(2,1)S(1)} %bitcast.35), channel_id=1, source_target_pairs={{0,1},{1,0},{2,3},{3,2},{4,5},{5,4},{6,7},{7,6},{8,9},{9,8},{10,11... | collective-permute-start | bytes 786440 | tf_op jit(solution)/shard_map/ppermute | solution.py:363
  26.7 0.1 fusion.1.count_ref
  27.5 0.1 copy.16
  27.6 0.1 squeeze.26
  27.6 0.1 copy.17
  27.7 0.1 squeeze.27
  27.8 0.1 pad_maximum_fusion.refs_4_
  27.9 4.7 %collective-permute-done.4.refs_1_ = bf16[512,256]{1,0:T(8,128)(2,1)S(1)} collective-permute-done((bf16[512,256]{1,0:T(8,128)(2,1)S(1)}, bf16[512,256]{1,0:T(8,128)(2,1)S(1)}, u32[]{:S(2)}, u32[]{:S(2)}) %collective-permute-start.4) | collective-permute-done | bytes 262176 | tf_op jit(solution)/shard_map/ppermute | solution.py:363
  32.6 2.8 %collective-permute-done.5.refs_2_ = bf16[512,256]{1,0:T(8,128)(2,1)} collective-permute-done((bf16[512,256]{1,0:T(8,128)(2,1)S(1)}, bf16[512,256]{1,0:T(8,128)(2,1)}, u32[]{:S(2)}, u32[]{:S(2)}) %collective-permute-start.5) | collective-permute-done | bytes 262176 | tf_op jit(solution)/shard_map/ppermute | solution.py:363
  35.4 0.0 collective-permute-done.refs_4_.refs_2_
  35.4 3.9 %collective-permute-done.1.refs_5_.refs_3_ = bf16[1024,256]{1,0:T(8,128)(2,1)S(1)} collective-permute-done((bf16[1024,256]{1,0:T(8,128)(2,1)}, bf16[1024,256]{1,0:T(8,128)(2,1)S(1)}, u32[]{:S(2)}, u32[]{:S(2)}) %collective-permute-start.1) | collective-permute-done | bytes 524320 | tf_op jit(solution)/shard_map/ppermute | solution.py:362
  39.3 0.0 collective-permute-done.2.refs_6_.refs_4_
  39.4 11.2 %shard_map.114 = (bf16[144,512]{1,0:T(8,128)(2,1)S(1)}, bf16[144,512]{1,0:T(8,128)(2,1)S(1)}, bf16[144,512]{1,0:T(8,128)(2,1)S(1)}) custom-call(s32[4]{0:T(128)S(1)} %fusion.1.count_ref, bf16[512,256]{1,0:T(8,128)(2,1)S(1)} %collective-permute-done.3.refs_0_, bf16[512,256]{1,0:T(8,128)(2,1)S(1)} %collective-permute-done.4.refs_1_, ...), custom_call_target="tpu_custom_call" | custom-call | flops 3221225472 | bytes 2883584 | tf_op jit(solution)/shard_map/pallas_call | solution.py:204
  50.6 2.9 %collective-permute-start.6 = (bf16[144,512]{1,0:T(8,128)(2,1)S(1)}, bf16[144,512]{1,0:T(8,128)(2,1)S(1)}, u32[]{:S(2)}, u32[]{:S(2)}) collective-permute-start(bf16[144,512]{1,0:T(8,128)(2,1)S(1)} %get-tuple-element.9.refs_6_), channel_id=1, source_target_pairs={{0,3},{1,2},{2,1},{3,0},{4,7},{5,6},{6,5},{7,4},{8,11},{9,10},{10,... | collective-permute-start | bytes 442376 | tf_op jit(solution)/shard_map/ppermute | solution.py:385
  53.5 1.9 %collective-permute-start.7 = (bf16[144,512]{1,0:T(8,128)(2,1)S(1)}, bf16[144,512]{1,0:T(8,128)(2,1)S(1)}, u32[]{:S(2)}, u32[]{:S(2)}) collective-permute-start(bf16[144,512]{1,0:T(8,128)(2,1)S(1)} %get-tuple-element.10), channel_id=1, source_target_pairs={{0,2},{1,3},{2,0},{3,1},{4,6},{5,7},{6,4},{7,5},{8,10},{9,11},{10,... | collective-permute-start | bytes 442376 | tf_op jit(solution)/shard_map/ppermute | solution.py:385
  55.4 5.3 %collective-permute-start.8 = (bf16[144,512]{1,0:T(8,128)(2,1)S(1)}, bf16[144,512]{1,0:T(8,128)(2,1)S(1)}, u32[]{:S(2)}, u32[]{:S(2)}) collective-permute-start(bf16[144,512]{1,0:T(8,128)(2,1)S(1)} %get-tuple-element.11), channel_id=1, source_target_pairs={{0,1},{1,0},{2,3},{3,2},{4,5},{5,4},{6,7},{7,6},{8,9},{9,8},{10,11... | collective-permute-start | bytes 442376 | tf_op jit(solution)/shard_map/ppermute | solution.py:385
  60.7 0.1 pad_maximum_fusion.1.scale_ref
  60.8 4.5 %shard_map.115.refs_0_ = bf16[144,512]{1,0:T(8,128)(2,1)S(1)} custom-call(s32[4]{0:T(128)S(1)} %fusion.1.count_ref, bf16[512,256]{1,0:T(8,128)(2,1)S(1)} %bitcast.36, bf16[1024,256]{1,0:T(8,128)(2,1)S(1)} %copy-done.1, bf16[1024,256]{1,0:T(8,128)(2,1)S(1)} %collective-permute-done.refs_4_.refs_2_, ...), custom_call_target="tpu_custom_call" | custom-call | flops 1073741824 | bytes 2359296 | tf_op jit(solution)/shard_map/pallas_call | solution.py:204
  65.3 0.0 collective-permute-done.6.refs_1_
  65.3 0.6 collective-permute-done.7.refs_2_
  65.9 0.4 collective-permute-done.8.refs_3_
  66.3 0.8 shard_map.116
  67.1 30.5 %all_to_all.5 = bf16[16,32,128]{2,1,0:T(8,128)(2,1)S(1)} all-to-all(bf16[16,32,128]{2,1,0:T(8,128)(2,1)S(1)} %shard_map.116), channel_id=1, replica_groups=mesh['cfg'=2,'zh'=4,'x'=4,'y'=4,'zl'=4] {'zh','x'}, dimensions={0} | all-to-all | bytes 262144 | tf_op jit(solution)/shard_map/all_to_all | solution.py:388
  97.6 1.9 %collective-permute-start.9 = (f32[32,128]{1,0:T(8,128)S(1)}, f32[32,128]{1,0:T(8,128)S(1)}, u32[]{:S(2)}, u32[]{:S(2)}) collective-permute-start(f32[32,128]{1,0:T(8,128)S(1)} %convert_reduce_fusion), channel_id=1, source_target_pairs={{0,256},{256,0},{1,257},{257,1},{2,258},{258,2},{3,259},{259,3},{4... | collective-permute-start | bytes 49160 | tf_op jit(solution)/shard_map/ppermute | solution.py:390
  99.5 1.1 %collective-permute-done.9 = f32[32,128]{1,0:T(8,128)S(1)} collective-permute-done((f32[32,128]{1,0:T(8,128)S(1)}, f32[32,128]{1,0:T(8,128)S(1)}, u32[]{:S(2)}, u32[]{:S(2)}) %collective-permute-start.9) | collective-permute-done | bytes 16416 | tf_op jit(solution)/shard_map/ppermute | solution.py:390
  100.7 0.1 subtract_convert_fusion
  100.7 2.2 %collective-permute-start.10 = (bf16[32,128]{1,0:T(8,128)(2,1)S(1)}, bf16[32,128]{1,0:T(8,128)(2,1)S(1)}, u32[]{:S(2)}, u32[]{:S(2)}) collective-permute-start(bf16[32,128]{1,0:T(8,128)(2,1)S(1)} %get-tuple-element.18._.own_ref), channel_id=1, source_target_pairs={{0,1},{1,2},{2,3},{3,4},{4,5},{5,6},{6,7},{7,8},{8,9},{9,10},{10,1... | collective-permute-start | bytes 24584 | tf_op jit(solution)/shard_map/ppermute | solution.py:393
  103.0 4.4 %collective-permute-start.11 = (bf16[32,128]{1,0:T(8,128)(2,1)S(1)}, bf16[32,128]{1,0:T(8,128)(2,1)S(1)}, u32[]{:S(2)}, u32[]{:S(2)}) collective-permute-start(bf16[32,128]{1,0:T(8,128)(2,1)S(1)} %get-tuple-element.18._.own_ref), channel_id=1, source_target_pairs={{0,2},{1,3},{2,4},{3,5},{4,6},{5,7},{6,8},{7,9},{8,10},{9,11},{10,... | collective-permute-start | bytes 24584 | tf_op jit(solution)/shard_map/ppermute | solution.py:394
  107.3 0.1 dynamic-slice
  107.4 0.1 reshape.37
  107.5 0.7 copy.19
  108.2 1.1 shard_map.117
  109.3 0.0 collective-permute-done.10.last_ref
  109.3 1.0 collective-permute-done.11.older_ref
  110.3 1.2 %shard_map.118 = bf16[2,32,384]{2,1,0:T(8,128)(2,1)} custom-call(s32[1]{0:T(128)} %bitcast.18.half_ref, bf16[32,128]{1,0:T(8,128)(2,1)S(1)} %get-tuple-element.18._.own_ref, bf16[32,128]{1,0:T(8,128)(2,1)S(1)} %collective-permute-done.10.last_ref, bf16[32,128]{1,0:T(8,128)(2,1)S(1)} %collective-permute-done.11.older_ref, ...), custom_call_target="tpu_custom_call" | custom-call | tf_op jit(solution)/shard_map/pallas_call | solution.py:345
  (7 shorter events, 0.1 us)
Async XLA Ops:
  0.6 27.3 %copy-start = (bf16[4096,64]{0,1:T(8,128)(2,1)S(1)}, bf16[4096,64]{0,1:T(8,128)(2,1)}, u32[]{:S(2)}) copy-start(bf16[4096,64]{0,1:T(8,128)(2,1)} %param.16) | copy-start | bytes 1572868
  0.6 20.5 %collective-permute-start.3 = (bf16[512,256]{1,0:T(8,128)(2,1)}, bf16[512,256]{1,0:T(8,128)(2,1)S(1)}, u32[]{:S(2)}, u32[]{:S(2)}) collective-permute-start(bf16[512,256]{1,0:T(8,128)(2,1)} %bitcast.33), channel_id=1, source_target_pairs={{0,3},{1,2},{2,1},{3,0},{4,7},{5,6},{6,5},{7,4},{8,11},{9,10},{10,... | collective-permute-start | bytes 786440 | tf_op jit(solution)/shard_map/ppermute | solution.py:363
  7.3 11.2 %copy-start.2 = (bf16[1,512,256]{2,1,0:T(8,128)(2,1)S(1)}, bf16[1,512,256]{2,1,0:T(8,128)(2,1)}, u32[]{:S(2)}) copy-start(bf16[1,512,256]{2,1,0:T(8,128)(2,1)} %param.10) | copy-start | bytes 786436
  7.3 13.8 %copy-start.3 = (f32[1,2,64,16]{2,3,1,0:T(8,128)S(1)}, f32[1,2,64,16]{2,3,1,0:T(8,128)}, u32[]{:S(2)}) copy-start(f32[1,2,64,16]{2,3,1,0:T(8,128)} %param.15) | copy-start | bytes 24580
  9.3 30.0 %copy-start.1 = (bf16[1024,256]{1,0:T(8,128)(2,1)S(1)}, bf16[1024,256]{1,0:T(8,128)(2,1)}, u32[]{:S(2)}) copy-start(bf16[1024,256]{1,0:T(8,128)(2,1)} %shard_map.113.refs_3_.refs_1_) | copy-start | bytes 1572868
  9.4 26.0 %collective-permute-start = (bf16[1024,256]{1,0:T(8,128)(2,1)}, bf16[1024,256]{1,0:T(8,128)(2,1)S(1)}, u32[]{:S(2)}, u32[]{:S(2)}) collective-permute-start(bf16[1024,256]{1,0:T(8,128)(2,1)} %shard_map.113.refs_3_.refs_1_), channel_id=1, source_target_pairs={{0,4},{4,8},{8,12},{12,0},{1,5},{5,9},{9,13},{13,1},{2,6},{6,10},{... | collective-permute-start | bytes 1572872 | tf_op jit(solution)/shard_map/ppermute | solution.py:362
  12.4 27.0 %collective-permute-start.1 = (bf16[1024,256]{1,0:T(8,128)(2,1)}, bf16[1024,256]{1,0:T(8,128)(2,1)S(1)}, u32[]{:S(2)}, u32[]{:S(2)}) collective-permute-start(bf16[1024,256]{1,0:T(8,128)(2,1)} %shard_map.113.refs_3_.refs_1_), channel_id=1, source_target_pairs={{0,12},{4,0},{8,4},{12,8},{1,13},{5,1},{9,5},{13,9},{2,14},{6,2},{... | collective-permute-start | bytes 1572872 | tf_op jit(solution)/shard_map/ppermute | solution.py:362
  15.3 24.0 %collective-permute-start.2 = (bf16[1024,256]{1,0:T(8,128)(2,1)}, bf16[1024,256]{1,0:T(8,128)(2,1)S(1)}, u32[]{:S(2)}, u32[]{:S(2)}) collective-permute-start(bf16[1024,256]{1,0:T(8,128)(2,1)} %shard_map.113.refs_3_.refs_1_), channel_id=1, source_target_pairs={{0,8},{4,12},{8,0},{12,4},{1,9},{5,13},{9,1},{13,5},{2,10},{6,14},... | collective-permute-start | bytes 1572872 | tf_op jit(solution)/shard_map/ppermute | solution.py:362
  18.5 14.1 %collective-permute-start.4 = (bf16[512,256]{1,0:T(8,128)(2,1)S(1)}, bf16[512,256]{1,0:T(8,128)(2,1)S(1)}, u32[]{:S(2)}, u32[]{:S(2)}) collective-permute-start(bf16[512,256]{1,0:T(8,128)(2,1)S(1)} %bitcast.34), channel_id=1, source_target_pairs={{0,2},{1,3},{2,0},{3,1},{4,6},{5,7},{6,4},{7,5},{8,10},{9,11},{10,... | collective-permute-start | bytes 786440 | tf_op jit(solution)/shard_map/ppermute | solution.py:363
  21.2 14.2 %collective-permute-start.5 = (bf16[512,256]{1,0:T(8,128)(2,1)S(1)}, bf16[512,256]{1,0:T(8,128)(2,1)}, u32[]{:S(2)}, u32[]{:S(2)}) collective-permute-start(bf16[512,256]{1,0:T(8,128)(2,1)S(1)} %bitcast.35), channel_id=1, source_target_pairs={{0,1},{1,0},{2,3},{3,2},{4,5},{5,4},{6,7},{7,6},{8,9},{9,8},{10,11... | collective-permute-start | bytes 786440 | tf_op jit(solution)/shard_map/ppermute | solution.py:363
  50.6 14.7 %collective-permute-start.6 = (bf16[144,512]{1,0:T(8,128)(2,1)S(1)}, bf16[144,512]{1,0:T(8,128)(2,1)S(1)}, u32[]{:S(2)}, u32[]{:S(2)}) collective-permute-start(bf16[144,512]{1,0:T(8,128)(2,1)S(1)} %get-tuple-element.9.refs_6_), channel_id=1, source_target_pairs={{0,3},{1,2},{2,1},{3,0},{4,7},{5,6},{6,5},{7,4},{8,11},{9,10},{10,... | collective-permute-start | bytes 442376 | tf_op jit(solution)/shard_map/ppermute | solution.py:385
  53.5 12.4 %collective-permute-start.7 = (bf16[144,512]{1,0:T(8,128)(2,1)S(1)}, bf16[144,512]{1,0:T(8,128)(2,1)S(1)}, u32[]{:S(2)}, u32[]{:S(2)}) collective-permute-start(bf16[144,512]{1,0:T(8,128)(2,1)S(1)} %get-tuple-element.10), channel_id=1, source_target_pairs={{0,2},{1,3},{2,0},{3,1},{4,6},{5,7},{6,4},{7,5},{8,10},{9,11},{10,... | collective-permute-start | bytes 442376 | tf_op jit(solution)/shard_map/ppermute | solution.py:385
  55.4 10.9 %collective-permute-start.8 = (bf16[144,512]{1,0:T(8,128)(2,1)S(1)}, bf16[144,512]{1,0:T(8,128)(2,1)S(1)}, u32[]{:S(2)}, u32[]{:S(2)}) collective-permute-start(bf16[144,512]{1,0:T(8,128)(2,1)S(1)} %get-tuple-element.11), channel_id=1, source_target_pairs={{0,1},{1,0},{2,3},{3,2},{4,5},{5,4},{6,7},{7,6},{8,9},{9,8},{10,11... | collective-permute-start | bytes 442376 | tf_op jit(solution)/shard_map/ppermute | solution.py:385
  97.6 3.1 %collective-permute-start.9 = (f32[32,128]{1,0:T(8,128)S(1)}, f32[32,128]{1,0:T(8,128)S(1)}, u32[]{:S(2)}, u32[]{:S(2)}) collective-permute-start(f32[32,128]{1,0:T(8,128)S(1)} %convert_reduce_fusion), channel_id=1, source_target_pairs={{0,256},{256,0},{1,257},{257,1},{2,258},{258,2},{3,259},{259,3},{4... | collective-permute-start | bytes 49160 | tf_op jit(solution)/shard_map/ppermute | solution.py:390
  100.7 8.5 %collective-permute-start.10 = (bf16[32,128]{1,0:T(8,128)(2,1)S(1)}, bf16[32,128]{1,0:T(8,128)(2,1)S(1)}, u32[]{:S(2)}, u32[]{:S(2)}) collective-permute-start(bf16[32,128]{1,0:T(8,128)(2,1)S(1)} %get-tuple-element.18._.own_ref), channel_id=1, source_target_pairs={{0,1},{1,2},{2,3},{3,4},{4,5},{5,6},{6,7},{7,8},{8,9},{9,10},{10,1... | collective-permute-start | bytes 24584 | tf_op jit(solution)/shard_map/ppermute | solution.py:393
  103.0 7.3 %collective-permute-start.11 = (bf16[32,128]{1,0:T(8,128)(2,1)S(1)}, bf16[32,128]{1,0:T(8,128)(2,1)S(1)}, u32[]{:S(2)}, u32[]{:S(2)}) collective-permute-start(bf16[32,128]{1,0:T(8,128)(2,1)S(1)} %get-tuple-element.18._.own_ref), channel_id=1, source_target_pairs={{0,2},{1,3},{2,4},{3,5},{4,6},{5,7},{6,8},{7,9},{8,10},{9,11},{10,... | collective-permute-start | bytes 24584 | tf_op jit(solution)/shard_map/ppermute | solution.py:394
